TPU v7x, 512 devices: a whole 4x4x16 slice. The times are simulated.
512 devices in a mesh: frame: 32 (over x_lo, z), atom: 16 (over y, x_hi, core).
Axes of the slice: x: 4 (x_hi: 2, x_lo: 2; x = x_hi * 2 + x_lo), y: 4, z: 16, core: 2. Of those that a mesh axis runs over, the one named last changes fastest.
Arguments:
- coords: float32 [3, 1536, 8192], P(None, 'frame', 'atom'), may hold values from -45 to 45
- weights: int32 [8192], P('atom'), may hold values from 1 to 32
Outputs:
- msd: float32 [1536, 1536], P('frame', 'atom')
All inputs are finite; a program needn't handle non-finite values.
Results may differ from a plain program's by a relative error of at most 0.0003.
Values sent between devices are 32-bit elements; how exact they have to be, the bound alone decides.
No kernel may reach another device: no remote copies, remote signals or barrier semaphores. Data moves between devices by JAX's collectives and lax.ppermute only.
A program may use at most 64 MiB of HBM per device.

v0:
```python
import jax
import jax.numpy as jnp
from jax import lax
from jax.sharding import PartitionSpec as P

NEWTON = 3


def shifted(block, axis, distance):
    devices = range(lax.axis_size(axis))
    route = [((i - distance) % len(devices), i) for i in devices]
    return lax.ppermute(block, axis, route)


def det_four(rows):
    a00, a01, a02, a03 = rows[0]
    a10, a11, a12, a13 = rows[1]
    a20, a21, a22, a23 = rows[2]
    a30, a31, a32, a33 = rows[3]
    s0 = a00 * a11 - a10 * a01
    s1 = a00 * a12 - a10 * a02
    s2 = a00 * a13 - a10 * a03
    s3 = a01 * a12 - a11 * a02
    s4 = a01 * a13 - a11 * a03
    s5 = a02 * a13 - a12 * a03
    t5 = a22 * a33 - a32 * a23
    t4 = a21 * a33 - a31 * a23
    t3 = a21 * a32 - a31 * a22
    t2 = a20 * a33 - a30 * a23
    t1 = a20 * a32 - a30 * a22
    t0 = a20 * a31 - a30 * a21
    return s0 * t5 - s1 * t4 + s2 * t3 + s3 * t2 - s4 * t1 + s5 * t0


def quaternion_fit(moment, spread_rows, spread_cols):
    sxx, sxy, sxz, syx, syy, syz, szx, szy, szz = [moment[k] for k in range(9)]
    coef_two = -2.0 * jnp.sum(moment * moment, axis=0)
    det_three = (
        sxx * (syy * szz - syz * szy)
        - sxy * (syx * szz - syz * szx)
        + sxz * (syx * szy - syy * szx)
    )
    coef_one = -8.0 * det_three
    rows = [
        [sxx + syy + szz, syz - szy, szx - sxz, sxy - syx],
        [syz - szy, sxx - syy - szz, sxy + syx, szx + sxz],
        [szx - sxz, sxy + syx, -sxx + syy - szz, syz + szy],
        [sxy - syx, szx + sxz, syz + szy, -sxx - syy + szz],
    ]
    coef_zero = det_four(rows)
    lam = 0.5 * (spread_rows + spread_cols)
    for turn in range(NEWTON):
        square = lam * lam
        value = (square + coef_two) * square + coef_one * lam + coef_zero
        slope = 4.0 * square * lam + 2.0 * coef_two * lam + coef_one
        lam = lam - value / slope
    return spread_rows + spread_cols - 2.0 * lam


def on_device(coords, weights):
    frame_rows = coords.shape[1]
    n_frame = lax.axis_size("frame")
    n_atom = lax.axis_size("atom")
    frames = frame_rows * n_frame
    mass = weights.astype(jnp.float32)
    sums, total = lax.psum((jnp.sum(coords * mass, axis=2), jnp.sum(mass)), "atom")
    centroid = sums / total
    centered = coords - centroid[:, :, None]
    spread = lax.psum(jnp.sum(mass * centered * centered, axis=(0, 2)), "atom") / total
    weighted = centered * mass
    mine = lax.axis_index("frame")
    payload = (centered,)

    def absorb(state, parcel, owner):
        tile, norm_list = state
        block = jnp.einsum("cia,dja->cdij", weighted, parcel[0], precision=lax.Precision.HIGHEST)
        block = block.reshape(9, frame_rows, frame_rows)
        start = owner * frame_rows
        zero = jnp.zeros((), jnp.int32)
        tile = lax.dynamic_update_slice(tile, block, (zero, zero, start))
        return (tile, norm_list)

    state = (jnp.zeros((9, frame_rows, frames), jnp.float32), jnp.zeros((frames,), jnp.float32))
    state = absorb(state, payload, mine)

    def advance(turn, carry):
        held, moving = carry
        moving = shifted((moving[0],), "frame", 1)
        return (absorb(held, moving, (mine - turn) % n_frame), moving)

    state, payload = lax.fori_loop(1, n_frame, advance, (state, payload))
    tile, norm_list = state
    norm_list = lax.all_gather(spread, "frame", axis=0, tiled=True)
    owned = lax.psum_scatter(tile, "atom", scatter_dimension=2, tiled=True)
    columns = frames // n_atom
    start = lax.axis_index("atom") * columns
    column_norms = lax.dynamic_slice_in_dim(norm_list, start, columns, 0)
    return quaternion_fit(owned / total, spread[:, None], column_norms[None, :])


def solution(mesh):
    placed = (P(None, "frame", "atom"), P("atom"))
    return jax.shard_map(
        on_device, mesh=mesh, in_specs=placed, out_specs=P("frame", "atom"), check_vma=False
    )
```

profile of v0, /device:TPU:7, one launch (start us, length us, event | category | flops | bytes accessed | tf_op | source)
XLA Modules:
  0.0 605.5 jit_solution(7174427796848994705)
XLA Ops:
  9.6 29.4 %all-reduce.1 = (f32[3,48]{1,0:T(4,128)S(1)}, f32[]{:T(128)}) all-reduce(f32[3,48]{1,0:T(4,128)S(1)} %multiply_reduce_fusion.1, f32[]{:T(128)} %convert_reduce_fusion), channel_id=1, replica_groups=mesh['frame'=32,'atom'=16] {'atom'}, use_global_device_ids=true, to_apply=%region_1.0 | all-reduce | flops 145 | bytes 1160 | tf_op jit(solution)/shard_map/psum | solution.py:66
  42.4 403.6 %while.17 = (s32[]{:T(128)}, f32[9,48,1536]{2,1,0:T(8,128)S(1)}, f32[3,48,512]{2,1,0:T(8,128)S(1)}, f32[3,48,512]{2,1,0:T(8,128)S(1)}, s32[]{:T(128)}, /*index=5...) while((s32[]{:T(128)}, f32[9,48,1536]{2,1,0:T(8,128)S(1)}, ...), condition=%wide.region_7.8_spmd, body=%wide.region_6.7_spmd.sunk | while | flops 127401984 | bytes 2774336 | solution.py:91
  42.4 4.9 collective-permute-start
  47.3 11.3 %collective-permute-done = f32[3,48,512]{2,1,0:T(8,128)S(1)} collective-permute-done((f32[3,48,512]{2,1,0:T(8,128)S(1)}, f32[3,48,512]{2,1,0:T(8,128)S(1)}, u32[]{:S(2)}, u32[]{:S(2)}) %collective-permute-start) | collective-permute-done | bytes 294944 | tf_op jit(solution)/shard_map/while/body/eval_jaxpr/ppermute | solution.py:12
  61.2 1.9 collective-permute-start
  63.1 7.6 %collective-permute-done = f32[3,48,512]{2,1,0:T(8,128)S(1)} collective-permute-done((f32[3,48,512]{2,1,0:T(8,128)S(1)}, f32[3,48,512]{2,1,0:T(8,128)S(1)}, u32[]{:S(2)}, u32[]{:S(2)}) %collective-permute-start) | collective-permute-done | bytes 294944 | tf_op jit(solution)/shard_map/while/body/eval_jaxpr/ppermute | solution.py:12
  73.3 1.9 collective-permute-start
  75.3 7.6 %collective-permute-done = f32[3,48,512]{2,1,0:T(8,128)S(1)} collective-permute-done((f32[3,48,512]{2,1,0:T(8,128)S(1)}, f32[3,48,512]{2,1,0:T(8,128)S(1)}, u32[]{:S(2)}, u32[]{:S(2)}) %collective-permute-start) | collective-permute-done | bytes 294944 | tf_op jit(solution)/shard_map/while/body/eval_jaxpr/ppermute | solution.py:12
  85.5 1.9 collective-permute-start
  87.5 7.6 %collective-permute-done = f32[3,48,512]{2,1,0:T(8,128)S(1)} collective-permute-done((f32[3,48,512]{2,1,0:T(8,128)S(1)}, f32[3,48,512]{2,1,0:T(8,128)S(1)}, u32[]{:S(2)}, u32[]{:S(2)}) %collective-permute-start) | collective-permute-done | bytes 294944 | tf_op jit(solution)/shard_map/while/body/eval_jaxpr/ppermute | solution.py:12
  97.7 1.9 collective-permute-start
  99.7 7.6 %collective-permute-done = f32[3,48,512]{2,1,0:T(8,128)S(1)} collective-permute-done((f32[3,48,512]{2,1,0:T(8,128)S(1)}, f32[3,48,512]{2,1,0:T(8,128)S(1)}, u32[]{:S(2)}, u32[]{:S(2)}) %collective-permute-start) | collective-permute-done | bytes 294944 | tf_op jit(solution)/shard_map/while/body/eval_jaxpr/ppermute | solution.py:12
  109.9 1.9 collective-permute-start
  111.9 8.7 %collective-permute-done = f32[3,48,512]{2,1,0:T(8,128)S(1)} collective-permute-done((f32[3,48,512]{2,1,0:T(8,128)S(1)}, f32[3,48,512]{2,1,0:T(8,128)S(1)}, u32[]{:S(2)}, u32[]{:S(2)}) %collective-permute-start) | collective-permute-done | bytes 294944 | tf_op jit(solution)/shard_map/while/body/eval_jaxpr/ppermute | solution.py:12
  123.2 1.9 collective-permute-start
  125.1 9.8 %collective-permute-done = f32[3,48,512]{2,1,0:T(8,128)S(1)} collective-permute-done((f32[3,48,512]{2,1,0:T(8,128)S(1)}, f32[3,48,512]{2,1,0:T(8,128)S(1)}, u32[]{:S(2)}, u32[]{:S(2)}) %collective-permute-start) | collective-permute-done | bytes 294944 | tf_op jit(solution)/shard_map/while/body/eval_jaxpr/ppermute | solution.py:12
  137.5 1.9 collective-permute-start
  139.4 10.9 %collective-permute-done = f32[3,48,512]{2,1,0:T(8,128)S(1)} collective-permute-done((f32[3,48,512]{2,1,0:T(8,128)S(1)}, f32[3,48,512]{2,1,0:T(8,128)S(1)}, u32[]{:S(2)}, u32[]{:S(2)}) %collective-permute-start) | collective-permute-done | bytes 294944 | tf_op jit(solution)/shard_map/while/body/eval_jaxpr/ppermute | solution.py:12
  151.6 1.9 collective-permute-start
  153.6 8.7 %collective-permute-done = f32[3,48,512]{2,1,0:T(8,128)S(1)} collective-permute-done((f32[3,48,512]{2,1,0:T(8,128)S(1)}, f32[3,48,512]{2,1,0:T(8,128)S(1)}, u32[]{:S(2)}, u32[]{:S(2)}) %collective-permute-start) | collective-permute-done | bytes 294944 | tf_op jit(solution)/shard_map/while/body/eval_jaxpr/ppermute | solution.py:12
  164.9 1.9 collective-permute-start
  166.8 9.1 %collective-permute-done = f32[3,48,512]{2,1,0:T(8,128)S(1)} collective-permute-done((f32[3,48,512]{2,1,0:T(8,128)S(1)}, f32[3,48,512]{2,1,0:T(8,128)S(1)}, u32[]{:S(2)}, u32[]{:S(2)}) %collective-permute-start) | collective-permute-done | bytes 294944 | tf_op jit(solution)/shard_map/while/body/eval_jaxpr/ppermute | solution.py:12
  178.5 1.9 collective-permute-start
  180.5 8.2 %collective-permute-done = f32[3,48,512]{2,1,0:T(8,128)S(1)} collective-permute-done((f32[3,48,512]{2,1,0:T(8,128)S(1)}, f32[3,48,512]{2,1,0:T(8,128)S(1)}, u32[]{:S(2)}, u32[]{:S(2)}) %collective-permute-start) | collective-permute-done | bytes 294944 | tf_op jit(solution)/shard_map/while/body/eval_jaxpr/ppermute | solution.py:12
  191.3 1.9 collective-permute-start
  193.2 7.6 %collective-permute-done = f32[3,48,512]{2,1,0:T(8,128)S(1)} collective-permute-done((f32[3,48,512]{2,1,0:T(8,128)S(1)}, f32[3,48,512]{2,1,0:T(8,128)S(1)}, u32[]{:S(2)}, u32[]{:S(2)}) %collective-permute-start) | collective-permute-done | bytes 294944 | tf_op jit(solution)/shard_map/while/body/eval_jaxpr/ppermute | solution.py:12
  203.4 1.9 collective-permute-start
  205.4 7.6 %collective-permute-done = f32[3,48,512]{2,1,0:T(8,128)S(1)} collective-permute-done((f32[3,48,512]{2,1,0:T(8,128)S(1)}, f32[3,48,512]{2,1,0:T(8,128)S(1)}, u32[]{:S(2)}, u32[]{:S(2)}) %collective-permute-start) | collective-permute-done | bytes 294944 | tf_op jit(solution)/shard_map/while/body/eval_jaxpr/ppermute | solution.py:12
  215.6 1.9 collective-permute-start
  217.6 7.6 %collective-permute-done = f32[3,48,512]{2,1,0:T(8,128)S(1)} collective-permute-done((f32[3,48,512]{2,1,0:T(8,128)S(1)}, f32[3,48,512]{2,1,0:T(8,128)S(1)}, u32[]{:S(2)}, u32[]{:S(2)}) %collective-permute-start) | collective-permute-done | bytes 294944 | tf_op jit(solution)/shard_map/while/body/eval_jaxpr/ppermute | solution.py:12
  227.8 1.9 collective-permute-start
  229.8 7.6 %collective-permute-done = f32[3,48,512]{2,1,0:T(8,128)S(1)} collective-permute-done((f32[3,48,512]{2,1,0:T(8,128)S(1)}, f32[3,48,512]{2,1,0:T(8,128)S(1)}, u32[]{:S(2)}, u32[]{:S(2)}) %collective-permute-start) | collective-permute-done | bytes 294944 | tf_op jit(solution)/shard_map/while/body/eval_jaxpr/ppermute | solution.py:12
  240.0 1.9 collective-permute-start
  242.0 7.6 %collective-permute-done = f32[3,48,512]{2,1,0:T(8,128)S(1)} collective-permute-done((f32[3,48,512]{2,1,0:T(8,128)S(1)}, f32[3,48,512]{2,1,0:T(8,128)S(1)}, u32[]{:S(2)}, u32[]{:S(2)}) %collective-permute-start) | collective-permute-done | bytes 294944 | tf_op jit(solution)/shard_map/while/body/eval_jaxpr/ppermute | solution.py:12
  250.8 1.9 collective-permute-start
  252.8 8.3 %collective-permute-done = f32[3,48,512]{2,1,0:T(8,128)S(1)} collective-permute-done((f32[3,48,512]{2,1,0:T(8,128)S(1)}, f32[3,48,512]{2,1,0:T(8,128)S(1)}, u32[]{:S(2)}, u32[]{:S(2)}) %collective-permute-start) | collective-permute-done | bytes 294944 | tf_op jit(solution)/shard_map/while/body/eval_jaxpr/ppermute | solution.py:12
  263.6 1.9 collective-permute-start
  265.5 9.5 %collective-permute-done = f32[3,48,512]{2,1,0:T(8,128)S(1)} collective-permute-done((f32[3,48,512]{2,1,0:T(8,128)S(1)}, f32[3,48,512]{2,1,0:T(8,128)S(1)}, u32[]{:S(2)}, u32[]{:S(2)}) %collective-permute-start) | collective-permute-done | bytes 294944 | tf_op jit(solution)/shard_map/while/body/eval_jaxpr/ppermute | solution.py:12
  277.5 1.9 collective-permute-start
  279.5 9.4 %collective-permute-done = f32[3,48,512]{2,1,0:T(8,128)S(1)} collective-permute-done((f32[3,48,512]{2,1,0:T(8,128)S(1)}, f32[3,48,512]{2,1,0:T(8,128)S(1)}, u32[]{:S(2)}, u32[]{:S(2)}) %collective-permute-start) | collective-permute-done | bytes 294944 | tf_op jit(solution)/shard_map/while/body/eval_jaxpr/ppermute | solution.py:12
  291.5 1.9 collective-permute-start
  293.4 10.4 %collective-permute-done = f32[3,48,512]{2,1,0:T(8,128)S(1)} collective-permute-done((f32[3,48,512]{2,1,0:T(8,128)S(1)}, f32[3,48,512]{2,1,0:T(8,128)S(1)}, u32[]{:S(2)}, u32[]{:S(2)}) %collective-permute-start) | collective-permute-done | bytes 294944 | tf_op jit(solution)/shard_map/while/body/eval_jaxpr/ppermute | solution.py:12
  306.4 1.9 collective-permute-start
  308.4 10.4 %collective-permute-done = f32[3,48,512]{2,1,0:T(8,128)S(1)} collective-permute-done((f32[3,48,512]{2,1,0:T(8,128)S(1)}, f32[3,48,512]{2,1,0:T(8,128)S(1)}, u32[]{:S(2)}, u32[]{:S(2)}) %collective-permute-start) | collective-permute-done | bytes 294944 | tf_op jit(solution)/shard_map/while/body/eval_jaxpr/ppermute | solution.py:12
  321.4 1.9 collective-permute-start
  323.4 9.5 %collective-permute-done = f32[3,48,512]{2,1,0:T(8,128)S(1)} collective-permute-done((f32[3,48,512]{2,1,0:T(8,128)S(1)}, f32[3,48,512]{2,1,0:T(8,128)S(1)}, u32[]{:S(2)}, u32[]{:S(2)}) %collective-permute-start) | collective-permute-done | bytes 294944 | tf_op jit(solution)/shard_map/while/body/eval_jaxpr/ppermute | solution.py:12
  335.5 1.9 collective-permute-start
  337.4 8.6 %collective-permute-done = f32[3,48,512]{2,1,0:T(8,128)S(1)} collective-permute-done((f32[3,48,512]{2,1,0:T(8,128)S(1)}, f32[3,48,512]{2,1,0:T(8,128)S(1)}, u32[]{:S(2)}, u32[]{:S(2)}) %collective-permute-start) | collective-permute-done | bytes 294944 | tf_op jit(solution)/shard_map/while/body/eval_jaxpr/ppermute | solution.py:12
  348.6 1.9 collective-permute-start
  350.6 7.6 %collective-permute-done = f32[3,48,512]{2,1,0:T(8,128)S(1)} collective-permute-done((f32[3,48,512]{2,1,0:T(8,128)S(1)}, f32[3,48,512]{2,1,0:T(8,128)S(1)}, u32[]{:S(2)}, u32[]{:S(2)}) %collective-permute-start) | collective-permute-done | bytes 294944 | tf_op jit(solution)/shard_map/while/body/eval_jaxpr/ppermute | solution.py:12
  361.4 7.6 %collective-permute-done = f32[3,48,512]{2,1,0:T(8,128)S(1)} collective-permute-done((f32[3,48,512]{2,1,0:T(8,128)S(1)}, f32[3,48,512]{2,1,0:T(8,128)S(1)}, u32[]{:S(2)}, u32[]{:S(2)}) %collective-permute-start) | collective-permute-done | bytes 294944 | tf_op jit(solution)/shard_map/while/body/eval_jaxpr/ppermute | solution.py:12
  373.6 7.6 %collective-permute-done = f32[3,48,512]{2,1,0:T(8,128)S(1)} collective-permute-done((f32[3,48,512]{2,1,0:T(8,128)S(1)}, f32[3,48,512]{2,1,0:T(8,128)S(1)}, u32[]{:S(2)}, u32[]{:S(2)}) %collective-permute-start) | collective-permute-done | bytes 294944 | tf_op jit(solution)/shard_map/while/body/eval_jaxpr/ppermute | solution.py:12
  385.8 7.6 %collective-permute-done = f32[3,48,512]{2,1,0:T(8,128)S(1)} collective-permute-done((f32[3,48,512]{2,1,0:T(8,128)S(1)}, f32[3,48,512]{2,1,0:T(8,128)S(1)}, u32[]{:S(2)}, u32[]{:S(2)}) %collective-permute-start) | collective-permute-done | bytes 294944 | tf_op jit(solution)/shard_map/while/body/eval_jaxpr/ppermute | solution.py:12
  398.0 7.6 %collective-permute-done = f32[3,48,512]{2,1,0:T(8,128)S(1)} collective-permute-done((f32[3,48,512]{2,1,0:T(8,128)S(1)}, f32[3,48,512]{2,1,0:T(8,128)S(1)}, u32[]{:S(2)}, u32[]{:S(2)}) %collective-permute-start) | collective-permute-done | bytes 294944 | tf_op jit(solution)/shard_map/while/body/eval_jaxpr/ppermute | solution.py:12
  408.2 1.9 collective-permute-start
  410.1 7.6 %collective-permute-done = f32[3,48,512]{2,1,0:T(8,128)S(1)} collective-permute-done((f32[3,48,512]{2,1,0:T(8,128)S(1)}, f32[3,48,512]{2,1,0:T(8,128)S(1)}, u32[]{:S(2)}, u32[]{:S(2)}) %collective-permute-start) | collective-permute-done | bytes 294944 | tf_op jit(solution)/shard_map/while/body/eval_jaxpr/ppermute | solution.py:12
  420.4 1.9 collective-permute-start
  422.3 7.7 %collective-permute-done = f32[3,48,512]{2,1,0:T(8,128)S(1)} collective-permute-done((f32[3,48,512]{2,1,0:T(8,128)S(1)}, f32[3,48,512]{2,1,0:T(8,128)S(1)}, u32[]{:S(2)}, u32[]{:S(2)}) %collective-permute-start) | collective-permute-done | bytes 294944 | tf_op jit(solution)/shard_map/while/body/eval_jaxpr/ppermute | solution.py:12
  434.6 8.8 %collective-permute-done = f32[3,48,512]{2,1,0:T(8,128)S(1)} collective-permute-done((f32[3,48,512]{2,1,0:T(8,128)S(1)}, f32[3,48,512]{2,1,0:T(8,128)S(1)}, u32[]{:S(2)}, u32[]{:S(2)}) %collective-permute-start) | collective-permute-done | bytes 294944 | tf_op jit(solution)/shard_map/while/body/eval_jaxpr/ppermute | solution.py:12
  446.0 8.7 %copy.9 = f32[9,48,1536]{1,0,2:T(8,128)} copy(f32[9,48,1536]{2,1,0:T(8,128)S(1)} %get-tuple-element.138) | data formatting | bytes 5308416
  454.6 9.4 %reshape.27 = f32[1536,432]{1,0:T(8,128)} reshape(f32[1536,9,48]{2,1,0:T(8,128)} %bitcast.69) | data formatting | bytes 5308416
  466.0 72.0 %psum.23 = f32[48]{0:T(128)S(1)} all-reduce(f32[48]{0:T(128)S(1)} %get-tuple-element.153), channel_id=1, replica_groups=mesh['frame'=32,'atom'=16] {'atom'}, use_global_device_ids=true, to_apply=%region_5.0 | all-reduce | flops 48 | bytes 384 | tf_op jit(solution)/shard_map/psum | solution.py:69
  538.7 48.6 %all-reduce = f32[1536]{0:T(1024)S(1)} all-reduce(f32[1536]{0:T(1024)S(1)} %get-tuple-element.151), channel_id=1, replica_groups=mesh['frame'=32,'atom'=16] {'frame'}, use_global_device_ids=true, to_apply=%add | all-reduce | flops 1536 | bytes 12288
  587.4 8.4 %reduce-scatter.4.cloned.1.call-done = f32[96,432]{1,0:T(8,128)} async-done(((f32[1536,432]{1,0:T(8,128)}), f32[96,432]{1,0:T(8,128)}) %reduce-scatter.4.cloned.1.call-update) | async-done | bytes 165904
  (149 shorter events, 96.2 us)
Async XLA Ops:
  6.5 589.3 %reduce-scatter.4.cloned.1.call-start = ((), (), s32[]{:S(2)}) async-start(), calls=%async_computation.1 | async-start | bytes 3342336
  42.4 16.2 %collective-permute-start = (f32[3,48,512]{2,1,0:T(8,128)S(1)}, f32[3,48,512]{2,1,0:T(8,128)S(1)}, u32[]{:S(2)}, u32[]{:S(2)}) collective-permute-start(f32[3,48,512]{2,1,0:T(8,128)S(1)} %get-tuple-element.201), channel_id=1, source_target_pairs={{496,0},{0,16},{16,32},{32,48},{48,64},{64,80},{80,96},{96,112},{1... | collective-permute-start | bytes 884744 | tf_op jit(solution)/shard_map/while/body/eval_jaxpr/ppermute | solution.py:12
  61.2 9.6 %collective-permute-start = (f32[3,48,512]{2,1,0:T(8,128)S(1)}, f32[3,48,512]{2,1,0:T(8,128)S(1)}, u32[]{:S(2)}, u32[]{:S(2)}) collective-permute-start(f32[3,48,512]{2,1,0:T(8,128)S(1)} %get-tuple-element.201), channel_id=1, source_target_pairs={{496,0},{0,16},{16,32},{32,48},{48,64},{64,80},{80,96},{96,112},{1... | collective-permute-start | bytes 884744 | tf_op jit(solution)/shard_map/while/body/eval_jaxpr/ppermute | solution.py:12
  73.3 9.6 %collective-permute-start = (f32[3,48,512]{2,1,0:T(8,128)S(1)}, f32[3,48,512]{2,1,0:T(8,128)S(1)}, u32[]{:S(2)}, u32[]{:S(2)}) collective-permute-start(f32[3,48,512]{2,1,0:T(8,128)S(1)} %get-tuple-element.201), channel_id=1, source_target_pairs={{496,0},{0,16},{16,32},{32,48},{48,64},{64,80},{80,96},{96,112},{1... | collective-permute-start | bytes 884744 | tf_op jit(solution)/shard_map/while/body/eval_jaxpr/ppermute | solution.py:12
  85.5 9.6 %collective-permute-start = (f32[3,48,512]{2,1,0:T(8,128)S(1)}, f32[3,48,512]{2,1,0:T(8,128)S(1)}, u32[]{:S(2)}, u32[]{:S(2)}) collective-permute-start(f32[3,48,512]{2,1,0:T(8,128)S(1)} %get-tuple-element.201), channel_id=1, source_target_pairs={{496,0},{0,16},{16,32},{32,48},{48,64},{64,80},{80,96},{96,112},{1... | collective-permute-start | bytes 884744 | tf_op jit(solution)/shard_map/while/body/eval_jaxpr/ppermute | solution.py:12
  97.7 9.6 %collective-permute-start = (f32[3,48,512]{2,1,0:T(8,128)S(1)}, f32[3,48,512]{2,1,0:T(8,128)S(1)}, u32[]{:S(2)}, u32[]{:S(2)}) collective-permute-start(f32[3,48,512]{2,1,0:T(8,128)S(1)} %get-tuple-element.201), channel_id=1, source_target_pairs={{496,0},{0,16},{16,32},{32,48},{48,64},{64,80},{80,96},{96,112},{1... | collective-permute-start | bytes 884744 | tf_op jit(solution)/shard_map/while/body/eval_jaxpr/ppermute | solution.py:12
  109.9 10.6 %collective-permute-start = (f32[3,48,512]{2,1,0:T(8,128)S(1)}, f32[3,48,512]{2,1,0:T(8,128)S(1)}, u32[]{:S(2)}, u32[]{:S(2)}) collective-permute-start(f32[3,48,512]{2,1,0:T(8,128)S(1)} %get-tuple-element.201), channel_id=1, source_target_pairs={{496,0},{0,16},{16,32},{32,48},{48,64},{64,80},{80,96},{96,112},{1... | collective-permute-start | bytes 884744 | tf_op jit(solution)/shard_map/while/body/eval_jaxpr/ppermute | solution.py:12
  123.2 11.7 %collective-permute-start = (f32[3,48,512]{2,1,0:T(8,128)S(1)}, f32[3,48,512]{2,1,0:T(8,128)S(1)}, u32[]{:S(2)}, u32[]{:S(2)}) collective-permute-start(f32[3,48,512]{2,1,0:T(8,128)S(1)} %get-tuple-element.201), channel_id=1, source_target_pairs={{496,0},{0,16},{16,32},{32,48},{48,64},{64,80},{80,96},{96,112},{1... | collective-permute-start | bytes 884744 | tf_op jit(solution)/shard_map/while/body/eval_jaxpr/ppermute | solution.py:12
  137.5 12.9 %collective-permute-start = (f32[3,48,512]{2,1,0:T(8,128)S(1)}, f32[3,48,512]{2,1,0:T(8,128)S(1)}, u32[]{:S(2)}, u32[]{:S(2)}) collective-permute-start(f32[3,48,512]{2,1,0:T(8,128)S(1)} %get-tuple-element.201), channel_id=1, source_target_pairs={{496,0},{0,16},{16,32},{32,48},{48,64},{64,80},{80,96},{96,112},{1... | collective-permute-start | bytes 884744 | tf_op jit(solution)/shard_map/while/body/eval_jaxpr/ppermute | solution.py:12
  151.6 10.6 %collective-permute-start = (f32[3,48,512]{2,1,0:T(8,128)S(1)}, f32[3,48,512]{2,1,0:T(8,128)S(1)}, u32[]{:S(2)}, u32[]{:S(2)}) collective-permute-start(f32[3,48,512]{2,1,0:T(8,128)S(1)} %get-tuple-element.201), channel_id=1, source_target_pairs={{496,0},{0,16},{16,32},{32,48},{48,64},{64,80},{80,96},{96,112},{1... | collective-permute-start | bytes 884744 | tf_op jit(solution)/shard_map/while/body/eval_jaxpr/ppermute | solution.py:12
  164.9 11.1 %collective-permute-start = (f32[3,48,512]{2,1,0:T(8,128)S(1)}, f32[3,48,512]{2,1,0:T(8,128)S(1)}, u32[]{:S(2)}, u32[]{:S(2)}) collective-permute-start(f32[3,48,512]{2,1,0:T(8,128)S(1)} %get-tuple-element.201), channel_id=1, source_target_pairs={{496,0},{0,16},{16,32},{32,48},{48,64},{64,80},{80,96},{96,112},{1... | collective-permute-start | bytes 884744 | tf_op jit(solution)/shard_map/while/body/eval_jaxpr/ppermute | solution.py:12
  178.5 10.1 %collective-permute-start = (f32[3,48,512]{2,1,0:T(8,128)S(1)}, f32[3,48,512]{2,1,0:T(8,128)S(1)}, u32[]{:S(2)}, u32[]{:S(2)}) collective-permute-start(f32[3,48,512]{2,1,0:T(8,128)S(1)} %get-tuple-element.201), channel_id=1, source_target_pairs={{496,0},{0,16},{16,32},{32,48},{48,64},{64,80},{80,96},{96,112},{1... | collective-permute-start | bytes 884744 | tf_op jit(solution)/shard_map/while/body/eval_jaxpr/ppermute | solution.py:12
  191.3 9.6 %collective-permute-start = (f32[3,48,512]{2,1,0:T(8,128)S(1)}, f32[3,48,512]{2,1,0:T(8,128)S(1)}, u32[]{:S(2)}, u32[]{:S(2)}) collective-permute-start(f32[3,48,512]{2,1,0:T(8,128)S(1)} %get-tuple-element.201), channel_id=1, source_target_pairs={{496,0},{0,16},{16,32},{32,48},{48,64},{64,80},{80,96},{96,112},{1... | collective-permute-start | bytes 884744 | tf_op jit(solution)/shard_map/while/body/eval_jaxpr/ppermute | solution.py:12
  203.4 9.6 %collective-permute-start = (f32[3,48,512]{2,1,0:T(8,128)S(1)}, f32[3,48,512]{2,1,0:T(8,128)S(1)}, u32[]{:S(2)}, u32[]{:S(2)}) collective-permute-start(f32[3,48,512]{2,1,0:T(8,128)S(1)} %get-tuple-element.201), channel_id=1, source_target_pairs={{496,0},{0,16},{16,32},{32,48},{48,64},{64,80},{80,96},{96,112},{1... | collective-permute-start | bytes 884744 | tf_op jit(solution)/shard_map/while/body/eval_jaxpr/ppermute | solution.py:12
  215.6 9.6 %collective-permute-start = (f32[3,48,512]{2,1,0:T(8,128)S(1)}, f32[3,48,512]{2,1,0:T(8,128)S(1)}, u32[]{:S(2)}, u32[]{:S(2)}) collective-permute-start(f32[3,48,512]{2,1,0:T(8,128)S(1)} %get-tuple-element.201), channel_id=1, source_target_pairs={{496,0},{0,16},{16,32},{32,48},{48,64},{64,80},{80,96},{96,112},{1... | collective-permute-start | bytes 884744 | tf_op jit(solution)/shard_map/while/body/eval_jaxpr/ppermute | solution.py:12
  227.8 9.6 %collective-permute-start = (f32[3,48,512]{2,1,0:T(8,128)S(1)}, f32[3,48,512]{2,1,0:T(8,128)S(1)}, u32[]{:S(2)}, u32[]{:S(2)}) collective-permute-start(f32[3,48,512]{2,1,0:T(8,128)S(1)} %get-tuple-element.201), channel_id=1, source_target_pairs={{496,0},{0,16},{16,32},{32,48},{48,64},{64,80},{80,96},{96,112},{1... | collective-permute-start | bytes 884744 | tf_op jit(solution)/shard_map/while/body/eval_jaxpr/ppermute | solution.py:12
  240.0 9.6 %collective-permute-start = (f32[3,48,512]{2,1,0:T(8,128)S(1)}, f32[3,48,512]{2,1,0:T(8,128)S(1)}, u32[]{:S(2)}, u32[]{:S(2)}) collective-permute-start(f32[3,48,512]{2,1,0:T(8,128)S(1)} %get-tuple-element.201), channel_id=1, source_target_pairs={{496,0},{0,16},{16,32},{32,48},{48,64},{64,80},{80,96},{96,112},{1... | collective-permute-start | bytes 884744 | tf_op jit(solution)/shard_map/while/body/eval_jaxpr/ppermute | solution.py:12
  250.8 10.3 %collective-permute-start = (f32[3,48,512]{2,1,0:T(8,128)S(1)}, f32[3,48,512]{2,1,0:T(8,128)S(1)}, u32[]{:S(2)}, u32[]{:S(2)}) collective-permute-start(f32[3,48,512]{2,1,0:T(8,128)S(1)} %get-tuple-element.201), channel_id=1, source_target_pairs={{496,0},{0,16},{16,32},{32,48},{48,64},{64,80},{80,96},{96,112},{1... | collective-permute-start | bytes 884744 | tf_op jit(solution)/shard_map/while/body/eval_jaxpr/ppermute | solution.py:12
  263.6 11.5 %collective-permute-start = (f32[3,48,512]{2,1,0:T(8,128)S(1)}, f32[3,48,512]{2,1,0:T(8,128)S(1)}, u32[]{:S(2)}, u32[]{:S(2)}) collective-permute-start(f32[3,48,512]{2,1,0:T(8,128)S(1)} %get-tuple-element.201), channel_id=1, source_target_pairs={{496,0},{0,16},{16,32},{32,48},{48,64},{64,80},{80,96},{96,112},{1... | collective-permute-start | bytes 884744 | tf_op jit(solution)/shard_map/while/body/eval_jaxpr/ppermute | solution.py:12
  277.5 11.3 %collective-permute-start = (f32[3,48,512]{2,1,0:T(8,128)S(1)}, f32[3,48,512]{2,1,0:T(8,128)S(1)}, u32[]{:S(2)}, u32[]{:S(2)}) collective-permute-start(f32[3,48,512]{2,1,0:T(8,128)S(1)} %get-tuple-element.201), channel_id=1, source_target_pairs={{496,0},{0,16},{16,32},{32,48},{48,64},{64,80},{80,96},{96,112},{1... | collective-permute-start | bytes 884744 | tf_op jit(solution)/shard_map/while/body/eval_jaxpr/ppermute | solution.py:12
  291.5 12.3 %collective-permute-start = (f32[3,48,512]{2,1,0:T(8,128)S(1)}, f32[3,48,512]{2,1,0:T(8,128)S(1)}, u32[]{:S(2)}, u32[]{:S(2)}) collective-permute-start(f32[3,48,512]{2,1,0:T(8,128)S(1)} %get-tuple-element.201), channel_id=1, source_target_pairs={{496,0},{0,16},{16,32},{32,48},{48,64},{64,80},{80,96},{96,112},{1... | collective-permute-start | bytes 884744 | tf_op jit(solution)/shard_map/while/body/eval_jaxpr/ppermute | solution.py:12
  306.4 12.4 %collective-permute-start = (f32[3,48,512]{2,1,0:T(8,128)S(1)}, f32[3,48,512]{2,1,0:T(8,128)S(1)}, u32[]{:S(2)}, u32[]{:S(2)}) collective-permute-start(f32[3,48,512]{2,1,0:T(8,128)S(1)} %get-tuple-element.201), channel_id=1, source_target_pairs={{496,0},{0,16},{16,32},{32,48},{48,64},{64,80},{80,96},{96,112},{1... | collective-permute-start | bytes 884744 | tf_op jit(solution)/shard_map/while/body/eval_jaxpr/ppermute | solution.py:12
  321.4 11.5 %collective-permute-start = (f32[3,48,512]{2,1,0:T(8,128)S(1)}, f32[3,48,512]{2,1,0:T(8,128)S(1)}, u32[]{:S(2)}, u32[]{:S(2)}) collective-permute-start(f32[3,48,512]{2,1,0:T(8,128)S(1)} %get-tuple-element.201), channel_id=1, source_target_pairs={{496,0},{0,16},{16,32},{32,48},{48,64},{64,80},{80,96},{96,112},{1... | collective-permute-start | bytes 884744 | tf_op jit(solution)/shard_map/while/body/eval_jaxpr/ppermute | solution.py:12
  335.5 10.5 %collective-permute-start = (f32[3,48,512]{2,1,0:T(8,128)S(1)}, f32[3,48,512]{2,1,0:T(8,128)S(1)}, u32[]{:S(2)}, u32[]{:S(2)}) collective-permute-start(f32[3,48,512]{2,1,0:T(8,128)S(1)} %get-tuple-element.201), channel_id=1, source_target_pairs={{496,0},{0,16},{16,32},{32,48},{48,64},{64,80},{80,96},{96,112},{1... | collective-permute-start | bytes 884744 | tf_op jit(solution)/shard_map/while/body/eval_jaxpr/ppermute | solution.py:12
  348.6 9.6 %collective-permute-start = (f32[3,48,512]{2,1,0:T(8,128)S(1)}, f32[3,48,512]{2,1,0:T(8,128)S(1)}, u32[]{:S(2)}, u32[]{:S(2)}) collective-permute-start(f32[3,48,512]{2,1,0:T(8,128)S(1)} %get-tuple-element.201), channel_id=1, source_target_pairs={{496,0},{0,16},{16,32},{32,48},{48,64},{64,80},{80,96},{96,112},{1... | collective-permute-start | bytes 884744 | tf_op jit(solution)/shard_map/while/body/eval_jaxpr/ppermute | solution.py:12
  359.5 9.6 %collective-permute-start = (f32[3,48,512]{2,1,0:T(8,128)S(1)}, f32[3,48,512]{2,1,0:T(8,128)S(1)}, u32[]{:S(2)}, u32[]{:S(2)}) collective-permute-start(f32[3,48,512]{2,1,0:T(8,128)S(1)} %get-tuple-element.201), channel_id=1, source_target_pairs={{496,0},{0,16},{16,32},{32,48},{48,64},{64,80},{80,96},{96,112},{1... | collective-permute-start | bytes 884744 | tf_op jit(solution)/shard_map/while/body/eval_jaxpr/ppermute | solution.py:12
  371.6 9.6 %collective-permute-start = (f32[3,48,512]{2,1,0:T(8,128)S(1)}, f32[3,48,512]{2,1,0:T(8,128)S(1)}, u32[]{:S(2)}, u32[]{:S(2)}) collective-permute-start(f32[3,48,512]{2,1,0:T(8,128)S(1)} %get-tuple-element.201), channel_id=1, source_target_pairs={{496,0},{0,16},{16,32},{32,48},{48,64},{64,80},{80,96},{96,112},{1... | collective-permute-start | bytes 884744 | tf_op jit(solution)/shard_map/while/body/eval_jaxpr/ppermute | solution.py:12
  383.8 9.6 %collective-permute-start = (f32[3,48,512]{2,1,0:T(8,128)S(1)}, f32[3,48,512]{2,1,0:T(8,128)S(1)}, u32[]{:S(2)}, u32[]{:S(2)}) collective-permute-start(f32[3,48,512]{2,1,0:T(8,128)S(1)} %get-tuple-element.201), channel_id=1, source_target_pairs={{496,0},{0,16},{16,32},{32,48},{48,64},{64,80},{80,96},{96,112},{1... | collective-permute-start | bytes 884744 | tf_op jit(solution)/shard_map/while/body/eval_jaxpr/ppermute | solution.py:12
  396.0 9.6 %collective-permute-start = (f32[3,48,512]{2,1,0:T(8,128)S(1)}, f32[3,48,512]{2,1,0:T(8,128)S(1)}, u32[]{:S(2)}, u32[]{:S(2)}) collective-permute-start(f32[3,48,512]{2,1,0:T(8,128)S(1)} %get-tuple-element.201), channel_id=1, source_target_pairs={{496,0},{0,16},{16,32},{32,48},{48,64},{64,80},{80,96},{96,112},{1... | collective-permute-start | bytes 884744 | tf_op jit(solution)/shard_map/while/body/eval_jaxpr/ppermute | solution.py:12
  408.2 9.6 %collective-permute-start = (f32[3,48,512]{2,1,0:T(8,128)S(1)}, f32[3,48,512]{2,1,0:T(8,128)S(1)}, u32[]{:S(2)}, u32[]{:S(2)}) collective-permute-start(f32[3,48,512]{2,1,0:T(8,128)S(1)} %get-tuple-element.201), channel_id=1, source_target_pairs={{496,0},{0,16},{16,32},{32,48},{48,64},{64,80},{80,96},{96,112},{1... | collective-permute-start | bytes 884744 | tf_op jit(solution)/shard_map/while/body/eval_jaxpr/ppermute | solution.py:12
  420.4 9.7 %collective-permute-start = (f32[3,48,512]{2,1,0:T(8,128)S(1)}, f32[3,48,512]{2,1,0:T(8,128)S(1)}, u32[]{:S(2)}, u32[]{:S(2)}) collective-permute-start(f32[3,48,512]{2,1,0:T(8,128)S(1)} %get-tuple-element.201), channel_id=1, source_target_pairs={{496,0},{0,16},{16,32},{32,48},{48,64},{64,80},{80,96},{96,112},{1... | collective-permute-start | bytes 884744 | tf_op jit(solution)/shard_map/while/body/eval_jaxpr/ppermute | solution.py:12
  432.6 10.7 %collective-permute-start = (f32[3,48,512]{2,1,0:T(8,128)S(1)}, f32[3,48,512]{2,1,0:T(8,128)S(1)}, u32[]{:S(2)}, u32[]{:S(2)}) collective-permute-start(f32[3,48,512]{2,1,0:T(8,128)S(1)} %get-tuple-element.201), channel_id=1, source_target_pairs={{496,0},{0,16},{16,32},{32,48},{48,64},{64,80},{80,96},{96,112},{1... | collective-permute-start | bytes 884744 | tf_op jit(solution)/shard_map/while/body/eval_jaxpr/ppermute | solution.py:12
Sparse Core Ops, SparseCore 0:
  464.2 131.5 reduce-scatter.3
where the time goes:
time: 616 us; the launch traced here: 606 us
  waiting for transfers between devices  272 us (44%)
  blocking collectives  150 us (24%)
  local copies, waits for them, and re-layouts  76.5 us (12%)
  starting transfers between devices  62.5 us (10%)
  matrix products  21.1 us (3%)
  between operations  14.1 us (2%)
  other arithmetic  7.02 us (1%)
    ppermute x31, waiting for transfers between devices, shifted(): return lax.ppermute(block, axis, route)  263 us
    psum x1, blocking collectives, on_device(): lax.psum(jnp.sum(mass * centered * centered, axis=(0, 2)), 'atom') / total  72 us
    ppermute x31, starting transfers between devices, shifted(): return lax.ppermute(block, axis, route)  62.5 us
    dynamic_update_slice x32, local copies, waits for them, and re-layouts, absorb(): tile = lax.dynamic_update_slice(tile, block, (zero, zero, start))  54.2 us
    unnamed x1, blocking collectives  48.6 us
    psum x1, blocking collectives, on_device(): lax.psum((jnp.sum(coords * mass, axis=2), jnp.sum(mass)), 'atom')  29.4 us
    dot_general x32, matrix products, absorb(): jnp.einsum('cia,dja->cdij', weighted, parcel[0], precision=lax.Precision....  21.1 us
    unnamed x6, local copies, waits for them, and re-layouts  20.7 us
  transfers between devices with their start and end apart: 32, of which 32 were waited for; matrix products, arithmetic and copies ran while one was open for 0% of the time, Pallas kernels for 0%

commit v1 on v0

v1 whole, which is shorter than its diff:
```python
import functools

import jax
import jax.numpy as jnp
import numpy as np
from jax import lax
from jax.experimental import pallas as pl
from jax.experimental.pallas import tpu as pltpu
from jax.sharding import PartitionSpec as P

NEWTON = 3
ROWS = 48
SIDE = 16
EXACT = lax.Precision.HIGHEST
VMEM_LIMIT = 40 * 1024 * 1024

OWN = (0, -2, -3, 4, 5)
OTHER = (0, -2, -3)
EARLY = (
    (2, 1), (1, 0), (2, 0), (0, 3), (1, 3), (2, 3),
    (1, 7), (0, 6), (0, 7), (3, 5), (3, 6), (3, 7),
)
LATE = ((0, 4), (4, 5), (2, 7), (2, 4))


def frame_block(column, z, index):
    if index < len(OWN):
        return column * SIDE + (z + OWN[index]) % SIDE
    return (1 - column) * SIDE + (z + OTHER[index - len(OWN)]) % SIDE


def routes():
    ends = []
    for column in range(2):
        for z in range(SIDE):
            for slot, (p, q) in enumerate(EARLY + LATE):
                if slot == len(EARLY) + 2 and column == 1:
                    p = 4
                a, b = frame_block(column, z, p), frame_block(column, z, q)
                if slot == len(EARLY) + 3 and z >= SIDE // 2:
                    ends.append(((a, a), (b, b)))
                else:
                    ends.append(((a, b), (b, a)))
    place = lambda end: end[0] * SIDE + end[1] // 2
    at = {}
    for device, pair in enumerate(ends):
        for which, end in enumerate(pair):
            at.setdefault(place(end), []).append((device, which))
    assert len(at) == len(ends) and all(len(v) == 2 for v in at.values())
    swapped = [None] * len(ends)
    for seed in range(len(ends)):
        device, enter = seed, 0
        while swapped[device] is None:
            swapped[device] = enter
            node = place(ends[device][1 - enter])
            device, enter = [e for e in at[node] if e != (device, 1 - enter)][0]
    first = [place(ends[d][swapped[d]]) for d in range(len(ends))]
    second = [place(ends[d][1 - swapped[d]]) for d in range(len(ends))]
    assert len(set(first)) == len(set(second)) == len(ends)
    half = [0] * len(ends)
    for d in range(len(ends)):
        half[first[d]] = ends[d][swapped[d]][1] % 2
        assert ends[d][1 - swapped[d]][1] % 2 == 1 - half[first[d]] or second[d] != first[d]
    return first, second, swapped, half


def lookup(step, values):
    out = jnp.int32(values[0])
    for k, value in enumerate(values):
        out = jnp.where(step == k, jnp.int32(value), out)
    return out


def iota(shape, axis):
    return lax.broadcasted_iota(jnp.int32, shape, axis)


def dot_t(a, b):
    return lax.dot_general(a, b, (((1,), (1,)), ((), ())), precision=EXACT, preferred_element_type=jnp.float32)


def stage(block, mass, slot, centered, weighted, feature):
    x = block[...]
    local = jnp.sum(mass)
    mean = jnp.sum(x * mass, axis=1, keepdims=True) / local
    x = x - mean
    wx = x * mass
    square = jnp.sum(wx * x, axis=1, keepdims=True)
    centered[slot, : 3 * ROWS] = x
    centered[slot, 3 * ROWS :] = jnp.zeros((256 - 3 * ROWS, x.shape[1]), jnp.float32)
    weighted[slot] = wx
    lane = iota((ROWS, 128), 1)
    square = square[:ROWS] + square[ROWS : 2 * ROWS] + square[2 * ROWS :]
    row, column = jnp.zeros((ROWS, 128), jnp.float32), jnp.zeros((ROWS, 128), jnp.float32)
    for c in range(3):
        part = mean[c * ROWS : (c + 1) * ROWS]
        row = jnp.where(lane == 48 + c, part, row)
        column = jnp.where(lane == 52 + c, part, column)
    row = jnp.where(lane == 51, local, row)
    row = jnp.where(lane == 56, square, row)
    column = jnp.where(lane == 57, square, column)
    feature[slot, 0] = row
    feature[slot, 1] = column


def rest_of(tail):
    return tail[:ROWS] + pltpu.roll(tail[ROWS : 2 * ROWS], 16, 1) + pltpu.roll(tail[2 * ROWS :], 32, 1)


def put_pair(out, slot, product, feature, p, q):
    out[slot, : 3 * ROWS] = product[:, :128]
    out[slot, 3 * ROWS :] = rest_of(product[:, 128:]) + feature[p, 0] + feature[q, 1]


def early_kernel(mass_ref, *refs):
    blocks, (out, centered, weighted, feature) = refs[:7], refs[7:]
    mass = mass_ref[...]
    index = (0, 1, 2, 3, 5, 6, 7)
    for k, block in enumerate(blocks):
        stage(block, mass, k, centered, weighted, feature)
    rows = [index.index(p) for p, _ in EARLY]
    columns = [index.index(q) for _, q in EARLY]

    def body(step, carry):
        p, q = lookup(step, rows), lookup(step, columns)
        put_pair(out, step, dot_t(weighted[p], centered[q]), feature, p, q)
        return carry

    lax.fori_loop(0, len(EARLY), body, 0)


def late_kernel(flags, mass_ref, *refs):
    blocks, (_, out, centered, weighted, feature) = refs[:5], refs[5:]
    mass = mass_ref[...]
    index = (0, 2, 4, 5, 7)
    for k, block in enumerate(blocks):
        stage(block, mass, k, centered, weighted, feature)
    column, diagonal = flags[0], flags[1]
    rows = [index.index(p) for p, _ in LATE]
    columns = [index.index(q) for _, q in LATE]

    def body(step, carry):
        p, q = lookup(step, rows), lookup(step, columns)
        p = jnp.where((step == 2) & (column == 1), jnp.int32(index.index(4)), p)
        put_pair(out, step, dot_t(weighted[p], centered[q]), feature, p, q)
        return carry

    lax.fori_loop(0, len(LATE), body, 0)

    @pl.when(diagonal == 1)
    def _():
        p, q = rows[3], columns[3]
        upper, lower = dot_t(weighted[p], centered[p]), dot_t(weighted[q], centered[q])
        i, j = iota((3 * ROWS, 256), 0) % ROWS, iota((3 * ROWS, 256), 1) % ROWS
        product = jnp.where(i <= j, upper, lower)
        put_pair(out, 3, product, feature, p, q)
        lane = iota((ROWS, 128), 1)
        on = jnp.where(i == j, lower, 0.0)
        ends = jnp.zeros((ROWS, 128), jnp.float32)
        at = iota((ROWS, 256), 1)
        for c in range(3):
            mine = on[c * ROWS : (c + 1) * ROWS]
            for d in range(3):
                inside = (at >= d * ROWS) & (at < (d + 1) * ROWS)
                value = jnp.sum(jnp.where(inside, mine, 0.0), axis=1, keepdims=True)
                ends = jnp.where(lane == 64 + 3 * c + d, value, ends)
        out[3, 3 * ROWS :] += ends


def det_four(rows):
    a00, a01, a02, a03 = rows[0]
    a10, a11, a12, a13 = rows[1]
    a20, a21, a22, a23 = rows[2]
    a30, a31, a32, a33 = rows[3]
    s0 = a00 * a11 - a10 * a01
    s1 = a00 * a12 - a10 * a02
    s2 = a00 * a13 - a10 * a03
    s3 = a01 * a12 - a11 * a02
    s4 = a01 * a13 - a11 * a03
    s5 = a02 * a13 - a12 * a03
    t5 = a22 * a33 - a32 * a23
    t4 = a21 * a33 - a31 * a23
    t3 = a21 * a32 - a31 * a22
    t2 = a20 * a33 - a30 * a23
    t1 = a20 * a32 - a30 * a22
    t0 = a20 * a31 - a30 * a21
    return s0 * t5 - s1 * t4 + s2 * t3 + s3 * t2 - s4 * t1 + s5 * t0


def quaternion_fit(moment, spread_rows, spread_cols):
    sxx, sxy, sxz, syx, syy, syz, szx, szy, szz = moment
    coef_two = -2.0 * sum(m * m for m in moment)
    det_three = (
        sxx * (syy * szz - syz * szy)
        - sxy * (syx * szz - syz * szx)
        + sxz * (syx * szy - syy * szx)
    )
    coef_one = -8.0 * det_three
    rows = [
        [sxx + syy + szz, syz - szy, szx - sxz, sxy - syx],
        [syz - szy, sxx - syy - szz, sxy + syx, szx + sxz],
        [szx - sxz, sxy + syx, -sxx + syy - szz, syz + szy],
        [sxy - syx, szx + sxz, syz + szy, -sxx - syy + szz],
    ]
    coef_zero = det_four(rows)
    lam = 0.5 * (spread_rows + spread_cols)
    for turn in range(NEWTON):
        square = lam * lam
        value = (square + coef_two) * square + coef_one * lam + coef_zero
        slope = 4.0 * square * lam + 2.0 * coef_two * lam + coef_one
        lam = lam - value / slope
    return spread_rows + spread_cols - 2.0 * lam


def square_tile(x):
    return jnp.concatenate([x, jnp.zeros((128 - x.shape[0], 128), jnp.float32)], axis=0)


def fit_kernel(flags, parts, first, second):
    diagonal, swap = flags[1] == 1, flags[2] == 1
    total = parts[0]
    for a in range(1, SIDE):
        total = total + parts[a]
    lane, row = iota((ROWS, 128), 1), iota((ROWS, 128), 0)
    rest = total[3 * ROWS :]

    gathered = jnp.zeros((ROWS, 128), jnp.float32)
    for a in range(SIDE):
        tile = jnp.where((lane >= 48) & (lane < 56), parts[a, 3 * ROWS :], 0.0)
        gathered = gathered + pltpu.roll(tile, (8 * a - 48) % 128, 1)

    def per_sender(which):
        pick = (iota((128, 128), 0) == 8 * iota((128, 128), 1) + which).astype(jnp.float32)
        return jnp.dot(gathered, pick, precision=EXACT, preferred_element_type=jnp.float32)

    mass = per_sender(3)
    whole = jnp.sum(mass, axis=1, keepdims=True)

    def offsets(base):
        out = []
        for c in range(3):
            mean = per_sender(base + c)
            centroid = jnp.sum(mass * mean, axis=1, keepdims=True) / whole
            out.append(jnp.where(lane < SIDE, mean - centroid, 0.0))
        return out

    off_p, off_q = offsets(0), offsets(4)

    def spread(off, at):
        within = jnp.sum(jnp.where(lane == at, rest, 0.0), axis=1, keepdims=True)
        between = jnp.sum(mass * sum(o * o for o in off), axis=1, keepdims=True)
        return (within + between) / whole

    spread_p, spread_q = spread(off_p, 56), spread(off_q, 57)

    def as_row(column):
        return jnp.sum(jnp.where(row == lane, column, 0.0), axis=0, keepdims=True)

    upper = row <= lane
    corner = lane == ROWS
    row_p, row_q = as_row(spread_p), as_row(spread_q)
    spread_rows = jnp.where(upper, spread_p, jnp.where(diagonal, spread_q, spread_p))
    spread_cols = jnp.where(upper, jnp.where(diagonal, row_p, row_q), row_q)
    spread_rows = jnp.where(corner, spread_q, spread_rows)
    spread_cols = jnp.where(corner, spread_q, spread_cols)

    low_rows = jnp.concatenate([mass * jnp.where(diagonal, q, p) for p, q in zip(off_p, off_q)], axis=0)
    up_rows = jnp.concatenate([mass * p for p in off_p], axis=0)
    moment = []
    between = []
    for d in range(3):
        up = dot_t(up_rows, square_tile(jnp.where(diagonal, off_p[d], off_q[d])))
        low = dot_t(low_rows, square_tile(off_q[d]))
        between.append((up, low))
    for c in range(3):
        main = total[c * ROWS : (c + 1) * ROWS]
        tail = pltpu.roll(rest, (32 - 16 * c) % 128, 1)
        shifted = [main, pltpu.roll(main, 128 - 48, 1), jnp.where(lane < 32, pltpu.roll(main, 128 - 96, 1), tail)]
        for d in range(3):
            up, low = (b[c * ROWS : (c + 1) * ROWS] for b in between[d])
            value = shifted[d] + jnp.where(upper, up, low)
            end = jnp.sum(jnp.where(lane == 64 + 3 * c + d, rest, 0.0), axis=1, keepdims=True)
            end = end + jnp.sum(mass * off_q[c] * off_q[d], axis=1, keepdims=True)
            moment.append(jnp.where(corner, end, value) / whole)
    msd = quaternion_fit(moment, spread_rows, spread_cols)
    corner_value = jnp.sum(jnp.where(corner, msd, 0.0), axis=1, keepdims=True)
    msd = jnp.where(lane < ROWS, msd, 0.0)
    turned = square_tile(msd).T[:ROWS]
    plain_a = jnp.where(diagonal, jnp.where(upper, msd, turned), msd)
    mirrored = jnp.where(row > lane, msd, jnp.where(row == lane, corner_value, turned))
    plain_b = jnp.where(diagonal, mirrored, turned)
    first[...] = jnp.where(swap, plain_b, plain_a)
    second[...] = jnp.where(swap, plain_a, plain_b)


def join_kernel(flags, first, second, out):
    lane = iota((ROWS, 128), 1)
    a, b = first[...], second[...]
    left = jnp.where(flags[3] == 1, b, a)
    right = jnp.where(flags[3] == 1, a, b)
    out[...] = jnp.where(lane < ROWS, left, pltpu.roll(right, ROWS, 1))[:, : 2 * ROWS]


def on_device(coords, weights):
    first, second, swapped, half = routes()
    frame, atom = lax.axis_index("frame"), lax.axis_index("atom")
    place = frame * SIDE + atom
    last = (atom == SIDE - 1).astype(jnp.int32)
    column, z = frame // SIDE, frame % SIDE
    late_diagonal = (z >= SIDE // 2).astype(jnp.int32)
    table = jnp.asarray(np.array(swapped) + 2 * np.array(half), jnp.int32)[place]
    build_flags = jnp.stack([column, late_diagonal]).astype(jnp.int32)
    fit_flags = jnp.stack([column, late_diagonal * last, table % 2, table // 2]).astype(jnp.int32)
    mass = weights.astype(jnp.float32)[None, :]

    def along(block, distance):
        route = [
            (c * SIDE + (k + distance) % SIDE, c * SIDE + k) for c in range(2) for k in range(SIDE)
        ]
        return lax.ppermute(block, "frame", route)

    def across(block):
        return lax.ppermute(block, "frame", [((f + SIDE) % (2 * SIDE), f) for f in range(2 * SIDE)])

    own = coords.reshape(3 * ROWS, coords.shape[2])
    plus4 = along(own, 4)
    minus2 = along(own, -2)
    other0 = across(own)
    minus3 = along(minus2, -1)
    other2 = across(minus2)
    other3 = across(minus3)
    plus5 = along(plus4, 1)

    atoms = own.shape[1]
    slots = len(EARLY) + len(LATE)
    result = jax.ShapeDtypeStruct((slots, 4 * ROWS, 128), jnp.float32)

    def scratch(n):
        return [
            pltpu.VMEM((n, 256, atoms), jnp.float32),
            pltpu.VMEM((n, 3 * ROWS, atoms), jnp.float32),
            pltpu.VMEM((n, 2, ROWS, 128), jnp.float32),
        ]

    smem = pl.BlockSpec(memory_space=pltpu.SMEM)
    params = pltpu.CompilerParams(vmem_limit_bytes=VMEM_LIMIT)
    whole = lambda *shape: pl.BlockSpec(shape, lambda i: (0,) * len(shape))
    block_spec = whole(3 * ROWS, atoms)
    pair_flops = 2 * 3 * ROWS * 256 * atoms * 6
    partial = pl.pallas_call(
        early_kernel,
        grid=(1,),
        out_shape=result,
        in_specs=[whole(1, atoms)] + [block_spec] * 7,
        out_specs=whole(len(EARLY), 4 * ROWS, 128),
        scratch_shapes=scratch(7),
        compiler_params=params,
        cost_estimate=pl.CostEstimate(flops=12 * pair_flops, bytes_accessed=4_000_000, transcendentals=0),
    )(mass, own, minus2, minus3, plus4, other0, other2, other3)
    partial = pl.pallas_call(
        late_kernel,
        grid=(1,),
        out_shape=result,
        in_specs=[smem, whole(1, atoms)] + [block_spec] * 5 + [pl.BlockSpec(memory_space=pl.ANY)],
        out_specs=pl.BlockSpec((len(LATE), 4 * ROWS, 128), lambda i: (len(EARLY) // len(LATE), 0, 0)),
        scratch_shapes=scratch(5),
        input_output_aliases={7: 0},
        compiler_params=params,
        cost_estimate=pl.CostEstimate(flops=6 * pair_flops, bytes_accessed=2_000_000, transcendentals=0),
    )(build_flags, mass, own, minus3, plus5, other0, other3, partial)

    parts = lax.all_to_all(partial, "atom", 0, 0, tiled=True)

    block = jax.ShapeDtypeStruct((ROWS, 128), jnp.float32)
    vmem = pl.BlockSpec(memory_space=pltpu.VMEM)
    one, two = pl.pallas_call(
        fit_kernel,
        out_shape=(block, block),
        in_specs=[smem, vmem],
        out_specs=(vmem, vmem),
        compiler_params=params,
    )(fit_flags, parts)
    one = lax.ppermute(one, ("frame", "atom"), list(enumerate(first)))
    two = lax.ppermute(two, ("frame", "atom"), list(enumerate(second)))
    return pl.pallas_call(
        join_kernel,
        out_shape=jax.ShapeDtypeStruct((ROWS, 2 * ROWS), jnp.float32),
        in_specs=[smem, vmem, vmem],
        out_specs=vmem,
        compiler_params=params,
    )(fit_flags, one, two)


def solution(mesh):
    placed = (P(None, "frame", "atom"), P("atom"))
    return jax.shard_map(
        on_device, mesh=mesh, in_specs=placed, out_specs=P("frame", "atom"), check_vma=False
    )
```

time: 616 us -> 136 us (0.22)
  the two profiles are of different devices: /device:TPU:7 before, /device:TPU:126 now
where the time goes in v1:
time: 136 us; the launch traced here: 135 us
  waiting for transfers between devices  57.8 us (42%)
  starting transfers between devices  53.4 us (39%)
  Pallas kernels  18.5 us (14%)
  between operations  2.76 us (2%)
  local copies, waits for them, and re-layouts  2.22 us (2%)
    ppermute x4, waiting for transfers between devices, along(): return lax.ppermute(block, 'frame', route)  31.1 us
    ppermute x4, starting transfers between devices, along(): return lax.ppermute(block, 'frame', route)  20.5 us
    ppermute x1, starting transfers between devices, on_device(): one = lax.ppermute(one, ('frame', 'atom'), list(enumerate(first)))  15.2 us
    all_to_all x1, waiting for transfers between devices, on_device(): parts = lax.all_to_all(partial, 'atom', 0, 0, tiled=True)  14.7 us
    ppermute x1, waiting for transfers between devices, on_device(): two = lax.ppermute(two, ('frame', 'atom'), list(enumerate(second)))  11.9 us
    pallas_call x1, Pallas kernels, on_device(): pl.pallas_call(early_kernel, grid=(1,), out_shape=result, in_specs=[whole...  10.6 us
    ppermute x3, starting transfers between devices, across(): lax.ppermute(block, 'frame', [((f + SIDE) % (2 * SIDE), f) for f in range...  8.58 us
    all_to_all x1, starting transfers between devices, on_device(): parts = lax.all_to_all(partial, 'atom', 0, 0, tiled=True)  7.11 us
  transfers between devices with their start and end apart: 10, of which 4 were waited for; matrix products, arithmetic and copies ran while one was open for 2% of the time, Pallas kernels for 8%

profile of v1, /device:TPU:126, one launch (start us, length us, event | category | flops | bytes accessed | tf_op | source)
XLA Modules:
  0.0 135.4 jit_solution(10165541389125909663)
XLA Ops:
  0.0 6.4 %collective-permute-start = (f32[144,512]{1,0:T(8,128)}, f32[144,512]{1,0:T(8,128)S(1)}, u32[]{:S(2)}, u32[]{:S(2)}) collective-permute-start(f32[144,512]{1,0:T(8,128)} %bitcast.10), channel_id=1, source_target_pairs={{224,0},{240,16},{0,32},{16,48},{32,64},{48,80},{64,96},{80,112},{... | collective-permute-start | bytes 884744 | tf_op jit(solution)/shard_map/ppermute | solution.py:320
  6.4 11.2 %collective-permute-done.refs_1_ = f32[144,512]{1,0:T(8,128)S(1)} collective-permute-done((f32[144,512]{1,0:T(8,128)}, f32[144,512]{1,0:T(8,128)S(1)}, u32[]{:S(2)}, u32[]{:S(2)}) %collective-permute-start) | collective-permute-done | bytes 294944 | tf_op jit(solution)/shard_map/ppermute | solution.py:320
  17.6 6.7 %collective-permute-start.1 = (f32[144,512]{1,0:T(8,128)S(1)}, f32[144,512]{1,0:T(8,128)S(1)}, u32[]{:S(2)}, u32[]{:S(2)}) collective-permute-start(f32[144,512]{1,0:T(8,128)S(1)} %collective-permute-done.refs_1_), channel_id=1, source_target_pairs={{240,0},{0,16},{16,32},{32,48},{48,64},{64,80},{80,96},{96,112},{1... | collective-permute-start | bytes 884744 | tf_op jit(solution)/shard_map/ppermute | solution.py:320
  24.3 5.6 %collective-permute-start.2 = (f32[144,512]{1,0:T(8,128)}, f32[144,512]{1,0:T(8,128)S(1)}, u32[]{:S(2)}, u32[]{:S(2)}) collective-permute-start(f32[144,512]{1,0:T(8,128)} %bitcast.11), channel_id=1, source_target_pairs={{64,0},{80,16},{96,32},{112,48},{128,64},{144,80},{160,96},{176,11... | collective-permute-start | bytes 884744 | tf_op jit(solution)/shard_map/ppermute | solution.py:320
  29.9 2.7 %collective-permute-start.4 = (f32[144,512]{1,0:T(8,128)}, f32[144,512]{1,0:T(8,128)S(1)}, u32[]{:S(2)}, u32[]{:S(2)}) collective-permute-start(f32[144,512]{1,0:T(8,128)} %bitcast.12), channel_id=1, source_target_pairs={{256,0},{272,16},{288,32},{304,48},{320,64},{336,80},{352,96},{368... | collective-permute-start | bytes 884744 | tf_op jit(solution)/shard_map/ppermute | solution.py:323
  32.6 3.1 %collective-permute-start.6 = (f32[144,512]{1,0:T(8,128)S(1)}, f32[144,512]{1,0:T(8,128)S(1)}, u32[]{:S(2)}, u32[]{:S(2)}) collective-permute-start(f32[144,512]{1,0:T(8,128)S(1)} %collective-permute-done.refs_1_), channel_id=1, source_target_pairs={{256,0},{272,16},{288,32},{304,48},{320,64},{336,80},{352,96},{368... | collective-permute-start | bytes 884744 | tf_op jit(solution)/shard_map/ppermute | solution.py:323
  35.7 0.0 collective-permute-done.1.refs_2_.refs_1_
  35.7 2.7 %collective-permute-start.5 = (f32[144,512]{1,0:T(8,128)S(1)}, f32[144,512]{1,0:T(8,128)S(1)}, u32[]{:S(2)}, u32[]{:S(2)}) collective-permute-start(f32[144,512]{1,0:T(8,128)S(1)} %collective-permute-done.1.refs_2_.refs_1_), channel_id=1, source_target_pairs={{256,0},{272,16},{288,32},{304,48},{320,64},{336,80},{352,96},{368... | collective-permute-start | bytes 884744 | tf_op jit(solution)/shard_map/ppermute | solution.py:323
  38.5 19.9 %collective-permute-done.2.refs_3_ = f32[144,512]{1,0:T(8,128)S(1)} collective-permute-done((f32[144,512]{1,0:T(8,128)}, f32[144,512]{1,0:T(8,128)S(1)}, u32[]{:S(2)}, u32[]{:S(2)}) %collective-permute-start.2) | collective-permute-done | bytes 294944 | tf_op jit(solution)/shard_map/ppermute | solution.py:320
  58.4 1.9 %collective-permute-start.3 = (f32[144,512]{1,0:T(8,128)S(1)}, f32[144,512]{1,0:T(8,128)S(1)}, u32[]{:S(2)}, u32[]{:S(2)}) collective-permute-start(f32[144,512]{1,0:T(8,128)S(1)} %collective-permute-done.2.refs_3_), channel_id=1, source_target_pairs={{16,0},{32,16},{48,32},{64,48},{80,64},{96,80},{112,96},{128,112},... | collective-permute-start | bytes 884744 | tf_op jit(solution)/shard_map/ppermute | solution.py:320
  60.3 0.1 pad_add_fusion.1.flags
  60.4 0.7 convert_element_type.8
  61.1 0.0 collective-permute-done.4.refs_4_.refs_3_
  61.1 0.0 collective-permute-done.6.refs_5_
  61.1 0.0 collective-permute-done.5.refs_6_.refs_4_
  61.1 0.0 copy-start
  61.1 1.0 copy-done
  62.0 10.6 %shard_map.37.refs_5_ = f32[16,192,128]{2,1,0:T(8,128)} custom-call(f32[1,512]{1,0:T(1,128)S(1)} %bitcast.8, f32[144,512]{1,0:T(8,128)S(1)} %bitcast.13, f32[144,512]{1,0:T(8,128)S(1)} %collective-permute-done.refs_1_, f32[144,512]{1,0:T(8,128)S(1)} %collective-permute-done.1.refs_2_.refs_1_, f32[144,512]{1,0:T(8,128)S(1)} %collective-permute-done.2.refs_3_, ...), custom_call_target="tpu_custom_call" | custom-call | flops 2717908992 | bytes 4000000 | tf_op jit(solution)/shard_map/pallas_call | solution.py:350
  72.6 0.0 collective-permute-done.3.refs_2_
  72.6 4.7 %shard_map.38 = f32[16,192,128]{2,1,0:T(8,128)} custom-call(s32[2]{0:T(128)S(1)} %pad_add_fusion.1.flags, f32[1,512]{1,0:T(1,128)S(1)} %bitcast.9, f32[144,512]{1,0:T(8,128)S(1)} %bitcast.14, f32[144,512]{1,0:T(8,128)S(1)} %collective-permute-done.1.refs_2_.refs_1_, f32[144,512]{1,0:T(8,128)S(1)} %collective-permute-done.3.refs_2_, ...), custom_call_target="tpu_custom_call", output_to_operand_aliasing={{}: (7, {})} | custom-call | flops 1358954496 | bytes 2000000 | tf_op jit(solution)/shard_map/pallas_call | solution.py:360
  77.3 7.1 %all-to-all-start = ((f32[16,192,128]{2,1,0:T(8,128)}), f32[16,192,128]{2,1,0:T(8,128)S(1)}, u32[]{:S(2)}, u32[]{:S(2)}) async-start(f32[16,192,128]{2,1,0:T(8,128)} %shard_map.38), calls=%async_computation | async-start | bytes 3145728 | tf_op jit(solution)/shard_map/all_to_all | solution.py:372
  84.4 1.3 dynamic_slice.3
  88.3 0.1 pad_add_fusion.flags
  88.4 14.7 %all-to-all-done.parts = f32[16,192,128]{2,1,0:T(8,128)S(1)} async-done(((f32[16,192,128]{2,1,0:T(8,128)}), f32[16,192,128]{2,1,0:T(8,128)S(1)}, u32[]{:S(2)}, u32[]{:S(2)}) %all-to-all-start) | async-done | bytes 1572896 | tf_op jit(solution)/shard_map/all_to_all | solution.py:372
  103.1 1.9 %shard_map.39 = (f32[48,128]{1,0:T(8,128)S(1)}, f32[48,128]{1,0:T(8,128)S(1)}) custom-call(s32[4]{0:T(128)S(1)} %pad_add_fusion.flags, f32[16,192,128]{2,1,0:T(8,128)S(1)} %all-to-all-done.parts), custom_call_target="tpu_custom_call" | custom-call | tf_op jit(solution)/shard_map/pallas_call | solution.py:376
  105.1 15.2 %collective-permute-start.7 = (f32[48,128]{1,0:T(8,128)S(1)}, f32[48,128]{1,0:T(8,128)S(1)}, u32[]{:S(2)}, u32[]{:S(2)}) collective-permute-start(f32[48,128]{1,0:T(8,128)S(1)} %get-tuple-element.7), channel_id=1, source_target_pairs={{0,215},{1,224},{2,208},{3,2},{4,226},{5,210},{6,238},{7,15},{8,14... | collective-permute-start | bytes 73736 | tf_op jit(solution)/shard_map/ppermute | solution.py:383
  120.3 1.9 %collective-permute-start.8 = (f32[48,128]{1,0:T(8,128)S(1)}, f32[48,128]{1,0:T(8,128)S(1)}, u32[]{:S(2)}, u32[]{:S(2)}) collective-permute-start(f32[48,128]{1,0:T(8,128)S(1)} %get-tuple-element.8), channel_id=1, source_target_pairs={{0,230},{1,7},{2,6},{3,64},{4,71},{5,70},{6,471},{7,480},{8,464},{... | collective-permute-start | bytes 73736 | tf_op jit(solution)/shard_map/ppermute | solution.py:384
  122.3 0.0 collective-permute-done.7.first
  122.3 11.9 %collective-permute-done.8.second = f32[48,128]{1,0:T(8,128)S(1)} collective-permute-done((f32[48,128]{1,0:T(8,128)S(1)}, f32[48,128]{1,0:T(8,128)S(1)}, u32[]{:S(2)}, u32[]{:S(2)}) %collective-permute-start.8) | collective-permute-done | bytes 24608 | tf_op jit(solution)/shard_map/ppermute | solution.py:384
  134.2 1.2 shard_map.40
Async XLA Ops:
  0.0 17.6 %collective-permute-start = (f32[144,512]{1,0:T(8,128)}, f32[144,512]{1,0:T(8,128)S(1)}, u32[]{:S(2)}, u32[]{:S(2)}) collective-permute-start(f32[144,512]{1,0:T(8,128)} %bitcast.10), channel_id=1, source_target_pairs={{224,0},{240,16},{0,32},{16,48},{32,64},{48,80},{64,96},{80,112},{... | collective-permute-start | bytes 884744 | tf_op jit(solution)/shard_map/ppermute | solution.py:320
  17.6 18.1 %collective-permute-start.1 = (f32[144,512]{1,0:T(8,128)S(1)}, f32[144,512]{1,0:T(8,128)S(1)}, u32[]{:S(2)}, u32[]{:S(2)}) collective-permute-start(f32[144,512]{1,0:T(8,128)S(1)} %collective-permute-done.refs_1_), channel_id=1, source_target_pairs={{240,0},{0,16},{16,32},{32,48},{48,64},{64,80},{80,96},{96,112},{1... | collective-permute-start | bytes 884744 | tf_op jit(solution)/shard_map/ppermute | solution.py:320
  24.3 34.1 %collective-permute-start.2 = (f32[144,512]{1,0:T(8,128)}, f32[144,512]{1,0:T(8,128)S(1)}, u32[]{:S(2)}, u32[]{:S(2)}) collective-permute-start(f32[144,512]{1,0:T(8,128)} %bitcast.11), channel_id=1, source_target_pairs={{64,0},{80,16},{96,32},{112,48},{128,64},{144,80},{160,96},{176,11... | collective-permute-start | bytes 884744 | tf_op jit(solution)/shard_map/ppermute | solution.py:320
  29.9 31.2 %collective-permute-start.4 = (f32[144,512]{1,0:T(8,128)}, f32[144,512]{1,0:T(8,128)S(1)}, u32[]{:S(2)}, u32[]{:S(2)}) collective-permute-start(f32[144,512]{1,0:T(8,128)} %bitcast.12), channel_id=1, source_target_pairs={{256,0},{272,16},{288,32},{304,48},{320,64},{336,80},{352,96},{368... | collective-permute-start | bytes 884744 | tf_op jit(solution)/shard_map/ppermute | solution.py:323
  32.6 28.5 %collective-permute-start.6 = (f32[144,512]{1,0:T(8,128)S(1)}, f32[144,512]{1,0:T(8,128)S(1)}, u32[]{:S(2)}, u32[]{:S(2)}) collective-permute-start(f32[144,512]{1,0:T(8,128)S(1)} %collective-permute-done.refs_1_), channel_id=1, source_target_pairs={{256,0},{272,16},{288,32},{304,48},{320,64},{336,80},{352,96},{368... | collective-permute-start | bytes 884744 | tf_op jit(solution)/shard_map/ppermute | solution.py:323
  35.7 25.3 %collective-permute-start.5 = (f32[144,512]{1,0:T(8,128)S(1)}, f32[144,512]{1,0:T(8,128)S(1)}, u32[]{:S(2)}, u32[]{:S(2)}) collective-permute-start(f32[144,512]{1,0:T(8,128)S(1)} %collective-permute-done.1.refs_2_.refs_1_), channel_id=1, source_target_pairs={{256,0},{272,16},{288,32},{304,48},{320,64},{336,80},{352,96},{368... | collective-permute-start | bytes 884744 | tf_op jit(solution)/shard_map/ppermute | solution.py:323
  58.4 14.2 %collective-permute-start.3 = (f32[144,512]{1,0:T(8,128)S(1)}, f32[144,512]{1,0:T(8,128)S(1)}, u32[]{:S(2)}, u32[]{:S(2)}) collective-permute-start(f32[144,512]{1,0:T(8,128)S(1)} %collective-permute-done.2.refs_3_), channel_id=1, source_target_pairs={{16,0},{32,16},{48,32},{64,48},{80,64},{96,80},{112,96},{128,112},... | collective-permute-start | bytes 884744 | tf_op jit(solution)/shard_map/ppermute | solution.py:320
  61.1 1.0 copy-start
  77.3 25.8 %all-to-all-start = ((f32[16,192,128]{2,1,0:T(8,128)}), f32[16,192,128]{2,1,0:T(8,128)S(1)}, u32[]{:S(2)}, u32[]{:S(2)}) async-start(f32[16,192,128]{2,1,0:T(8,128)} %shard_map.38), calls=%async_computation | async-start | bytes 3145728 | tf_op jit(solution)/shard_map/all_to_all | solution.py:372
  105.1 17.2 %collective-permute-start.7 = (f32[48,128]{1,0:T(8,128)S(1)}, f32[48,128]{1,0:T(8,128)S(1)}, u32[]{:S(2)}, u32[]{:S(2)}) collective-permute-start(f32[48,128]{1,0:T(8,128)S(1)} %get-tuple-element.7), channel_id=1, source_target_pairs={{0,215},{1,224},{2,208},{3,2},{4,226},{5,210},{6,238},{7,15},{8,14... | collective-permute-start | bytes 73736 | tf_op jit(solution)/shard_map/ppermute | solution.py:383
  120.3 13.9 %collective-permute-start.8 = (f32[48,128]{1,0:T(8,128)S(1)}, f32[48,128]{1,0:T(8,128)S(1)}, u32[]{:S(2)}, u32[]{:S(2)}) collective-permute-start(f32[48,128]{1,0:T(8,128)S(1)} %get-tuple-element.8), channel_id=1, source_target_pairs={{0,230},{1,7},{2,6},{3,64},{4,71},{5,70},{6,471},{7,480},{8,464},{... | collective-permute-start | bytes 73736 | tf_op jit(solution)/shard_map/ppermute | solution.py:384

commit v2 on v1

--- a/solution.py
+++ b/solution.py
@@ -14,13 +14,13 @@
 EXACT = lax.Precision.HIGHEST
 VMEM_LIMIT = 40 * 1024 * 1024
 
-OWN = (0, -2, -3, 4, 5)
-OTHER = (0, -2, -3)
+OWN = (0, -1, -3, 4, 5)
+OTHER = (0, -1, -3)
 EARLY = (
-    (2, 1), (1, 0), (2, 0), (0, 3), (1, 3), (2, 3),
-    (1, 7), (0, 6), (0, 7), (3, 5), (3, 6), (3, 7),
+    (1, 0), (2, 1), (2, 0), (0, 3), (1, 3), (2, 3),
+    (0, 6), (1, 7), (0, 7), (3, 5), (3, 6), (3, 7),
 )
-LATE = ((0, 4), (4, 5), (2, 7), (2, 4))
+LATE = ((1, 4), (4, 6), (2, 7), (2, 4))
 
 
 def frame_block(column, z, index):
@@ -79,16 +79,30 @@
     return lax.dot_general(a, b, (((1,), (1,)), ((), ())), precision=EXACT, preferred_element_type=jnp.float32)
 
 
+def product(a, b):
+    return lax.dot_general(a, b, (((1,), (1,)), ((), ())), preferred_element_type=jnp.float32)
+
+
+def halves(x):
+    high = x.astype(jnp.bfloat16)
+    return high, (x - high.astype(jnp.float32)).astype(jnp.bfloat16)
+
+
 def stage(block, mass, slot, centered, weighted, feature):
     x = block[...]
+    atoms = x.shape[1]
     local = jnp.sum(mass)
     mean = jnp.sum(x * mass, axis=1, keepdims=True) / local
     x = x - mean
     wx = x * mass
     square = jnp.sum(wx * x, axis=1, keepdims=True)
-    centered[slot, : 3 * ROWS] = x
-    centered[slot, 3 * ROWS :] = jnp.zeros((256 - 3 * ROWS, x.shape[1]), jnp.float32)
-    weighted[slot] = wx
+    high, low = halves(x)
+    for k, part in enumerate((high, low, high)):
+        centered[slot, : 3 * ROWS, k * atoms : (k + 1) * atoms] = part
+    centered[slot, 3 * ROWS :] = jnp.zeros((256 - 3 * ROWS, 3 * atoms), jnp.bfloat16)
+    high, low = halves(wx)
+    for k, part in enumerate((high, high, low)):
+        weighted[slot, :, k * atoms : (k + 1) * atoms] = part
     lane = iota((ROWS, 128), 1)
     square = square[:ROWS] + square[ROWS : 2 * ROWS] + square[2 * ROWS :]
     row, column = jnp.zeros((ROWS, 128), jnp.float32), jnp.zeros((ROWS, 128), jnp.float32)
@@ -107,14 +121,14 @@
     return tail[:ROWS] + pltpu.roll(tail[ROWS : 2 * ROWS], 16, 1) + pltpu.roll(tail[2 * ROWS :], 32, 1)
 
 
-def put_pair(out, slot, product, feature, p, q):
-    out[slot, : 3 * ROWS] = product[:, :128]
-    out[slot, 3 * ROWS :] = rest_of(product[:, 128:]) + feature[p, 0] + feature[q, 1]
+def put_pair(out, slot, value, feature, p, q):
+    out[slot, : 3 * ROWS] = value[:, :128]
+    out[slot, 3 * ROWS :] = rest_of(value[:, 128:]) + feature[p, 0] + feature[q, 1]
 
 
 def early_kernel(mass_ref, *refs):
     blocks, (out, centered, weighted, feature) = refs[:7], refs[7:]
-    mass = mass_ref[...]
+    mass = mass_ref[...].astype(jnp.float32)
     index = (0, 1, 2, 3, 5, 6, 7)
     for k, block in enumerate(blocks):
         stage(block, mass, k, centered, weighted, feature)
@@ -123,7 +137,7 @@
 
     def body(step, carry):
         p, q = lookup(step, rows), lookup(step, columns)
-        put_pair(out, step, dot_t(weighted[p], centered[q]), feature, p, q)
+        put_pair(out, step, product(weighted[p], centered[q]), feature, p, q)
         return carry
 
     lax.fori_loop(0, len(EARLY), body, 0)
@@ -131,8 +145,8 @@
 
 def late_kernel(flags, mass_ref, *refs):
     blocks, (_, out, centered, weighted, feature) = refs[:5], refs[5:]
-    mass = mass_ref[...]
-    index = (0, 2, 4, 5, 7)
+    mass = mass_ref[...].astype(jnp.float32)
+    index = (1, 2, 4, 6, 7)
     for k, block in enumerate(blocks):
         stage(block, mass, k, centered, weighted, feature)
     column, diagonal = flags[0], flags[1]
@@ -142,7 +156,7 @@
     def body(step, carry):
         p, q = lookup(step, rows), lookup(step, columns)
         p = jnp.where((step == 2) & (column == 1), jnp.int32(index.index(4)), p)
-        put_pair(out, step, dot_t(weighted[p], centered[q]), feature, p, q)
+        put_pair(out, step, product(weighted[p], centered[q]), feature, p, q)
         return carry
 
     lax.fori_loop(0, len(LATE), body, 0)
@@ -150,10 +164,9 @@
     @pl.when(diagonal == 1)
     def _():
         p, q = rows[3], columns[3]
-        upper, lower = dot_t(weighted[p], centered[p]), dot_t(weighted[q], centered[q])
+        upper, lower = product(weighted[p], centered[p]), product(weighted[q], centered[q])
         i, j = iota((3 * ROWS, 256), 0) % ROWS, iota((3 * ROWS, 256), 1) % ROWS
-        product = jnp.where(i <= j, upper, lower)
-        put_pair(out, 3, product, feature, p, q)
+        put_pair(out, 3, jnp.where(i <= j, upper, lower), feature, p, q)
         lane = iota((ROWS, 128), 1)
         on = jnp.where(i == j, lower, 0.0)
         ends = jnp.zeros((ROWS, 128), jnp.float32)
@@ -311,7 +324,7 @@
     table = jnp.asarray(np.array(swapped) + 2 * np.array(half), jnp.int32)[place]
     build_flags = jnp.stack([column, late_diagonal]).astype(jnp.int32)
     fit_flags = jnp.stack([column, late_diagonal * last, table % 2, table // 2]).astype(jnp.int32)
-    mass = weights.astype(jnp.float32)[None, :]
+    mass = weights[None, :]
 
     def along(block, distance):
         route = [
@@ -324,10 +337,10 @@
 
     own = coords.reshape(3 * ROWS, coords.shape[2])
     plus4 = along(own, 4)
-    minus2 = along(own, -2)
+    minus3 = along(own, -3)
+    minus1 = along(own, -1)
     other0 = across(own)
-    minus3 = along(minus2, -1)
-    other2 = across(minus2)
+    other1 = across(minus1)
     other3 = across(minus3)
     plus5 = along(plus4, 1)
 
@@ -337,8 +350,8 @@
 
     def scratch(n):
         return [
-            pltpu.VMEM((n, 256, atoms), jnp.float32),
-            pltpu.VMEM((n, 3 * ROWS, atoms), jnp.float32),
+            pltpu.VMEM((n, 256, 3 * atoms), jnp.bfloat16),
+            pltpu.VMEM((n, 3 * ROWS, 3 * atoms), jnp.bfloat16),
             pltpu.VMEM((n, 2, ROWS, 128), jnp.float32),
         ]
 
@@ -346,7 +359,7 @@
     params = pltpu.CompilerParams(vmem_limit_bytes=VMEM_LIMIT)
     whole = lambda *shape: pl.BlockSpec(shape, lambda i: (0,) * len(shape))
     block_spec = whole(3 * ROWS, atoms)
-    pair_flops = 2 * 3 * ROWS * 256 * atoms * 6
+    pair_flops = 2 * 3 * ROWS * 256 * atoms * 3
     partial = pl.pallas_call(
         early_kernel,
         grid=(1,),
@@ -356,7 +369,7 @@
         scratch_shapes=scratch(7),
         compiler_params=params,
         cost_estimate=pl.CostEstimate(flops=12 * pair_flops, bytes_accessed=4_000_000, transcendentals=0),
-    )(mass, own, minus2, minus3, plus4, other0, other2, other3)
+    )(mass, own, minus1, minus3, plus4, other0, other1, other3)
     partial = pl.pallas_call(
         late_kernel,
         grid=(1,),
@@ -367,7 +380,7 @@
         input_output_aliases={7: 0},
         compiler_params=params,
         cost_estimate=pl.CostEstimate(flops=6 * pair_flops, bytes_accessed=2_000_000, transcendentals=0),
-    )(build_flags, mass, own, minus3, plus5, other0, other3, partial)
+    )(build_flags, mass, minus1, minus3, plus5, other1, other3, partial)
 
     parts = lax.all_to_all(partial, "atom", 0, 0, tiled=True)
 

time: 136 us -> 118 us (0.87)
  waiting for transfers between devices: 57.8 us -> 45.7 us
  Pallas kernels: 18.5 us -> 15.2 us
  starting transfers between devices: 53.4 us -> 50.4 us
    ppermute x4, waiting for transfers between devices: 31.1 us -> 17.5 us  [along(): return lax.ppermute(block, 'frame', route)]
    pallas_call x1, Pallas kernels: 10.6 us -> 7.98 us  [on_device(): pl.pallas_call(early_kernel, grid=(1,), out_shape=result, in_specs=[whole...]
    ppermute x3, waiting for transfers between devices: 0.01 us -> 2.5 us  [across(): lax.ppermute(block, 'frame', [((f + SIDE) % (2 * SIDE), f) for f in range...]
    ppermute x4, starting transfers between devices: 20.5 us -> 18.4 us  [along(): return lax.ppermute(block, 'frame', route)]
  transfers between devices with their start and end apart: 10 -> 10, of which waited for: 4 -> 6; matrix products, arithmetic and copies ran while one was open for 2% -> 1% of each run, Pallas kernels for 8% -> 7%
where the time goes in v2:
time: 118 us; the launch traced here: 117 us
  starting transfers between devices  50.4 us (43%)
  waiting for transfers between devices  45.7 us (39%)
  Pallas kernels  15.2 us (13%)
  local copies, waits for them, and re-layouts  2.91 us (2%)
  between operations  2.75 us (2%)
    ppermute x4, starting transfers between devices, along(): return lax.ppermute(block, 'frame', route)  18.4 us
    ppermute x4, waiting for transfers between devices, along(): return lax.ppermute(block, 'frame', route)  17.5 us
    ppermute x1, starting transfers between devices, on_device(): one = lax.ppermute(one, ('frame', 'atom'), list(enumerate(first)))  14.8 us
    all_to_all x1, waiting for transfers between devices, on_device(): parts = lax.all_to_all(partial, 'atom', 0, 0, tiled=True)  14.7 us
    ppermute x1, waiting for transfers between devices, on_device(): two = lax.ppermute(two, ('frame', 'atom'), list(enumerate(second)))  11 us
    ppermute x3, starting transfers between devices, across(): lax.ppermute(block, 'frame', [((f + SIDE) % (2 * SIDE), f) for f in range...  8.19 us
    pallas_call x1, Pallas kernels, on_device(): pl.pallas_call(early_kernel, grid=(1,), out_shape=result, in_specs=[whole...  7.98 us
    all_to_all x1, starting transfers between devices, on_device(): parts = lax.all_to_all(partial, 'atom', 0, 0, tiled=True)  7.11 us
  transfers between devices with their start and end apart: 10, of which 6 were waited for; matrix products, arithmetic and copies ran while one was open for 1% of the time, Pallas kernels for 7%

profile of v2, /device:TPU:126, one launch (start us, length us, event | category | flops | bytes accessed | tf_op | source)
XLA Modules:
  0.0 117.1 jit_solution(7113281690934331825)
XLA Ops:
  0.0 7.7 %collective-permute-start.1 = (f32[144,512]{1,0:T(8,128)}, f32[144,512]{1,0:T(8,128)S(1)}, u32[]{:S(2)}, u32[]{:S(2)}) collective-permute-start(f32[144,512]{1,0:T(8,128)} %bitcast.10), channel_id=1, source_target_pairs={{208,0},{224,16},{240,32},{0,48},{16,64},{32,80},{48,96},{64,112},... | collective-permute-start | bytes 884744 | tf_op jit(solution)/shard_map/ppermute | solution.py:333
  7.7 3.8 %collective-permute-start = (f32[144,512]{1,0:T(8,128)}, f32[144,512]{1,0:T(8,128)S(1)}, u32[]{:S(2)}, u32[]{:S(2)}) collective-permute-start(f32[144,512]{1,0:T(8,128)} %bitcast.11), channel_id=1, source_target_pairs={{240,0},{0,16},{16,32},{32,48},{48,64},{64,80},{80,96},{96,112},{1... | collective-permute-start | bytes 884744 | tf_op jit(solution)/shard_map/ppermute | solution.py:333
  11.6 2.3 %collective-permute-start.2 = (f32[144,512]{1,0:T(8,128)}, f32[144,512]{1,0:T(8,128)S(1)}, u32[]{:S(2)}, u32[]{:S(2)}) collective-permute-start(f32[144,512]{1,0:T(8,128)} %bitcast.12), channel_id=1, source_target_pairs={{64,0},{80,16},{96,32},{112,48},{128,64},{144,80},{160,96},{176,11... | collective-permute-start | bytes 884744 | tf_op jit(solution)/shard_map/ppermute | solution.py:333
  13.9 2.7 %collective-permute-start.6 = (f32[144,512]{1,0:T(8,128)}, f32[144,512]{1,0:T(8,128)S(1)}, u32[]{:S(2)}, u32[]{:S(2)}) collective-permute-start(f32[144,512]{1,0:T(8,128)} %bitcast.13), channel_id=1, source_target_pairs={{256,0},{272,16},{288,32},{304,48},{320,64},{336,80},{352,96},{368... | collective-permute-start | bytes 884744 | tf_op jit(solution)/shard_map/ppermute | solution.py:336
  16.6 11.3 %collective-permute-done.1.refs_2_.refs_1_ = f32[144,512]{1,0:T(8,128)S(1)} collective-permute-done((f32[144,512]{1,0:T(8,128)}, f32[144,512]{1,0:T(8,128)S(1)}, u32[]{:S(2)}, u32[]{:S(2)}) %collective-permute-start.1) | collective-permute-done | bytes 294944 | tf_op jit(solution)/shard_map/ppermute | solution.py:333
  27.9 2.7 %collective-permute-start.5 = (f32[144,512]{1,0:T(8,128)S(1)}, f32[144,512]{1,0:T(8,128)S(1)}, u32[]{:S(2)}, u32[]{:S(2)}) collective-permute-start(f32[144,512]{1,0:T(8,128)S(1)} %collective-permute-done.1.refs_2_.refs_1_), channel_id=1, source_target_pairs={{256,0},{272,16},{288,32},{304,48},{320,64},{336,80},{352,96},{368... | collective-permute-start | bytes 884744 | tf_op jit(solution)/shard_map/ppermute | solution.py:336
  30.7 2.5 %collective-permute-done.refs_1_.refs_0_ = f32[144,512]{1,0:T(8,128)S(1)} collective-permute-done((f32[144,512]{1,0:T(8,128)}, f32[144,512]{1,0:T(8,128)S(1)}, u32[]{:S(2)}, u32[]{:S(2)}) %collective-permute-start) | collective-permute-done | bytes 294944 | tf_op jit(solution)/shard_map/ppermute | solution.py:333
  33.2 2.7 %collective-permute-start.4 = (f32[144,512]{1,0:T(8,128)S(1)}, f32[144,512]{1,0:T(8,128)S(1)}, u32[]{:S(2)}, u32[]{:S(2)}) collective-permute-start(f32[144,512]{1,0:T(8,128)S(1)} %collective-permute-done.refs_1_.refs_0_), channel_id=1, source_target_pairs={{256,0},{272,16},{288,32},{304,48},{320,64},{336,80},{352,96},{368... | collective-permute-start | bytes 884744 | tf_op jit(solution)/shard_map/ppermute | solution.py:336
  35.9 0.0 collective-permute-done.2.refs_3_
  35.9 4.5 %collective-permute-start.3 = (f32[144,512]{1,0:T(8,128)S(1)}, f32[144,512]{1,0:T(8,128)S(1)}, u32[]{:S(2)}, u32[]{:S(2)}) collective-permute-start(f32[144,512]{1,0:T(8,128)S(1)} %collective-permute-done.2.refs_3_), channel_id=1, source_target_pairs={{16,0},{32,16},{48,32},{64,48},{80,64},{96,80},{112,96},{128,112},... | collective-permute-start | bytes 884744 | tf_op jit(solution)/shard_map/ppermute | solution.py:333
  40.4 0.1 pad_add_fusion.1.flags
  40.5 0.0 collective-permute-done.6.refs_4_
  40.5 0.0 collective-permute-done.5.refs_6_.refs_4_
  40.5 2.5 %collective-permute-done.4.refs_5_.refs_3_ = f32[144,512]{1,0:T(8,128)S(1)} collective-permute-done((f32[144,512]{1,0:T(8,128)S(1)}, f32[144,512]{1,0:T(8,128)S(1)}, u32[]{:S(2)}, u32[]{:S(2)}) %collective-permute-start.4) | collective-permute-done | bytes 294944 | tf_op jit(solution)/shard_map/ppermute | solution.py:336
  43.0 0.0 copy-start
  43.0 0.7 copy-done
  43.7 0.0 copy-start.1
  43.7 1.0 copy-done.1
  44.6 8.0 %shard_map.37.refs_5_ = f32[16,192,128]{2,1,0:T(8,128)} custom-call(s32[1,512]{1,0:T(1,128)S(1)} %bitcast.8, f32[144,512]{1,0:T(8,128)S(1)} %bitcast.14, f32[144,512]{1,0:T(8,128)S(1)} %collective-permute-done.refs_1_.refs_0_, f32[144,512]{1,0:T(8,128)S(1)} %collective-permute-done.1.refs_2_.refs_1_, f32[144,512]{1,0:T(8,128)S(1)} %collective-permute-done.2.refs_3_, ...), custom_call_target="tpu_custom_call" | custom-call | flops 1358954496 | bytes 4000000 | tf_op jit(solution)/shard_map/pallas_call | solution.py:363
  52.6 3.7 %collective-permute-done.3.refs_2_ = f32[144,512]{1,0:T(8,128)S(1)} collective-permute-done((f32[144,512]{1,0:T(8,128)S(1)}, f32[144,512]{1,0:T(8,128)S(1)}, u32[]{:S(2)}, u32[]{:S(2)}) %collective-permute-start.3) | collective-permute-done | bytes 294944 | tf_op jit(solution)/shard_map/ppermute | solution.py:333
  56.3 4.1 %shard_map.38 = f32[16,192,128]{2,1,0:T(8,128)} custom-call(s32[2]{0:T(128)S(1)} %pad_add_fusion.1.flags, s32[1,512]{1,0:T(1,128)S(1)} %bitcast.9, f32[144,512]{1,0:T(8,128)S(1)} %collective-permute-done.refs_1_.refs_0_, f32[144,512]{1,0:T(8,128)S(1)} %collective-permute-done.1.refs_2_.refs_1_, ...), custom_call_target="tpu_custom_call", output_to_operand_aliasing={{}: (7, {})} | custom-call | flops 679477248 | bytes 2000000 | tf_op jit(solution)/shard_map/pallas_call | solution.py:373
  60.4 7.1 %all-to-all-start = ((f32[16,192,128]{2,1,0:T(8,128)}), f32[16,192,128]{2,1,0:T(8,128)S(1)}, u32[]{:S(2)}, u32[]{:S(2)}) async-start(f32[16,192,128]{2,1,0:T(8,128)} %shard_map.38), calls=%async_computation | async-start | bytes 3145728 | tf_op jit(solution)/shard_map/all_to_all | solution.py:385
  67.5 1.3 %dynamic_slice.3 = s32[1]{0:T(128)} dynamic-slice(s32[512]{0:T(512)} %constant.61.clone, s32[]{:T(128)S(6)} %select_n.23), dynamic_slice_sizes={1} | dynamic-slice | bytes 12 | tf_op jit(solution)/shard_map/dynamic_slice | solution.py:324
  71.4 0.1 pad_add_fusion.flags
  71.4 14.7 %all-to-all-done.parts = f32[16,192,128]{2,1,0:T(8,128)S(1)} async-done(((f32[16,192,128]{2,1,0:T(8,128)}), f32[16,192,128]{2,1,0:T(8,128)S(1)}, u32[]{:S(2)}, u32[]{:S(2)}) %all-to-all-start) | async-done | bytes 1572896 | tf_op jit(solution)/shard_map/all_to_all | solution.py:385
  86.2 1.9 %shard_map.39 = (f32[48,128]{1,0:T(8,128)S(1)}, f32[48,128]{1,0:T(8,128)S(1)}) custom-call(s32[4]{0:T(128)S(1)} %pad_add_fusion.flags, f32[16,192,128]{2,1,0:T(8,128)S(1)} %all-to-all-done.parts), custom_call_target="tpu_custom_call" | custom-call | tf_op jit(solution)/shard_map/pallas_call | solution.py:389
  88.1 14.8 %collective-permute-start.7 = (f32[48,128]{1,0:T(8,128)S(1)}, f32[48,128]{1,0:T(8,128)S(1)}, u32[]{:S(2)}, u32[]{:S(2)}) collective-permute-start(f32[48,128]{1,0:T(8,128)S(1)} %get-tuple-element.7), channel_id=1, source_target_pairs={{0,240},{1,215},{2,208},{3,2},{4,242},{5,210},{6,15},{7,254},{8,14... | collective-permute-start | bytes 73736 | tf_op jit(solution)/shard_map/ppermute | solution.py:396
  102.9 1.9 %collective-permute-start.8 = (f32[48,128]{1,0:T(8,128)S(1)}, f32[48,128]{1,0:T(8,128)S(1)}, u32[]{:S(2)}, u32[]{:S(2)}) collective-permute-start(f32[48,128]{1,0:T(8,128)S(1)} %get-tuple-element.8), channel_id=1, source_target_pairs={{0,7},{1,246},{2,6},{3,64},{4,71},{5,70},{6,496},{7,471},{8,464},{... | collective-permute-start | bytes 73736 | tf_op jit(solution)/shard_map/ppermute | solution.py:397
  104.9 0.0 collective-permute-done.7.first
  104.9 11.0 %collective-permute-done.8.second = f32[48,128]{1,0:T(8,128)S(1)} collective-permute-done((f32[48,128]{1,0:T(8,128)S(1)}, f32[48,128]{1,0:T(8,128)S(1)}, u32[]{:S(2)}, u32[]{:S(2)}) %collective-permute-start.8) | collective-permute-done | bytes 24608 | tf_op jit(solution)/shard_map/ppermute | solution.py:397
  115.9 1.2 %shard_map.40 = f32[48,96]{1,0:T(8,128)} custom-call(s32[4]{0:T(128)S(1)} %pad_add_fusion.flags, f32[48,128]{1,0:T(8,128)S(1)} %collective-permute-done.7.first, f32[48,128]{1,0:T(8,128)S(1)} %collective-permute-done.8.second), custom_call_target="tpu_custom_call" | custom-call | tf_op jit(solution)/shard_map/pallas_call | solution.py:398
Async XLA Ops:
  0.0 27.9 %collective-permute-start.1 = (f32[144,512]{1,0:T(8,128)}, f32[144,512]{1,0:T(8,128)S(1)}, u32[]{:S(2)}, u32[]{:S(2)}) collective-permute-start(f32[144,512]{1,0:T(8,128)} %bitcast.10), channel_id=1, source_target_pairs={{208,0},{224,16},{240,32},{0,48},{16,64},{32,80},{48,96},{64,112},... | collective-permute-start | bytes 884744 | tf_op jit(solution)/shard_map/ppermute | solution.py:333
  7.7 25.4 %collective-permute-start = (f32[144,512]{1,0:T(8,128)}, f32[144,512]{1,0:T(8,128)S(1)}, u32[]{:S(2)}, u32[]{:S(2)}) collective-permute-start(f32[144,512]{1,0:T(8,128)} %bitcast.11), channel_id=1, source_target_pairs={{240,0},{0,16},{16,32},{32,48},{48,64},{64,80},{80,96},{96,112},{1... | collective-permute-start | bytes 884744 | tf_op jit(solution)/shard_map/ppermute | solution.py:333
  11.6 24.3 %collective-permute-start.2 = (f32[144,512]{1,0:T(8,128)}, f32[144,512]{1,0:T(8,128)S(1)}, u32[]{:S(2)}, u32[]{:S(2)}) collective-permute-start(f32[144,512]{1,0:T(8,128)} %bitcast.12), channel_id=1, source_target_pairs={{64,0},{80,16},{96,32},{112,48},{128,64},{144,80},{160,96},{176,11... | collective-permute-start | bytes 884744 | tf_op jit(solution)/shard_map/ppermute | solution.py:333
  13.9 26.6 %collective-permute-start.6 = (f32[144,512]{1,0:T(8,128)}, f32[144,512]{1,0:T(8,128)S(1)}, u32[]{:S(2)}, u32[]{:S(2)}) collective-permute-start(f32[144,512]{1,0:T(8,128)} %bitcast.13), channel_id=1, source_target_pairs={{256,0},{272,16},{288,32},{304,48},{320,64},{336,80},{352,96},{368... | collective-permute-start | bytes 884744 | tf_op jit(solution)/shard_map/ppermute | solution.py:336
  27.9 12.6 %collective-permute-start.5 = (f32[144,512]{1,0:T(8,128)S(1)}, f32[144,512]{1,0:T(8,128)S(1)}, u32[]{:S(2)}, u32[]{:S(2)}) collective-permute-start(f32[144,512]{1,0:T(8,128)S(1)} %collective-permute-done.1.refs_2_.refs_1_), channel_id=1, source_target_pairs={{256,0},{272,16},{288,32},{304,48},{320,64},{336,80},{352,96},{368... | collective-permute-start | bytes 884744 | tf_op jit(solution)/shard_map/ppermute | solution.py:336
  33.2 9.8 %collective-permute-start.4 = (f32[144,512]{1,0:T(8,128)S(1)}, f32[144,512]{1,0:T(8,128)S(1)}, u32[]{:S(2)}, u32[]{:S(2)}) collective-permute-start(f32[144,512]{1,0:T(8,128)S(1)} %collective-permute-done.refs_1_.refs_0_), channel_id=1, source_target_pairs={{256,0},{272,16},{288,32},{304,48},{320,64},{336,80},{352,96},{368... | collective-permute-start | bytes 884744 | tf_op jit(solution)/shard_map/ppermute | solution.py:336
  35.9 20.4 %collective-permute-start.3 = (f32[144,512]{1,0:T(8,128)S(1)}, f32[144,512]{1,0:T(8,128)S(1)}, u32[]{:S(2)}, u32[]{:S(2)}) collective-permute-start(f32[144,512]{1,0:T(8,128)S(1)} %collective-permute-done.2.refs_3_), channel_id=1, source_target_pairs={{16,0},{32,16},{48,32},{64,48},{80,64},{96,80},{112,96},{128,112},... | collective-permute-start | bytes 884744 | tf_op jit(solution)/shard_map/ppermute | solution.py:333
  43.0 0.7 copy-start
  43.7 1.0 copy-start.1
  60.4 25.8 %all-to-all-start = ((f32[16,192,128]{2,1,0:T(8,128)}), f32[16,192,128]{2,1,0:T(8,128)S(1)}, u32[]{:S(2)}, u32[]{:S(2)}) async-start(f32[16,192,128]{2,1,0:T(8,128)} %shard_map.38), calls=%async_computation | async-start | bytes 3145728 | tf_op jit(solution)/shard_map/all_to_all | solution.py:385
  88.1 16.7 %collective-permute-start.7 = (f32[48,128]{1,0:T(8,128)S(1)}, f32[48,128]{1,0:T(8,128)S(1)}, u32[]{:S(2)}, u32[]{:S(2)}) collective-permute-start(f32[48,128]{1,0:T(8,128)S(1)} %get-tuple-element.7), channel_id=1, source_target_pairs={{0,240},{1,215},{2,208},{3,2},{4,242},{5,210},{6,15},{7,254},{8,14... | collective-permute-start | bytes 73736 | tf_op jit(solution)/shard_map/ppermute | solution.py:396
  102.9 12.9 %collective-permute-start.8 = (f32[48,128]{1,0:T(8,128)S(1)}, f32[48,128]{1,0:T(8,128)S(1)}, u32[]{:S(2)}, u32[]{:S(2)}) collective-permute-start(f32[48,128]{1,0:T(8,128)S(1)} %get-tuple-element.8), channel_id=1, source_target_pairs={{0,7},{1,246},{2,6},{3,64},{4,71},{5,70},{6,496},{7,471},{8,464},{... | collective-permute-start | bytes 73736 | tf_op jit(solution)/shard_map/ppermute | solution.py:397

commit v3 on v2

--- a/solution.py
+++ b/solution.py
@@ -14,13 +14,18 @@
 EXACT = lax.Precision.HIGHEST
 VMEM_LIMIT = 40 * 1024 * 1024
 
-OWN = (0, -1, -3, 4, 5)
-OTHER = (0, -1, -3)
+OWN = (0, 2, 4, -3, -4)
+OTHER = (2, 4, -3)
+STACK = (3, 0, 4, 2)
 EARLY = (
-    (1, 0), (2, 1), (2, 0), (0, 3), (1, 3), (2, 3),
-    (0, 6), (1, 7), (0, 7), (3, 5), (3, 6), (3, 7),
+    (3, 1), (0, 1), (4, 1),
+    (3, 2), (0, 2), (4, 2),
+    (3, 5), (0, 5), (4, 5),
+    (0, 3), (4, 3),
+    (0, 7), (4, 7), (2, 7),
 )
-LATE = ((1, 4), (4, 6), (2, 7), (2, 4))
+DIAGONAL = EARLY.index((4, 2))
+LATE = ((0, 6), (2, 6))
 
 
 def frame_block(column, z, index):
@@ -34,10 +39,10 @@
     for column in range(2):
         for z in range(SIDE):
             for slot, (p, q) in enumerate(EARLY + LATE):
-                if slot == len(EARLY) + 2 and column == 1:
+                if slot == len(EARLY) + 1 and column == 1:
                     p = 4
                 a, b = frame_block(column, z, p), frame_block(column, z, q)
-                if slot == len(EARLY) + 3 and z >= SIDE // 2:
+                if slot == DIAGONAL and z >= SIDE // 2:
                     ends.append(((a, a), (b, b)))
                 else:
                     ends.append(((a, b), (b, a)))
@@ -88,96 +93,108 @@
     return high, (x - high.astype(jnp.float32)).astype(jnp.bfloat16)
 
 
-def stage(block, mass, slot, centered, weighted, feature):
-    x = block[...]
-    atoms = x.shape[1]
+def stage(x, mass):
     local = jnp.sum(mass)
     mean = jnp.sum(x * mass, axis=1, keepdims=True) / local
     x = x - mean
     wx = x * mass
     square = jnp.sum(wx * x, axis=1, keepdims=True)
+    return x, wx, mean, square[:ROWS] + square[ROWS : 2 * ROWS] + square[2 * ROWS :], local
+
+
+def stage_rows(block, mass, at, weighted, feature):
+    atoms = block.shape[1]
+    _, wx, mean, square, local = stage(block[...], mass)
+    high, low = halves(wx)
+    for k, part in enumerate((high, high, low)):
+        weighted[at * 3 * ROWS : (at + 1) * 3 * ROWS, k * atoms : (k + 1) * atoms] = part
+    lane = iota((ROWS, 128), 1)
+    out = jnp.where(lane == 51, local, jnp.where(lane == 56, square, 0.0))
+    for c in range(3):
+        out = jnp.where(lane == 48 + c, mean[c * ROWS : (c + 1) * ROWS], out)
+    feature[at] = out
+
+
+def stage_columns(block, mass, at, centered, feature):
+    atoms = block.shape[1]
+    x, _, mean, square, _ = stage(block[...], mass)
     high, low = halves(x)
     for k, part in enumerate((high, low, high)):
-        centered[slot, : 3 * ROWS, k * atoms : (k + 1) * atoms] = part
-    centered[slot, 3 * ROWS :] = jnp.zeros((256 - 3 * ROWS, 3 * atoms), jnp.bfloat16)
-    high, low = halves(wx)
-    for k, part in enumerate((high, high, low)):
-        weighted[slot, :, k * atoms : (k + 1) * atoms] = part
+        centered[at, : 3 * ROWS, k * atoms : (k + 1) * atoms] = part
     lane = iota((ROWS, 128), 1)
-    square = square[:ROWS] + square[ROWS : 2 * ROWS] + square[2 * ROWS :]
-    row, column = jnp.zeros((ROWS, 128), jnp.float32), jnp.zeros((ROWS, 128), jnp.float32)
+    out = jnp.where(lane == 57, square, 0.0)
     for c in range(3):
-        part = mean[c * ROWS : (c + 1) * ROWS]
-        row = jnp.where(lane == 48 + c, part, row)
-        column = jnp.where(lane == 52 + c, part, column)
-    row = jnp.where(lane == 51, local, row)
-    row = jnp.where(lane == 56, square, row)
-    column = jnp.where(lane == 57, square, column)
-    feature[slot, 0] = row
-    feature[slot, 1] = column
+        out = jnp.where(lane == 52 + c, mean[c * ROWS : (c + 1) * ROWS], out)
+    feature[at] = out
 
 
 def rest_of(tail):
+    tail = jnp.where(iota((3 * ROWS, 128), 1) < 16, tail, 0.0)
     return tail[:ROWS] + pltpu.roll(tail[ROWS : 2 * ROWS], 16, 1) + pltpu.roll(tail[2 * ROWS :], 32, 1)
 
 
-def put_pair(out, slot, value, feature, p, q):
+def put_pair(out, slot, value, feature):
     out[slot, : 3 * ROWS] = value[:, :128]
-    out[slot, 3 * ROWS :] = rest_of(value[:, 128:]) + feature[p, 0] + feature[q, 1]
-
-
-def early_kernel(mass_ref, *refs):
-    blocks, (out, centered, weighted, feature) = refs[:7], refs[7:]
+    out[slot, 3 * ROWS :] = rest_of(value[:, 128:]) + feature
+
+
+def put_group(out, first, pairs, weighted, columns, row_feature, column_feature):
+    start = STACK.index(pairs[0][0])
+    rows = weighted[start * 3 * ROWS : (start + len(pairs)) * 3 * ROWS]
+    values = product(rows, columns)
+    for k in range(len(pairs)):
+        value = values[k * 3 * ROWS : (k + 1) * 3 * ROWS]
+        put_pair(out, first + k, value, row_feature[start + k] + column_feature)
+
+
+def early_kernel(flags, mass_ref, *refs):
+    blocks, (out, weighted, centered, row_feature, column_feature) = refs[:7], refs[7:]
+    blocks = dict(zip((0, 1, 2, 3, 4, 5, 7), blocks))
     mass = mass_ref[...].astype(jnp.float32)
-    index = (0, 1, 2, 3, 5, 6, 7)
-    for k, block in enumerate(blocks):
-        stage(block, mass, k, centered, weighted, feature)
-    rows = [index.index(p) for p, _ in EARLY]
-    columns = [index.index(q) for _, q in EARLY]
-
-    def body(step, carry):
-        p, q = lookup(step, rows), lookup(step, columns)
-        put_pair(out, step, product(weighted[p], centered[q]), feature, p, q)
-        return carry
-
-    lax.fori_loop(0, len(EARLY), body, 0)
-
-
-def late_kernel(flags, mass_ref, *refs):
-    blocks, (_, out, centered, weighted, feature) = refs[:5], refs[5:]
-    mass = mass_ref[...].astype(jnp.float32)
-    index = (1, 2, 4, 6, 7)
-    for k, block in enumerate(blocks):
-        stage(block, mass, k, centered, weighted, feature)
-    column, diagonal = flags[0], flags[1]
-    rows = [index.index(p) for p, _ in LATE]
-    columns = [index.index(q) for _, q in LATE]
-
-    def body(step, carry):
-        p, q = lookup(step, rows), lookup(step, columns)
-        p = jnp.where((step == 2) & (column == 1), jnp.int32(index.index(4)), p)
-        put_pair(out, step, product(weighted[p], centered[q]), feature, p, q)
-        return carry
-
-    lax.fori_loop(0, len(LATE), body, 0)
-
-    @pl.when(diagonal == 1)
+    for at, k in enumerate(STACK):
+        stage_rows(blocks[k], mass, at, weighted, row_feature)
+    order = (1, 2, 5, 3, 7)
+    for at, k in enumerate(order):
+        stage_columns(blocks[k], mass, at, centered, column_feature)
+    first = 0
+    for at, k in enumerate(order):
+        pairs = [pair for pair in EARLY if pair[1] == k]
+        assert tuple(EARLY[first : first + len(pairs)]) == tuple(pairs)
+        assert tuple(STACK[STACK.index(pairs[0][0]) :][: len(pairs)]) == tuple(p for p, _ in pairs)
+        put_group(out, first, pairs, weighted, centered[at], row_feature, column_feature[at])
+        first += len(pairs)
+
+    @pl.when(flags[1] == 1)
     def _():
-        p, q = rows[3], columns[3]
-        upper, lower = product(weighted[p], centered[p]), product(weighted[q], centered[q])
+        stage_columns(blocks[4], mass, 5, centered, column_feature)
+        p, q = STACK.index(4), STACK.index(2)
+        upper = product(weighted[p * 3 * ROWS : (p + 1) * 3 * ROWS], centered[5])
+        lower = product(weighted[q * 3 * ROWS : (q + 1) * 3 * ROWS], centered[order.index(2)])
         i, j = iota((3 * ROWS, 256), 0) % ROWS, iota((3 * ROWS, 256), 1) % ROWS
-        put_pair(out, 3, jnp.where(i <= j, upper, lower), feature, p, q)
+        at = iota((ROWS, 256), 1)
+        on = jnp.where((i == j) & (iota((3 * ROWS, 256), 1) < 3 * ROWS), lower, 0.0)
         lane = iota((ROWS, 128), 1)
-        on = jnp.where(i == j, lower, 0.0)
-        ends = jnp.zeros((ROWS, 128), jnp.float32)
-        at = iota((ROWS, 256), 1)
+        ends = row_feature[p] + column_feature[order.index(2)]
         for c in range(3):
             mine = on[c * ROWS : (c + 1) * ROWS]
             for d in range(3):
                 inside = (at >= d * ROWS) & (at < (d + 1) * ROWS)
                 value = jnp.sum(jnp.where(inside, mine, 0.0), axis=1, keepdims=True)
                 ends = jnp.where(lane == 64 + 3 * c + d, value, ends)
-        out[3, 3 * ROWS :] += ends
+        put_pair(out, DIAGONAL, jnp.where(i <= j, upper, lower), ends)
+
+
+def late_kernel(flags, mass_ref, *refs):
+    blocks, (_, out, weighted, centered, row_feature, column_feature) = refs[:4], refs[4:]
+    mass = mass_ref[...].astype(jnp.float32)
+    for at, block in enumerate(blocks[:3]):
+        stage_rows(block, mass, at, weighted, row_feature)
+    stage_columns(blocks[3], mass, 0, centered, column_feature)
+    values = product(weighted[...], centered[0])
+    put_pair(out, 0, values[: 3 * ROWS], row_feature[0] + column_feature[0])
+    other = flags[0] == 1
+    value = jnp.where(other, values[3 * ROWS : 6 * ROWS], values[6 * ROWS :])
+    put_pair(out, 1, value, jnp.where(other, row_feature[1], row_feature[2]) + column_feature[0])
 
 
 def det_four(rows):
@@ -318,7 +335,7 @@
     first, second, swapped, half = routes()
     frame, atom = lax.axis_index("frame"), lax.axis_index("atom")
     place = frame * SIDE + atom
-    last = (atom == SIDE - 1).astype(jnp.int32)
+    last = (atom == DIAGONAL).astype(jnp.int32)
     column, z = frame // SIDE, frame % SIDE
     late_diagonal = (z >= SIDE // 2).astype(jnp.int32)
     table = jnp.asarray(np.array(swapped) + 2 * np.array(half), jnp.int32)[place]
@@ -336,23 +353,24 @@
         return lax.ppermute(block, "frame", [((f + SIDE) % (2 * SIDE), f) for f in range(2 * SIDE)])
 
     own = coords.reshape(3 * ROWS, coords.shape[2])
-    plus4 = along(own, 4)
+    plus2 = along(own, 2)
     minus3 = along(own, -3)
-    minus1 = along(own, -1)
-    other0 = across(own)
-    other1 = across(minus1)
+    plus4 = along(plus2, 2)
+    minus4 = along(minus3, -1)
+    other2 = across(plus2)
     other3 = across(minus3)
-    plus5 = along(plus4, 1)
+    other4 = across(plus4)
 
     atoms = own.shape[1]
     slots = len(EARLY) + len(LATE)
     result = jax.ShapeDtypeStruct((slots, 4 * ROWS, 128), jnp.float32)
 
-    def scratch(n):
+    def scratch(rows, columns):
         return [
-            pltpu.VMEM((n, 256, 3 * atoms), jnp.bfloat16),
-            pltpu.VMEM((n, 3 * ROWS, 3 * atoms), jnp.bfloat16),
-            pltpu.VMEM((n, 2, ROWS, 128), jnp.float32),
+            pltpu.VMEM((rows * 3 * ROWS, 3 * atoms), jnp.bfloat16),
+            pltpu.VMEM((columns, 256, 3 * atoms), jnp.bfloat16),
+            pltpu.VMEM((rows, ROWS, 128), jnp.float32),
+            pltpu.VMEM((columns, ROWS, 128), jnp.float32),
         ]
 
     smem = pl.BlockSpec(memory_space=pltpu.SMEM)
@@ -364,23 +382,23 @@
         early_kernel,
         grid=(1,),
         out_shape=result,
-        in_specs=[whole(1, atoms)] + [block_spec] * 7,
+        in_specs=[smem, whole(1, atoms)] + [block_spec] * 7,
         out_specs=whole(len(EARLY), 4 * ROWS, 128),
-        scratch_shapes=scratch(7),
+        scratch_shapes=scratch(4, 6),
         compiler_params=params,
-        cost_estimate=pl.CostEstimate(flops=12 * pair_flops, bytes_accessed=4_000_000, transcendentals=0),
-    )(mass, own, minus1, minus3, plus4, other0, other1, other3)
+        cost_estimate=pl.CostEstimate(flops=14 * pair_flops, bytes_accessed=4_000_000, transcendentals=0),
+    )(build_flags, mass, own, plus2, plus4, minus3, minus4, other2, other3)
     partial = pl.pallas_call(
         late_kernel,
         grid=(1,),
         out_shape=result,
-        in_specs=[smem, whole(1, atoms)] + [block_spec] * 5 + [pl.BlockSpec(memory_space=pl.ANY)],
+        in_specs=[smem, whole(1, atoms)] + [block_spec] * 4 + [pl.BlockSpec(memory_space=pl.ANY)],
         out_specs=pl.BlockSpec((len(LATE), 4 * ROWS, 128), lambda i: (len(EARLY) // len(LATE), 0, 0)),
-        scratch_shapes=scratch(5),
-        input_output_aliases={7: 0},
+        scratch_shapes=scratch(3, 1),
+        input_output_aliases={6: 0},
         compiler_params=params,
-        cost_estimate=pl.CostEstimate(flops=6 * pair_flops, bytes_accessed=2_000_000, transcendentals=0),
-    )(build_flags, mass, minus1, minus3, plus5, other1, other3, partial)
+        cost_estimate=pl.CostEstimate(flops=3 * pair_flops, bytes_accessed=2_000_000, transcendentals=0),
+    )(build_flags, mass, own, minus4, plus4, other4, partial)
 
     parts = lax.all_to_all(partial, "atom", 0, 0, tiled=True)
 

time: 118 us -> 111 us (0.941)
  the two profiles are of different devices: /device:TPU:126 before, /device:TPU:32 now
where the time goes in v3:
time: 111 us; the launch traced here: 110 us
  waiting for transfers between devices  49.1 us (44%)
  starting transfers between devices  45.8 us (41%)
  Pallas kernels  9.53 us (9%)
  local copies, waits for them, and re-layouts  2.91 us (3%)
  between operations  2.76 us (2%)
    ppermute x4, starting transfers between devices, along(): return lax.ppermute(block, 'frame', route)  22.4 us
    all_to_all x1, waiting for transfers between devices, on_device(): parts = lax.all_to_all(partial, 'atom', 0, 0, tiled=True)  19.7 us
    ppermute x4, waiting for transfers between devices, along(): return lax.ppermute(block, 'frame', route)  16.8 us
    ppermute x3, starting transfers between devices, across(): lax.ppermute(block, 'frame', [((f + SIDE) % (2 * SIDE), f) for f in range...  9.23 us
    ppermute x1, waiting for transfers between devices, on_device(): two = lax.ppermute(two, ('frame', 'atom'), list(enumerate(second)))  9.08 us
    all_to_all x1, starting transfers between devices, on_device(): parts = lax.all_to_all(partial, 'atom', 0, 0, tiled=True)  6.74 us
    ppermute x1, starting transfers between devices, on_device(): one = lax.ppermute(one, ('frame', 'atom'), list(enumerate(first)))  5.49 us
    pallas_call x1, Pallas kernels, on_device(): pl.pallas_call(early_kernel, grid=(1,), out_shape=result, in_specs=[smem,...  4.23 us
  transfers between devices with their start and end apart: 10, of which 7 were waited for; matrix products, arithmetic and copies ran while one was open for 1% of the time, Pallas kernels for 4%

profile of v3, /device:TPU:32, one launch (start us, length us, event | category | flops | bytes accessed | tf_op | source)
XLA Modules:
  0.0 110.3 jit_solution(8088204390567394767)
XLA Ops:
  0.0 10.9 %collective-permute-start.2 = (f32[144,512]{1,0:T(8,128)}, f32[144,512]{1,0:T(8,128)S(1)}, u32[]{:S(2)}, u32[]{:S(2)}) collective-permute-start(f32[144,512]{1,0:T(8,128)} %bitcast.8), channel_id=1, source_target_pairs={{32,0},{48,16},{64,32},{80,48},{96,64},{112,80},{128,96},{144,112}... | collective-permute-start | bytes 884744 | tf_op jit(solution)/shard_map/ppermute | solution.py:350
  10.9 1.9 %collective-permute-start = (f32[144,512]{1,0:T(8,128)}, f32[144,512]{1,0:T(8,128)S(1)}, u32[]{:S(2)}, u32[]{:S(2)}) collective-permute-start(f32[144,512]{1,0:T(8,128)} %bitcast.9), channel_id=1, source_target_pairs={{208,0},{224,16},{240,32},{0,48},{16,64},{32,80},{48,96},{64,112},... | collective-permute-start | bytes 884744 | tf_op jit(solution)/shard_map/ppermute | solution.py:350
  12.9 7.6 %collective-permute-done.2.refs_1_ = f32[144,512]{1,0:T(8,128)S(1)} collective-permute-done((f32[144,512]{1,0:T(8,128)}, f32[144,512]{1,0:T(8,128)S(1)}, u32[]{:S(2)}, u32[]{:S(2)}) %collective-permute-start.2) | collective-permute-done | bytes 294944 | tf_op jit(solution)/shard_map/ppermute | solution.py:350
  20.5 6.4 %collective-permute-start.3 = (f32[144,512]{1,0:T(8,128)S(1)}, f32[144,512]{1,0:T(8,128)S(1)}, u32[]{:S(2)}, u32[]{:S(2)}) collective-permute-start(f32[144,512]{1,0:T(8,128)S(1)} %collective-permute-done.2.refs_1_), channel_id=1, source_target_pairs={{32,0},{48,16},{64,32},{80,48},{96,64},{112,80},{128,96},{144,112}... | collective-permute-start | bytes 884744 | tf_op jit(solution)/shard_map/ppermute | solution.py:350
  27.0 3.4 %collective-permute-start.5 = (f32[144,512]{1,0:T(8,128)S(1)}, f32[144,512]{1,0:T(8,128)S(1)}, u32[]{:S(2)}, u32[]{:S(2)}) collective-permute-start(f32[144,512]{1,0:T(8,128)S(1)} %collective-permute-done.2.refs_1_), channel_id=1, source_target_pairs={{256,0},{272,16},{288,32},{304,48},{320,64},{336,80},{352,96},{368... | collective-permute-start | bytes 884744 | tf_op jit(solution)/shard_map/ppermute | solution.py:353
  30.4 0.0 collective-permute-done.refs_3_
  30.4 2.4 %collective-permute-start.6 = (f32[144,512]{1,0:T(8,128)S(1)}, f32[144,512]{1,0:T(8,128)S(1)}, u32[]{:S(2)}, u32[]{:S(2)}) collective-permute-start(f32[144,512]{1,0:T(8,128)S(1)} %collective-permute-done.refs_3_), channel_id=1, source_target_pairs={{256,0},{272,16},{288,32},{304,48},{320,64},{336,80},{352,96},{368... | collective-permute-start | bytes 884744 | tf_op jit(solution)/shard_map/ppermute | solution.py:353
  32.8 3.2 %collective-permute-start.1 = (f32[144,512]{1,0:T(8,128)S(1)}, f32[144,512]{1,0:T(8,128)S(1)}, u32[]{:S(2)}, u32[]{:S(2)}) collective-permute-start(f32[144,512]{1,0:T(8,128)S(1)} %collective-permute-done.refs_3_), channel_id=1, source_target_pairs={{240,0},{0,16},{16,32},{32,48},{48,64},{64,80},{80,96},{96,112},{1... | collective-permute-start | bytes 884744 | tf_op jit(solution)/shard_map/ppermute | solution.py:350
  36.0 3.7 %collective-permute-done.3.refs_2_ = f32[144,512]{1,0:T(8,128)S(1)} collective-permute-done((f32[144,512]{1,0:T(8,128)S(1)}, f32[144,512]{1,0:T(8,128)S(1)}, u32[]{:S(2)}, u32[]{:S(2)}) %collective-permute-start.3) | collective-permute-done | bytes 294944 | tf_op jit(solution)/shard_map/ppermute | solution.py:350
  39.7 3.4 %collective-permute-start.4 = (f32[144,512]{1,0:T(8,128)S(1)}, f32[144,512]{1,0:T(8,128)S(1)}, u32[]{:S(2)}, u32[]{:S(2)}) collective-permute-start(f32[144,512]{1,0:T(8,128)S(1)} %collective-permute-done.3.refs_2_), channel_id=1, source_target_pairs={{256,0},{272,16},{288,32},{304,48},{320,64},{336,80},{352,96},{368... | collective-permute-start | bytes 884744 | tf_op jit(solution)/shard_map/ppermute | solution.py:353
  43.1 0.1 pad_add_fusion.1.flags
  43.2 0.0 collective-permute-done.5.refs_5_
  43.2 1.0 collective-permute-done.6.refs_6_
  44.2 5.5 %collective-permute-done.1.refs_4_.refs_1_ = f32[144,512]{1,0:T(8,128)S(1)} collective-permute-done((f32[144,512]{1,0:T(8,128)S(1)}, f32[144,512]{1,0:T(8,128)S(1)}, u32[]{:S(2)}, u32[]{:S(2)}) %collective-permute-start.1) | collective-permute-done | bytes 294944 | tf_op jit(solution)/shard_map/ppermute | solution.py:350
  49.6 0.0 copy-start
  49.6 1.0 copy-done
  50.6 0.0 copy-start.1
  50.6 0.7 copy-done.1
  51.3 4.2 %shard_map.37.refs_4_ = f32[16,192,128]{2,1,0:T(8,128)} custom-call(s32[2]{0:T(128)S(1)} %pad_add_fusion.1.flags, s32[1,512]{1,0:T(1,128)S(1)} %bitcast.12, f32[144,512]{1,0:T(8,128)S(1)} %bitcast.10, f32[144,512]{1,0:T(8,128)S(1)} %collective-permute-done.2.refs_1_, f32[144,512]{1,0:T(8,128)S(1)} %collective-permute-done.3.refs_2_, ...), custom_call_target="tpu_custom_call" | custom-call | flops 1585446912 | bytes 4000000 | tf_op jit(solution)/shard_map/pallas_call | solution.py:381
  55.5 0.0 collective-permute-done.4.refs_3_
  55.5 2.1 %shard_map.38 = f32[16,192,128]{2,1,0:T(8,128)} custom-call(s32[2]{0:T(128)S(1)} %pad_add_fusion.1.flags, s32[1,512]{1,0:T(1,128)S(1)} %bitcast.13, f32[144,512]{1,0:T(8,128)S(1)} %bitcast.11, f32[144,512]{1,0:T(8,128)S(1)} %collective-permute-done.1.refs_4_.refs_1_, f32[144,512]{1,0:T(8,128)S(1)} %collective-permute-done.3.refs_2_, ...), custom_call_target="tpu_custom_call", output_to_operand_aliasing={{}: (6, {})} | custom-call | flops 339738624 | bytes 2000000 | tf_op jit(solution)/shard_map/pallas_call | solution.py:391
  57.6 6.7 %all-to-all-start = ((f32[16,192,128]{2,1,0:T(8,128)}), f32[16,192,128]{2,1,0:T(8,128)S(1)}, u32[]{:S(2)}, u32[]{:S(2)}) async-start(f32[16,192,128]{2,1,0:T(8,128)} %shard_map.38), calls=%async_computation | async-start | bytes 3145728 | tf_op jit(solution)/shard_map/all_to_all | solution.py:403
  64.4 1.3 %dynamic_slice.3 = s32[1]{0:T(128)} dynamic-slice(s32[512]{0:T(512)} %constant.62.clone, s32[]{:T(128)S(6)} %select_n.23), dynamic_slice_sizes={1} | dynamic-slice | bytes 12 | tf_op jit(solution)/shard_map/dynamic_slice | solution.py:341
  68.3 0.1 pad_add_fusion.flags
  68.4 19.7 %all-to-all-done.parts = f32[16,192,128]{2,1,0:T(8,128)S(1)} async-done(((f32[16,192,128]{2,1,0:T(8,128)}), f32[16,192,128]{2,1,0:T(8,128)S(1)}, u32[]{:S(2)}, u32[]{:S(2)}) %all-to-all-start) | async-done | bytes 1572896 | tf_op jit(solution)/shard_map/all_to_all | solution.py:403
  88.1 1.9 %shard_map.39 = (f32[48,128]{1,0:T(8,128)S(1)}, f32[48,128]{1,0:T(8,128)S(1)}) custom-call(s32[4]{0:T(128)S(1)} %pad_add_fusion.flags, f32[16,192,128]{2,1,0:T(8,128)S(1)} %all-to-all-done.parts), custom_call_target="tpu_custom_call" | custom-call | tf_op jit(solution)/shard_map/pallas_call | solution.py:407
  90.0 5.5 %collective-permute-start.7 = (f32[48,128]{1,0:T(8,128)S(1)}, f32[48,128]{1,0:T(8,128)S(1)}, u32[]{:S(2)}, u32[]{:S(2)}) collective-permute-start(f32[48,128]{1,0:T(8,128)S(1)} %get-tuple-element.7), channel_id=1, source_target_pairs={{0,209},{1,1},{2,38},{3,210},{4,2},{5,70},{6,217},{7,9},{8,294},{9... | collective-permute-start | bytes 73736 | tf_op jit(solution)/shard_map/ppermute | solution.py:414
  95.5 1.9 %collective-permute-start.8 = (f32[48,128]{1,0:T(8,128)S(1)}, f32[48,128]{1,0:T(8,128)S(1)}, u32[]{:S(2)}, u32[]{:S(2)}) collective-permute-start(f32[48,128]{1,0:T(8,128)S(1)} %get-tuple-element.8), channel_id=1, source_target_pairs={{0,38},{1,32},{2,193},{3,70},{4,64},{5,194},{6,294},{7,288},{8,201... | collective-permute-start | bytes 73736 | tf_op jit(solution)/shard_map/ppermute | solution.py:415
  97.4 2.5 %collective-permute-done.7.first = f32[48,128]{1,0:T(8,128)S(1)} collective-permute-done((f32[48,128]{1,0:T(8,128)S(1)}, f32[48,128]{1,0:T(8,128)S(1)}, u32[]{:S(2)}, u32[]{:S(2)}) %collective-permute-start.7) | collective-permute-done | bytes 24608 | tf_op jit(solution)/shard_map/ppermute | solution.py:414
  100.0 9.1 %collective-permute-done.8.second = f32[48,128]{1,0:T(8,128)S(1)} collective-permute-done((f32[48,128]{1,0:T(8,128)S(1)}, f32[48,128]{1,0:T(8,128)S(1)}, u32[]{:S(2)}, u32[]{:S(2)}) %collective-permute-start.8) | collective-permute-done | bytes 24608 | tf_op jit(solution)/shard_map/ppermute | solution.py:415
  109.0 1.2 %shard_map.40 = f32[48,96]{1,0:T(8,128)} custom-call(s32[4]{0:T(128)S(1)} %pad_add_fusion.flags, f32[48,128]{1,0:T(8,128)S(1)} %collective-permute-done.7.first, f32[48,128]{1,0:T(8,128)S(1)} %collective-permute-done.8.second), custom_call_target="tpu_custom_call" | custom-call | tf_op jit(solution)/shard_map/pallas_call | solution.py:416
Async XLA Ops:
  0.0 20.5 %collective-permute-start.2 = (f32[144,512]{1,0:T(8,128)}, f32[144,512]{1,0:T(8,128)S(1)}, u32[]{:S(2)}, u32[]{:S(2)}) collective-permute-start(f32[144,512]{1,0:T(8,128)} %bitcast.8), channel_id=1, source_target_pairs={{32,0},{48,16},{64,32},{80,48},{96,64},{112,80},{128,96},{144,112}... | collective-permute-start | bytes 884744 | tf_op jit(solution)/shard_map/ppermute | solution.py:350
  10.9 19.4 %collective-permute-start = (f32[144,512]{1,0:T(8,128)}, f32[144,512]{1,0:T(8,128)S(1)}, u32[]{:S(2)}, u32[]{:S(2)}) collective-permute-start(f32[144,512]{1,0:T(8,128)} %bitcast.9), channel_id=1, source_target_pairs={{208,0},{224,16},{240,32},{0,48},{16,64},{32,80},{48,96},{64,112},... | collective-permute-start | bytes 884744 | tf_op jit(solution)/shard_map/ppermute | solution.py:350
  20.5 19.2 %collective-permute-start.3 = (f32[144,512]{1,0:T(8,128)S(1)}, f32[144,512]{1,0:T(8,128)S(1)}, u32[]{:S(2)}, u32[]{:S(2)}) collective-permute-start(f32[144,512]{1,0:T(8,128)S(1)} %collective-permute-done.2.refs_1_), channel_id=1, source_target_pairs={{32,0},{48,16},{64,32},{80,48},{96,64},{112,80},{128,96},{144,112}... | collective-permute-start | bytes 884744 | tf_op jit(solution)/shard_map/ppermute | solution.py:350
  27.0 16.2 %collective-permute-start.5 = (f32[144,512]{1,0:T(8,128)S(1)}, f32[144,512]{1,0:T(8,128)S(1)}, u32[]{:S(2)}, u32[]{:S(2)}) collective-permute-start(f32[144,512]{1,0:T(8,128)S(1)} %collective-permute-done.2.refs_1_), channel_id=1, source_target_pairs={{256,0},{272,16},{288,32},{304,48},{320,64},{336,80},{352,96},{368... | collective-permute-start | bytes 884744 | tf_op jit(solution)/shard_map/ppermute | solution.py:353
  30.4 13.8 %collective-permute-start.6 = (f32[144,512]{1,0:T(8,128)S(1)}, f32[144,512]{1,0:T(8,128)S(1)}, u32[]{:S(2)}, u32[]{:S(2)}) collective-permute-start(f32[144,512]{1,0:T(8,128)S(1)} %collective-permute-done.refs_3_), channel_id=1, source_target_pairs={{256,0},{272,16},{288,32},{304,48},{320,64},{336,80},{352,96},{368... | collective-permute-start | bytes 884744 | tf_op jit(solution)/shard_map/ppermute | solution.py:353
  32.8 16.8 %collective-permute-start.1 = (f32[144,512]{1,0:T(8,128)S(1)}, f32[144,512]{1,0:T(8,128)S(1)}, u32[]{:S(2)}, u32[]{:S(2)}) collective-permute-start(f32[144,512]{1,0:T(8,128)S(1)} %collective-permute-done.refs_3_), channel_id=1, source_target_pairs={{240,0},{0,16},{16,32},{32,48},{48,64},{64,80},{80,96},{96,112},{1... | collective-permute-start | bytes 884744 | tf_op jit(solution)/shard_map/ppermute | solution.py:350
  39.7 15.8 %collective-permute-start.4 = (f32[144,512]{1,0:T(8,128)S(1)}, f32[144,512]{1,0:T(8,128)S(1)}, u32[]{:S(2)}, u32[]{:S(2)}) collective-permute-start(f32[144,512]{1,0:T(8,128)S(1)} %collective-permute-done.3.refs_2_), channel_id=1, source_target_pairs={{256,0},{272,16},{288,32},{304,48},{320,64},{336,80},{352,96},{368... | collective-permute-start | bytes 884744 | tf_op jit(solution)/shard_map/ppermute | solution.py:353
  49.6 1.0 copy-start
  50.6 0.7 copy-start.1
  57.6 30.4 %all-to-all-start = ((f32[16,192,128]{2,1,0:T(8,128)}), f32[16,192,128]{2,1,0:T(8,128)S(1)}, u32[]{:S(2)}, u32[]{:S(2)}) async-start(f32[16,192,128]{2,1,0:T(8,128)} %shard_map.38), calls=%async_computation | async-start | bytes 3145728 | tf_op jit(solution)/shard_map/all_to_all | solution.py:403
  90.0 10.0 %collective-permute-start.7 = (f32[48,128]{1,0:T(8,128)S(1)}, f32[48,128]{1,0:T(8,128)S(1)}, u32[]{:S(2)}, u32[]{:S(2)}) collective-permute-start(f32[48,128]{1,0:T(8,128)S(1)} %get-tuple-element.7), channel_id=1, source_target_pairs={{0,209},{1,1},{2,38},{3,210},{4,2},{5,70},{6,217},{7,9},{8,294},{9... | collective-permute-start | bytes 73736 | tf_op jit(solution)/shard_map/ppermute | solution.py:414
  95.5 13.5 %collective-permute-start.8 = (f32[48,128]{1,0:T(8,128)S(1)}, f32[48,128]{1,0:T(8,128)S(1)}, u32[]{:S(2)}, u32[]{:S(2)}) collective-permute-start(f32[48,128]{1,0:T(8,128)S(1)} %get-tuple-element.8), channel_id=1, source_target_pairs={{0,38},{1,32},{2,193},{3,70},{4,64},{5,194},{6,294},{7,288},{8,201... | collective-permute-start | bytes 73736 | tf_op jit(solution)/shard_map/ppermute | solution.py:415

commit v4 on v3

--- a/solution.py
+++ b/solution.py
@@ -26,6 +26,8 @@
 )
 DIAGONAL = EARLY.index((4, 2))
 LATE = ((0, 6), (2, 6))
+POSITION = (11, 4, 12, 5, 0, 2, 10, 3, 1, 9, 6, 8, 13, 7, 14, 15)
+CHIPS = SIDE // 2
 
 
 def frame_block(column, z, index):
@@ -34,18 +36,57 @@
     return (1 - column) * SIDE + (z + OTHER[index - len(OWN)]) % SIDE
 
 
+def ends_of(column, z, pair):
+    p, q = (EARLY + LATE)[pair]
+    if pair == len(EARLY) + 1 and column == 1:
+        p = 4
+    a, b = frame_block(column, z, p), frame_block(column, z, q)
+    if pair == DIAGONAL and z >= SIDE // 2:
+        return ((a, a), (b, b))
+    return ((a, b), (b, a))
+
+
+def around(a, b, n):
+    return min((a - b) % n, (b - a) % n)
+
+
+def distance(column, z, chip, end):
+    to_column, to_z = divmod(end[0], SIDE)
+    to_chip = end[1] // 4
+    x, to_x = 2 * (chip % 2) + column, 2 * (to_chip % 2) + to_column
+    return around(z, to_z, SIDE) + around(chip // 2, to_chip // 2, 4) + around(x, to_x, 4)
+
+
+def order_of_chips(column, z):
+    cost = [[0] * CHIPS for _ in range(CHIPS)]
+    for k in range(CHIPS):
+        for chip in range(CHIPS):
+            for pair in POSITION[2 * k : 2 * k + 2]:
+                far = max(distance(column, z, chip, end) for end in ends_of(column, z, pair))
+                cost[k][chip] = max(cost[k][chip], 4**far)
+    best = {0: (0, ())}
+    for k in range(CHIPS):
+        later = {}
+        for taken, (value, order) in best.items():
+            for chip in range(CHIPS):
+                if not taken >> chip & 1:
+                    entry = (value + cost[k][chip], order + (chip,))
+                    key = taken | 1 << chip
+                    later[key] = min(later.get(key, entry), entry)
+        best = later
+    return best[(1 << CHIPS) - 1][1]
+
+
 def routes():
-    ends = []
+    orders, ends, diagonal = [], [], []
     for column in range(2):
         for z in range(SIDE):
-            for slot, (p, q) in enumerate(EARLY + LATE):
-                if slot == len(EARLY) + 1 and column == 1:
-                    p = 4
-                a, b = frame_block(column, z, p), frame_block(column, z, q)
-                if slot == DIAGONAL and z >= SIDE // 2:
-                    ends.append(((a, a), (b, b)))
-                else:
-                    ends.append(((a, b), (b, a)))
+            order = order_of_chips(column, z)
+            orders.append(order)
+            for device in range(SIDE):
+                pair = POSITION[2 * order.index(device // 2) + device % 2]
+                ends.append(ends_of(column, z, pair))
+                diagonal.append(int(pair == DIAGONAL and z >= SIDE // 2))
     place = lambda end: end[0] * SIDE + end[1] // 2
     at = {}
     for device, pair in enumerate(ends):
@@ -65,8 +106,8 @@
     half = [0] * len(ends)
     for d in range(len(ends)):
         half[first[d]] = ends[d][swapped[d]][1] % 2
-        assert ends[d][1 - swapped[d]][1] % 2 == 1 - half[first[d]] or second[d] != first[d]
-    return first, second, swapped, half
+    table = [a + 2 * b + 4 * c for a, b, c in zip(swapped, half, diagonal)]
+    return orders, first, second, table
 
 
 def lookup(step, values):
@@ -102,27 +143,27 @@
     return x, wx, mean, square[:ROWS] + square[ROWS : 2 * ROWS] + square[2 * ROWS :], local
 
 
-def stage_rows(block, mass, at, weighted, feature):
+def stage_rows(block, mass, at, core, weighted, feature):
     atoms = block.shape[1]
     _, wx, mean, square, local = stage(block[...], mass)
     high, low = halves(wx)
     for k, part in enumerate((high, high, low)):
         weighted[at * 3 * ROWS : (at + 1) * 3 * ROWS, k * atoms : (k + 1) * atoms] = part
-    lane = iota((ROWS, 128), 1)
-    out = jnp.where(lane == 51, local, jnp.where(lane == 56, square, 0.0))
+    lane = iota((ROWS, 128), 1) - 8 * core
+    out = jnp.where(lane == 51, local, jnp.where(lane == 64 - 8 * core, square, 0.0))
     for c in range(3):
         out = jnp.where(lane == 48 + c, mean[c * ROWS : (c + 1) * ROWS], out)
     feature[at] = out
 
 
-def stage_columns(block, mass, at, centered, feature):
+def stage_columns(block, mass, at, core, centered, feature):
     atoms = block.shape[1]
     x, _, mean, square, _ = stage(block[...], mass)
     high, low = halves(x)
     for k, part in enumerate((high, low, high)):
         centered[at, : 3 * ROWS, k * atoms : (k + 1) * atoms] = part
-    lane = iota((ROWS, 128), 1)
-    out = jnp.where(lane == 57, square, 0.0)
+    lane = iota((ROWS, 128), 1) - 8 * core
+    out = jnp.where(lane == 65 - 8 * core, square, 0.0)
     for c in range(3):
         out = jnp.where(lane == 52 + c, mean[c * ROWS : (c + 1) * ROWS], out)
     feature[at] = out
@@ -133,40 +174,48 @@
     return tail[:ROWS] + pltpu.roll(tail[ROWS : 2 * ROWS], 16, 1) + pltpu.roll(tail[2 * ROWS :], 32, 1)
 
 
-def put_pair(out, slot, value, feature):
-    out[slot, : 3 * ROWS] = value[:, :128]
-    out[slot, 3 * ROWS :] = rest_of(value[:, 128:]) + feature
-
-
-def put_group(out, first, pairs, weighted, columns, row_feature, column_feature):
+def put_pair(out, pair, core, value, feature):
+    k, owner = divmod(POSITION.index(pair), 2)
+    k = k % out[0].shape[0]
+    rest = rest_of(value[:, 128:]) + feature
+    for ref, here in zip(out, (core == owner, core != owner)):
+
+        @pl.when(here)
+        def _():
+            ref[k, : 3 * ROWS] = value[:, :128]
+            ref[k, 3 * ROWS :] = rest
+
+
+def put_group(out, first, pairs, core, weighted, columns, row_feature, column_feature):
     start = STACK.index(pairs[0][0])
     rows = weighted[start * 3 * ROWS : (start + len(pairs)) * 3 * ROWS]
     values = product(rows, columns)
     for k in range(len(pairs)):
         value = values[k * 3 * ROWS : (k + 1) * 3 * ROWS]
-        put_pair(out, first + k, value, row_feature[start + k] + column_feature)
+        put_pair(out, first + k, core, value, row_feature[start + k] + column_feature)
 
 
 def early_kernel(flags, mass_ref, *refs):
-    blocks, (out, weighted, centered, row_feature, column_feature) = refs[:7], refs[7:]
+    blocks, out, (weighted, centered, row_feature, column_feature) = refs[:7], refs[7:9], refs[9:]
+    core = flags[2]
     blocks = dict(zip((0, 1, 2, 3, 4, 5, 7), blocks))
     mass = mass_ref[...].astype(jnp.float32)
     for at, k in enumerate(STACK):
-        stage_rows(blocks[k], mass, at, weighted, row_feature)
+        stage_rows(blocks[k], mass, at, core, weighted, row_feature)
     order = (1, 2, 5, 3, 7)
     for at, k in enumerate(order):
-        stage_columns(blocks[k], mass, at, centered, column_feature)
+        stage_columns(blocks[k], mass, at, core, centered, column_feature)
     first = 0
     for at, k in enumerate(order):
         pairs = [pair for pair in EARLY if pair[1] == k]
         assert tuple(EARLY[first : first + len(pairs)]) == tuple(pairs)
         assert tuple(STACK[STACK.index(pairs[0][0]) :][: len(pairs)]) == tuple(p for p, _ in pairs)
-        put_group(out, first, pairs, weighted, centered[at], row_feature, column_feature[at])
+        put_group(out, first, pairs, core, weighted, centered[at], row_feature, column_feature[at])
         first += len(pairs)
 
     @pl.when(flags[1] == 1)
     def _():
-        stage_columns(blocks[4], mass, 5, centered, column_feature)
+        stage_columns(blocks[4], mass, 5, core, centered, column_feature)
         p, q = STACK.index(4), STACK.index(2)
         upper = product(weighted[p * 3 * ROWS : (p + 1) * 3 * ROWS], centered[5])
         lower = product(weighted[q * 3 * ROWS : (q + 1) * 3 * ROWS], centered[order.index(2)])
@@ -180,21 +229,23 @@
             for d in range(3):
                 inside = (at >= d * ROWS) & (at < (d + 1) * ROWS)
                 value = jnp.sum(jnp.where(inside, mine, 0.0), axis=1, keepdims=True)
-                ends = jnp.where(lane == 64 + 3 * c + d, value, ends)
-        put_pair(out, DIAGONAL, jnp.where(i <= j, upper, lower), ends)
+                ends = jnp.where(lane == 66 + 3 * c + d, value, ends)
+        put_pair(out, DIAGONAL, core, jnp.where(i <= j, upper, lower), ends)
 
 
 def late_kernel(flags, mass_ref, *refs):
-    blocks, (_, out, weighted, centered, row_feature, column_feature) = refs[:4], refs[4:]
+    blocks, out, (weighted, centered, row_feature, column_feature) = refs[:4], refs[6:8], refs[8:]
+    core = flags[2]
     mass = mass_ref[...].astype(jnp.float32)
     for at, block in enumerate(blocks[:3]):
-        stage_rows(block, mass, at, weighted, row_feature)
-    stage_columns(blocks[3], mass, 0, centered, column_feature)
+        stage_rows(block, mass, at, core, weighted, row_feature)
+    stage_columns(blocks[3], mass, 0, core, centered, column_feature)
     values = product(weighted[...], centered[0])
-    put_pair(out, 0, values[: 3 * ROWS], row_feature[0] + column_feature[0])
+    first = len(EARLY)
+    put_pair(out, first, core, values[: 3 * ROWS], row_feature[0] + column_feature[0])
     other = flags[0] == 1
     value = jnp.where(other, values[3 * ROWS : 6 * ROWS], values[6 * ROWS :])
-    put_pair(out, 1, value, jnp.where(other, row_feature[1], row_feature[2]) + column_feature[0])
+    put_pair(out, first + 1, core, value, jnp.where(other, row_feature[1], row_feature[2]) + column_feature[0])
 
 
 def det_four(rows):
@@ -247,17 +298,17 @@
 
 
 def fit_kernel(flags, parts, first, second):
-    diagonal, swap = flags[1] == 1, flags[2] == 1
+    diagonal, swap = flags[2] == 1, flags[0] == 1
     total = parts[0]
-    for a in range(1, SIDE):
+    for a in range(1, CHIPS):
         total = total + parts[a]
     lane, row = iota((ROWS, 128), 1), iota((ROWS, 128), 0)
     rest = total[3 * ROWS :]
 
     gathered = jnp.zeros((ROWS, 128), jnp.float32)
-    for a in range(SIDE):
-        tile = jnp.where((lane >= 48) & (lane < 56), parts[a, 3 * ROWS :], 0.0)
-        gathered = gathered + pltpu.roll(tile, (8 * a - 48) % 128, 1)
+    for a in range(CHIPS):
+        tile = jnp.where((lane >= 48) & (lane < 64), parts[a, 3 * ROWS :], 0.0)
+        gathered = gathered + pltpu.roll(tile, (16 * a - 48) % 128, 1)
 
     def per_sender(which):
         pick = (iota((128, 128), 0) == 8 * iota((128, 128), 1) + which).astype(jnp.float32)
@@ -281,7 +332,7 @@
         between = jnp.sum(mass * sum(o * o for o in off), axis=1, keepdims=True)
         return (within + between) / whole
 
-    spread_p, spread_q = spread(off_p, 56), spread(off_q, 57)
+    spread_p, spread_q = spread(off_p, 64), spread(off_q, 65)
 
     def as_row(column):
         return jnp.sum(jnp.where(row == lane, column, 0.0), axis=0, keepdims=True)
@@ -309,7 +360,7 @@
         for d in range(3):
             up, low = (b[c * ROWS : (c + 1) * ROWS] for b in between[d])
             value = shifted[d] + jnp.where(upper, up, low)
-            end = jnp.sum(jnp.where(lane == 64 + 3 * c + d, rest, 0.0), axis=1, keepdims=True)
+            end = jnp.sum(jnp.where(lane == 66 + 3 * c + d, rest, 0.0), axis=1, keepdims=True)
             end = end + jnp.sum(mass * off_q[c] * off_q[d], axis=1, keepdims=True)
             moment.append(jnp.where(corner, end, value) / whole)
     msd = quaternion_fit(moment, spread_rows, spread_cols)
@@ -326,21 +377,17 @@
 def join_kernel(flags, first, second, out):
     lane = iota((ROWS, 128), 1)
     a, b = first[...], second[...]
-    left = jnp.where(flags[3] == 1, b, a)
-    right = jnp.where(flags[3] == 1, a, b)
+    left = jnp.where(flags[1] == 1, b, a)
+    right = jnp.where(flags[1] == 1, a, b)
     out[...] = jnp.where(lane < ROWS, left, pltpu.roll(right, ROWS, 1))[:, : 2 * ROWS]
 
 
 def on_device(coords, weights):
-    first, second, swapped, half = routes()
+    orders, first, second, table = routes()
     frame, atom = lax.axis_index("frame"), lax.axis_index("atom")
-    place = frame * SIDE + atom
-    last = (atom == DIAGONAL).astype(jnp.int32)
-    column, z = frame // SIDE, frame % SIDE
-    late_diagonal = (z >= SIDE // 2).astype(jnp.int32)
-    table = jnp.asarray(np.array(swapped) + 2 * np.array(half), jnp.int32)[place]
-    build_flags = jnp.stack([column, late_diagonal]).astype(jnp.int32)
-    fit_flags = jnp.stack([column, late_diagonal * last, table % 2, table // 2]).astype(jnp.int32)
+    build_flags = jnp.stack([frame // SIDE, (frame % SIDE) // (SIDE // 2), atom % 2]).astype(jnp.int32)
+    mine = jnp.asarray(np.array(table), jnp.int32)[frame * SIDE + atom]
+    fit_flags = jnp.stack([mine & 1, mine >> 1 & 1, mine >> 2])
     mass = weights[None, :]
 
     def along(block, distance):
@@ -362,8 +409,7 @@
     other4 = across(plus4)
 
     atoms = own.shape[1]
-    slots = len(EARLY) + len(LATE)
-    result = jax.ShapeDtypeStruct((slots, 4 * ROWS, 128), jnp.float32)
+    result = [jax.ShapeDtypeStruct((CHIPS, 4 * ROWS, 128), jnp.float32)] * 2
 
     def scratch(rows, columns):
         return [
@@ -383,24 +429,28 @@
         grid=(1,),
         out_shape=result,
         in_specs=[smem, whole(1, atoms)] + [block_spec] * 7,
-        out_specs=whole(len(EARLY), 4 * ROWS, 128),
+        out_specs=[whole(len(EARLY) // 2, 4 * ROWS, 128)] * 2,
         scratch_shapes=scratch(4, 6),
         compiler_params=params,
         cost_estimate=pl.CostEstimate(flops=14 * pair_flops, bytes_accessed=4_000_000, transcendentals=0),
     )(build_flags, mass, own, plus2, plus4, minus3, minus4, other2, other3)
-    partial = pl.pallas_call(
+    keep, send = pl.pallas_call(
         late_kernel,
         grid=(1,),
         out_shape=result,
-        in_specs=[smem, whole(1, atoms)] + [block_spec] * 4 + [pl.BlockSpec(memory_space=pl.ANY)],
-        out_specs=pl.BlockSpec((len(LATE), 4 * ROWS, 128), lambda i: (len(EARLY) // len(LATE), 0, 0)),
+        in_specs=[smem, whole(1, atoms)] + [block_spec] * 4 + [pl.BlockSpec(memory_space=pl.ANY)] * 2,
+        out_specs=[pl.BlockSpec((1, 4 * ROWS, 128), lambda i: (CHIPS - 1, 0, 0))] * 2,
         scratch_shapes=scratch(3, 1),
-        input_output_aliases={6: 0},
+        input_output_aliases={6: 0, 7: 1},
         compiler_params=params,
         cost_estimate=pl.CostEstimate(flops=3 * pair_flops, bytes_accessed=2_000_000, transcendentals=0),
-    )(build_flags, mass, own, minus4, plus4, other4, partial)
-
-    parts = lax.all_to_all(partial, "atom", 0, 0, tiled=True)
+    )(build_flags, mass, own, minus4, plus4, other4, *partial)
+
+    taken = lax.ppermute(send, "atom", [(a, a ^ 1) for a in range(SIDE)])
+    groups = [[f * SIDE + 2 * chip + c for chip in orders[f]] for f in range(2 * SIDE) for c in range(2)]
+    parts = lax.all_to_all(
+        keep + taken, ("frame", "atom"), 0, 0, axis_index_groups=groups, tiled=True
+    )
 
     block = jax.ShapeDtypeStruct((ROWS, 128), jnp.float32)
     vmem = pl.BlockSpec(memory_space=pltpu.VMEM)

time: 111 us -> 105 us (0.946)
  the two profiles are of different devices: /device:TPU:32 before, /device:TPU:7 now
where the time goes in v4:
time: 105 us
  starting transfers between devices  49.6 us (47%)
  waiting for transfers between devices  39.4 us (38%)
  Pallas kernels  10.5 us (10%)
  local copies, waits for them, and re-layouts  2.23 us (2%)
  between operations  2.14 us (2%)
  other arithmetic  1.16 us (1%)
    ppermute x4, starting transfers between devices, along(): return lax.ppermute(block, 'frame', route)  21.5 us
    ppermute x4, waiting for transfers between devices, along(): return lax.ppermute(block, 'frame', route)  18.8 us
    ppermute x1, waiting for transfers between devices, on_device(): two = lax.ppermute(two, ('frame', 'atom'), list(enumerate(second)))  9.22 us
    ppermute x3, starting transfers between devices, across(): lax.ppermute(block, 'frame', [((f + SIDE) % (2 * SIDE), f) for f in range...  7.73 us
    all_to_all x1, starting transfers between devices, on_device(): lax.all_to_all(keep + taken, ('frame', 'atom'), 0, 0, axis_index_groups=g...  7.59 us
    ppermute x1, starting transfers between devices, on_device(): one = lax.ppermute(one, ('frame', 'atom'), list(enumerate(first)))  7.26 us
    all_to_all x1, waiting for transfers between devices, on_device(): lax.all_to_all(keep + taken, ('frame', 'atom'), 0, 0, axis_index_groups=g...  6.92 us
    pallas_call x1, Pallas kernels, on_device(): pl.pallas_call(early_kernel, grid=(1,), out_shape=result, in_specs=[smem,...  5.89 us
  transfers between devices with their start and end apart: 11, of which 7 were waited for; matrix products, arithmetic and copies ran while one was open for 1% of the time, Pallas kernels for 6%

profile of v4, /device:TPU:7, one launch (start us, length us, event | category | flops | bytes accessed | tf_op | source)
XLA Modules:
  0.0 105.0 jit_solution(15762010672961131344)
XLA Ops:
  0.0 11.6 %collective-permute-start.2 = (f32[144,512]{1,0:T(8,128)}, f32[144,512]{1,0:T(8,128)S(1)}, u32[]{:S(2)}, u32[]{:S(2)}) collective-permute-start(f32[144,512]{1,0:T(8,128)} %bitcast.5), channel_id=1, source_target_pairs={{32,0},{48,16},{64,32},{80,48},{96,64},{112,80},{128,96},{144,112}... | collective-permute-start | bytes 884744 | tf_op jit(solution)/shard_map/ppermute | solution.py:397
  11.6 1.9 %collective-permute-start = (f32[144,512]{1,0:T(8,128)}, f32[144,512]{1,0:T(8,128)S(1)}, u32[]{:S(2)}, u32[]{:S(2)}) collective-permute-start(f32[144,512]{1,0:T(8,128)} %bitcast.6), channel_id=1, source_target_pairs={{208,0},{224,16},{240,32},{0,48},{16,64},{32,80},{48,96},{64,112},... | collective-permute-start | bytes 884744 | tf_op jit(solution)/shard_map/ppermute | solution.py:397
  13.5 10.4 %collective-permute-done.2.refs_1_ = f32[144,512]{1,0:T(8,128)S(1)} collective-permute-done((f32[144,512]{1,0:T(8,128)}, f32[144,512]{1,0:T(8,128)S(1)}, u32[]{:S(2)}, u32[]{:S(2)}) %collective-permute-start.2) | collective-permute-done | bytes 294944 | tf_op jit(solution)/shard_map/ppermute | solution.py:397
  23.9 6.1 %collective-permute-start.3 = (f32[144,512]{1,0:T(8,128)S(1)}, f32[144,512]{1,0:T(8,128)S(1)}, u32[]{:S(2)}, u32[]{:S(2)}) collective-permute-start(f32[144,512]{1,0:T(8,128)S(1)} %collective-permute-done.2.refs_1_), channel_id=1, source_target_pairs={{32,0},{48,16},{64,32},{80,48},{96,64},{112,80},{128,96},{144,112}... | collective-permute-start | bytes 884744 | tf_op jit(solution)/shard_map/ppermute | solution.py:397
  30.0 2.5 %collective-permute-start.5 = (f32[144,512]{1,0:T(8,128)S(1)}, f32[144,512]{1,0:T(8,128)S(1)}, u32[]{:S(2)}, u32[]{:S(2)}) collective-permute-start(f32[144,512]{1,0:T(8,128)S(1)} %collective-permute-done.2.refs_1_), channel_id=1, source_target_pairs={{256,0},{272,16},{288,32},{304,48},{320,64},{336,80},{352,96},{368... | collective-permute-start | bytes 884744 | tf_op jit(solution)/shard_map/ppermute | solution.py:400
  32.5 5.0 %collective-permute-done.refs_3_ = f32[144,512]{1,0:T(8,128)S(1)} collective-permute-done((f32[144,512]{1,0:T(8,128)}, f32[144,512]{1,0:T(8,128)S(1)}, u32[]{:S(2)}, u32[]{:S(2)}) %collective-permute-start) | collective-permute-done | bytes 294944 | tf_op jit(solution)/shard_map/ppermute | solution.py:397
  37.5 2.4 %collective-permute-start.6 = (f32[144,512]{1,0:T(8,128)S(1)}, f32[144,512]{1,0:T(8,128)S(1)}, u32[]{:S(2)}, u32[]{:S(2)}) collective-permute-start(f32[144,512]{1,0:T(8,128)S(1)} %collective-permute-done.refs_3_), channel_id=1, source_target_pairs={{256,0},{272,16},{288,32},{304,48},{320,64},{336,80},{352,96},{368... | collective-permute-start | bytes 884744 | tf_op jit(solution)/shard_map/ppermute | solution.py:400
  39.9 1.9 %collective-permute-start.1 = (f32[144,512]{1,0:T(8,128)S(1)}, f32[144,512]{1,0:T(8,128)S(1)}, u32[]{:S(2)}, u32[]{:S(2)}) collective-permute-start(f32[144,512]{1,0:T(8,128)S(1)} %collective-permute-done.refs_3_), channel_id=1, source_target_pairs={{240,0},{0,16},{16,32},{32,48},{48,64},{64,80},{80,96},{96,112},{1... | collective-permute-start | bytes 884744 | tf_op jit(solution)/shard_map/ppermute | solution.py:397
  41.9 0.0 collective-permute-done.3.refs_2_
  41.9 2.8 %collective-permute-start.4 = (f32[144,512]{1,0:T(8,128)S(1)}, f32[144,512]{1,0:T(8,128)S(1)}, u32[]{:S(2)}, u32[]{:S(2)}) collective-permute-start(f32[144,512]{1,0:T(8,128)S(1)} %collective-permute-done.3.refs_2_), channel_id=1, source_target_pairs={{256,0},{272,16},{288,32},{304,48},{320,64},{336,80},{352,96},{368... | collective-permute-start | bytes 884744 | tf_op jit(solution)/shard_map/ppermute | solution.py:400
  44.8 0.0 copy-start.1
  44.8 0.1 pad_add_fusion.1.flags
  44.8 0.0 collective-permute-done.5.refs_5_
  44.8 2.6 %collective-permute-done.6.refs_6_ = f32[144,512]{1,0:T(8,128)S(1)} collective-permute-done((f32[144,512]{1,0:T(8,128)S(1)}, f32[144,512]{1,0:T(8,128)S(1)}, u32[]{:S(2)}, u32[]{:S(2)}) %collective-permute-start.6) | collective-permute-done | bytes 294944 | tf_op jit(solution)/shard_map/ppermute | solution.py:400
  47.5 3.4 %collective-permute-done.1.refs_4_.refs_1_ = f32[144,512]{1,0:T(8,128)S(1)} collective-permute-done((f32[144,512]{1,0:T(8,128)S(1)}, f32[144,512]{1,0:T(8,128)S(1)}, u32[]{:S(2)}, u32[]{:S(2)}) %collective-permute-start.1) | collective-permute-done | bytes 294944 | tf_op jit(solution)/shard_map/ppermute | solution.py:397
  50.8 0.0 copy-done.1
  50.8 0.0 copy-start
  50.8 1.0 copy-done
  51.8 5.9 %shard_map.37 = (f32[8,192,128]{2,1,0:T(8,128)S(1)}, f32[8,192,128]{2,1,0:T(8,128)S(1)}) custom-call(s32[3]{0:T(128)S(1)} %pad_add_fusion.1.flags, s32[1,512]{1,0:T(1,128)S(1)} %bitcast.9, f32[144,512]{1,0:T(8,128)S(1)} %bitcast.7, f32[144,512]{1,0:T(8,128)S(1)} %collective-permute-done.2.refs_1_, f32[144,512]{1,0:T(8,128)S(1)} %collective-permute-done.3.refs_2_, ...), custom_call_target="tpu_custom_call" | custom-call | flops 1585446912 | bytes 4000000 | tf_op jit(solution)/shard_map/pallas_call | solution.py:427
  57.7 0.0 collective-permute-done.4.refs_3_
  57.7 1.5 %shard_map.38 = (f32[8,192,128]{2,1,0:T(8,128)S(1)}, f32[8,192,128]{2,1,0:T(8,128)S(1)}) custom-call(s32[3]{0:T(128)S(1)} %pad_add_fusion.1.flags, s32[1,512]{1,0:T(1,128)S(1)} %bitcast.10, f32[144,512]{1,0:T(8,128)S(1)} %bitcast.8, f32[144,512]{1,0:T(8,128)S(1)} %collective-permute-done.1.refs_4_.refs_1_, ...), custom_call_target="tpu_custom_call", output_to_operand_aliasing={{0}: (6, {}), {1}: (7, {})} | custom-call | flops 339738624 | bytes 2000000 | tf_op jit(solution)/shard_map/pallas_call | solution.py:437
  59.1 3.6 %collective-permute-start.7 = (f32[8,192,128]{2,1,0:T(8,128)S(1)}, f32[8,192,128]{2,1,0:T(8,128)S(1)}, u32[]{:S(2)}, u32[]{:S(2)}) collective-permute-start(f32[8,192,128]{2,1,0:T(8,128)S(1)} %get-tuple-element.14), channel_id=1, source_target_pairs={{0,1},{1,0},{2,3},{3,2},{4,5},{5,4},{6,7},{7,6},{8,9},{9,8},{10,11... | collective-permute-start | bytes 2359304 | tf_op jit(solution)/shard_map/ppermute | solution.py:449
  62.7 1.9 %collective-permute-done.7 = f32[8,192,128]{2,1,0:T(8,128)S(1)} collective-permute-done((f32[8,192,128]{2,1,0:T(8,128)S(1)}, f32[8,192,128]{2,1,0:T(8,128)S(1)}, u32[]{:S(2)}, u32[]{:S(2)}) %collective-permute-start.7) | collective-permute-done | bytes 786464 | tf_op jit(solution)/shard_map/ppermute | solution.py:449
  64.6 1.0 add.22
  65.6 7.6 %all-to-all-start = ((f32[8,192,128]{2,1,0:T(8,128)}), f32[8,192,128]{2,1,0:T(8,128)S(1)}, u32[]{:S(2)}, u32[]{:S(2)}) async-start(f32[8,192,128]{2,1,0:T(8,128)} %add.22), calls=%async_computation | async-start | bytes 1572864 | tf_op jit(solution)/shard_map/all_to_all | solution.py:451
  73.2 1.3 %dynamic_slice.3 = s32[1]{0:T(128)} dynamic-slice(s32[512]{0:T(512)} %constant.67.clone, s32[]{:T(128)S(6)} %select_n.21), dynamic_slice_sizes={1} | dynamic-slice | bytes 12 | tf_op jit(solution)/shard_map/dynamic_slice | solution.py:389
  76.4 0.1 pad_add_fusion.flags
  76.5 6.9 %all-to-all-done.parts = f32[8,192,128]{2,1,0:T(8,128)S(1)} async-done(((f32[8,192,128]{2,1,0:T(8,128)}), f32[8,192,128]{2,1,0:T(8,128)S(1)}, u32[]{:S(2)}, u32[]{:S(2)}) %all-to-all-start) | async-done | bytes 786464 | tf_op jit(solution)/shard_map/all_to_all | solution.py:451
  83.4 1.9 %shard_map.39 = (f32[48,128]{1,0:T(8,128)S(1)}, f32[48,128]{1,0:T(8,128)S(1)}) custom-call(s32[3]{0:T(128)S(1)} %pad_add_fusion.flags, f32[8,192,128]{2,1,0:T(8,128)S(1)} %all-to-all-done.parts), custom_call_target="tpu_custom_call" | custom-call | tf_op jit(solution)/shard_map/pallas_call | solution.py:457
  85.3 7.3 %collective-permute-start.8 = (f32[48,128]{1,0:T(8,128)S(1)}, f32[48,128]{1,0:T(8,128)S(1)}, u32[]{:S(2)}, u32[]{:S(2)}) collective-permute-start(f32[48,128]{1,0:T(8,128)S(1)} %get-tuple-element.15), channel_id=1, source_target_pairs={{0,14},{1,2},{2,206},{3,194},{4,209},{5,38},{6,10},{7,74},{8,217},... | collective-permute-start | bytes 73736 | tf_op jit(solution)/shard_map/ppermute | solution.py:464
  92.6 1.9 %collective-permute-start.9 = (f32[48,128]{1,0:T(8,128)S(1)}, f32[48,128]{1,0:T(8,128)S(1)}, u32[]{:S(2)}, u32[]{:S(2)}) collective-permute-start(f32[48,128]{1,0:T(8,128)S(1)} %get-tuple-element.16), channel_id=1, source_target_pairs={{0,464},{1,64},{2,470},{3,70},{4,38},{5,193},{6,320},{7,322},{8,29... | collective-permute-start | bytes 73736 | tf_op jit(solution)/shard_map/ppermute | solution.py:465
  94.5 0.0 collective-permute-done.8.first
  94.5 9.2 %collective-permute-done.9.second = f32[48,128]{1,0:T(8,128)S(1)} collective-permute-done((f32[48,128]{1,0:T(8,128)S(1)}, f32[48,128]{1,0:T(8,128)S(1)}, u32[]{:S(2)}, u32[]{:S(2)}) %collective-permute-start.9) | collective-permute-done | bytes 24608 | tf_op jit(solution)/shard_map/ppermute | solution.py:465
  103.8 1.2 %shard_map.40 = f32[48,96]{1,0:T(8,128)} custom-call(s32[3]{0:T(128)S(1)} %pad_add_fusion.flags, f32[48,128]{1,0:T(8,128)S(1)} %collective-permute-done.8.first, f32[48,128]{1,0:T(8,128)S(1)} %collective-permute-done.9.second), custom_call_target="tpu_custom_call" | custom-call | tf_op jit(solution)/shard_map/pallas_call | solution.py:466
Async XLA Ops:
  0.0 23.9 %collective-permute-start.2 = (f32[144,512]{1,0:T(8,128)}, f32[144,512]{1,0:T(8,128)S(1)}, u32[]{:S(2)}, u32[]{:S(2)}) collective-permute-start(f32[144,512]{1,0:T(8,128)} %bitcast.5), channel_id=1, source_target_pairs={{32,0},{48,16},{64,32},{80,48},{96,64},{112,80},{128,96},{144,112}... | collective-permute-start | bytes 884744 | tf_op jit(solution)/shard_map/ppermute | solution.py:397
  11.6 25.9 %collective-permute-start = (f32[144,512]{1,0:T(8,128)}, f32[144,512]{1,0:T(8,128)S(1)}, u32[]{:S(2)}, u32[]{:S(2)}) collective-permute-start(f32[144,512]{1,0:T(8,128)} %bitcast.6), channel_id=1, source_target_pairs={{208,0},{224,16},{240,32},{0,48},{16,64},{32,80},{48,96},{64,112},... | collective-permute-start | bytes 884744 | tf_op jit(solution)/shard_map/ppermute | solution.py:397
  23.9 17.9 %collective-permute-start.3 = (f32[144,512]{1,0:T(8,128)S(1)}, f32[144,512]{1,0:T(8,128)S(1)}, u32[]{:S(2)}, u32[]{:S(2)}) collective-permute-start(f32[144,512]{1,0:T(8,128)S(1)} %collective-permute-done.2.refs_1_), channel_id=1, source_target_pairs={{32,0},{48,16},{64,32},{80,48},{96,64},{112,80},{128,96},{144,112}... | collective-permute-start | bytes 884744 | tf_op jit(solution)/shard_map/ppermute | solution.py:397
  30.0 14.8 %collective-permute-start.5 = (f32[144,512]{1,0:T(8,128)S(1)}, f32[144,512]{1,0:T(8,128)S(1)}, u32[]{:S(2)}, u32[]{:S(2)}) collective-permute-start(f32[144,512]{1,0:T(8,128)S(1)} %collective-permute-done.2.refs_1_), channel_id=1, source_target_pairs={{256,0},{272,16},{288,32},{304,48},{320,64},{336,80},{352,96},{368... | collective-permute-start | bytes 884744 | tf_op jit(solution)/shard_map/ppermute | solution.py:400
  37.5 10.0 %collective-permute-start.6 = (f32[144,512]{1,0:T(8,128)S(1)}, f32[144,512]{1,0:T(8,128)S(1)}, u32[]{:S(2)}, u32[]{:S(2)}) collective-permute-start(f32[144,512]{1,0:T(8,128)S(1)} %collective-permute-done.refs_3_), channel_id=1, source_target_pairs={{256,0},{272,16},{288,32},{304,48},{320,64},{336,80},{352,96},{368... | collective-permute-start | bytes 884744 | tf_op jit(solution)/shard_map/ppermute | solution.py:400
  39.9 10.9 %collective-permute-start.1 = (f32[144,512]{1,0:T(8,128)S(1)}, f32[144,512]{1,0:T(8,128)S(1)}, u32[]{:S(2)}, u32[]{:S(2)}) collective-permute-start(f32[144,512]{1,0:T(8,128)S(1)} %collective-permute-done.refs_3_), channel_id=1, source_target_pairs={{240,0},{0,16},{16,32},{32,48},{48,64},{64,80},{80,96},{96,112},{1... | collective-permute-start | bytes 884744 | tf_op jit(solution)/shard_map/ppermute | solution.py:397
  41.9 15.8 %collective-permute-start.4 = (f32[144,512]{1,0:T(8,128)S(1)}, f32[144,512]{1,0:T(8,128)S(1)}, u32[]{:S(2)}, u32[]{:S(2)}) collective-permute-start(f32[144,512]{1,0:T(8,128)S(1)} %collective-permute-done.3.refs_2_), channel_id=1, source_target_pairs={{256,0},{272,16},{288,32},{304,48},{320,64},{336,80},{352,96},{368... | collective-permute-start | bytes 884744 | tf_op jit(solution)/shard_map/ppermute | solution.py:400
  44.8 6.0 %copy-start.1 = (s32[512]{0:T(512)S(1)}, s32[512]{0:T(512)}, u32[]{:S(2)}) copy-start(s32[512]{0:T(512)} %param.4) | copy-start | bytes 6148
  50.8 1.0 copy-start
  59.1 5.5 %collective-permute-start.7 = (f32[8,192,128]{2,1,0:T(8,128)S(1)}, f32[8,192,128]{2,1,0:T(8,128)S(1)}, u32[]{:S(2)}, u32[]{:S(2)}) collective-permute-start(f32[8,192,128]{2,1,0:T(8,128)S(1)} %get-tuple-element.14), channel_id=1, source_target_pairs={{0,1},{1,0},{2,3},{3,2},{4,5},{5,4},{6,7},{7,6},{8,9},{9,8},{10,11... | collective-permute-start | bytes 2359304 | tf_op jit(solution)/shard_map/ppermute | solution.py:449
  65.6 17.8 %all-to-all-start = ((f32[8,192,128]{2,1,0:T(8,128)}), f32[8,192,128]{2,1,0:T(8,128)S(1)}, u32[]{:S(2)}, u32[]{:S(2)}) async-start(f32[8,192,128]{2,1,0:T(8,128)} %add.22), calls=%async_computation | async-start | bytes 1572864 | tf_op jit(solution)/shard_map/all_to_all | solution.py:451
  85.3 9.2 %collective-permute-start.8 = (f32[48,128]{1,0:T(8,128)S(1)}, f32[48,128]{1,0:T(8,128)S(1)}, u32[]{:S(2)}, u32[]{:S(2)}) collective-permute-start(f32[48,128]{1,0:T(8,128)S(1)} %get-tuple-element.15), channel_id=1, source_target_pairs={{0,14},{1,2},{2,206},{3,194},{4,209},{5,38},{6,10},{7,74},{8,217},... | collective-permute-start | bytes 73736 | tf_op jit(solution)/shard_map/ppermute | solution.py:464
  92.6 11.2 %collective-permute-start.9 = (f32[48,128]{1,0:T(8,128)S(1)}, f32[48,128]{1,0:T(8,128)S(1)}, u32[]{:S(2)}, u32[]{:S(2)}) collective-permute-start(f32[48,128]{1,0:T(8,128)S(1)} %get-tuple-element.16), channel_id=1, source_target_pairs={{0,464},{1,64},{2,470},{3,70},{4,38},{5,193},{6,320},{7,322},{8,29... | collective-permute-start | bytes 73736 | tf_op jit(solution)/shard_map/ppermute | solution.py:465

commit v5 on v4

--- a/solution.py
+++ b/solution.py
@@ -17,16 +17,19 @@
 OWN = (0, 2, 4, -3, -4)
 OTHER = (2, 4, -3)
 STACK = (3, 0, 4, 2)
-EARLY = (
+SAME = (
     (3, 1), (0, 1), (4, 1),
     (3, 2), (0, 2), (4, 2),
+    (0, 3), (4, 3),
+)
+CROSS = (
     (3, 5), (0, 5), (4, 5),
-    (0, 3), (4, 3),
     (0, 7), (4, 7), (2, 7),
 )
-DIAGONAL = EARLY.index((4, 2))
 LATE = ((0, 6), (2, 6))
-POSITION = (11, 4, 12, 5, 0, 2, 10, 3, 1, 9, 6, 8, 13, 7, 14, 15)
+PAIRS = SAME + CROSS + LATE
+DIAGONAL = PAIRS.index((4, 2))
+POSITION = (11, 4, 12, 5, 0, 2, 7, 3, 1, 6, 8, 10, 13, 9, 14, 15)
 CHIPS = SIDE // 2
 
 
@@ -37,8 +40,8 @@
 
 
 def ends_of(column, z, pair):
-    p, q = (EARLY + LATE)[pair]
-    if pair == len(EARLY) + 1 and column == 1:
+    p, q = PAIRS[pair]
+    if pair == len(PAIRS) - 1 and column == 1:
         p = 4
     a, b = frame_block(column, z, p), frame_block(column, z, q)
     if pair == DIAGONAL and z >= SIDE // 2:
@@ -176,54 +179,47 @@
 
 def put_pair(out, pair, core, value, feature):
     k, owner = divmod(POSITION.index(pair), 2)
-    k = k % out[0].shape[0]
-    rest = rest_of(value[:, 128:]) + feature
-    for ref, here in zip(out, (core == owner, core != owner)):
-
-        @pl.when(here)
-        def _():
-            ref[k, : 3 * ROWS] = value[:, :128]
-            ref[k, 3 * ROWS :] = rest
-
-
-def put_group(out, first, pairs, core, weighted, columns, row_feature, column_feature):
-    start = STACK.index(pairs[0][0])
-    rows = weighted[start * 3 * ROWS : (start + len(pairs)) * 3 * ROWS]
-    values = product(rows, columns)
-    for k in range(len(pairs)):
-        value = values[k * 3 * ROWS : (k + 1) * 3 * ROWS]
-        put_pair(out, first + k, core, value, row_feature[start + k] + column_feature)
-
-
-def early_kernel(flags, mass_ref, *refs):
-    blocks, out, (weighted, centered, row_feature, column_feature) = refs[:7], refs[7:9], refs[9:]
+    at = jnp.where(core == owner, k, CHIPS + k)
+    out[at, : 3 * ROWS] = value[:, :128]
+    out[at, 3 * ROWS :] = rest_of(value[:, 128:]) + feature
+
+
+def put_groups(out, pairs, order, core, weighted, centered, row_feature, column_feature):
+    for at, k in enumerate(order):
+        group = [pair for pair in pairs if pair[1] == k]
+        start = STACK.index(group[0][0])
+        assert STACK[start : start + len(group)] == tuple(p for p, _ in group)
+        values = product(weighted[start * 3 * ROWS : (start + len(group)) * 3 * ROWS], centered[at])
+        for n, pair in enumerate(group):
+            value = values[n * 3 * ROWS : (n + 1) * 3 * ROWS]
+            put_pair(out, PAIRS.index(pair), core, value, row_feature[start + n] + column_feature[at])
+
+
+def same_kernel(flags, mass_ref, own_hbm, plus2, plus4, minus3, minus4, out, weighted, row_feature, own, arrived, centered, column_feature):
+    fetch = pltpu.make_async_copy(own_hbm, own, arrived)
+    fetch.start()
     core = flags[2]
-    blocks = dict(zip((0, 1, 2, 3, 4, 5, 7), blocks))
     mass = mass_ref[...].astype(jnp.float32)
-    for at, k in enumerate(STACK):
-        stage_rows(blocks[k], mass, at, core, weighted, row_feature)
-    order = (1, 2, 5, 3, 7)
-    for at, k in enumerate(order):
-        stage_columns(blocks[k], mass, at, core, centered, column_feature)
-    first = 0
-    for at, k in enumerate(order):
-        pairs = [pair for pair in EARLY if pair[1] == k]
-        assert tuple(EARLY[first : first + len(pairs)]) == tuple(pairs)
-        assert tuple(STACK[STACK.index(pairs[0][0]) :][: len(pairs)]) == tuple(p for p, _ in pairs)
-        put_group(out, first, pairs, core, weighted, centered[at], row_feature, column_feature[at])
-        first += len(pairs)
+    order = (1, 2, 3)
+    for at, block in enumerate((plus2, plus4, minus3)):
+        stage_columns(block, mass, at, core, centered, column_feature)
+    for at, block in ((0, minus3), (2, minus4), (3, plus4)):
+        stage_rows(block, mass, at, core, weighted, row_feature)
+    fetch.wait()
+    stage_rows(own, mass, STACK.index(0), core, weighted, row_feature)
+    put_groups(out, SAME, order, core, weighted, centered, row_feature, column_feature)
 
     @pl.when(flags[1] == 1)
     def _():
-        stage_columns(blocks[4], mass, 5, core, centered, column_feature)
-        p, q = STACK.index(4), STACK.index(2)
-        upper = product(weighted[p * 3 * ROWS : (p + 1) * 3 * ROWS], centered[5])
-        lower = product(weighted[q * 3 * ROWS : (q + 1) * 3 * ROWS], centered[order.index(2)])
+        stage_columns(minus4, mass, 3, core, centered, column_feature)
+        p, q, last = STACK.index(4), STACK.index(2), order.index(2)
+        upper = product(weighted[p * 3 * ROWS : (p + 1) * 3 * ROWS], centered[3])
+        lower = product(weighted[q * 3 * ROWS : (q + 1) * 3 * ROWS], centered[last])
         i, j = iota((3 * ROWS, 256), 0) % ROWS, iota((3 * ROWS, 256), 1) % ROWS
         at = iota((ROWS, 256), 1)
         on = jnp.where((i == j) & (iota((3 * ROWS, 256), 1) < 3 * ROWS), lower, 0.0)
         lane = iota((ROWS, 128), 1)
-        ends = row_feature[p] + column_feature[order.index(2)]
+        ends = row_feature[p] + column_feature[last]
         for c in range(3):
             mine = on[c * ROWS : (c + 1) * ROWS]
             for d in range(3):
@@ -233,19 +229,34 @@
         put_pair(out, DIAGONAL, core, jnp.where(i <= j, upper, lower), ends)
 
 
-def late_kernel(flags, mass_ref, *refs):
-    blocks, out, (weighted, centered, row_feature, column_feature) = refs[:4], refs[6:8], refs[8:]
+def cross_kernel(flags, mass_ref, weighted, row_feature, other2, other3, _, out, centered, column_feature):
     core = flags[2]
     mass = mass_ref[...].astype(jnp.float32)
-    for at, block in enumerate(blocks[:3]):
-        stage_rows(block, mass, at, core, weighted, row_feature)
-    stage_columns(blocks[3], mass, 0, core, centered, column_feature)
-    values = product(weighted[...], centered[0])
-    first = len(EARLY)
-    put_pair(out, first, core, values[: 3 * ROWS], row_feature[0] + column_feature[0])
+    for at, block in enumerate((other2, other3)):
+        stage_columns(block, mass, at, core, centered, column_feature)
+    put_groups(out, CROSS, (5, 7), core, weighted, centered, row_feature, column_feature)
+
+
+def late_kernel(flags, mass_ref, weighted, row_feature, other4, sums, send, keep, last, centered, column_feature):
+    core = flags[2]
+    mass = mass_ref[...].astype(jnp.float32)
+    stage_columns(other4, mass, 0, core, centered, column_feature)
+    values = product(weighted[3 * ROWS :], centered[0])
     other = flags[0] == 1
-    value = jnp.where(other, values[3 * ROWS : 6 * ROWS], values[6 * ROWS :])
-    put_pair(out, first + 1, core, value, jnp.where(other, row_feature[1], row_feature[2]) + column_feature[0])
+    for n in range(2):
+        rows = values[: 3 * ROWS] if n == 0 else jnp.where(other, values[3 * ROWS : 6 * ROWS], values[6 * ROWS :])
+        feature = row_feature[1] if n == 0 else jnp.where(other, row_feature[2], row_feature[3])
+        at = jnp.where(core == n, 0, 1)
+        last[at, : 3 * ROWS] = rows[:, :128]
+        last[at, 3 * ROWS :] = rest_of(rows[:, 128:]) + feature + column_feature[0]
+    keep[0] = last[0]
+    send[CHIPS - 1] = last[1]
+    send[: CHIPS - 1] = sums[CHIPS : 2 * CHIPS - 1]
+
+
+def merge_kernel(sums, keep, taken, out):
+    out[: CHIPS - 1] = sums[: CHIPS - 1] + taken[: CHIPS - 1]
+    out[CHIPS - 1] = keep[0] + taken[CHIPS - 1]
 
 
 def det_four(rows):
@@ -409,51 +420,63 @@
     other4 = across(plus4)
 
     atoms = own.shape[1]
-    result = [jax.ShapeDtypeStruct((CHIPS, 4 * ROWS, 128), jnp.float32)] * 2
-
-    def scratch(rows, columns):
-        return [
-            pltpu.VMEM((rows * 3 * ROWS, 3 * atoms), jnp.bfloat16),
-            pltpu.VMEM((columns, 256, 3 * atoms), jnp.bfloat16),
-            pltpu.VMEM((rows, ROWS, 128), jnp.float32),
-            pltpu.VMEM((columns, ROWS, 128), jnp.float32),
-        ]
-
     smem = pl.BlockSpec(memory_space=pltpu.SMEM)
+    vmem = pl.BlockSpec(memory_space=pltpu.VMEM)
     params = pltpu.CompilerParams(vmem_limit_bytes=VMEM_LIMIT)
-    whole = lambda *shape: pl.BlockSpec(shape, lambda i: (0,) * len(shape))
-    block_spec = whole(3 * ROWS, atoms)
-    pair_flops = 2 * 3 * ROWS * 256 * atoms * 3
-    partial = pl.pallas_call(
-        early_kernel,
-        grid=(1,),
-        out_shape=result,
-        in_specs=[smem, whole(1, atoms)] + [block_spec] * 7,
-        out_specs=[whole(len(EARLY) // 2, 4 * ROWS, 128)] * 2,
-        scratch_shapes=scratch(4, 6),
+
+    def columns_scratch(n):
+        return [pltpu.VMEM((n, 256, 3 * atoms), jnp.bfloat16), pltpu.VMEM((n, ROWS, 128), jnp.float32)]
+
+    def cost(pairs):
+        return pl.CostEstimate(flops=pairs * 2 * 3 * ROWS * 256 * atoms * 3, bytes_accessed=4_000_000, transcendentals=0)
+
+    def sums_of(n):
+        return jax.ShapeDtypeStruct((n, 4 * ROWS, 128), jnp.float32)
+
+    sums, weighted, row_feature = pl.pallas_call(
+        same_kernel,
+        out_shape=[
+            sums_of(2 * CHIPS),
+            jax.ShapeDtypeStruct((len(STACK) * 3 * ROWS, 3 * atoms), jnp.bfloat16),
+            jax.ShapeDtypeStruct((len(STACK), ROWS, 128), jnp.float32),
+        ],
+        in_specs=[smem, vmem, pl.BlockSpec(memory_space=pltpu.HBM)] + [vmem] * 4,
+        out_specs=[vmem] * 3,
+        scratch_shapes=[pltpu.VMEM(own.shape, jnp.float32), pltpu.SemaphoreType.DMA(())] + columns_scratch(4),
         compiler_params=params,
-        cost_estimate=pl.CostEstimate(flops=14 * pair_flops, bytes_accessed=4_000_000, transcendentals=0),
-    )(build_flags, mass, own, plus2, plus4, minus3, minus4, other2, other3)
-    keep, send = pl.pallas_call(
+        cost_estimate=cost(len(SAME) + 1),
+    )(build_flags, mass, own, plus2, plus4, minus3, minus4)
+    sums = pl.pallas_call(
+        cross_kernel,
+        out_shape=sums_of(2 * CHIPS),
+        in_specs=[smem] + [vmem] * 6,
+        out_specs=vmem,
+        scratch_shapes=columns_scratch(2),
+        input_output_aliases={6: 0},
+        compiler_params=params,
+        cost_estimate=cost(len(CROSS)),
+    )(build_flags, mass, weighted, row_feature, other2, other3, sums)
+    send, keep = pl.pallas_call(
         late_kernel,
-        grid=(1,),
-        out_shape=result,
-        in_specs=[smem, whole(1, atoms)] + [block_spec] * 4 + [pl.BlockSpec(memory_space=pl.ANY)] * 2,
-        out_specs=[pl.BlockSpec((1, 4 * ROWS, 128), lambda i: (CHIPS - 1, 0, 0))] * 2,
-        scratch_shapes=scratch(3, 1),
-        input_output_aliases={6: 0, 7: 1},
+        out_shape=[sums_of(CHIPS), sums_of(1)],
+        in_specs=[smem] + [vmem] * 5,
+        out_specs=[vmem] * 2,
+        scratch_shapes=[pltpu.VMEM((2, 4 * ROWS, 128), jnp.float32)] + columns_scratch(1),
         compiler_params=params,
-        cost_estimate=pl.CostEstimate(flops=3 * pair_flops, bytes_accessed=2_000_000, transcendentals=0),
-    )(build_flags, mass, own, minus4, plus4, other4, *partial)
-
+        cost_estimate=cost(len(LATE) + 1),
+    )(build_flags, mass, weighted, row_feature, other4, sums)
     taken = lax.ppermute(send, "atom", [(a, a ^ 1) for a in range(SIDE)])
+    merged = pl.pallas_call(
+        merge_kernel,
+        out_shape=sums_of(CHIPS),
+        in_specs=[vmem] * 3,
+        out_specs=vmem,
+        compiler_params=params,
+    )(sums, keep, taken)
     groups = [[f * SIDE + 2 * chip + c for chip in orders[f]] for f in range(2 * SIDE) for c in range(2)]
-    parts = lax.all_to_all(
-        keep + taken, ("frame", "atom"), 0, 0, axis_index_groups=groups, tiled=True
-    )
+    parts = lax.all_to_all(merged, ("frame", "atom"), 0, 0, axis_index_groups=groups, tiled=True)
 
     block = jax.ShapeDtypeStruct((ROWS, 128), jnp.float32)
-    vmem = pl.BlockSpec(memory_space=pltpu.VMEM)
     one, two = pl.pallas_call(
         fit_kernel,
         out_shape=(block, block),

time: 105 us -> 110 us (1.048)
  waiting for transfers between devices: 39.4 us -> 44.5 us
    ppermute x3, waiting for transfers between devices: 2.61 us -> 7.26 us  [across(): lax.ppermute(block, 'frame', [((f + SIDE) % (2 * SIDE), f) for f in range...]
    pallas_call x2 -> x4, Pallas kernels: 7.35 us -> 6.8 us  [the longest x1 2.64 us: on_device(): pl.pallas_call(same_kernel, out_shape=[sums_of(2 * CHIPS), jax.ShapeDtype...]
  transfers between devices with their start and end apart: 11 -> 11, of which waited for: 7 -> 8; matrix products, arithmetic and copies ran while one was open for 1% -> 1% of each run, Pallas kernels for 6% -> 4%
where the time goes in v5:
time: 110 us
  starting transfers between devices  50 us (45%)
  waiting for transfers between devices  44.5 us (40%)
  Pallas kernels  9.92 us (9%)
  local copies, waits for them, and re-layouts  2.91 us (3%)
  between operations  2.13 us (2%)
    ppermute x4, starting transfers between devices, along(): return lax.ppermute(block, 'frame', route)  21.5 us
    ppermute x4, waiting for transfers between devices, along(): return lax.ppermute(block, 'frame', route)  19.2 us
    ppermute x1, waiting for transfers between devices, on_device(): two = lax.ppermute(two, ('frame', 'atom'), list(enumerate(second)))  9.22 us
    ppermute x1, starting transfers between devices, on_device(): one = lax.ppermute(one, ('frame', 'atom'), list(enumerate(first)))  7.89 us
    ppermute x3, starting transfers between devices, across(): lax.ppermute(block, 'frame', [((f + SIDE) % (2 * SIDE), f) for f in range...  7.74 us
    all_to_all x1, starting transfers between devices, on_device(): lax.all_to_all(merged, ('frame', 'atom'), 0, 0, axis_index_groups=groups,...  7.59 us
    ppermute x3, waiting for transfers between devices, across(): lax.ppermute(block, 'frame', [((f + SIDE) % (2 * SIDE), f) for f in range...  7.26 us
    all_to_all x1, waiting for transfers between devices, on_device(): lax.all_to_all(merged, ('frame', 'atom'), 0, 0, axis_index_groups=groups,...  6.92 us
  transfers between devices with their start and end apart: 11, of which 8 were waited for; matrix products, arithmetic and copies ran while one was open for 1% of the time, Pallas kernels for 4%

profile of v5, /device:TPU:7, one launch (start us, length us, event | category | flops | bytes accessed | tf_op | source)
XLA Modules:
  0.0 109.6 jit_solution(12308852233169341887)
XLA Ops:
  0.0 11.6 %collective-permute-start = (f32[144,512]{1,0:T(8,128)}, f32[144,512]{1,0:T(8,128)S(1)}, u32[]{:S(2)}, u32[]{:S(2)}) collective-permute-start(f32[144,512]{1,0:T(8,128)} %bitcast.8), channel_id=1, source_target_pairs={{32,0},{48,16},{64,32},{80,48},{96,64},{112,80},{128,96},{144,112}... | collective-permute-start | bytes 884744 | tf_op jit(solution)/shard_map/ppermute | solution.py:408
  11.6 1.9 %collective-permute-start.2 = (f32[144,512]{1,0:T(8,128)}, f32[144,512]{1,0:T(8,128)S(1)}, u32[]{:S(2)}, u32[]{:S(2)}) collective-permute-start(f32[144,512]{1,0:T(8,128)} %bitcast.9), channel_id=1, source_target_pairs={{208,0},{224,16},{240,32},{0,48},{16,64},{32,80},{48,96},{64,112},... | collective-permute-start | bytes 884744 | tf_op jit(solution)/shard_map/ppermute | solution.py:408
  13.5 10.4 %collective-permute-done.plus2 = f32[144,512]{1,0:T(8,128)S(1)} collective-permute-done((f32[144,512]{1,0:T(8,128)}, f32[144,512]{1,0:T(8,128)S(1)}, u32[]{:S(2)}, u32[]{:S(2)}) %collective-permute-start) | collective-permute-done | bytes 294944 | tf_op jit(solution)/shard_map/ppermute | solution.py:408
  23.9 6.1 %collective-permute-start.1 = (f32[144,512]{1,0:T(8,128)S(1)}, f32[144,512]{1,0:T(8,128)S(1)}, u32[]{:S(2)}, u32[]{:S(2)}) collective-permute-start(f32[144,512]{1,0:T(8,128)S(1)} %collective-permute-done.plus2), channel_id=1, source_target_pairs={{32,0},{48,16},{64,32},{80,48},{96,64},{112,80},{128,96},{144,112}... | collective-permute-start | bytes 884744 | tf_op jit(solution)/shard_map/ppermute | solution.py:408
  30.0 7.5 %collective-permute-done.2.minus3 = f32[144,512]{1,0:T(8,128)S(1)} collective-permute-done((f32[144,512]{1,0:T(8,128)}, f32[144,512]{1,0:T(8,128)S(1)}, u32[]{:S(2)}, u32[]{:S(2)}) %collective-permute-start.2) | collective-permute-done | bytes 294944 | tf_op jit(solution)/shard_map/ppermute | solution.py:408
  37.5 1.9 %collective-permute-start.3 = (f32[144,512]{1,0:T(8,128)S(1)}, f32[144,512]{1,0:T(8,128)S(1)}, u32[]{:S(2)}, u32[]{:S(2)}) collective-permute-start(f32[144,512]{1,0:T(8,128)S(1)} %collective-permute-done.2.minus3), channel_id=1, source_target_pairs={{240,0},{0,16},{16,32},{32,48},{48,64},{64,80},{80,96},{96,112},{1... | collective-permute-start | bytes 884744 | tf_op jit(solution)/shard_map/ppermute | solution.py:408
  39.4 2.5 %collective-permute-start.5 = (f32[144,512]{1,0:T(8,128)S(1)}, f32[144,512]{1,0:T(8,128)S(1)}, u32[]{:S(2)}, u32[]{:S(2)}) collective-permute-start(f32[144,512]{1,0:T(8,128)S(1)} %collective-permute-done.2.minus3), channel_id=1, source_target_pairs={{256,0},{272,16},{288,32},{304,48},{320,64},{336,80},{352,96},{368... | collective-permute-start | bytes 884744 | tf_op jit(solution)/shard_map/ppermute | solution.py:411
  41.9 2.8 %collective-permute-start.4 = (f32[144,512]{1,0:T(8,128)S(1)}, f32[144,512]{1,0:T(8,128)S(1)}, u32[]{:S(2)}, u32[]{:S(2)}) collective-permute-start(f32[144,512]{1,0:T(8,128)S(1)} %collective-permute-done.plus2), channel_id=1, source_target_pairs={{256,0},{272,16},{288,32},{304,48},{320,64},{336,80},{352,96},{368... | collective-permute-start | bytes 884744 | tf_op jit(solution)/shard_map/ppermute | solution.py:411
  44.7 0.0 collective-permute-done.1.plus4
  44.8 2.5 %collective-permute-start.6 = (f32[144,512]{1,0:T(8,128)S(1)}, f32[144,512]{1,0:T(8,128)S(1)}, u32[]{:S(2)}, u32[]{:S(2)}) collective-permute-start(f32[144,512]{1,0:T(8,128)S(1)} %collective-permute-done.1.plus4), channel_id=1, source_target_pairs={{256,0},{272,16},{288,32},{304,48},{320,64},{336,80},{352,96},{368... | collective-permute-start | bytes 884744 | tf_op jit(solution)/shard_map/ppermute | solution.py:411
  47.3 0.1 pad_add_fusion.1.flags
  47.3 1.3 %collective-permute-done.3.minus4 = f32[144,512]{1,0:T(8,128)S(1)} collective-permute-done((f32[144,512]{1,0:T(8,128)S(1)}, f32[144,512]{1,0:T(8,128)S(1)}, u32[]{:S(2)}, u32[]{:S(2)}) %collective-permute-start.3) | collective-permute-done | bytes 294944 | tf_op jit(solution)/shard_map/ppermute | solution.py:408
  48.6 0.0 copy-start
  48.6 0.7 copy-done
  49.3 0.0 copy-start.1
  49.3 1.0 copy-done.1
  50.3 2.6 %shard_map.37 = (f32[16,192,128]{2,1,0:T(8,128)S(1)}, bf16[576,1536]{1,0:T(8,128)(2,1)S(1)}, f32[4,48,128]{2,1,0:T(8,128)S(1)}) custom-call(s32[3]{0:T(128)S(1)} %pad_add_fusion.1.flags, s32[1,512]{1,0:T(1,128)S(1)} %bitcast.5, f32[144,512]{1,0:T(8,128)S(1)} %bitcast.10, f32[144,512]{1,0:T(8,128)S(1)} %collective-permute-done.plus2, ...), custom_call_target="tpu_custom_call" | custom-call | flops 1019215872 | bytes 4000000 | tf_op jit(solution)/shard_map/pallas_call | solution.py:436
  52.9 0.0 collective-permute-done.5.other3
  52.9 2.7 %collective-permute-done.4.other2 = f32[144,512]{1,0:T(8,128)S(1)} collective-permute-done((f32[144,512]{1,0:T(8,128)S(1)}, f32[144,512]{1,0:T(8,128)S(1)}, u32[]{:S(2)}, u32[]{:S(2)}) %collective-permute-start.4) | collective-permute-done | bytes 294944 | tf_op jit(solution)/shard_map/ppermute | solution.py:411
  55.7 1.8 %shard_map.38.sums = f32[16,192,128]{2,1,0:T(8,128)S(1)} custom-call(s32[3]{0:T(128)S(1)} %pad_add_fusion.1.flags, s32[1,512]{1,0:T(1,128)S(1)} %bitcast.6, bf16[576,1536]{1,0:T(8,128)(2,1)S(1)} %get-tuple-element.12.weighted, f32[4,48,128]{2,1,0:T(8,128)S(1)} %get-tuple-element.13.row_feature, ...), custom_call_target="tpu_custom_call", output_to_operand_aliasing={{}: (6, {})} | custom-call | flops 679477248 | bytes 4000000 | tf_op jit(solution)/shard_map/pallas_call | solution.py:449
  57.5 4.5 %collective-permute-done.6.other4 = f32[144,512]{1,0:T(8,128)S(1)} collective-permute-done((f32[144,512]{1,0:T(8,128)S(1)}, f32[144,512]{1,0:T(8,128)S(1)}, u32[]{:S(2)}, u32[]{:S(2)}) %collective-permute-start.6) | collective-permute-done | bytes 294944 | tf_op jit(solution)/shard_map/ppermute | solution.py:411
  62.0 1.4 %shard_map.39 = (f32[8,192,128]{2,1,0:T(8,128)S(1)}, f32[1,192,128]{2,1,0:T(8,128)S(1)}) custom-call(s32[3]{0:T(128)S(1)} %pad_add_fusion.1.flags, s32[1,512]{1,0:T(1,128)S(1)} %bitcast.7, bf16[576,1536]{1,0:T(8,128)(2,1)S(1)} %get-tuple-element.12.weighted, f32[4,48,128]{2,1,0:T(8,128)S(1)} %get-tuple-element.13.row_feature, ...), custom_call_target="tpu_custom_call" | custom-call | flops 339738624 | bytes 4000000 | tf_op jit(solution)/shard_map/pallas_call | solution.py:459
  63.4 3.3 %collective-permute-start.7 = (f32[8,192,128]{2,1,0:T(8,128)S(1)}, f32[8,192,128]{2,1,0:T(8,128)S(1)}, u32[]{:S(2)}, u32[]{:S(2)}) collective-permute-start(f32[8,192,128]{2,1,0:T(8,128)S(1)} %get-tuple-element.16), channel_id=1, source_target_pairs={{0,1},{1,0},{2,3},{3,2},{4,5},{5,4},{6,7},{7,6},{8,9},{9,8},{10,11... | collective-permute-start | bytes 2359304 | tf_op jit(solution)/shard_map/ppermute | solution.py:468
  66.7 1.9 %collective-permute-done.7.taken = f32[8,192,128]{2,1,0:T(8,128)S(1)} collective-permute-done((f32[8,192,128]{2,1,0:T(8,128)S(1)}, f32[8,192,128]{2,1,0:T(8,128)S(1)}, u32[]{:S(2)}, u32[]{:S(2)}) %collective-permute-start.7) | collective-permute-done | bytes 786464 | tf_op jit(solution)/shard_map/ppermute | solution.py:468
  68.6 1.0 shard_map.40
  69.6 7.6 %all-to-all-start = ((f32[8,192,128]{2,1,0:T(8,128)}), f32[8,192,128]{2,1,0:T(8,128)S(1)}, u32[]{:S(2)}, u32[]{:S(2)}) async-start(f32[8,192,128]{2,1,0:T(8,128)} %shard_map.40), calls=%async_computation | async-start | bytes 1572864 | tf_op jit(solution)/shard_map/all_to_all | solution.py:477
  77.2 1.3 %dynamic_slice.3 = s32[1]{0:T(128)} dynamic-slice(s32[512]{0:T(512)} %constant.67.clone, s32[]{:T(128)S(6)} %select_n.21), dynamic_slice_sizes={1} | dynamic-slice | bytes 12 | tf_op jit(solution)/shard_map/dynamic_slice | solution.py:400
  80.4 0.1 pad_add_fusion.flags
  80.5 6.9 %all-to-all-done.parts = f32[8,192,128]{2,1,0:T(8,128)S(1)} async-done(((f32[8,192,128]{2,1,0:T(8,128)}), f32[8,192,128]{2,1,0:T(8,128)S(1)}, u32[]{:S(2)}, u32[]{:S(2)}) %all-to-all-start) | async-done | bytes 786464 | tf_op jit(solution)/shard_map/all_to_all | solution.py:477
  87.4 1.9 %shard_map.41 = (f32[48,128]{1,0:T(8,128)S(1)}, f32[48,128]{1,0:T(8,128)S(1)}) custom-call(s32[3]{0:T(128)S(1)} %pad_add_fusion.flags, f32[8,192,128]{2,1,0:T(8,128)S(1)} %all-to-all-done.parts), custom_call_target="tpu_custom_call" | custom-call | tf_op jit(solution)/shard_map/pallas_call | solution.py:480
  89.3 7.9 %collective-permute-start.8 = (f32[48,128]{1,0:T(8,128)S(1)}, f32[48,128]{1,0:T(8,128)S(1)}, u32[]{:S(2)}, u32[]{:S(2)}) collective-permute-start(f32[48,128]{1,0:T(8,128)S(1)} %get-tuple-element.17), channel_id=1, source_target_pairs={{0,14},{1,2},{2,206},{3,194},{4,209},{5,38},{6,10},{7,74},{8,217},... | collective-permute-start | bytes 73736 | tf_op jit(solution)/shard_map/ppermute | solution.py:487
  97.2 1.9 %collective-permute-start.9 = (f32[48,128]{1,0:T(8,128)S(1)}, f32[48,128]{1,0:T(8,128)S(1)}, u32[]{:S(2)}, u32[]{:S(2)}) collective-permute-start(f32[48,128]{1,0:T(8,128)S(1)} %get-tuple-element.18), channel_id=1, source_target_pairs={{0,464},{1,64},{2,470},{3,70},{4,38},{5,193},{6,320},{7,322},{8,29... | collective-permute-start | bytes 73736 | tf_op jit(solution)/shard_map/ppermute | solution.py:488
  99.1 0.0 collective-permute-done.8.first
  99.1 9.2 %collective-permute-done.9.second = f32[48,128]{1,0:T(8,128)S(1)} collective-permute-done((f32[48,128]{1,0:T(8,128)S(1)}, f32[48,128]{1,0:T(8,128)S(1)}, u32[]{:S(2)}, u32[]{:S(2)}) %collective-permute-start.9) | collective-permute-done | bytes 24608 | tf_op jit(solution)/shard_map/ppermute | solution.py:488
  108.3 1.2 %shard_map.42 = f32[48,96]{1,0:T(8,128)} custom-call(s32[3]{0:T(128)S(1)} %pad_add_fusion.flags, f32[48,128]{1,0:T(8,128)S(1)} %collective-permute-done.8.first, f32[48,128]{1,0:T(8,128)S(1)} %collective-permute-done.9.second), custom_call_target="tpu_custom_call" | custom-call | tf_op jit(solution)/shard_map/pallas_call | solution.py:489
Async XLA Ops:
  0.0 23.9 %collective-permute-start = (f32[144,512]{1,0:T(8,128)}, f32[144,512]{1,0:T(8,128)S(1)}, u32[]{:S(2)}, u32[]{:S(2)}) collective-permute-start(f32[144,512]{1,0:T(8,128)} %bitcast.8), channel_id=1, source_target_pairs={{32,0},{48,16},{64,32},{80,48},{96,64},{112,80},{128,96},{144,112}... | collective-permute-start | bytes 884744 | tf_op jit(solution)/shard_map/ppermute | solution.py:408
  11.6 26.0 %collective-permute-start.2 = (f32[144,512]{1,0:T(8,128)}, f32[144,512]{1,0:T(8,128)S(1)}, u32[]{:S(2)}, u32[]{:S(2)}) collective-permute-start(f32[144,512]{1,0:T(8,128)} %bitcast.9), channel_id=1, source_target_pairs={{208,0},{224,16},{240,32},{0,48},{16,64},{32,80},{48,96},{64,112},... | collective-permute-start | bytes 884744 | tf_op jit(solution)/shard_map/ppermute | solution.py:408
  23.9 20.8 %collective-permute-start.1 = (f32[144,512]{1,0:T(8,128)S(1)}, f32[144,512]{1,0:T(8,128)S(1)}, u32[]{:S(2)}, u32[]{:S(2)}) collective-permute-start(f32[144,512]{1,0:T(8,128)S(1)} %collective-permute-done.plus2), channel_id=1, source_target_pairs={{32,0},{48,16},{64,32},{80,48},{96,64},{112,80},{128,96},{144,112}... | collective-permute-start | bytes 884744 | tf_op jit(solution)/shard_map/ppermute | solution.py:408
  37.5 11.1 %collective-permute-start.3 = (f32[144,512]{1,0:T(8,128)S(1)}, f32[144,512]{1,0:T(8,128)S(1)}, u32[]{:S(2)}, u32[]{:S(2)}) collective-permute-start(f32[144,512]{1,0:T(8,128)S(1)} %collective-permute-done.2.minus3), channel_id=1, source_target_pairs={{240,0},{0,16},{16,32},{32,48},{48,64},{64,80},{80,96},{96,112},{1... | collective-permute-start | bytes 884744 | tf_op jit(solution)/shard_map/ppermute | solution.py:408
  39.4 13.5 %collective-permute-start.5 = (f32[144,512]{1,0:T(8,128)S(1)}, f32[144,512]{1,0:T(8,128)S(1)}, u32[]{:S(2)}, u32[]{:S(2)}) collective-permute-start(f32[144,512]{1,0:T(8,128)S(1)} %collective-permute-done.2.minus3), channel_id=1, source_target_pairs={{256,0},{272,16},{288,32},{304,48},{320,64},{336,80},{352,96},{368... | collective-permute-start | bytes 884744 | tf_op jit(solution)/shard_map/ppermute | solution.py:411
  41.9 13.8 %collective-permute-start.4 = (f32[144,512]{1,0:T(8,128)S(1)}, f32[144,512]{1,0:T(8,128)S(1)}, u32[]{:S(2)}, u32[]{:S(2)}) collective-permute-start(f32[144,512]{1,0:T(8,128)S(1)} %collective-permute-done.plus2), channel_id=1, source_target_pairs={{256,0},{272,16},{288,32},{304,48},{320,64},{336,80},{352,96},{368... | collective-permute-start | bytes 884744 | tf_op jit(solution)/shard_map/ppermute | solution.py:411
  44.8 17.2 %collective-permute-start.6 = (f32[144,512]{1,0:T(8,128)S(1)}, f32[144,512]{1,0:T(8,128)S(1)}, u32[]{:S(2)}, u32[]{:S(2)}) collective-permute-start(f32[144,512]{1,0:T(8,128)S(1)} %collective-permute-done.1.plus4), channel_id=1, source_target_pairs={{256,0},{272,16},{288,32},{304,48},{320,64},{336,80},{352,96},{368... | collective-permute-start | bytes 884744 | tf_op jit(solution)/shard_map/ppermute | solution.py:411
  48.6 0.7 copy-start
  49.3 1.0 copy-start.1
  63.4 5.2 %collective-permute-start.7 = (f32[8,192,128]{2,1,0:T(8,128)S(1)}, f32[8,192,128]{2,1,0:T(8,128)S(1)}, u32[]{:S(2)}, u32[]{:S(2)}) collective-permute-start(f32[8,192,128]{2,1,0:T(8,128)S(1)} %get-tuple-element.16), channel_id=1, source_target_pairs={{0,1},{1,0},{2,3},{3,2},{4,5},{5,4},{6,7},{7,6},{8,9},{9,8},{10,11... | collective-permute-start | bytes 2359304 | tf_op jit(solution)/shard_map/ppermute | solution.py:468
  69.6 17.8 %all-to-all-start = ((f32[8,192,128]{2,1,0:T(8,128)}), f32[8,192,128]{2,1,0:T(8,128)S(1)}, u32[]{:S(2)}, u32[]{:S(2)}) async-start(f32[8,192,128]{2,1,0:T(8,128)} %shard_map.40), calls=%async_computation | async-start | bytes 1572864 | tf_op jit(solution)/shard_map/all_to_all | solution.py:477
  89.3 9.8 %collective-permute-start.8 = (f32[48,128]{1,0:T(8,128)S(1)}, f32[48,128]{1,0:T(8,128)S(1)}, u32[]{:S(2)}, u32[]{:S(2)}) collective-permute-start(f32[48,128]{1,0:T(8,128)S(1)} %get-tuple-element.17), channel_id=1, source_target_pairs={{0,14},{1,2},{2,206},{3,194},{4,209},{5,38},{6,10},{7,74},{8,217},... | collective-permute-start | bytes 73736 | tf_op jit(solution)/shard_map/ppermute | solution.py:487
  97.2 11.2 %collective-permute-start.9 = (f32[48,128]{1,0:T(8,128)S(1)}, f32[48,128]{1,0:T(8,128)S(1)}, u32[]{:S(2)}, u32[]{:S(2)}) collective-permute-start(f32[48,128]{1,0:T(8,128)S(1)} %get-tuple-element.18), channel_id=1, source_target_pairs={{0,464},{1,64},{2,470},{3,70},{4,38},{5,193},{6,320},{7,322},{8,29... | collective-permute-start | bytes 73736 | tf_op jit(solution)/shard_map/ppermute | solution.py:488

commit v6 on v5

--- a/solution.py
+++ b/solution.py
@@ -17,17 +17,15 @@
 OWN = (0, 2, 4, -3, -4)
 OTHER = (2, 4, -3)
 STACK = (3, 0, 4, 2)
-SAME = (
+EARLY = (
     (3, 1), (0, 1), (4, 1),
     (3, 2), (0, 2), (4, 2),
     (0, 3), (4, 3),
-)
-CROSS = (
     (3, 5), (0, 5), (4, 5),
     (0, 7), (4, 7), (2, 7),
 )
 LATE = ((0, 6), (2, 6))
-PAIRS = SAME + CROSS + LATE
+PAIRS = EARLY + LATE
 DIAGONAL = PAIRS.index((4, 2))
 POSITION = (11, 4, 12, 5, 0, 2, 7, 3, 1, 6, 8, 10, 13, 9, 14, 15)
 CHIPS = SIDE // 2
@@ -195,25 +193,33 @@
             put_pair(out, PAIRS.index(pair), core, value, row_feature[start + n] + column_feature[at])
 
 
-def same_kernel(flags, mass_ref, own_hbm, plus2, plus4, minus3, minus4, out, weighted, row_feature, own, arrived, centered, column_feature):
-    fetch = pltpu.make_async_copy(own_hbm, own, arrived)
-    fetch.start()
+def first_kernel(flags, mass_ref, own, plus2, other2, other3, weighted, row_feature, centered, column_feature):
     core = flags[2]
     mass = mass_ref[...].astype(jnp.float32)
-    order = (1, 2, 3)
-    for at, block in enumerate((plus2, plus4, minus3)):
+    stage_rows(own, mass, STACK.index(0), core, weighted, row_feature)
+    for at, block in enumerate((plus2, other2, other3)):
+        stage_columns(block, mass, at, core, centered, column_feature)
+
+
+def early_kernel(
+    flags, mass_ref, plus4, minus3, minus4, first_centered, first_feature, _, __,
+    out, weighted, row_feature, centered, column_feature,
+):
+    core = flags[2]
+    mass = mass_ref[...].astype(jnp.float32)
+    order = (2, 3)
+    for at, block in enumerate((plus4, minus3)):
         stage_columns(block, mass, at, core, centered, column_feature)
     for at, block in ((0, minus3), (2, minus4), (3, plus4)):
         stage_rows(block, mass, at, core, weighted, row_feature)
-    fetch.wait()
-    stage_rows(own, mass, STACK.index(0), core, weighted, row_feature)
-    put_groups(out, SAME, order, core, weighted, centered, row_feature, column_feature)
+    put_groups(out, EARLY, (1, 5, 7), core, weighted, first_centered, row_feature, first_feature)
+    put_groups(out, EARLY, order, core, weighted, centered, row_feature, column_feature)
 
     @pl.when(flags[1] == 1)
     def _():
-        stage_columns(minus4, mass, 3, core, centered, column_feature)
+        stage_columns(minus4, mass, 2, core, centered, column_feature)
         p, q, last = STACK.index(4), STACK.index(2), order.index(2)
-        upper = product(weighted[p * 3 * ROWS : (p + 1) * 3 * ROWS], centered[3])
+        upper = product(weighted[p * 3 * ROWS : (p + 1) * 3 * ROWS], centered[2])
         lower = product(weighted[q * 3 * ROWS : (q + 1) * 3 * ROWS], centered[last])
         i, j = iota((3 * ROWS, 256), 0) % ROWS, iota((3 * ROWS, 256), 1) % ROWS
         at = iota((ROWS, 256), 1)
@@ -227,14 +233,6 @@
                 value = jnp.sum(jnp.where(inside, mine, 0.0), axis=1, keepdims=True)
                 ends = jnp.where(lane == 66 + 3 * c + d, value, ends)
         put_pair(out, DIAGONAL, core, jnp.where(i <= j, upper, lower), ends)
-
-
-def cross_kernel(flags, mass_ref, weighted, row_feature, other2, other3, _, out, centered, column_feature):
-    core = flags[2]
-    mass = mass_ref[...].astype(jnp.float32)
-    for at, block in enumerate((other2, other3)):
-        stage_columns(block, mass, at, core, centered, column_feature)
-    put_groups(out, CROSS, (5, 7), core, weighted, centered, row_feature, column_feature)
 
 
 def late_kernel(flags, mass_ref, weighted, row_feature, other4, sums, send, keep, last, centered, column_feature):
@@ -433,29 +431,32 @@
     def sums_of(n):
         return jax.ShapeDtypeStruct((n, 4 * ROWS, 128), jnp.float32)
 
+    staged = [
+        jax.ShapeDtypeStruct((len(STACK) * 3 * ROWS, 3 * atoms), jnp.bfloat16),
+        jax.ShapeDtypeStruct((len(STACK), ROWS, 128), jnp.float32),
+    ]
+    columns = [
+        jax.ShapeDtypeStruct((3, 256, 3 * atoms), jnp.bfloat16),
+        jax.ShapeDtypeStruct((3, ROWS, 128), jnp.float32),
+    ]
+    weighted, row_feature, centered, column_feature = pl.pallas_call(
+        first_kernel,
+        out_shape=staged + columns,
+        in_specs=[smem] + [vmem] * 5,
+        out_specs=[vmem] * 4,
+        compiler_params=params,
+        cost_estimate=cost(len(EARLY)),
+    )(build_flags, mass, own, plus2, other2, other3)
     sums, weighted, row_feature = pl.pallas_call(
-        same_kernel,
-        out_shape=[
-            sums_of(2 * CHIPS),
-            jax.ShapeDtypeStruct((len(STACK) * 3 * ROWS, 3 * atoms), jnp.bfloat16),
-            jax.ShapeDtypeStruct((len(STACK), ROWS, 128), jnp.float32),
-        ],
-        in_specs=[smem, vmem, pl.BlockSpec(memory_space=pltpu.HBM)] + [vmem] * 4,
+        early_kernel,
+        out_shape=[sums_of(2 * CHIPS)] + staged,
+        in_specs=[smem] + [vmem] * 8,
         out_specs=[vmem] * 3,
-        scratch_shapes=[pltpu.VMEM(own.shape, jnp.float32), pltpu.SemaphoreType.DMA(())] + columns_scratch(4),
+        scratch_shapes=columns_scratch(3),
+        input_output_aliases={7: 1, 8: 2},
         compiler_params=params,
-        cost_estimate=cost(len(SAME) + 1),
-    )(build_flags, mass, own, plus2, plus4, minus3, minus4)
-    sums = pl.pallas_call(
-        cross_kernel,
-        out_shape=sums_of(2 * CHIPS),
-        in_specs=[smem] + [vmem] * 6,
-        out_specs=vmem,
-        scratch_shapes=columns_scratch(2),
-        input_output_aliases={6: 0},
-        compiler_params=params,
-        cost_estimate=cost(len(CROSS)),
-    )(build_flags, mass, weighted, row_feature, other2, other3, sums)
+        cost_estimate=cost(len(EARLY) + 1),
+    )(build_flags, mass, plus4, minus3, minus4, centered, column_feature, weighted, row_feature)
     send, keep = pl.pallas_call(
         late_kernel,
         out_shape=[sums_of(CHIPS), sums_of(1)],

time: 110 us -> 103 us (0.936)
  waiting for transfers between devices: 44.5 us -> 36.8 us
    ppermute x3, waiting for transfers between devices: 7.26 us -> 2.73 us  [across(): lax.ppermute(block, 'frame', [((f + SIDE) % (2 * SIDE), f) for f in range...]
    ppermute x4, waiting for transfers between devices: 19.2 us -> 16 us  [along(): return lax.ppermute(block, 'frame', route)]
where the time goes in v6:
time: 103 us; the launch traced here: 102 us
  starting transfers between devices  51 us (50%)
  waiting for transfers between devices  36.8 us (36%)
  Pallas kernels  9.4 us (9%)
  local copies, waits for them, and re-layouts  2.91 us (3%)
  between operations  2.12 us (2%)
    ppermute x4, starting transfers between devices, along(): return lax.ppermute(block, 'frame', route)  21.5 us
    ppermute x4, waiting for transfers between devices, along(): return lax.ppermute(block, 'frame', route)  16 us
    ppermute x1, waiting for transfers between devices, on_device(): two = lax.ppermute(two, ('frame', 'atom'), list(enumerate(second)))  9.22 us
    ppermute x1, starting transfers between devices, on_device(): one = lax.ppermute(one, ('frame', 'atom'), list(enumerate(first)))  8.82 us
    ppermute x3, starting transfers between devices, across(): lax.ppermute(block, 'frame', [((f + SIDE) % (2 * SIDE), f) for f in range...  7.72 us
    all_to_all x1, starting transfers between devices, on_device(): lax.all_to_all(merged, ('frame', 'atom'), 0, 0, axis_index_groups=groups,...  7.59 us
    all_to_all x1, waiting for transfers between devices, on_device(): lax.all_to_all(merged, ('frame', 'atom'), 0, 0, axis_index_groups=groups,...  6.92 us
    ppermute x1, starting transfers between devices, on_device(): taken = lax.ppermute(send, 'atom', [(a, a ^ 1) for a in range(SIDE)])  3.49 us
  transfers between devices with their start and end apart: 11, of which 8 were waited for; matrix products, arithmetic and copies ran while one was open for 1% of the time, Pallas kernels for 4%

profile of v6, /device:TPU:7, one launch (start us, length us, event | category | flops | bytes accessed | tf_op | source)
XLA Modules:
  0.0 102.4 jit_solution(6464953303807236107)
XLA Ops:
  0.0 11.6 %collective-permute-start = (f32[144,512]{1,0:T(8,128)}, f32[144,512]{1,0:T(8,128)S(1)}, u32[]{:S(2)}, u32[]{:S(2)}) collective-permute-start(f32[144,512]{1,0:T(8,128)} %bitcast.8), channel_id=1, source_target_pairs={{32,0},{48,16},{64,32},{80,48},{96,64},{112,80},{128,96},{144,112}... | collective-permute-start | bytes 884744 | tf_op jit(solution)/shard_map/ppermute | solution.py:406
  11.6 1.9 %collective-permute-start.2 = (f32[144,512]{1,0:T(8,128)}, f32[144,512]{1,0:T(8,128)S(1)}, u32[]{:S(2)}, u32[]{:S(2)}) collective-permute-start(f32[144,512]{1,0:T(8,128)} %bitcast.9), channel_id=1, source_target_pairs={{208,0},{224,16},{240,32},{0,48},{16,64},{32,80},{48,96},{64,112},... | collective-permute-start | bytes 884744 | tf_op jit(solution)/shard_map/ppermute | solution.py:406
  13.5 10.4 %collective-permute-done.plus2 = f32[144,512]{1,0:T(8,128)S(1)} collective-permute-done((f32[144,512]{1,0:T(8,128)}, f32[144,512]{1,0:T(8,128)S(1)}, u32[]{:S(2)}, u32[]{:S(2)}) %collective-permute-start) | collective-permute-done | bytes 294944 | tf_op jit(solution)/shard_map/ppermute | solution.py:406
  23.9 6.1 %collective-permute-start.1 = (f32[144,512]{1,0:T(8,128)S(1)}, f32[144,512]{1,0:T(8,128)S(1)}, u32[]{:S(2)}, u32[]{:S(2)}) collective-permute-start(f32[144,512]{1,0:T(8,128)S(1)} %collective-permute-done.plus2), channel_id=1, source_target_pairs={{32,0},{48,16},{64,32},{80,48},{96,64},{112,80},{128,96},{144,112}... | collective-permute-start | bytes 884744 | tf_op jit(solution)/shard_map/ppermute | solution.py:406
  30.0 2.5 %collective-permute-start.4 = (f32[144,512]{1,0:T(8,128)S(1)}, f32[144,512]{1,0:T(8,128)S(1)}, u32[]{:S(2)}, u32[]{:S(2)}) collective-permute-start(f32[144,512]{1,0:T(8,128)S(1)} %collective-permute-done.plus2), channel_id=1, source_target_pairs={{256,0},{272,16},{288,32},{304,48},{320,64},{336,80},{352,96},{368... | collective-permute-start | bytes 884744 | tf_op jit(solution)/shard_map/ppermute | solution.py:409
  32.5 5.0 %collective-permute-done.2.minus3 = f32[144,512]{1,0:T(8,128)S(1)} collective-permute-done((f32[144,512]{1,0:T(8,128)}, f32[144,512]{1,0:T(8,128)S(1)}, u32[]{:S(2)}, u32[]{:S(2)}) %collective-permute-start.2) | collective-permute-done | bytes 294944 | tf_op jit(solution)/shard_map/ppermute | solution.py:406
  37.5 2.4 %collective-permute-start.5 = (f32[144,512]{1,0:T(8,128)S(1)}, f32[144,512]{1,0:T(8,128)S(1)}, u32[]{:S(2)}, u32[]{:S(2)}) collective-permute-start(f32[144,512]{1,0:T(8,128)S(1)} %collective-permute-done.2.minus3), channel_id=1, source_target_pairs={{256,0},{272,16},{288,32},{304,48},{320,64},{336,80},{352,96},{368... | collective-permute-start | bytes 884744 | tf_op jit(solution)/shard_map/ppermute | solution.py:409
  39.9 1.9 %collective-permute-start.3 = (f32[144,512]{1,0:T(8,128)S(1)}, f32[144,512]{1,0:T(8,128)S(1)}, u32[]{:S(2)}, u32[]{:S(2)}) collective-permute-start(f32[144,512]{1,0:T(8,128)S(1)} %collective-permute-done.2.minus3), channel_id=1, source_target_pairs={{240,0},{0,16},{16,32},{32,48},{48,64},{64,80},{80,96},{96,112},{1... | collective-permute-start | bytes 884744 | tf_op jit(solution)/shard_map/ppermute | solution.py:406
  41.9 0.1 pad_add_fusion.1.flags
  42.0 0.0 collective-permute-done.1.plus4
  42.0 2.8 %collective-permute-start.6 = (f32[144,512]{1,0:T(8,128)S(1)}, f32[144,512]{1,0:T(8,128)S(1)}, u32[]{:S(2)}, u32[]{:S(2)}) collective-permute-start(f32[144,512]{1,0:T(8,128)S(1)} %collective-permute-done.1.plus4), channel_id=1, source_target_pairs={{256,0},{272,16},{288,32},{304,48},{320,64},{336,80},{352,96},{368... | collective-permute-start | bytes 884744 | tf_op jit(solution)/shard_map/ppermute | solution.py:409
  44.8 0.0 collective-permute-done.4.other2
  44.8 2.6 %collective-permute-done.5.other3 = f32[144,512]{1,0:T(8,128)S(1)} collective-permute-done((f32[144,512]{1,0:T(8,128)S(1)}, f32[144,512]{1,0:T(8,128)S(1)}, u32[]{:S(2)}, u32[]{:S(2)}) %collective-permute-start.5) | collective-permute-done | bytes 294944 | tf_op jit(solution)/shard_map/ppermute | solution.py:409
  47.5 0.0 copy-start
  47.5 0.7 copy-done
  48.1 0.0 copy-start.1
  48.1 1.0 copy-done.1
  49.1 1.1 %shard_map.37 = (bf16[576,1536]{1,0:T(8,128)(2,1)S(1)}, f32[4,48,128]{2,1,0:T(8,128)S(1)}, bf16[3,256,1536]{2,1,0:T(8,128)(2,1)S(1)}, f32[3,48,128]{2,1,0:T(8,128)S(1)}) custom-call(s32[3]{0:T(128)S(1)} %pad_add_fusion.1.flags, s32[1,512]{1,0:T(1,128)S(1)} %bitcast.5, f32[144,512]{1,0:T(8,128)S(1)} %bitcast.10, f32[144,512]{1,0:T(8,128)S(1)} %collective-permute-done.plus2, ...), custom_call_target="tpu_custom_call" | custom-call | flops 1585446912 | bytes 4000000 | tf_op jit(solution)/shard_map/pallas_call | solution.py:442
  50.2 0.6 collective-permute-done.3.minus4
  50.8 2.8 %shard_map.38 = (f32[16,192,128]{2,1,0:T(8,128)S(1)}, bf16[576,1536]{1,0:T(8,128)(2,1)S(1)}, f32[4,48,128]{2,1,0:T(8,128)S(1)}) custom-call(s32[3]{0:T(128)S(1)} %pad_add_fusion.1.flags, s32[1,512]{1,0:T(1,128)S(1)} %bitcast.6, f32[144,512]{1,0:T(8,128)S(1)} %collective-permute-done.1.plus4, ...), custom_call_target="tpu_custom_call", output_to_operand_aliasing={{1}: (7, {}), {2}: (8, {})} | custom-call | flops 1698693120 | bytes 4000000 | tf_op jit(solution)/shard_map/pallas_call | solution.py:450
  53.7 0.1 collective-permute-done.6.other4
  53.8 1.4 %shard_map.39 = (f32[8,192,128]{2,1,0:T(8,128)S(1)}, f32[1,192,128]{2,1,0:T(8,128)S(1)}) custom-call(s32[3]{0:T(128)S(1)} %pad_add_fusion.1.flags, s32[1,512]{1,0:T(1,128)S(1)} %bitcast.7, bf16[576,1536]{1,0:T(8,128)(2,1)S(1)} %get-tuple-element.21.weighted, f32[4,48,128]{2,1,0:T(8,128)S(1)} %get-tuple-element.22.row_feature, ...), custom_call_target="tpu_custom_call" | custom-call | flops 339738624 | bytes 4000000 | tf_op jit(solution)/shard_map/pallas_call | solution.py:460
  55.1 3.5 %collective-permute-start.7 = (f32[8,192,128]{2,1,0:T(8,128)S(1)}, f32[8,192,128]{2,1,0:T(8,128)S(1)}, u32[]{:S(2)}, u32[]{:S(2)}) collective-permute-start(f32[8,192,128]{2,1,0:T(8,128)S(1)} %get-tuple-element.24), channel_id=1, source_target_pairs={{0,1},{1,0},{2,3},{3,2},{4,5},{5,4},{6,7},{7,6},{8,9},{9,8},{10,11... | collective-permute-start | bytes 2359304 | tf_op jit(solution)/shard_map/ppermute | solution.py:469
  58.6 1.9 %collective-permute-done.7.taken = f32[8,192,128]{2,1,0:T(8,128)S(1)} collective-permute-done((f32[8,192,128]{2,1,0:T(8,128)S(1)}, f32[8,192,128]{2,1,0:T(8,128)S(1)}, u32[]{:S(2)}, u32[]{:S(2)}) %collective-permute-start.7) | collective-permute-done | bytes 786464 | tf_op jit(solution)/shard_map/ppermute | solution.py:469
  60.5 1.0 shard_map.40
  61.5 7.6 %all-to-all-start = ((f32[8,192,128]{2,1,0:T(8,128)}), f32[8,192,128]{2,1,0:T(8,128)S(1)}, u32[]{:S(2)}, u32[]{:S(2)}) async-start(f32[8,192,128]{2,1,0:T(8,128)} %shard_map.40), calls=%async_computation | async-start | bytes 1572864 | tf_op jit(solution)/shard_map/all_to_all | solution.py:478
  69.1 1.3 %dynamic_slice.3 = s32[1]{0:T(128)} dynamic-slice(s32[512]{0:T(512)} %constant.67.clone, s32[]{:T(128)S(6)} %select_n.21), dynamic_slice_sizes={1} | dynamic-slice | bytes 12 | tf_op jit(solution)/shard_map/dynamic_slice | solution.py:398
  72.3 0.1 pad_add_fusion.flags
  72.4 6.9 %all-to-all-done.parts = f32[8,192,128]{2,1,0:T(8,128)S(1)} async-done(((f32[8,192,128]{2,1,0:T(8,128)}), f32[8,192,128]{2,1,0:T(8,128)S(1)}, u32[]{:S(2)}, u32[]{:S(2)}) %all-to-all-start) | async-done | bytes 786464 | tf_op jit(solution)/shard_map/all_to_all | solution.py:478
  79.3 1.9 %shard_map.41 = (f32[48,128]{1,0:T(8,128)S(1)}, f32[48,128]{1,0:T(8,128)S(1)}) custom-call(s32[3]{0:T(128)S(1)} %pad_add_fusion.flags, f32[8,192,128]{2,1,0:T(8,128)S(1)} %all-to-all-done.parts), custom_call_target="tpu_custom_call" | custom-call | tf_op jit(solution)/shard_map/pallas_call | solution.py:481
  81.2 8.8 %collective-permute-start.8 = (f32[48,128]{1,0:T(8,128)S(1)}, f32[48,128]{1,0:T(8,128)S(1)}, u32[]{:S(2)}, u32[]{:S(2)}) collective-permute-start(f32[48,128]{1,0:T(8,128)S(1)} %get-tuple-element.25), channel_id=1, source_target_pairs={{0,14},{1,2},{2,206},{3,194},{4,209},{5,38},{6,10},{7,74},{8,217},... | collective-permute-start | bytes 73736 | tf_op jit(solution)/shard_map/ppermute | solution.py:488
  90.0 1.9 %collective-permute-start.9 = (f32[48,128]{1,0:T(8,128)S(1)}, f32[48,128]{1,0:T(8,128)S(1)}, u32[]{:S(2)}, u32[]{:S(2)}) collective-permute-start(f32[48,128]{1,0:T(8,128)S(1)} %get-tuple-element.26), channel_id=1, source_target_pairs={{0,464},{1,64},{2,470},{3,70},{4,38},{5,193},{6,320},{7,322},{8,29... | collective-permute-start | bytes 73736 | tf_op jit(solution)/shard_map/ppermute | solution.py:489
  92.0 0.0 collective-permute-done.8.first
  92.0 9.2 %collective-permute-done.9.second = f32[48,128]{1,0:T(8,128)S(1)} collective-permute-done((f32[48,128]{1,0:T(8,128)S(1)}, f32[48,128]{1,0:T(8,128)S(1)}, u32[]{:S(2)}, u32[]{:S(2)}) %collective-permute-start.9) | collective-permute-done | bytes 24608 | tf_op jit(solution)/shard_map/ppermute | solution.py:489
  101.2 1.2 %shard_map.42 = f32[48,96]{1,0:T(8,128)} custom-call(s32[3]{0:T(128)S(1)} %pad_add_fusion.flags, f32[48,128]{1,0:T(8,128)S(1)} %collective-permute-done.8.first, f32[48,128]{1,0:T(8,128)S(1)} %collective-permute-done.9.second), custom_call_target="tpu_custom_call" | custom-call | tf_op jit(solution)/shard_map/pallas_call | solution.py:490
Async XLA Ops:
  0.0 23.9 %collective-permute-start = (f32[144,512]{1,0:T(8,128)}, f32[144,512]{1,0:T(8,128)S(1)}, u32[]{:S(2)}, u32[]{:S(2)}) collective-permute-start(f32[144,512]{1,0:T(8,128)} %bitcast.8), channel_id=1, source_target_pairs={{32,0},{48,16},{64,32},{80,48},{96,64},{112,80},{128,96},{144,112}... | collective-permute-start | bytes 884744 | tf_op jit(solution)/shard_map/ppermute | solution.py:406
  11.6 25.9 %collective-permute-start.2 = (f32[144,512]{1,0:T(8,128)}, f32[144,512]{1,0:T(8,128)S(1)}, u32[]{:S(2)}, u32[]{:S(2)}) collective-permute-start(f32[144,512]{1,0:T(8,128)} %bitcast.9), channel_id=1, source_target_pairs={{208,0},{224,16},{240,32},{0,48},{16,64},{32,80},{48,96},{64,112},... | collective-permute-start | bytes 884744 | tf_op jit(solution)/shard_map/ppermute | solution.py:406
  23.9 18.1 %collective-permute-start.1 = (f32[144,512]{1,0:T(8,128)S(1)}, f32[144,512]{1,0:T(8,128)S(1)}, u32[]{:S(2)}, u32[]{:S(2)}) collective-permute-start(f32[144,512]{1,0:T(8,128)S(1)} %collective-permute-done.plus2), channel_id=1, source_target_pairs={{32,0},{48,16},{64,32},{80,48},{96,64},{112,80},{128,96},{144,112}... | collective-permute-start | bytes 884744 | tf_op jit(solution)/shard_map/ppermute | solution.py:406
  30.0 14.8 %collective-permute-start.4 = (f32[144,512]{1,0:T(8,128)S(1)}, f32[144,512]{1,0:T(8,128)S(1)}, u32[]{:S(2)}, u32[]{:S(2)}) collective-permute-start(f32[144,512]{1,0:T(8,128)S(1)} %collective-permute-done.plus2), channel_id=1, source_target_pairs={{256,0},{272,16},{288,32},{304,48},{320,64},{336,80},{352,96},{368... | collective-permute-start | bytes 884744 | tf_op jit(solution)/shard_map/ppermute | solution.py:409
  37.5 10.0 %collective-permute-start.5 = (f32[144,512]{1,0:T(8,128)S(1)}, f32[144,512]{1,0:T(8,128)S(1)}, u32[]{:S(2)}, u32[]{:S(2)}) collective-permute-start(f32[144,512]{1,0:T(8,128)S(1)} %collective-permute-done.2.minus3), channel_id=1, source_target_pairs={{256,0},{272,16},{288,32},{304,48},{320,64},{336,80},{352,96},{368... | collective-permute-start | bytes 884744 | tf_op jit(solution)/shard_map/ppermute | solution.py:409
  39.9 10.9 %collective-permute-start.3 = (f32[144,512]{1,0:T(8,128)S(1)}, f32[144,512]{1,0:T(8,128)S(1)}, u32[]{:S(2)}, u32[]{:S(2)}) collective-permute-start(f32[144,512]{1,0:T(8,128)S(1)} %collective-permute-done.2.minus3), channel_id=1, source_target_pairs={{240,0},{0,16},{16,32},{32,48},{48,64},{64,80},{80,96},{96,112},{1... | collective-permute-start | bytes 884744 | tf_op jit(solution)/shard_map/ppermute | solution.py:406
  42.0 11.8 %collective-permute-start.6 = (f32[144,512]{1,0:T(8,128)S(1)}, f32[144,512]{1,0:T(8,128)S(1)}, u32[]{:S(2)}, u32[]{:S(2)}) collective-permute-start(f32[144,512]{1,0:T(8,128)S(1)} %collective-permute-done.1.plus4), channel_id=1, source_target_pairs={{256,0},{272,16},{288,32},{304,48},{320,64},{336,80},{352,96},{368... | collective-permute-start | bytes 884744 | tf_op jit(solution)/shard_map/ppermute | solution.py:409
  47.5 0.7 copy-start
  48.1 1.0 copy-start.1
  55.1 5.4 %collective-permute-start.7 = (f32[8,192,128]{2,1,0:T(8,128)S(1)}, f32[8,192,128]{2,1,0:T(8,128)S(1)}, u32[]{:S(2)}, u32[]{:S(2)}) collective-permute-start(f32[8,192,128]{2,1,0:T(8,128)S(1)} %get-tuple-element.24), channel_id=1, source_target_pairs={{0,1},{1,0},{2,3},{3,2},{4,5},{5,4},{6,7},{7,6},{8,9},{9,8},{10,11... | collective-permute-start | bytes 2359304 | tf_op jit(solution)/shard_map/ppermute | solution.py:469
  61.5 17.8 %all-to-all-start = ((f32[8,192,128]{2,1,0:T(8,128)}), f32[8,192,128]{2,1,0:T(8,128)S(1)}, u32[]{:S(2)}, u32[]{:S(2)}) async-start(f32[8,192,128]{2,1,0:T(8,128)} %shard_map.40), calls=%async_computation | async-start | bytes 1572864 | tf_op jit(solution)/shard_map/all_to_all | solution.py:478
  81.2 10.8 %collective-permute-start.8 = (f32[48,128]{1,0:T(8,128)S(1)}, f32[48,128]{1,0:T(8,128)S(1)}, u32[]{:S(2)}, u32[]{:S(2)}) collective-permute-start(f32[48,128]{1,0:T(8,128)S(1)} %get-tuple-element.25), channel_id=1, source_target_pairs={{0,14},{1,2},{2,206},{3,194},{4,209},{5,38},{6,10},{7,74},{8,217},... | collective-permute-start | bytes 73736 | tf_op jit(solution)/shard_map/ppermute | solution.py:488
  90.0 11.2 %collective-permute-start.9 = (f32[48,128]{1,0:T(8,128)S(1)}, f32[48,128]{1,0:T(8,128)S(1)}, u32[]{:S(2)}, u32[]{:S(2)}) collective-permute-start(f32[48,128]{1,0:T(8,128)S(1)} %get-tuple-element.26), channel_id=1, source_target_pairs={{0,464},{1,64},{2,470},{3,70},{4,38},{5,193},{6,320},{7,322},{8,29... | collective-permute-start | bytes 73736 | tf_op jit(solution)/shard_map/ppermute | solution.py:489

commit v7 on v6

--- a/solution.py
+++ b/solution.py
@@ -27,7 +27,7 @@
 LATE = ((0, 6), (2, 6))
 PAIRS = EARLY + LATE
 DIAGONAL = PAIRS.index((4, 2))
-POSITION = (11, 4, 12, 5, 0, 2, 7, 3, 1, 6, 8, 10, 13, 9, 14, 15)
+POSITION = (13, 9, 5, 3, 8, 10, 11, 4, 12, 7, 2, 0, 6, 1, 14, 15)
 CHIPS = SIDE // 2
 
 
@@ -63,8 +63,8 @@
     for k in range(CHIPS):
         for chip in range(CHIPS):
             for pair in POSITION[2 * k : 2 * k + 2]:
-                far = max(distance(column, z, chip, end) for end in ends_of(column, z, pair))
-                cost[k][chip] = max(cost[k][chip], 4**far)
+                far = [distance(column, z, chip, end) for end in ends_of(column, z, pair)]
+                cost[k][chip] += 2 ** sum(far) + 2 * 4 ** max(far)
     best = {0: (0, ())}
     for k in range(CHIPS):
         later = {}
@@ -307,7 +307,7 @@
 
 
 def fit_kernel(flags, parts, first, second):
-    diagonal, swap = flags[2] == 1, flags[0] == 1
+    diagonal, swap = flags[1] == 1, flags[0] == 1
     total = parts[0]
     for a in range(1, CHIPS):
         total = total + parts[a]
@@ -319,9 +319,10 @@
         tile = jnp.where((lane >= 48) & (lane < 64), parts[a, 3 * ROWS :], 0.0)
         gathered = gathered + pltpu.roll(tile, (16 * a - 48) % 128, 1)
 
+    sender = lane % 8 == 0
+
     def per_sender(which):
-        pick = (iota((128, 128), 0) == 8 * iota((128, 128), 1) + which).astype(jnp.float32)
-        return jnp.dot(gathered, pick, precision=EXACT, preferred_element_type=jnp.float32)
+        return jnp.where(sender, pltpu.roll(gathered, (128 - which) % 128, 1), 0.0)
 
     mass = per_sender(3)
     whole = jnp.sum(mass, axis=1, keepdims=True)
@@ -331,7 +332,7 @@
         for c in range(3):
             mean = per_sender(base + c)
             centroid = jnp.sum(mass * mean, axis=1, keepdims=True) / whole
-            out.append(jnp.where(lane < SIDE, mean - centroid, 0.0))
+            out.append(jnp.where(sender, mean - centroid, 0.0))
         return out
 
     off_p, off_q = offsets(0), offsets(4)
@@ -354,13 +355,17 @@
     spread_rows = jnp.where(corner, spread_q, spread_rows)
     spread_cols = jnp.where(corner, spread_q, spread_cols)
 
-    low_rows = jnp.concatenate([mass * jnp.where(diagonal, q, p) for p, q in zip(off_p, off_q)], axis=0)
-    up_rows = jnp.concatenate([mass * p for p in off_p], axis=0)
+    def parts_of(blocks, first):
+        high, low = halves(jnp.concatenate(blocks, axis=0))
+        return jnp.concatenate([high, high, low] if first else [high, low, high], axis=1)
+
+    up_rows = parts_of([mass * p for p in off_p], True)
+    low_rows = parts_of([mass * jnp.where(diagonal, q, p) for p, q in zip(off_p, off_q)], True)
     moment = []
     between = []
     for d in range(3):
-        up = dot_t(up_rows, square_tile(jnp.where(diagonal, off_p[d], off_q[d])))
-        low = dot_t(low_rows, square_tile(off_q[d]))
+        up = product(up_rows, parts_of([square_tile(jnp.where(diagonal, off_p[d], off_q[d]))], False))
+        low = product(low_rows, parts_of([square_tile(off_q[d])], False))
         between.append((up, low))
     for c in range(3):
         main = total[c * ROWS : (c + 1) * ROWS]
@@ -383,20 +388,12 @@
     second[...] = jnp.where(swap, plain_a, plain_b)
 
 
-def join_kernel(flags, first, second, out):
-    lane = iota((ROWS, 128), 1)
-    a, b = first[...], second[...]
-    left = jnp.where(flags[1] == 1, b, a)
-    right = jnp.where(flags[1] == 1, a, b)
-    out[...] = jnp.where(lane < ROWS, left, pltpu.roll(right, ROWS, 1))[:, : 2 * ROWS]
-
-
 def on_device(coords, weights):
     orders, first, second, table = routes()
     frame, atom = lax.axis_index("frame"), lax.axis_index("atom")
     build_flags = jnp.stack([frame // SIDE, (frame % SIDE) // (SIDE // 2), atom % 2]).astype(jnp.int32)
     mine = jnp.asarray(np.array(table), jnp.int32)[frame * SIDE + atom]
-    fit_flags = jnp.stack([mine & 1, mine >> 1 & 1, mine >> 2])
+    fit_flags = jnp.stack([mine & 1, mine >> 2])
     mass = weights[None, :]
 
     def along(block, distance):
@@ -487,13 +484,9 @@
     )(fit_flags, parts)
     one = lax.ppermute(one, ("frame", "atom"), list(enumerate(first)))
     two = lax.ppermute(two, ("frame", "atom"), list(enumerate(second)))
-    return pl.pallas_call(
-        join_kernel,
-        out_shape=jax.ShapeDtypeStruct((ROWS, 2 * ROWS), jnp.float32),
-        in_specs=[smem, vmem, vmem],
-        out_specs=vmem,
-        compiler_params=params,
-    )(fit_flags, one, two)
+    left = jnp.where(mine >> 1 & 1, two, one)
+    right = jnp.where(mine >> 1 & 1, one, two)
+    return jnp.concatenate([left[:, :ROWS], right[:, :ROWS]], axis=1)
 
 
 def solution(mesh):

time: 103 us -> 100 us (0.971)
  waiting for transfers between devices: 36.8 us -> 34.4 us
  Pallas kernels: 9.4 us -> 7.73 us
    ppermute x1, waiting for transfers between devices: 9.22 us -> 0.01 us  [on_device(): two = lax.ppermute(two, ('frame', 'atom'), list(enumerate(second)))]
    ppermute x1, starting transfers between devices: 1.92 us -> 10.8 us  [on_device(): two = lax.ppermute(two, ('frame', 'atom'), list(enumerate(second)))]
    ppermute x1, starting transfers between devices: 8.82 us -> 1.92 us  [on_device(): one = lax.ppermute(one, ('frame', 'atom'), list(enumerate(first)))]
    ppermute x1, waiting for transfers between devices: 0.01 us -> 5.89 us  [on_device(): one = lax.ppermute(one, ('frame', 'atom'), list(enumerate(first)))]
    all_to_all x1, starting transfers between devices: 7.59 us -> 5.43 us  [on_device(): lax.all_to_all(merged, ('frame', 'atom'), 0, 0, axis_index_groups=groups,...]
    pallas_call x1 -> x0, Pallas kernels: 1.23 us -> none  [on_device(): pl.pallas_call(join_kernel, out_shape=jax.ShapeDtypeStruct((ROWS, 2 * ROW...]
where the time goes in v7:
time: 100 us; the launch traced here: 98.9 us
  starting transfers between devices  50.8 us (51%)
  waiting for transfers between devices  34.4 us (34%)
  Pallas kernels  7.73 us (8%)
  local copies, waits for them, and re-layouts  2.91 us (3%)
  between operations  2.13 us (2%)
    ppermute x4, starting transfers between devices, along(): return lax.ppermute(block, 'frame', route)  21.5 us
    ppermute x4, waiting for transfers between devices, along(): return lax.ppermute(block, 'frame', route)  16 us
    ppermute x1, starting transfers between devices, on_device(): two = lax.ppermute(two, ('frame', 'atom'), list(enumerate(second)))  10.8 us
    all_to_all x1, waiting for transfers between devices, on_device(): lax.all_to_all(merged, ('frame', 'atom'), 0, 0, axis_index_groups=groups,...  7.9 us
    ppermute x3, starting transfers between devices, across(): lax.ppermute(block, 'frame', [((f + SIDE) % (2 * SIDE), f) for f in range...  7.72 us
    ppermute x1, waiting for transfers between devices, on_device(): one = lax.ppermute(one, ('frame', 'atom'), list(enumerate(first)))  5.89 us
    all_to_all x1, starting transfers between devices, on_device(): lax.all_to_all(merged, ('frame', 'atom'), 0, 0, axis_index_groups=groups,...  5.43 us
    ppermute x1, starting transfers between devices, on_device(): taken = lax.ppermute(send, 'atom', [(a, a ^ 1) for a in range(SIDE)])  3.49 us
  transfers between devices with their start and end apart: 11, of which 8 were waited for; matrix products, arithmetic and copies ran while one was open for 1% of the time, Pallas kernels for 4%

profile of v7, /device:TPU:7, one launch (start us, length us, event | category | flops | bytes accessed | tf_op | source)
XLA Modules:
  0.0 98.9 jit_solution(6442296718290058438)
XLA Ops:
  0.0 11.6 %collective-permute-start = (f32[144,512]{1,0:T(8,128)}, f32[144,512]{1,0:T(8,128)S(1)}, u32[]{:S(2)}, u32[]{:S(2)}) collective-permute-start(f32[144,512]{1,0:T(8,128)} %bitcast.9), channel_id=1, source_target_pairs={{32,0},{48,16},{64,32},{80,48},{96,64},{112,80},{128,96},{144,112}... | collective-permute-start | bytes 884744 | tf_op jit(solution)/shard_map/ppermute | solution.py:403
  11.6 1.9 %collective-permute-start.2 = (f32[144,512]{1,0:T(8,128)}, f32[144,512]{1,0:T(8,128)S(1)}, u32[]{:S(2)}, u32[]{:S(2)}) collective-permute-start(f32[144,512]{1,0:T(8,128)} %bitcast.10), channel_id=1, source_target_pairs={{208,0},{224,16},{240,32},{0,48},{16,64},{32,80},{48,96},{64,112},... | collective-permute-start | bytes 884744 | tf_op jit(solution)/shard_map/ppermute | solution.py:403
  13.5 10.4 %collective-permute-done.plus2 = f32[144,512]{1,0:T(8,128)S(1)} collective-permute-done((f32[144,512]{1,0:T(8,128)}, f32[144,512]{1,0:T(8,128)S(1)}, u32[]{:S(2)}, u32[]{:S(2)}) %collective-permute-start) | collective-permute-done | bytes 294944 | tf_op jit(solution)/shard_map/ppermute | solution.py:403
  23.9 6.1 %collective-permute-start.1 = (f32[144,512]{1,0:T(8,128)S(1)}, f32[144,512]{1,0:T(8,128)S(1)}, u32[]{:S(2)}, u32[]{:S(2)}) collective-permute-start(f32[144,512]{1,0:T(8,128)S(1)} %collective-permute-done.plus2), channel_id=1, source_target_pairs={{32,0},{48,16},{64,32},{80,48},{96,64},{112,80},{128,96},{144,112}... | collective-permute-start | bytes 884744 | tf_op jit(solution)/shard_map/ppermute | solution.py:403
  30.0 2.5 %collective-permute-start.4 = (f32[144,512]{1,0:T(8,128)S(1)}, f32[144,512]{1,0:T(8,128)S(1)}, u32[]{:S(2)}, u32[]{:S(2)}) collective-permute-start(f32[144,512]{1,0:T(8,128)S(1)} %collective-permute-done.plus2), channel_id=1, source_target_pairs={{256,0},{272,16},{288,32},{304,48},{320,64},{336,80},{352,96},{368... | collective-permute-start | bytes 884744 | tf_op jit(solution)/shard_map/ppermute | solution.py:406
  32.5 5.0 %collective-permute-done.2.minus3 = f32[144,512]{1,0:T(8,128)S(1)} collective-permute-done((f32[144,512]{1,0:T(8,128)}, f32[144,512]{1,0:T(8,128)S(1)}, u32[]{:S(2)}, u32[]{:S(2)}) %collective-permute-start.2) | collective-permute-done | bytes 294944 | tf_op jit(solution)/shard_map/ppermute | solution.py:403
  37.5 2.4 %collective-permute-start.5 = (f32[144,512]{1,0:T(8,128)S(1)}, f32[144,512]{1,0:T(8,128)S(1)}, u32[]{:S(2)}, u32[]{:S(2)}) collective-permute-start(f32[144,512]{1,0:T(8,128)S(1)} %collective-permute-done.2.minus3), channel_id=1, source_target_pairs={{256,0},{272,16},{288,32},{304,48},{320,64},{336,80},{352,96},{368... | collective-permute-start | bytes 884744 | tf_op jit(solution)/shard_map/ppermute | solution.py:406
  39.9 1.9 %collective-permute-start.3 = (f32[144,512]{1,0:T(8,128)S(1)}, f32[144,512]{1,0:T(8,128)S(1)}, u32[]{:S(2)}, u32[]{:S(2)}) collective-permute-start(f32[144,512]{1,0:T(8,128)S(1)} %collective-permute-done.2.minus3), channel_id=1, source_target_pairs={{240,0},{0,16},{16,32},{32,48},{48,64},{64,80},{80,96},{96,112},{1... | collective-permute-start | bytes 884744 | tf_op jit(solution)/shard_map/ppermute | solution.py:403
  41.9 0.1 pad_add_fusion.1.flags
  42.0 0.0 collective-permute-done.1.plus4
  42.0 2.8 %collective-permute-start.6 = (f32[144,512]{1,0:T(8,128)S(1)}, f32[144,512]{1,0:T(8,128)S(1)}, u32[]{:S(2)}, u32[]{:S(2)}) collective-permute-start(f32[144,512]{1,0:T(8,128)S(1)} %collective-permute-done.1.plus4), channel_id=1, source_target_pairs={{256,0},{272,16},{288,32},{304,48},{320,64},{336,80},{352,96},{368... | collective-permute-start | bytes 884744 | tf_op jit(solution)/shard_map/ppermute | solution.py:406
  44.8 0.0 collective-permute-done.4.other2
  44.8 2.6 %collective-permute-done.5.other3 = f32[144,512]{1,0:T(8,128)S(1)} collective-permute-done((f32[144,512]{1,0:T(8,128)S(1)}, f32[144,512]{1,0:T(8,128)S(1)}, u32[]{:S(2)}, u32[]{:S(2)}) %collective-permute-start.5) | collective-permute-done | bytes 294944 | tf_op jit(solution)/shard_map/ppermute | solution.py:406
  47.5 0.0 copy-start
  47.5 0.7 copy-done
  48.1 0.0 copy-start.1
  48.1 1.0 copy-done.1
  49.1 1.1 %shard_map.37 = (bf16[576,1536]{1,0:T(8,128)(2,1)S(1)}, f32[4,48,128]{2,1,0:T(8,128)S(1)}, bf16[3,256,1536]{2,1,0:T(8,128)(2,1)S(1)}, f32[3,48,128]{2,1,0:T(8,128)S(1)}) custom-call(s32[3]{0:T(128)S(1)} %pad_add_fusion.1.flags, s32[1,512]{1,0:T(1,128)S(1)} %bitcast.6, f32[144,512]{1,0:T(8,128)S(1)} %bitcast.11, f32[144,512]{1,0:T(8,128)S(1)} %collective-permute-done.plus2, ...), custom_call_target="tpu_custom_call" | custom-call | flops 1585446912 | bytes 4000000 | tf_op jit(solution)/shard_map/pallas_call | solution.py:439
  50.2 0.6 collective-permute-done.3.minus4
  50.8 2.8 %shard_map.38 = (f32[16,192,128]{2,1,0:T(8,128)S(1)}, bf16[576,1536]{1,0:T(8,128)(2,1)S(1)}, f32[4,48,128]{2,1,0:T(8,128)S(1)}) custom-call(s32[3]{0:T(128)S(1)} %pad_add_fusion.1.flags, s32[1,512]{1,0:T(1,128)S(1)} %bitcast.7, f32[144,512]{1,0:T(8,128)S(1)} %collective-permute-done.1.plus4, ...), custom_call_target="tpu_custom_call", output_to_operand_aliasing={{1}: (7, {}), {2}: (8, {})} | custom-call | flops 1698693120 | bytes 4000000 | tf_op jit(solution)/shard_map/pallas_call | solution.py:447
  53.7 0.1 collective-permute-done.6.other4
  53.8 1.4 %shard_map.39 = (f32[8,192,128]{2,1,0:T(8,128)S(1)}, f32[1,192,128]{2,1,0:T(8,128)S(1)}) custom-call(s32[3]{0:T(128)S(1)} %pad_add_fusion.1.flags, s32[1,512]{1,0:T(1,128)S(1)} %bitcast.8, bf16[576,1536]{1,0:T(8,128)(2,1)S(1)} %get-tuple-element.21.weighted, f32[4,48,128]{2,1,0:T(8,128)S(1)} %get-tuple-element.22.row_feature, ...), custom_call_target="tpu_custom_call" | custom-call | flops 339738624 | bytes 4000000 | tf_op jit(solution)/shard_map/pallas_call | solution.py:457
  55.1 3.5 %collective-permute-start.7 = (f32[8,192,128]{2,1,0:T(8,128)S(1)}, f32[8,192,128]{2,1,0:T(8,128)S(1)}, u32[]{:S(2)}, u32[]{:S(2)}) collective-permute-start(f32[8,192,128]{2,1,0:T(8,128)S(1)} %get-tuple-element.24), channel_id=1, source_target_pairs={{0,1},{1,0},{2,3},{3,2},{4,5},{5,4},{6,7},{7,6},{8,9},{9,8},{10,11... | collective-permute-start | bytes 2359304 | tf_op jit(solution)/shard_map/ppermute | solution.py:466
  58.6 1.9 %collective-permute-done.7.taken = f32[8,192,128]{2,1,0:T(8,128)S(1)} collective-permute-done((f32[8,192,128]{2,1,0:T(8,128)S(1)}, f32[8,192,128]{2,1,0:T(8,128)S(1)}, u32[]{:S(2)}, u32[]{:S(2)}) %collective-permute-start.7) | collective-permute-done | bytes 786464 | tf_op jit(solution)/shard_map/ppermute | solution.py:466
  60.5 1.0 shard_map.40
  61.5 5.4 %all-to-all-start = ((f32[8,192,128]{2,1,0:T(8,128)}), f32[8,192,128]{2,1,0:T(8,128)S(1)}, u32[]{:S(2)}, u32[]{:S(2)}) async-start(f32[8,192,128]{2,1,0:T(8,128)} %shard_map.40), calls=%async_computation | async-start | bytes 1572864 | tf_op jit(solution)/shard_map/all_to_all | solution.py:475
  66.9 1.3 %dynamic_slice.3 = s32[1]{0:T(128)} dynamic-slice(s32[512]{0:T(512)} %constant.72.clone, s32[]{:T(128)S(6)} %select_n.33), dynamic_slice_sizes={1} | dynamic-slice | bytes 12 | tf_op jit(solution)/shard_map/dynamic_slice | solution.py:395
  69.5 0.1 pad_add_fusion.flags
  69.6 7.9 %all-to-all-done.parts = f32[8,192,128]{2,1,0:T(8,128)S(1)} async-done(((f32[8,192,128]{2,1,0:T(8,128)}), f32[8,192,128]{2,1,0:T(8,128)S(1)}, u32[]{:S(2)}, u32[]{:S(2)}) %all-to-all-start) | async-done | bytes 786464 | tf_op jit(solution)/shard_map/all_to_all | solution.py:475
  77.5 1.5 %shard_map.41 = (f32[48,128]{1,0:T(8,128)S(1)}, f32[48,128]{1,0:T(8,128)S(1)}) custom-call(s32[2]{0:T(128)S(1)} %pad_add_fusion.flags, f32[8,192,128]{2,1,0:T(8,128)S(1)} %all-to-all-done.parts), custom_call_target="tpu_custom_call" | custom-call | tf_op jit(solution)/shard_map/pallas_call | solution.py:478
  78.9 10.8 %collective-permute-start.8 = (f32[48,128]{1,0:T(8,128)S(1)}, f32[48,128]{1,0:T(8,128)S(1)}, u32[]{:S(2)}, u32[]{:S(2)}) collective-permute-start(f32[48,128]{1,0:T(8,128)S(1)} %get-tuple-element.25), channel_id=1, source_target_pairs={{0,464},{1,64},{2,320},{3,322},{4,38},{5,209},{6,70},{7,210},{8,29... | collective-permute-start | bytes 73736 | tf_op jit(solution)/shard_map/ppermute | solution.py:486
  89.7 1.9 %collective-permute-start.9 = (f32[48,128]{1,0:T(8,128)S(1)}, f32[48,128]{1,0:T(8,128)S(1)}, u32[]{:S(2)}, u32[]{:S(2)}) collective-permute-start(f32[48,128]{1,0:T(8,128)S(1)} %get-tuple-element.26), channel_id=1, source_target_pairs={{0,14},{1,2},{2,10},{3,74},{4,193},{5,38},{6,194},{7,70},{8,217},{... | collective-permute-start | bytes 73736 | tf_op jit(solution)/shard_map/ppermute | solution.py:485
  92.3 0.0 collective-permute-done.8
  92.3 5.9 %collective-permute-done.9 = f32[48,128]{1,0:T(8,128)S(1)} collective-permute-done((f32[48,128]{1,0:T(8,128)S(1)}, f32[48,128]{1,0:T(8,128)S(1)}, u32[]{:S(2)}, u32[]{:S(2)}) %collective-permute-start.9) | collective-permute-done | bytes 24608 | tf_op jit(solution)/shard_map/ppermute | solution.py:485
  98.2 0.7 pad_maximum_fusion
  (1 shorter events, 0.0 us)
Async XLA Ops:
  0.0 23.9 %collective-permute-start = (f32[144,512]{1,0:T(8,128)}, f32[144,512]{1,0:T(8,128)S(1)}, u32[]{:S(2)}, u32[]{:S(2)}) collective-permute-start(f32[144,512]{1,0:T(8,128)} %bitcast.9), channel_id=1, source_target_pairs={{32,0},{48,16},{64,32},{80,48},{96,64},{112,80},{128,96},{144,112}... | collective-permute-start | bytes 884744 | tf_op jit(solution)/shard_map/ppermute | solution.py:403
  11.6 25.9 %collective-permute-start.2 = (f32[144,512]{1,0:T(8,128)}, f32[144,512]{1,0:T(8,128)S(1)}, u32[]{:S(2)}, u32[]{:S(2)}) collective-permute-start(f32[144,512]{1,0:T(8,128)} %bitcast.10), channel_id=1, source_target_pairs={{208,0},{224,16},{240,32},{0,48},{16,64},{32,80},{48,96},{64,112},... | collective-permute-start | bytes 884744 | tf_op jit(solution)/shard_map/ppermute | solution.py:403
  23.9 18.1 %collective-permute-start.1 = (f32[144,512]{1,0:T(8,128)S(1)}, f32[144,512]{1,0:T(8,128)S(1)}, u32[]{:S(2)}, u32[]{:S(2)}) collective-permute-start(f32[144,512]{1,0:T(8,128)S(1)} %collective-permute-done.plus2), channel_id=1, source_target_pairs={{32,0},{48,16},{64,32},{80,48},{96,64},{112,80},{128,96},{144,112}... | collective-permute-start | bytes 884744 | tf_op jit(solution)/shard_map/ppermute | solution.py:403
  30.0 14.8 %collective-permute-start.4 = (f32[144,512]{1,0:T(8,128)S(1)}, f32[144,512]{1,0:T(8,128)S(1)}, u32[]{:S(2)}, u32[]{:S(2)}) collective-permute-start(f32[144,512]{1,0:T(8,128)S(1)} %collective-permute-done.plus2), channel_id=1, source_target_pairs={{256,0},{272,16},{288,32},{304,48},{320,64},{336,80},{352,96},{368... | collective-permute-start | bytes 884744 | tf_op jit(solution)/shard_map/ppermute | solution.py:406
  37.5 10.0 %collective-permute-start.5 = (f32[144,512]{1,0:T(8,128)S(1)}, f32[144,512]{1,0:T(8,128)S(1)}, u32[]{:S(2)}, u32[]{:S(2)}) collective-permute-start(f32[144,512]{1,0:T(8,128)S(1)} %collective-permute-done.2.minus3), channel_id=1, source_target_pairs={{256,0},{272,16},{288,32},{304,48},{320,64},{336,80},{352,96},{368... | collective-permute-start | bytes 884744 | tf_op jit(solution)/shard_map/ppermute | solution.py:406
  39.9 10.9 %collective-permute-start.3 = (f32[144,512]{1,0:T(8,128)S(1)}, f32[144,512]{1,0:T(8,128)S(1)}, u32[]{:S(2)}, u32[]{:S(2)}) collective-permute-start(f32[144,512]{1,0:T(8,128)S(1)} %collective-permute-done.2.minus3), channel_id=1, source_target_pairs={{240,0},{0,16},{16,32},{32,48},{48,64},{64,80},{80,96},{96,112},{1... | collective-permute-start | bytes 884744 | tf_op jit(solution)/shard_map/ppermute | solution.py:403
  42.0 11.8 %collective-permute-start.6 = (f32[144,512]{1,0:T(8,128)S(1)}, f32[144,512]{1,0:T(8,128)S(1)}, u32[]{:S(2)}, u32[]{:S(2)}) collective-permute-start(f32[144,512]{1,0:T(8,128)S(1)} %collective-permute-done.1.plus4), channel_id=1, source_target_pairs={{256,0},{272,16},{288,32},{304,48},{320,64},{336,80},{352,96},{368... | collective-permute-start | bytes 884744 | tf_op jit(solution)/shard_map/ppermute | solution.py:406
  47.5 0.7 copy-start
  48.1 1.0 copy-start.1
  55.1 5.4 %collective-permute-start.7 = (f32[8,192,128]{2,1,0:T(8,128)S(1)}, f32[8,192,128]{2,1,0:T(8,128)S(1)}, u32[]{:S(2)}, u32[]{:S(2)}) collective-permute-start(f32[8,192,128]{2,1,0:T(8,128)S(1)} %get-tuple-element.24), channel_id=1, source_target_pairs={{0,1},{1,0},{2,3},{3,2},{4,5},{5,4},{6,7},{7,6},{8,9},{9,8},{10,11... | collective-permute-start | bytes 2359304 | tf_op jit(solution)/shard_map/ppermute | solution.py:466
  61.5 16.0 %all-to-all-start = ((f32[8,192,128]{2,1,0:T(8,128)}), f32[8,192,128]{2,1,0:T(8,128)S(1)}, u32[]{:S(2)}, u32[]{:S(2)}) async-start(f32[8,192,128]{2,1,0:T(8,128)} %shard_map.40), calls=%async_computation | async-start | bytes 1572864 | tf_op jit(solution)/shard_map/all_to_all | solution.py:475
  78.9 13.4 %collective-permute-start.8 = (f32[48,128]{1,0:T(8,128)S(1)}, f32[48,128]{1,0:T(8,128)S(1)}, u32[]{:S(2)}, u32[]{:S(2)}) collective-permute-start(f32[48,128]{1,0:T(8,128)S(1)} %get-tuple-element.25), channel_id=1, source_target_pairs={{0,464},{1,64},{2,320},{3,322},{4,38},{5,209},{6,70},{7,210},{8,29... | collective-permute-start | bytes 73736 | tf_op jit(solution)/shard_map/ppermute | solution.py:486
  89.7 8.5 %collective-permute-start.9 = (f32[48,128]{1,0:T(8,128)S(1)}, f32[48,128]{1,0:T(8,128)S(1)}, u32[]{:S(2)}, u32[]{:S(2)}) collective-permute-start(f32[48,128]{1,0:T(8,128)S(1)} %get-tuple-element.26), channel_id=1, source_target_pairs={{0,14},{1,2},{2,10},{3,74},{4,193},{5,38},{6,194},{7,70},{8,217},{... | collective-permute-start | bytes 73736 | tf_op jit(solution)/shard_map/ppermute | solution.py:485

commit v8 on v7

--- a/solution.py
+++ b/solution.py
@@ -29,6 +29,7 @@
 DIAGONAL = PAIRS.index((4, 2))
 POSITION = (13, 9, 5, 3, 8, 10, 11, 4, 12, 7, 2, 0, 6, 1, 14, 15)
 CHIPS = SIDE // 2
+SUM_ROWS = 3 * ROWS + 32
 
 
 def frame_block(column, z, index):
@@ -175,11 +176,23 @@
     return tail[:ROWS] + pltpu.roll(tail[ROWS : 2 * ROWS], 16, 1) + pltpu.roll(tail[2 * ROWS :], 32, 1)
 
 
+def packed(rest):
+    lane, tail = iota((16, 128), 1), rest[32:]
+    low = pltpu.roll(jnp.where(lane < 48, tail, 0.0), 80, 1)
+    high = pltpu.roll(jnp.where(lane < 48, 0.0, tail), 32, 1)
+    return rest[:32] + jnp.concatenate([low, high], axis=0)
+
+
+def unpacked(rows):
+    tail = jnp.where(iota((16, 128), 1) < 48, pltpu.roll(rows[:16], 48, 1), pltpu.roll(rows[16:], 96, 1))
+    return jnp.concatenate([rows, tail], axis=0)
+
+
 def put_pair(out, pair, core, value, feature):
     k, owner = divmod(POSITION.index(pair), 2)
     at = jnp.where(core == owner, k, CHIPS + k)
     out[at, : 3 * ROWS] = value[:, :128]
-    out[at, 3 * ROWS :] = rest_of(value[:, 128:]) + feature
+    out[at, 3 * ROWS :] = packed(rest_of(value[:, 128:]) + feature)
 
 
 def put_groups(out, pairs, order, core, weighted, centered, row_feature, column_feature):
@@ -246,7 +259,7 @@
         feature = row_feature[1] if n == 0 else jnp.where(other, row_feature[2], row_feature[3])
         at = jnp.where(core == n, 0, 1)
         last[at, : 3 * ROWS] = rows[:, :128]
-        last[at, 3 * ROWS :] = rest_of(rows[:, 128:]) + feature + column_feature[0]
+        last[at, 3 * ROWS :] = packed(rest_of(rows[:, 128:]) + feature + column_feature[0])
     keep[0] = last[0]
     send[CHIPS - 1] = last[1]
     send[: CHIPS - 1] = sums[CHIPS : 2 * CHIPS - 1]
@@ -312,11 +325,11 @@
     for a in range(1, CHIPS):
         total = total + parts[a]
     lane, row = iota((ROWS, 128), 1), iota((ROWS, 128), 0)
-    rest = total[3 * ROWS :]
+    rest = unpacked(total[3 * ROWS :])
 
     gathered = jnp.zeros((ROWS, 128), jnp.float32)
     for a in range(CHIPS):
-        tile = jnp.where((lane >= 48) & (lane < 64), parts[a, 3 * ROWS :], 0.0)
+        tile = jnp.where((lane >= 48) & (lane < 64), unpacked(parts[a, 3 * ROWS :]), 0.0)
         gathered = gathered + pltpu.roll(tile, (16 * a - 48) % 128, 1)
 
     sender = lane % 8 == 0
@@ -384,8 +397,9 @@
     plain_a = jnp.where(diagonal, jnp.where(upper, msd, turned), msd)
     mirrored = jnp.where(row > lane, msd, jnp.where(row == lane, corner_value, turned))
     plain_b = jnp.where(diagonal, mirrored, turned)
-    first[...] = jnp.where(swap, plain_b, plain_a)
-    second[...] = jnp.where(swap, plain_a, plain_b)
+    for out, here, there in ((first, plain_a, plain_b), (second, plain_b, plain_a)):
+        value = jnp.where(swap, there, here)
+        out[...] = value[: ROWS // 2] + pltpu.roll(value[ROWS // 2 :], 64, 1)
 
 
 def on_device(coords, weights):
@@ -426,7 +440,7 @@
         return pl.CostEstimate(flops=pairs * 2 * 3 * ROWS * 256 * atoms * 3, bytes_accessed=4_000_000, transcendentals=0)
 
     def sums_of(n):
-        return jax.ShapeDtypeStruct((n, 4 * ROWS, 128), jnp.float32)
+        return jax.ShapeDtypeStruct((n, SUM_ROWS, 128), jnp.float32)
 
     staged = [
         jax.ShapeDtypeStruct((len(STACK) * 3 * ROWS, 3 * atoms), jnp.bfloat16),
@@ -459,7 +473,7 @@
         out_shape=[sums_of(CHIPS), sums_of(1)],
         in_specs=[smem] + [vmem] * 5,
         out_specs=[vmem] * 2,
-        scratch_shapes=[pltpu.VMEM((2, 4 * ROWS, 128), jnp.float32)] + columns_scratch(1),
+        scratch_shapes=[pltpu.VMEM((2, SUM_ROWS, 128), jnp.float32)] + columns_scratch(1),
         compiler_params=params,
         cost_estimate=cost(len(LATE) + 1),
     )(build_flags, mass, weighted, row_feature, other4, sums)
@@ -474,7 +488,7 @@
     groups = [[f * SIDE + 2 * chip + c for chip in orders[f]] for f in range(2 * SIDE) for c in range(2)]
     parts = lax.all_to_all(merged, ("frame", "atom"), 0, 0, axis_index_groups=groups, tiled=True)
 
-    block = jax.ShapeDtypeStruct((ROWS, 128), jnp.float32)
+    block = jax.ShapeDtypeStruct((ROWS // 2, 128), jnp.float32)
     one, two = pl.pallas_call(
         fit_kernel,
         out_shape=(block, block),
@@ -486,7 +500,9 @@
     two = lax.ppermute(two, ("frame", "atom"), list(enumerate(second)))
     left = jnp.where(mine >> 1 & 1, two, one)
     right = jnp.where(mine >> 1 & 1, one, two)
-    return jnp.concatenate([left[:, :ROWS], right[:, :ROWS]], axis=1)
+    upper = jnp.concatenate([left[:, :ROWS], right[:, :ROWS]], axis=1)
+    lower = jnp.concatenate([left[:, 64 : 64 + ROWS], right[:, 64 : 64 + ROWS]], axis=1)
+    return jnp.concatenate([upper, lower], axis=0)
 
 
 def solution(mesh):

time: 100 us -> 99.8 us (level)
  transfers between devices with their start and end apart: 11 -> 11, of which waited for: 8 -> 7; matrix products, arithmetic and copies ran while one was open for 1% -> 1% of each run, Pallas kernels for 4% -> 4%
where the time goes in v8:
time: 99.8 us; the launch traced here: 98.1 us
  starting transfers between devices  50.6 us (51%)
  waiting for transfers between devices  33.6 us (34%)
  Pallas kernels  8 us (8%)
  local copies, waits for them, and re-layouts  2.98 us (3%)
  between operations  2.12 us (2%)
    ppermute x4, starting transfers between devices, along(): return lax.ppermute(block, 'frame', route)  21.5 us
    ppermute x4, waiting for transfers between devices, along(): return lax.ppermute(block, 'frame', route)  16 us
    ppermute x1, starting transfers between devices, on_device(): two = lax.ppermute(two, ('frame', 'atom'), list(enumerate(second)))  10.5 us
    ppermute x3, starting transfers between devices, across(): lax.ppermute(block, 'frame', [((f + SIDE) % (2 * SIDE), f) for f in range...  7.72 us
    all_to_all x1, waiting for transfers between devices, on_device(): lax.all_to_all(merged, ('frame', 'atom'), 0, 0, axis_index_groups=groups,...  7.37 us
    ppermute x1, waiting for transfers between devices, on_device(): one = lax.ppermute(one, ('frame', 'atom'), list(enumerate(first)))  5.76 us
    all_to_all x1, starting transfers between devices, on_device(): lax.all_to_all(merged, ('frame', 'atom'), 0, 0, axis_index_groups=groups,...  5.42 us
    ppermute x1, starting transfers between devices, on_device(): taken = lax.ppermute(send, 'atom', [(a, a ^ 1) for a in range(SIDE)])  3.56 us
  transfers between devices with their start and end apart: 11, of which 7 were waited for; matrix products, arithmetic and copies ran while one was open for 1% of the time, Pallas kernels for 4%

profile of v8, /device:TPU:7, one launch (start us, length us, event | category | flops | bytes accessed | tf_op | source)
XLA Modules:
  0.0 98.1 jit_solution(16998270173963481463)
XLA Ops:
  0.0 11.6 %collective-permute-start = (f32[144,512]{1,0:T(8,128)}, f32[144,512]{1,0:T(8,128)S(1)}, u32[]{:S(2)}, u32[]{:S(2)}) collective-permute-start(f32[144,512]{1,0:T(8,128)} %bitcast.9), channel_id=1, source_target_pairs={{32,0},{48,16},{64,32},{80,48},{96,64},{112,80},{128,96},{144,112}... | collective-permute-start | bytes 884744 | tf_op jit(solution)/shard_map/ppermute | solution.py:417
  11.6 1.9 %collective-permute-start.2 = (f32[144,512]{1,0:T(8,128)}, f32[144,512]{1,0:T(8,128)S(1)}, u32[]{:S(2)}, u32[]{:S(2)}) collective-permute-start(f32[144,512]{1,0:T(8,128)} %bitcast.10), channel_id=1, source_target_pairs={{208,0},{224,16},{240,32},{0,48},{16,64},{32,80},{48,96},{64,112},... | collective-permute-start | bytes 884744 | tf_op jit(solution)/shard_map/ppermute | solution.py:417
  13.5 10.4 %collective-permute-done.plus2 = f32[144,512]{1,0:T(8,128)S(1)} collective-permute-done((f32[144,512]{1,0:T(8,128)}, f32[144,512]{1,0:T(8,128)S(1)}, u32[]{:S(2)}, u32[]{:S(2)}) %collective-permute-start) | collective-permute-done | bytes 294944 | tf_op jit(solution)/shard_map/ppermute | solution.py:417
  23.9 6.1 %collective-permute-start.1 = (f32[144,512]{1,0:T(8,128)S(1)}, f32[144,512]{1,0:T(8,128)S(1)}, u32[]{:S(2)}, u32[]{:S(2)}) collective-permute-start(f32[144,512]{1,0:T(8,128)S(1)} %collective-permute-done.plus2), channel_id=1, source_target_pairs={{32,0},{48,16},{64,32},{80,48},{96,64},{112,80},{128,96},{144,112}... | collective-permute-start | bytes 884744 | tf_op jit(solution)/shard_map/ppermute | solution.py:417
  30.0 2.5 %collective-permute-start.4 = (f32[144,512]{1,0:T(8,128)S(1)}, f32[144,512]{1,0:T(8,128)S(1)}, u32[]{:S(2)}, u32[]{:S(2)}) collective-permute-start(f32[144,512]{1,0:T(8,128)S(1)} %collective-permute-done.plus2), channel_id=1, source_target_pairs={{256,0},{272,16},{288,32},{304,48},{320,64},{336,80},{352,96},{368... | collective-permute-start | bytes 884744 | tf_op jit(solution)/shard_map/ppermute | solution.py:420
  32.5 5.0 %collective-permute-done.2.minus3 = f32[144,512]{1,0:T(8,128)S(1)} collective-permute-done((f32[144,512]{1,0:T(8,128)}, f32[144,512]{1,0:T(8,128)S(1)}, u32[]{:S(2)}, u32[]{:S(2)}) %collective-permute-start.2) | collective-permute-done | bytes 294944 | tf_op jit(solution)/shard_map/ppermute | solution.py:417
  37.5 2.4 %collective-permute-start.5 = (f32[144,512]{1,0:T(8,128)S(1)}, f32[144,512]{1,0:T(8,128)S(1)}, u32[]{:S(2)}, u32[]{:S(2)}) collective-permute-start(f32[144,512]{1,0:T(8,128)S(1)} %collective-permute-done.2.minus3), channel_id=1, source_target_pairs={{256,0},{272,16},{288,32},{304,48},{320,64},{336,80},{352,96},{368... | collective-permute-start | bytes 884744 | tf_op jit(solution)/shard_map/ppermute | solution.py:420
  39.9 1.9 %collective-permute-start.3 = (f32[144,512]{1,0:T(8,128)S(1)}, f32[144,512]{1,0:T(8,128)S(1)}, u32[]{:S(2)}, u32[]{:S(2)}) collective-permute-start(f32[144,512]{1,0:T(8,128)S(1)} %collective-permute-done.2.minus3), channel_id=1, source_target_pairs={{240,0},{0,16},{16,32},{32,48},{48,64},{64,80},{80,96},{96,112},{1... | collective-permute-start | bytes 884744 | tf_op jit(solution)/shard_map/ppermute | solution.py:417
  41.9 0.1 pad_add_fusion.1.flags
  42.0 0.0 collective-permute-done.1.plus4
  42.0 2.8 %collective-permute-start.6 = (f32[144,512]{1,0:T(8,128)S(1)}, f32[144,512]{1,0:T(8,128)S(1)}, u32[]{:S(2)}, u32[]{:S(2)}) collective-permute-start(f32[144,512]{1,0:T(8,128)S(1)} %collective-permute-done.1.plus4), channel_id=1, source_target_pairs={{256,0},{272,16},{288,32},{304,48},{320,64},{336,80},{352,96},{368... | collective-permute-start | bytes 884744 | tf_op jit(solution)/shard_map/ppermute | solution.py:420
  44.8 0.0 collective-permute-done.4.other2
  44.8 2.6 %collective-permute-done.5.other3 = f32[144,512]{1,0:T(8,128)S(1)} collective-permute-done((f32[144,512]{1,0:T(8,128)S(1)}, f32[144,512]{1,0:T(8,128)S(1)}, u32[]{:S(2)}, u32[]{:S(2)}) %collective-permute-start.5) | collective-permute-done | bytes 294944 | tf_op jit(solution)/shard_map/ppermute | solution.py:420
  47.5 0.0 copy-start
  47.5 0.7 copy-done
  48.1 0.0 copy-start.1
  48.1 1.0 copy-done.1
  49.1 1.1 %shard_map.37 = (bf16[576,1536]{1,0:T(8,128)(2,1)S(1)}, f32[4,48,128]{2,1,0:T(8,128)S(1)}, bf16[3,256,1536]{2,1,0:T(8,128)(2,1)S(1)}, f32[3,48,128]{2,1,0:T(8,128)S(1)}) custom-call(s32[3]{0:T(128)S(1)} %pad_add_fusion.1.flags, s32[1,512]{1,0:T(1,128)S(1)} %bitcast.6, f32[144,512]{1,0:T(8,128)S(1)} %bitcast.11, f32[144,512]{1,0:T(8,128)S(1)} %collective-permute-done.plus2, ...), custom_call_target="tpu_custom_call" | custom-call | flops 1585446912 | bytes 4000000 | tf_op jit(solution)/shard_map/pallas_call | solution.py:453
  50.2 0.6 collective-permute-done.3.minus4
  50.8 2.9 %shard_map.38 = (f32[16,176,128]{2,1,0:T(8,128)S(1)}, bf16[576,1536]{1,0:T(8,128)(2,1)S(1)}, f32[4,48,128]{2,1,0:T(8,128)S(1)}) custom-call(s32[3]{0:T(128)S(1)} %pad_add_fusion.1.flags, s32[1,512]{1,0:T(1,128)S(1)} %bitcast.7, f32[144,512]{1,0:T(8,128)S(1)} %collective-permute-done.1.plus4, ...), custom_call_target="tpu_custom_call", output_to_operand_aliasing={{1}: (7, {}), {2}: (8, {})} | custom-call | flops 1698693120 | bytes 4000000 | tf_op jit(solution)/shard_map/pallas_call | solution.py:461
  53.7 0.0 collective-permute-done.6.other4
  53.8 1.4 %shard_map.39 = (f32[8,176,128]{2,1,0:T(8,128)S(1)}, f32[1,176,128]{2,1,0:T(8,128)S(1)}) custom-call(s32[3]{0:T(128)S(1)} %pad_add_fusion.1.flags, s32[1,512]{1,0:T(1,128)S(1)} %bitcast.8, bf16[576,1536]{1,0:T(8,128)(2,1)S(1)} %get-tuple-element.21.weighted, f32[4,48,128]{2,1,0:T(8,128)S(1)} %get-tuple-element.22.row_feature, ...), custom_call_target="tpu_custom_call" | custom-call | flops 339738624 | bytes 4000000 | tf_op jit(solution)/shard_map/pallas_call | solution.py:471
  55.2 3.6 %collective-permute-start.7 = (f32[8,176,128]{2,1,0:T(8,128)S(1)}, f32[8,176,128]{2,1,0:T(8,128)S(1)}, u32[]{:S(2)}, u32[]{:S(2)}) collective-permute-start(f32[8,176,128]{2,1,0:T(8,128)S(1)} %get-tuple-element.24), channel_id=1, source_target_pairs={{0,1},{1,0},{2,3},{3,2},{4,5},{5,4},{6,7},{7,6},{8,9},{9,8},{10,11... | collective-permute-start | bytes 2162696 | tf_op jit(solution)/shard_map/ppermute | solution.py:480
  58.8 1.8 %collective-permute-done.7.taken = f32[8,176,128]{2,1,0:T(8,128)S(1)} collective-permute-done((f32[8,176,128]{2,1,0:T(8,128)S(1)}, f32[8,176,128]{2,1,0:T(8,128)S(1)}, u32[]{:S(2)}, u32[]{:S(2)}) %collective-permute-start.7) | collective-permute-done | bytes 720928 | tf_op jit(solution)/shard_map/ppermute | solution.py:480
  60.6 1.0 shard_map.40
  61.5 5.4 %all-to-all-start = ((f32[8,176,128]{2,1,0:T(8,128)}), f32[8,176,128]{2,1,0:T(8,128)S(1)}, u32[]{:S(2)}, u32[]{:S(2)}) async-start(f32[8,176,128]{2,1,0:T(8,128)} %shard_map.40), calls=%async_computation | async-start | bytes 1441792 | tf_op jit(solution)/shard_map/all_to_all | solution.py:489
  67.0 1.3 %dynamic_slice.3 = s32[1]{0:T(128)} dynamic-slice(s32[512]{0:T(512)} %constant.72.clone, s32[]{:T(128)S(6)} %select_n.33), dynamic_slice_sizes={1} | dynamic-slice | bytes 12 | tf_op jit(solution)/shard_map/dynamic_slice | solution.py:409
  69.5 0.1 pad_add_fusion.flags
  69.6 7.4 %all-to-all-done.parts = f32[8,176,128]{2,1,0:T(8,128)S(1)} async-done(((f32[8,176,128]{2,1,0:T(8,128)}), f32[8,176,128]{2,1,0:T(8,128)S(1)}, u32[]{:S(2)}, u32[]{:S(2)}) %all-to-all-start) | async-done | bytes 720928 | tf_op jit(solution)/shard_map/all_to_all | solution.py:489
  77.0 1.6 %shard_map.41 = (f32[24,128]{1,0:T(8,128)S(1)}, f32[24,128]{1,0:T(8,128)S(1)}) custom-call(s32[2]{0:T(128)S(1)} %pad_add_fusion.flags, f32[8,176,128]{2,1,0:T(8,128)S(1)} %all-to-all-done.parts), custom_call_target="tpu_custom_call" | custom-call | tf_op jit(solution)/shard_map/pallas_call | solution.py:492
  78.5 10.5 %collective-permute-start.8 = (f32[24,128]{1,0:T(8,128)S(1)}, f32[24,128]{1,0:T(8,128)S(1)}, u32[]{:S(2)}, u32[]{:S(2)}) collective-permute-start(f32[24,128]{1,0:T(8,128)S(1)} %get-tuple-element.25), channel_id=1, source_target_pairs={{0,464},{1,64},{2,320},{3,322},{4,38},{5,209},{6,70},{7,210},{8,29... | collective-permute-start | bytes 36872 | tf_op jit(solution)/shard_map/ppermute | solution.py:500
  89.0 1.9 %collective-permute-start.9 = (f32[24,128]{1,0:T(8,128)S(1)}, f32[24,128]{1,0:T(8,128)S(1)}, u32[]{:S(2)}, u32[]{:S(2)}) collective-permute-start(f32[24,128]{1,0:T(8,128)S(1)} %get-tuple-element.26), channel_id=1, source_target_pairs={{0,14},{1,2},{2,10},{3,74},{4,193},{5,38},{6,194},{7,70},{8,217},{... | collective-permute-start | bytes 36872 | tf_op jit(solution)/shard_map/ppermute | solution.py:499
  91.6 0.0 collective-permute-done.8
  91.6 5.8 %collective-permute-done.9 = f32[24,128]{1,0:T(8,128)S(1)} collective-permute-done((f32[24,128]{1,0:T(8,128)S(1)}, f32[24,128]{1,0:T(8,128)S(1)}, u32[]{:S(2)}, u32[]{:S(2)}) %collective-permute-start.9) | collective-permute-done | bytes 12320 | tf_op jit(solution)/shard_map/ppermute | solution.py:499
  97.4 0.1 fusion
  97.4 0.7 maximum_maximum_fusion
  (1 shorter events, 0.0 us)
Async XLA Ops:
  0.0 23.9 %collective-permute-start = (f32[144,512]{1,0:T(8,128)}, f32[144,512]{1,0:T(8,128)S(1)}, u32[]{:S(2)}, u32[]{:S(2)}) collective-permute-start(f32[144,512]{1,0:T(8,128)} %bitcast.9), channel_id=1, source_target_pairs={{32,0},{48,16},{64,32},{80,48},{96,64},{112,80},{128,96},{144,112}... | collective-permute-start | bytes 884744 | tf_op jit(solution)/shard_map/ppermute | solution.py:417
  11.6 25.9 %collective-permute-start.2 = (f32[144,512]{1,0:T(8,128)}, f32[144,512]{1,0:T(8,128)S(1)}, u32[]{:S(2)}, u32[]{:S(2)}) collective-permute-start(f32[144,512]{1,0:T(8,128)} %bitcast.10), channel_id=1, source_target_pairs={{208,0},{224,16},{240,32},{0,48},{16,64},{32,80},{48,96},{64,112},... | collective-permute-start | bytes 884744 | tf_op jit(solution)/shard_map/ppermute | solution.py:417
  23.9 18.1 %collective-permute-start.1 = (f32[144,512]{1,0:T(8,128)S(1)}, f32[144,512]{1,0:T(8,128)S(1)}, u32[]{:S(2)}, u32[]{:S(2)}) collective-permute-start(f32[144,512]{1,0:T(8,128)S(1)} %collective-permute-done.plus2), channel_id=1, source_target_pairs={{32,0},{48,16},{64,32},{80,48},{96,64},{112,80},{128,96},{144,112}... | collective-permute-start | bytes 884744 | tf_op jit(solution)/shard_map/ppermute | solution.py:417
  30.0 14.8 %collective-permute-start.4 = (f32[144,512]{1,0:T(8,128)S(1)}, f32[144,512]{1,0:T(8,128)S(1)}, u32[]{:S(2)}, u32[]{:S(2)}) collective-permute-start(f32[144,512]{1,0:T(8,128)S(1)} %collective-permute-done.plus2), channel_id=1, source_target_pairs={{256,0},{272,16},{288,32},{304,48},{320,64},{336,80},{352,96},{368... | collective-permute-start | bytes 884744 | tf_op jit(solution)/shard_map/ppermute | solution.py:420
  37.5 10.0 %collective-permute-start.5 = (f32[144,512]{1,0:T(8,128)S(1)}, f32[144,512]{1,0:T(8,128)S(1)}, u32[]{:S(2)}, u32[]{:S(2)}) collective-permute-start(f32[144,512]{1,0:T(8,128)S(1)} %collective-permute-done.2.minus3), channel_id=1, source_target_pairs={{256,0},{272,16},{288,32},{304,48},{320,64},{336,80},{352,96},{368... | collective-permute-start | bytes 884744 | tf_op jit(solution)/shard_map/ppermute | solution.py:420
  39.9 10.9 %collective-permute-start.3 = (f32[144,512]{1,0:T(8,128)S(1)}, f32[144,512]{1,0:T(8,128)S(1)}, u32[]{:S(2)}, u32[]{:S(2)}) collective-permute-start(f32[144,512]{1,0:T(8,128)S(1)} %collective-permute-done.2.minus3), channel_id=1, source_target_pairs={{240,0},{0,16},{16,32},{32,48},{48,64},{64,80},{80,96},{96,112},{1... | collective-permute-start | bytes 884744 | tf_op jit(solution)/shard_map/ppermute | solution.py:417
  42.0 11.8 %collective-permute-start.6 = (f32[144,512]{1,0:T(8,128)S(1)}, f32[144,512]{1,0:T(8,128)S(1)}, u32[]{:S(2)}, u32[]{:S(2)}) collective-permute-start(f32[144,512]{1,0:T(8,128)S(1)} %collective-permute-done.1.plus4), channel_id=1, source_target_pairs={{256,0},{272,16},{288,32},{304,48},{320,64},{336,80},{352,96},{368... | collective-permute-start | bytes 884744 | tf_op jit(solution)/shard_map/ppermute | solution.py:420
  47.5 0.7 copy-start
  48.1 1.0 copy-start.1
  55.2 5.4 %collective-permute-start.7 = (f32[8,176,128]{2,1,0:T(8,128)S(1)}, f32[8,176,128]{2,1,0:T(8,128)S(1)}, u32[]{:S(2)}, u32[]{:S(2)}) collective-permute-start(f32[8,176,128]{2,1,0:T(8,128)S(1)} %get-tuple-element.24), channel_id=1, source_target_pairs={{0,1},{1,0},{2,3},{3,2},{4,5},{5,4},{6,7},{7,6},{8,9},{9,8},{10,11... | collective-permute-start | bytes 2162696 | tf_op jit(solution)/shard_map/ppermute | solution.py:480
  61.5 15.4 %all-to-all-start = ((f32[8,176,128]{2,1,0:T(8,128)}), f32[8,176,128]{2,1,0:T(8,128)S(1)}, u32[]{:S(2)}, u32[]{:S(2)}) async-start(f32[8,176,128]{2,1,0:T(8,128)} %shard_map.40), calls=%async_computation | async-start | bytes 1441792 | tf_op jit(solution)/shard_map/all_to_all | solution.py:489
  78.5 13.0 %collective-permute-start.8 = (f32[24,128]{1,0:T(8,128)S(1)}, f32[24,128]{1,0:T(8,128)S(1)}, u32[]{:S(2)}, u32[]{:S(2)}) collective-permute-start(f32[24,128]{1,0:T(8,128)S(1)} %get-tuple-element.25), channel_id=1, source_target_pairs={{0,464},{1,64},{2,320},{3,322},{4,38},{5,209},{6,70},{7,210},{8,29... | collective-permute-start | bytes 36872 | tf_op jit(solution)/shard_map/ppermute | solution.py:500
  89.0 8.3 %collective-permute-start.9 = (f32[24,128]{1,0:T(8,128)S(1)}, f32[24,128]{1,0:T(8,128)S(1)}, u32[]{:S(2)}, u32[]{:S(2)}) collective-permute-start(f32[24,128]{1,0:T(8,128)S(1)} %get-tuple-element.26), channel_id=1, source_target_pairs={{0,14},{1,2},{2,10},{3,74},{4,193},{5,38},{6,194},{7,70},{8,217},{... | collective-permute-start | bytes 36872 | tf_op jit(solution)/shard_map/ppermute | solution.py:499

commit v9 on v8

--- a/solution.py
+++ b/solution.py
@@ -43,7 +43,7 @@
     if pair == len(PAIRS) - 1 and column == 1:
         p = 4
     a, b = frame_block(column, z, p), frame_block(column, z, q)
-    if pair == DIAGONAL and z >= SIDE // 2:
+    if pair == DIAGONAL and z < SIDE // 2:
         return ((a, a), (b, b))
     return ((a, b), (b, a))
 
@@ -88,7 +88,7 @@
             for device in range(SIDE):
                 pair = POSITION[2 * order.index(device // 2) + device % 2]
                 ends.append(ends_of(column, z, pair))
-                diagonal.append(int(pair == DIAGONAL and z >= SIDE // 2))
+                diagonal.append(int(pair == DIAGONAL and z < SIDE // 2))
     place = lambda end: end[0] * SIDE + end[1] // 2
     at = {}
     for device, pair in enumerate(ends):
@@ -405,7 +405,7 @@
 def on_device(coords, weights):
     orders, first, second, table = routes()
     frame, atom = lax.axis_index("frame"), lax.axis_index("atom")
-    build_flags = jnp.stack([frame // SIDE, (frame % SIDE) // (SIDE // 2), atom % 2]).astype(jnp.int32)
+    build_flags = jnp.stack([frame // SIDE, 1 - (frame % SIDE) // (SIDE // 2), atom % 2]).astype(jnp.int32)
     mine = jnp.asarray(np.array(table), jnp.int32)[frame * SIDE + atom]
     fit_flags = jnp.stack([mine & 1, mine >> 2])
     mass = weights[None, :]

time: 99.8 us -> 98.9 us (level)
  starting transfers between devices: 50.6 us -> 48.8 us
    ppermute x1, starting transfers between devices: 10.5 us -> 8.62 us  [on_device(): two = lax.ppermute(two, ('frame', 'atom'), list(enumerate(second)))]
  transfers between devices with their start and end apart: 11 -> 11, of which waited for: 7 -> 7; matrix products, arithmetic and copies ran while one was open for 1% -> 1% of each run, Pallas kernels for 4% -> 5%
where the time goes in v9:
time: 98.9 us; the launch traced here: 97.2 us
  starting transfers between devices  48.8 us (49%)
  waiting for transfers between devices  33.6 us (34%)
  Pallas kernels  8.92 us (9%)
  local copies, waits for them, and re-layouts  2.98 us (3%)
  between operations  2.12 us (2%)
    ppermute x4, starting transfers between devices, along(): return lax.ppermute(block, 'frame', route)  21.5 us
    ppermute x4, waiting for transfers between devices, along(): return lax.ppermute(block, 'frame', route)  16 us
    ppermute x1, starting transfers between devices, on_device(): two = lax.ppermute(two, ('frame', 'atom'), list(enumerate(second)))  8.62 us
    ppermute x3, starting transfers between devices, across(): lax.ppermute(block, 'frame', [((f + SIDE) % (2 * SIDE), f) for f in range...  7.72 us
    all_to_all x1, waiting for transfers between devices, on_device(): lax.all_to_all(merged, ('frame', 'atom'), 0, 0, axis_index_groups=groups,...  7.37 us
    ppermute x1, waiting for transfers between devices, on_device(): one = lax.ppermute(one, ('frame', 'atom'), list(enumerate(first)))  5.76 us
    all_to_all x1, starting transfers between devices, on_device(): lax.all_to_all(merged, ('frame', 'atom'), 0, 0, axis_index_groups=groups,...  5.43 us
    pallas_call x1, Pallas kernels, on_device(): pl.pallas_call(early_kernel, out_shape=[sums_of(2 * CHIPS)] + staged, in_...  3.86 us
  transfers between devices with their start and end apart: 11, of which 7 were waited for; matrix products, arithmetic and copies ran while one was open for 1% of the time, Pallas kernels for 5%

profile of v9, /device:TPU:7, one launch (start us, length us, event | category | flops | bytes accessed | tf_op | source)
XLA Modules:
  0.0 97.2 jit_solution(9206169835380881497)
XLA Ops:
  0.0 11.6 %collective-permute-start = (f32[144,512]{1,0:T(8,128)}, f32[144,512]{1,0:T(8,128)S(1)}, u32[]{:S(2)}, u32[]{:S(2)}) collective-permute-start(f32[144,512]{1,0:T(8,128)} %bitcast.9), channel_id=1, source_target_pairs={{32,0},{48,16},{64,32},{80,48},{96,64},{112,80},{128,96},{144,112}... | collective-permute-start | bytes 884744 | tf_op jit(solution)/shard_map/ppermute | solution.py:417
  11.6 1.9 %collective-permute-start.2 = (f32[144,512]{1,0:T(8,128)}, f32[144,512]{1,0:T(8,128)S(1)}, u32[]{:S(2)}, u32[]{:S(2)}) collective-permute-start(f32[144,512]{1,0:T(8,128)} %bitcast.10), channel_id=1, source_target_pairs={{208,0},{224,16},{240,32},{0,48},{16,64},{32,80},{48,96},{64,112},... | collective-permute-start | bytes 884744 | tf_op jit(solution)/shard_map/ppermute | solution.py:417
  13.5 10.4 %collective-permute-done.plus2 = f32[144,512]{1,0:T(8,128)S(1)} collective-permute-done((f32[144,512]{1,0:T(8,128)}, f32[144,512]{1,0:T(8,128)S(1)}, u32[]{:S(2)}, u32[]{:S(2)}) %collective-permute-start) | collective-permute-done | bytes 294944 | tf_op jit(solution)/shard_map/ppermute | solution.py:417
  23.9 6.1 %collective-permute-start.1 = (f32[144,512]{1,0:T(8,128)S(1)}, f32[144,512]{1,0:T(8,128)S(1)}, u32[]{:S(2)}, u32[]{:S(2)}) collective-permute-start(f32[144,512]{1,0:T(8,128)S(1)} %collective-permute-done.plus2), channel_id=1, source_target_pairs={{32,0},{48,16},{64,32},{80,48},{96,64},{112,80},{128,96},{144,112}... | collective-permute-start | bytes 884744 | tf_op jit(solution)/shard_map/ppermute | solution.py:417
  30.0 2.5 %collective-permute-start.4 = (f32[144,512]{1,0:T(8,128)S(1)}, f32[144,512]{1,0:T(8,128)S(1)}, u32[]{:S(2)}, u32[]{:S(2)}) collective-permute-start(f32[144,512]{1,0:T(8,128)S(1)} %collective-permute-done.plus2), channel_id=1, source_target_pairs={{256,0},{272,16},{288,32},{304,48},{320,64},{336,80},{352,96},{368... | collective-permute-start | bytes 884744 | tf_op jit(solution)/shard_map/ppermute | solution.py:420
  32.5 5.0 %collective-permute-done.2.minus3 = f32[144,512]{1,0:T(8,128)S(1)} collective-permute-done((f32[144,512]{1,0:T(8,128)}, f32[144,512]{1,0:T(8,128)S(1)}, u32[]{:S(2)}, u32[]{:S(2)}) %collective-permute-start.2) | collective-permute-done | bytes 294944 | tf_op jit(solution)/shard_map/ppermute | solution.py:417
  37.5 2.4 %collective-permute-start.5 = (f32[144,512]{1,0:T(8,128)S(1)}, f32[144,512]{1,0:T(8,128)S(1)}, u32[]{:S(2)}, u32[]{:S(2)}) collective-permute-start(f32[144,512]{1,0:T(8,128)S(1)} %collective-permute-done.2.minus3), channel_id=1, source_target_pairs={{256,0},{272,16},{288,32},{304,48},{320,64},{336,80},{352,96},{368... | collective-permute-start | bytes 884744 | tf_op jit(solution)/shard_map/ppermute | solution.py:420
  39.9 1.9 %collective-permute-start.3 = (f32[144,512]{1,0:T(8,128)S(1)}, f32[144,512]{1,0:T(8,128)S(1)}, u32[]{:S(2)}, u32[]{:S(2)}) collective-permute-start(f32[144,512]{1,0:T(8,128)S(1)} %collective-permute-done.2.minus3), channel_id=1, source_target_pairs={{240,0},{0,16},{16,32},{32,48},{48,64},{64,80},{80,96},{96,112},{1... | collective-permute-start | bytes 884744 | tf_op jit(solution)/shard_map/ppermute | solution.py:417
  41.9 0.1 pad_add_fusion.1.flags
  42.0 0.0 collective-permute-done.1.plus4
  42.0 2.8 %collective-permute-start.6 = (f32[144,512]{1,0:T(8,128)S(1)}, f32[144,512]{1,0:T(8,128)S(1)}, u32[]{:S(2)}, u32[]{:S(2)}) collective-permute-start(f32[144,512]{1,0:T(8,128)S(1)} %collective-permute-done.1.plus4), channel_id=1, source_target_pairs={{256,0},{272,16},{288,32},{304,48},{320,64},{336,80},{352,96},{368... | collective-permute-start | bytes 884744 | tf_op jit(solution)/shard_map/ppermute | solution.py:420
  44.8 0.0 collective-permute-done.4.other2
  44.8 2.6 %collective-permute-done.5.other3 = f32[144,512]{1,0:T(8,128)S(1)} collective-permute-done((f32[144,512]{1,0:T(8,128)S(1)}, f32[144,512]{1,0:T(8,128)S(1)}, u32[]{:S(2)}, u32[]{:S(2)}) %collective-permute-start.5) | collective-permute-done | bytes 294944 | tf_op jit(solution)/shard_map/ppermute | solution.py:420
  47.5 0.0 copy-start
  47.5 0.7 copy-done
  48.1 0.0 copy-start.1
  48.1 1.0 copy-done.1
  49.1 1.1 %shard_map.37 = (bf16[576,1536]{1,0:T(8,128)(2,1)S(1)}, f32[4,48,128]{2,1,0:T(8,128)S(1)}, bf16[3,256,1536]{2,1,0:T(8,128)(2,1)S(1)}, f32[3,48,128]{2,1,0:T(8,128)S(1)}) custom-call(s32[3]{0:T(128)S(1)} %pad_add_fusion.1.flags, s32[1,512]{1,0:T(1,128)S(1)} %bitcast.6, f32[144,512]{1,0:T(8,128)S(1)} %bitcast.11, f32[144,512]{1,0:T(8,128)S(1)} %collective-permute-done.plus2, ...), custom_call_target="tpu_custom_call" | custom-call | flops 1585446912 | bytes 4000000 | tf_op jit(solution)/shard_map/pallas_call | solution.py:453
  50.2 0.6 collective-permute-done.3.minus4
  50.8 3.9 %shard_map.38 = (f32[16,176,128]{2,1,0:T(8,128)S(1)}, bf16[576,1536]{1,0:T(8,128)(2,1)S(1)}, f32[4,48,128]{2,1,0:T(8,128)S(1)}) custom-call(s32[3]{0:T(128)S(1)} %pad_add_fusion.1.flags, s32[1,512]{1,0:T(1,128)S(1)} %bitcast.7, f32[144,512]{1,0:T(8,128)S(1)} %collective-permute-done.1.plus4, ...), custom_call_target="tpu_custom_call", output_to_operand_aliasing={{1}: (7, {}), {2}: (8, {})} | custom-call | flops 1698693120 | bytes 4000000 | tf_op jit(solution)/shard_map/pallas_call | solution.py:461
  54.7 0.0 collective-permute-done.6.other4
  54.7 1.4 %shard_map.39 = (f32[8,176,128]{2,1,0:T(8,128)S(1)}, f32[1,176,128]{2,1,0:T(8,128)S(1)}) custom-call(s32[3]{0:T(128)S(1)} %pad_add_fusion.1.flags, s32[1,512]{1,0:T(1,128)S(1)} %bitcast.8, bf16[576,1536]{1,0:T(8,128)(2,1)S(1)} %get-tuple-element.21.weighted, f32[4,48,128]{2,1,0:T(8,128)S(1)} %get-tuple-element.22.row_feature, ...), custom_call_target="tpu_custom_call" | custom-call | flops 339738624 | bytes 4000000 | tf_op jit(solution)/shard_map/pallas_call | solution.py:471
  56.1 3.6 %collective-permute-start.7 = (f32[8,176,128]{2,1,0:T(8,128)S(1)}, f32[8,176,128]{2,1,0:T(8,128)S(1)}, u32[]{:S(2)}, u32[]{:S(2)}) collective-permute-start(f32[8,176,128]{2,1,0:T(8,128)S(1)} %get-tuple-element.24), channel_id=1, source_target_pairs={{0,1},{1,0},{2,3},{3,2},{4,5},{5,4},{6,7},{7,6},{8,9},{9,8},{10,11... | collective-permute-start | bytes 2162696 | tf_op jit(solution)/shard_map/ppermute | solution.py:480
  59.7 1.8 %collective-permute-done.7.taken = f32[8,176,128]{2,1,0:T(8,128)S(1)} collective-permute-done((f32[8,176,128]{2,1,0:T(8,128)S(1)}, f32[8,176,128]{2,1,0:T(8,128)S(1)}, u32[]{:S(2)}, u32[]{:S(2)}) %collective-permute-start.7) | collective-permute-done | bytes 720928 | tf_op jit(solution)/shard_map/ppermute | solution.py:480
  61.5 1.0 shard_map.40
  62.5 5.4 %all-to-all-start = ((f32[8,176,128]{2,1,0:T(8,128)}), f32[8,176,128]{2,1,0:T(8,128)S(1)}, u32[]{:S(2)}, u32[]{:S(2)}) async-start(f32[8,176,128]{2,1,0:T(8,128)} %shard_map.40), calls=%async_computation | async-start | bytes 1441792 | tf_op jit(solution)/shard_map/all_to_all | solution.py:489
  67.9 1.3 %dynamic_slice.3 = s32[1]{0:T(128)} dynamic-slice(s32[512]{0:T(512)} %constant.72.clone, s32[]{:T(128)S(6)} %select_n.33), dynamic_slice_sizes={1} | dynamic-slice | bytes 12 | tf_op jit(solution)/shard_map/dynamic_slice | solution.py:409
  70.4 0.1 pad_add_fusion.flags
  70.5 7.4 %all-to-all-done.parts = f32[8,176,128]{2,1,0:T(8,128)S(1)} async-done(((f32[8,176,128]{2,1,0:T(8,128)}), f32[8,176,128]{2,1,0:T(8,128)S(1)}, u32[]{:S(2)}, u32[]{:S(2)}) %all-to-all-start) | async-done | bytes 720928 | tf_op jit(solution)/shard_map/all_to_all | solution.py:489
  77.9 1.6 %shard_map.41 = (f32[24,128]{1,0:T(8,128)S(1)}, f32[24,128]{1,0:T(8,128)S(1)}) custom-call(s32[2]{0:T(128)S(1)} %pad_add_fusion.flags, f32[8,176,128]{2,1,0:T(8,128)S(1)} %all-to-all-done.parts), custom_call_target="tpu_custom_call" | custom-call | tf_op jit(solution)/shard_map/pallas_call | solution.py:492
  79.5 8.6 %collective-permute-start.8 = (f32[24,128]{1,0:T(8,128)S(1)}, f32[24,128]{1,0:T(8,128)S(1)}, u32[]{:S(2)}, u32[]{:S(2)}) collective-permute-start(f32[24,128]{1,0:T(8,128)S(1)} %get-tuple-element.25), channel_id=1, source_target_pairs={{0,464},{1,64},{2,320},{3,322},{4,38},{5,209},{6,66},{7,70},{8,294... | collective-permute-start | bytes 36872 | tf_op jit(solution)/shard_map/ppermute | solution.py:500
  88.1 1.9 %collective-permute-start.9 = (f32[24,128]{1,0:T(8,128)S(1)}, f32[24,128]{1,0:T(8,128)S(1)}, u32[]{:S(2)}, u32[]{:S(2)}) collective-permute-start(f32[24,128]{1,0:T(8,128)S(1)} %get-tuple-element.26), channel_id=1, source_target_pairs={{0,14},{1,2},{2,10},{3,74},{4,193},{5,38},{6,198},{7,210},{8,217},... | collective-permute-start | bytes 36872 | tf_op jit(solution)/shard_map/ppermute | solution.py:499
  90.7 0.0 collective-permute-done.8
  90.7 5.8 %collective-permute-done.9 = f32[24,128]{1,0:T(8,128)S(1)} collective-permute-done((f32[24,128]{1,0:T(8,128)S(1)}, f32[24,128]{1,0:T(8,128)S(1)}, u32[]{:S(2)}, u32[]{:S(2)}) %collective-permute-start.9) | collective-permute-done | bytes 12320 | tf_op jit(solution)/shard_map/ppermute | solution.py:499
  96.5 0.1 fusion
  96.5 0.7 maximum_maximum_fusion
  (1 shorter events, 0.0 us)
Async XLA Ops:
  0.0 23.9 %collective-permute-start = (f32[144,512]{1,0:T(8,128)}, f32[144,512]{1,0:T(8,128)S(1)}, u32[]{:S(2)}, u32[]{:S(2)}) collective-permute-start(f32[144,512]{1,0:T(8,128)} %bitcast.9), channel_id=1, source_target_pairs={{32,0},{48,16},{64,32},{80,48},{96,64},{112,80},{128,96},{144,112}... | collective-permute-start | bytes 884744 | tf_op jit(solution)/shard_map/ppermute | solution.py:417
  11.6 25.9 %collective-permute-start.2 = (f32[144,512]{1,0:T(8,128)}, f32[144,512]{1,0:T(8,128)S(1)}, u32[]{:S(2)}, u32[]{:S(2)}) collective-permute-start(f32[144,512]{1,0:T(8,128)} %bitcast.10), channel_id=1, source_target_pairs={{208,0},{224,16},{240,32},{0,48},{16,64},{32,80},{48,96},{64,112},... | collective-permute-start | bytes 884744 | tf_op jit(solution)/shard_map/ppermute | solution.py:417
  23.9 18.1 %collective-permute-start.1 = (f32[144,512]{1,0:T(8,128)S(1)}, f32[144,512]{1,0:T(8,128)S(1)}, u32[]{:S(2)}, u32[]{:S(2)}) collective-permute-start(f32[144,512]{1,0:T(8,128)S(1)} %collective-permute-done.plus2), channel_id=1, source_target_pairs={{32,0},{48,16},{64,32},{80,48},{96,64},{112,80},{128,96},{144,112}... | collective-permute-start | bytes 884744 | tf_op jit(solution)/shard_map/ppermute | solution.py:417
  30.0 14.8 %collective-permute-start.4 = (f32[144,512]{1,0:T(8,128)S(1)}, f32[144,512]{1,0:T(8,128)S(1)}, u32[]{:S(2)}, u32[]{:S(2)}) collective-permute-start(f32[144,512]{1,0:T(8,128)S(1)} %collective-permute-done.plus2), channel_id=1, source_target_pairs={{256,0},{272,16},{288,32},{304,48},{320,64},{336,80},{352,96},{368... | collective-permute-start | bytes 884744 | tf_op jit(solution)/shard_map/ppermute | solution.py:420
  37.5 10.0 %collective-permute-start.5 = (f32[144,512]{1,0:T(8,128)S(1)}, f32[144,512]{1,0:T(8,128)S(1)}, u32[]{:S(2)}, u32[]{:S(2)}) collective-permute-start(f32[144,512]{1,0:T(8,128)S(1)} %collective-permute-done.2.minus3), channel_id=1, source_target_pairs={{256,0},{272,16},{288,32},{304,48},{320,64},{336,80},{352,96},{368... | collective-permute-start | bytes 884744 | tf_op jit(solution)/shard_map/ppermute | solution.py:420
  39.9 10.9 %collective-permute-start.3 = (f32[144,512]{1,0:T(8,128)S(1)}, f32[144,512]{1,0:T(8,128)S(1)}, u32[]{:S(2)}, u32[]{:S(2)}) collective-permute-start(f32[144,512]{1,0:T(8,128)S(1)} %collective-permute-done.2.minus3), channel_id=1, source_target_pairs={{240,0},{0,16},{16,32},{32,48},{48,64},{64,80},{80,96},{96,112},{1... | collective-permute-start | bytes 884744 | tf_op jit(solution)/shard_map/ppermute | solution.py:417
  42.0 12.7 %collective-permute-start.6 = (f32[144,512]{1,0:T(8,128)S(1)}, f32[144,512]{1,0:T(8,128)S(1)}, u32[]{:S(2)}, u32[]{:S(2)}) collective-permute-start(f32[144,512]{1,0:T(8,128)S(1)} %collective-permute-done.1.plus4), channel_id=1, source_target_pairs={{256,0},{272,16},{288,32},{304,48},{320,64},{336,80},{352,96},{368... | collective-permute-start | bytes 884744 | tf_op jit(solution)/shard_map/ppermute | solution.py:420
  47.5 0.7 copy-start
  48.1 1.0 copy-start.1
  56.1 5.4 %collective-permute-start.7 = (f32[8,176,128]{2,1,0:T(8,128)S(1)}, f32[8,176,128]{2,1,0:T(8,128)S(1)}, u32[]{:S(2)}, u32[]{:S(2)}) collective-permute-start(f32[8,176,128]{2,1,0:T(8,128)S(1)} %get-tuple-element.24), channel_id=1, source_target_pairs={{0,1},{1,0},{2,3},{3,2},{4,5},{5,4},{6,7},{7,6},{8,9},{9,8},{10,11... | collective-permute-start | bytes 2162696 | tf_op jit(solution)/shard_map/ppermute | solution.py:480
  62.5 15.4 %all-to-all-start = ((f32[8,176,128]{2,1,0:T(8,128)}), f32[8,176,128]{2,1,0:T(8,128)S(1)}, u32[]{:S(2)}, u32[]{:S(2)}) async-start(f32[8,176,128]{2,1,0:T(8,128)} %shard_map.40), calls=%async_computation | async-start | bytes 1441792 | tf_op jit(solution)/shard_map/all_to_all | solution.py:489
  79.5 11.2 %collective-permute-start.8 = (f32[24,128]{1,0:T(8,128)S(1)}, f32[24,128]{1,0:T(8,128)S(1)}, u32[]{:S(2)}, u32[]{:S(2)}) collective-permute-start(f32[24,128]{1,0:T(8,128)S(1)} %get-tuple-element.25), channel_id=1, source_target_pairs={{0,464},{1,64},{2,320},{3,322},{4,38},{5,209},{6,66},{7,70},{8,294... | collective-permute-start | bytes 36872 | tf_op jit(solution)/shard_map/ppermute | solution.py:500
  88.1 8.3 %collective-permute-start.9 = (f32[24,128]{1,0:T(8,128)S(1)}, f32[24,128]{1,0:T(8,128)S(1)}, u32[]{:S(2)}, u32[]{:S(2)}) collective-permute-start(f32[24,128]{1,0:T(8,128)S(1)} %get-tuple-element.26), channel_id=1, source_target_pairs={{0,14},{1,2},{2,10},{3,74},{4,193},{5,38},{6,198},{7,210},{8,217},... | collective-permute-start | bytes 36872 | tf_op jit(solution)/shard_map/ppermute | solution.py:499

commit v10 on v9

--- a/solution.py
+++ b/solution.py
@@ -38,12 +38,16 @@
     return (1 - column) * SIDE + (z + OTHER[index - len(OWN)]) % SIDE
 
 
+def two_diagonals(z):
+    return (z + SIDE - 2) % SIDE < SIDE // 2
+
+
 def ends_of(column, z, pair):
     p, q = PAIRS[pair]
     if pair == len(PAIRS) - 1 and column == 1:
         p = 4
     a, b = frame_block(column, z, p), frame_block(column, z, q)
-    if pair == DIAGONAL and z < SIDE // 2:
+    if pair == DIAGONAL and two_diagonals(z):
         return ((a, a), (b, b))
     return ((a, b), (b, a))
 
@@ -88,7 +92,7 @@
             for device in range(SIDE):
                 pair = POSITION[2 * order.index(device // 2) + device % 2]
                 ends.append(ends_of(column, z, pair))
-                diagonal.append(int(pair == DIAGONAL and z < SIDE // 2))
+                diagonal.append(int(pair == DIAGONAL and two_diagonals(z)))
     place = lambda end: end[0] * SIDE + end[1] // 2
     at = {}
     for device, pair in enumerate(ends):
@@ -206,33 +210,33 @@
             put_pair(out, PAIRS.index(pair), core, value, row_feature[start + n] + column_feature[at])
 
 
-def first_kernel(flags, mass_ref, own, plus2, other2, other3, weighted, row_feature, centered, column_feature):
+def first_kernel(flags, mass_ref, own, plus2, other2, weighted, row_feature, centered, column_feature):
     core = flags[2]
     mass = mass_ref[...].astype(jnp.float32)
     stage_rows(own, mass, STACK.index(0), core, weighted, row_feature)
-    for at, block in enumerate((plus2, other2, other3)):
+    for at, block in enumerate((plus2, other2)):
         stage_columns(block, mass, at, core, centered, column_feature)
 
 
 def early_kernel(
-    flags, mass_ref, plus4, minus3, minus4, first_centered, first_feature, _, __,
+    flags, mass_ref, other3, plus4, minus3, minus4, first_centered, first_feature, _, __,
     out, weighted, row_feature, centered, column_feature,
 ):
     core = flags[2]
     mass = mass_ref[...].astype(jnp.float32)
-    order = (2, 3)
-    for at, block in enumerate((plus4, minus3)):
+    order = (2, 3, 7)
+    for at, block in enumerate((plus4, minus3, other3)):
         stage_columns(block, mass, at, core, centered, column_feature)
     for at, block in ((0, minus3), (2, minus4), (3, plus4)):
         stage_rows(block, mass, at, core, weighted, row_feature)
-    put_groups(out, EARLY, (1, 5, 7), core, weighted, first_centered, row_feature, first_feature)
+    put_groups(out, EARLY, (1, 5), core, weighted, first_centered, row_feature, first_feature)
     put_groups(out, EARLY, order, core, weighted, centered, row_feature, column_feature)
 
     @pl.when(flags[1] == 1)
     def _():
-        stage_columns(minus4, mass, 2, core, centered, column_feature)
+        stage_columns(minus4, mass, 3, core, centered, column_feature)
         p, q, last = STACK.index(4), STACK.index(2), order.index(2)
-        upper = product(weighted[p * 3 * ROWS : (p + 1) * 3 * ROWS], centered[2])
+        upper = product(weighted[p * 3 * ROWS : (p + 1) * 3 * ROWS], centered[3])
         lower = product(weighted[q * 3 * ROWS : (q + 1) * 3 * ROWS], centered[last])
         i, j = iota((3 * ROWS, 256), 0) % ROWS, iota((3 * ROWS, 256), 1) % ROWS
         at = iota((ROWS, 256), 1)
@@ -405,7 +409,7 @@
 def on_device(coords, weights):
     orders, first, second, table = routes()
     frame, atom = lax.axis_index("frame"), lax.axis_index("atom")
-    build_flags = jnp.stack([frame // SIDE, 1 - (frame % SIDE) // (SIDE // 2), atom % 2]).astype(jnp.int32)
+    build_flags = jnp.stack([frame // SIDE, two_diagonals(frame % SIDE), atom % 2]).astype(jnp.int32)
     mine = jnp.asarray(np.array(table), jnp.int32)[frame * SIDE + atom]
     fit_flags = jnp.stack([mine & 1, mine >> 2])
     mass = weights[None, :]
@@ -447,27 +451,27 @@
         jax.ShapeDtypeStruct((len(STACK), ROWS, 128), jnp.float32),
     ]
     columns = [
-        jax.ShapeDtypeStruct((3, 256, 3 * atoms), jnp.bfloat16),
-        jax.ShapeDtypeStruct((3, ROWS, 128), jnp.float32),
+        jax.ShapeDtypeStruct((2, 256, 3 * atoms), jnp.bfloat16),
+        jax.ShapeDtypeStruct((2, ROWS, 128), jnp.float32),
     ]
     weighted, row_feature, centered, column_feature = pl.pallas_call(
         first_kernel,
         out_shape=staged + columns,
-        in_specs=[smem] + [vmem] * 5,
+        in_specs=[smem] + [vmem] * 4,
         out_specs=[vmem] * 4,
         compiler_params=params,
         cost_estimate=cost(len(EARLY)),
-    )(build_flags, mass, own, plus2, other2, other3)
+    )(build_flags, mass, own, plus2, other2)
     sums, weighted, row_feature = pl.pallas_call(
         early_kernel,
         out_shape=[sums_of(2 * CHIPS)] + staged,
-        in_specs=[smem] + [vmem] * 8,
+        in_specs=[smem] + [vmem] * 9,
         out_specs=[vmem] * 3,
-        scratch_shapes=columns_scratch(3),
-        input_output_aliases={7: 1, 8: 2},
+        scratch_shapes=columns_scratch(4),
+        input_output_aliases={8: 1, 9: 2},
         compiler_params=params,
         cost_estimate=cost(len(EARLY) + 1),
-    )(build_flags, mass, plus4, minus3, minus4, centered, column_feature, weighted, row_feature)
+    )(build_flags, mass, other3, plus4, minus3, minus4, centered, column_feature, weighted, row_feature)
     send, keep = pl.pallas_call(
         late_kernel,
         out_shape=[sums_of(CHIPS), sums_of(1)],

time: 98.9 us -> 98.5 us (level)
  Pallas kernels: 8.92 us -> 7.92 us
    ppermute x4, waiting for transfers between devices: 16 us -> 18.7 us  [along(): return lax.ppermute(block, 'frame', route)]
    ppermute x3, waiting for transfers between devices: 2.62 us -> 0.04 us  [across(): lax.ppermute(block, 'frame', [((f + SIDE) % (2 * SIDE), f) for f in range...]
  transfers between devices with their start and end apart: 11 -> 11, of which waited for: 7 -> 6; matrix products, arithmetic and copies ran while one was open for 1% -> 1% of each run, Pallas kernels for 5% -> 4%
where the time goes in v10:
time: 98.5 us; the launch traced here: 96.9 us
  starting transfers between devices  49.3 us (50%)
  waiting for transfers between devices  33.7 us (34%)
  Pallas kernels  7.92 us (8%)
  local copies, waits for them, and re-layouts  2.98 us (3%)
  between operations  2.13 us (2%)
    ppermute x4, starting transfers between devices, along(): return lax.ppermute(block, 'frame', route)  21.5 us
    ppermute x4, waiting for transfers between devices, along(): return lax.ppermute(block, 'frame', route)  18.7 us
    ppermute x1, starting transfers between devices, on_device(): two = lax.ppermute(two, ('frame', 'atom'), list(enumerate(second)))  9.47 us
    ppermute x3, starting transfers between devices, across(): lax.ppermute(block, 'frame', [((f + SIDE) % (2 * SIDE), f) for f in range...  7.72 us
    all_to_all x1, waiting for transfers between devices, on_device(): lax.all_to_all(merged, ('frame', 'atom'), 0, 0, axis_index_groups=groups,...  7.37 us
    ppermute x1, waiting for transfers between devices, on_device(): one = lax.ppermute(one, ('frame', 'atom'), list(enumerate(first)))  5.76 us
    all_to_all x1, starting transfers between devices, on_device(): lax.all_to_all(merged, ('frame', 'atom'), 0, 0, axis_index_groups=groups,...  5.13 us
    ppermute x1, starting transfers between devices, on_device(): taken = lax.ppermute(send, 'atom', [(a, a ^ 1) for a in range(SIDE)])  3.54 us
  transfers between devices with their start and end apart: 11, of which 6 were waited for; matrix products, arithmetic and copies ran while one was open for 1% of the time, Pallas kernels for 4%

profile of v10, /device:TPU:7, one launch (start us, length us, event | category | flops | bytes accessed | tf_op | source)
XLA Modules:
  0.0 96.9 jit_solution(12367714391987042421)
XLA Ops:
  0.0 11.6 %collective-permute-start.2 = (f32[144,512]{1,0:T(8,128)}, f32[144,512]{1,0:T(8,128)S(1)}, u32[]{:S(2)}, u32[]{:S(2)}) collective-permute-start(f32[144,512]{1,0:T(8,128)} %bitcast.9), channel_id=1, source_target_pairs={{32,0},{48,16},{64,32},{80,48},{96,64},{112,80},{128,96},{144,112}... | collective-permute-start | bytes 884744 | tf_op jit(solution)/shard_map/ppermute | solution.py:421
  11.6 1.9 %collective-permute-start = (f32[144,512]{1,0:T(8,128)}, f32[144,512]{1,0:T(8,128)S(1)}, u32[]{:S(2)}, u32[]{:S(2)}) collective-permute-start(f32[144,512]{1,0:T(8,128)} %bitcast.10), channel_id=1, source_target_pairs={{208,0},{224,16},{240,32},{0,48},{16,64},{32,80},{48,96},{64,112},... | collective-permute-start | bytes 884744 | tf_op jit(solution)/shard_map/ppermute | solution.py:421
  13.5 10.4 %collective-permute-done.2.plus2 = f32[144,512]{1,0:T(8,128)S(1)} collective-permute-done((f32[144,512]{1,0:T(8,128)}, f32[144,512]{1,0:T(8,128)S(1)}, u32[]{:S(2)}, u32[]{:S(2)}) %collective-permute-start.2) | collective-permute-done | bytes 294944 | tf_op jit(solution)/shard_map/ppermute | solution.py:421
  23.9 6.1 %collective-permute-start.3 = (f32[144,512]{1,0:T(8,128)S(1)}, f32[144,512]{1,0:T(8,128)S(1)}, u32[]{:S(2)}, u32[]{:S(2)}) collective-permute-start(f32[144,512]{1,0:T(8,128)S(1)} %collective-permute-done.2.plus2), channel_id=1, source_target_pairs={{32,0},{48,16},{64,32},{80,48},{96,64},{112,80},{128,96},{144,112}... | collective-permute-start | bytes 884744 | tf_op jit(solution)/shard_map/ppermute | solution.py:421
  30.0 2.5 %collective-permute-start.5 = (f32[144,512]{1,0:T(8,128)S(1)}, f32[144,512]{1,0:T(8,128)S(1)}, u32[]{:S(2)}, u32[]{:S(2)}) collective-permute-start(f32[144,512]{1,0:T(8,128)S(1)} %collective-permute-done.2.plus2), channel_id=1, source_target_pairs={{256,0},{272,16},{288,32},{304,48},{320,64},{336,80},{352,96},{368... | collective-permute-start | bytes 884744 | tf_op jit(solution)/shard_map/ppermute | solution.py:424
  32.5 5.0 %collective-permute-done.minus3 = f32[144,512]{1,0:T(8,128)S(1)} collective-permute-done((f32[144,512]{1,0:T(8,128)}, f32[144,512]{1,0:T(8,128)S(1)}, u32[]{:S(2)}, u32[]{:S(2)}) %collective-permute-start) | collective-permute-done | bytes 294944 | tf_op jit(solution)/shard_map/ppermute | solution.py:421
  37.5 2.4 %collective-permute-start.1 = (f32[144,512]{1,0:T(8,128)S(1)}, f32[144,512]{1,0:T(8,128)S(1)}, u32[]{:S(2)}, u32[]{:S(2)}) collective-permute-start(f32[144,512]{1,0:T(8,128)S(1)} %collective-permute-done.minus3), channel_id=1, source_target_pairs={{256,0},{272,16},{288,32},{304,48},{320,64},{336,80},{352,96},{368... | collective-permute-start | bytes 884744 | tf_op jit(solution)/shard_map/ppermute | solution.py:424
  39.9 1.9 %collective-permute-start.4 = (f32[144,512]{1,0:T(8,128)S(1)}, f32[144,512]{1,0:T(8,128)S(1)}, u32[]{:S(2)}, u32[]{:S(2)}) collective-permute-start(f32[144,512]{1,0:T(8,128)S(1)} %collective-permute-done.minus3), channel_id=1, source_target_pairs={{240,0},{0,16},{16,32},{32,48},{48,64},{64,80},{80,96},{96,112},{1... | collective-permute-start | bytes 884744 | tf_op jit(solution)/shard_map/ppermute | solution.py:421
  41.9 0.1 pad_add_fusion.1.flags
  42.0 0.0 collective-permute-done.3.plus4
  42.0 2.8 %collective-permute-start.6 = (f32[144,512]{1,0:T(8,128)S(1)}, f32[144,512]{1,0:T(8,128)S(1)}, u32[]{:S(2)}, u32[]{:S(2)}) collective-permute-start(f32[144,512]{1,0:T(8,128)S(1)} %collective-permute-done.3.plus4), channel_id=1, source_target_pairs={{256,0},{272,16},{288,32},{304,48},{320,64},{336,80},{352,96},{368... | collective-permute-start | bytes 884744 | tf_op jit(solution)/shard_map/ppermute | solution.py:424
  44.8 0.0 collective-permute-done.5.other2
  44.8 0.0 copy-start
  44.8 0.7 copy-done
  45.5 0.0 copy-start.1
  45.5 1.0 copy-done.1
  46.5 1.0 %shard_map.37 = (bf16[576,1536]{1,0:T(8,128)(2,1)S(1)}, f32[4,48,128]{2,1,0:T(8,128)S(1)}, bf16[2,256,1536]{2,1,0:T(8,128)(2,1)S(1)}, f32[2,48,128]{2,1,0:T(8,128)S(1)}) custom-call(s32[3]{0:T(128)S(1)} %pad_add_fusion.1.flags, s32[1,512]{1,0:T(1,128)S(1)} %bitcast.6, f32[144,512]{1,0:T(8,128)S(1)} %bitcast.11, f32[144,512]{1,0:T(8,128)S(1)} %collective-permute-done.2.plus2, ...), custom_call_target="tpu_custom_call" | custom-call | flops 1585446912 | bytes 4000000 | tf_op jit(solution)/shard_map/pallas_call | solution.py:457
  47.5 0.0 collective-permute-done.1.other3
  47.5 3.3 %collective-permute-done.4.minus4 = f32[144,512]{1,0:T(8,128)S(1)} collective-permute-done((f32[144,512]{1,0:T(8,128)S(1)}, f32[144,512]{1,0:T(8,128)S(1)}, u32[]{:S(2)}, u32[]{:S(2)}) %collective-permute-start.4) | collective-permute-done | bytes 294944 | tf_op jit(solution)/shard_map/ppermute | solution.py:421
  50.8 2.9 %shard_map.38 = (f32[16,176,128]{2,1,0:T(8,128)S(1)}, bf16[576,1536]{1,0:T(8,128)(2,1)S(1)}, f32[4,48,128]{2,1,0:T(8,128)S(1)}) custom-call(s32[3]{0:T(128)S(1)} %pad_add_fusion.1.flags, s32[1,512]{1,0:T(1,128)S(1)} %bitcast.7, f32[144,512]{1,0:T(8,128)S(1)} %collective-permute-done.1.other3, ...), custom_call_target="tpu_custom_call", output_to_operand_aliasing={{1}: (8, {}), {2}: (9, {})} | custom-call | flops 1698693120 | bytes 4000000 | tf_op jit(solution)/shard_map/pallas_call | solution.py:465
  53.7 0.0 collective-permute-done.6.other4
  53.8 1.4 %shard_map.39 = (f32[8,176,128]{2,1,0:T(8,128)S(1)}, f32[1,176,128]{2,1,0:T(8,128)S(1)}) custom-call(s32[3]{0:T(128)S(1)} %pad_add_fusion.1.flags, s32[1,512]{1,0:T(1,128)S(1)} %bitcast.8, bf16[576,1536]{1,0:T(8,128)(2,1)S(1)} %get-tuple-element.21.weighted, f32[4,48,128]{2,1,0:T(8,128)S(1)} %get-tuple-element.22.row_feature, ...), custom_call_target="tpu_custom_call" | custom-call | flops 339738624 | bytes 4000000 | tf_op jit(solution)/shard_map/pallas_call | solution.py:475
  55.2 3.5 %collective-permute-start.7 = (f32[8,176,128]{2,1,0:T(8,128)S(1)}, f32[8,176,128]{2,1,0:T(8,128)S(1)}, u32[]{:S(2)}, u32[]{:S(2)}) collective-permute-start(f32[8,176,128]{2,1,0:T(8,128)S(1)} %get-tuple-element.24), channel_id=1, source_target_pairs={{0,1},{1,0},{2,3},{3,2},{4,5},{5,4},{6,7},{7,6},{8,9},{9,8},{10,11... | collective-permute-start | bytes 2162696 | tf_op jit(solution)/shard_map/ppermute | solution.py:484
  58.8 1.8 %collective-permute-done.7.taken = f32[8,176,128]{2,1,0:T(8,128)S(1)} collective-permute-done((f32[8,176,128]{2,1,0:T(8,128)S(1)}, f32[8,176,128]{2,1,0:T(8,128)S(1)}, u32[]{:S(2)}, u32[]{:S(2)}) %collective-permute-start.7) | collective-permute-done | bytes 720928 | tf_op jit(solution)/shard_map/ppermute | solution.py:484
  60.5 1.0 %shard_map.40 = f32[8,176,128]{2,1,0:T(8,128)} custom-call(f32[16,176,128]{2,1,0:T(8,128)S(1)} %get-tuple-element.20.sums, f32[1,176,128]{2,1,0:T(8,128)S(1)} %get-tuple-element.23.keep, f32[8,176,128]{2,1,0:T(8,128)S(1)} %collective-permute-done.7.taken), custom_call_target="tpu_custom_call" | custom-call | tf_op jit(solution)/shard_map/pallas_call | solution.py:485
  61.5 5.1 %all-to-all-start = ((f32[8,176,128]{2,1,0:T(8,128)}), f32[8,176,128]{2,1,0:T(8,128)S(1)}, u32[]{:S(2)}, u32[]{:S(2)}) async-start(f32[8,176,128]{2,1,0:T(8,128)} %shard_map.40), calls=%async_computation | async-start | bytes 1441792 | tf_op jit(solution)/shard_map/all_to_all | solution.py:493
  66.7 1.3 %dynamic_slice.3 = s32[1]{0:T(128)} dynamic-slice(s32[512]{0:T(512)} %constant.70.clone, s32[]{:T(128)S(6)} %select_n.34), dynamic_slice_sizes={1} | dynamic-slice | bytes 12 | tf_op jit(solution)/shard_map/dynamic_slice | solution.py:413
  69.2 0.1 pad_add_fusion.flags
  69.3 7.4 %all-to-all-done.parts = f32[8,176,128]{2,1,0:T(8,128)S(1)} async-done(((f32[8,176,128]{2,1,0:T(8,128)}), f32[8,176,128]{2,1,0:T(8,128)S(1)}, u32[]{:S(2)}, u32[]{:S(2)}) %all-to-all-start) | async-done | bytes 720928 | tf_op jit(solution)/shard_map/all_to_all | solution.py:493
  76.7 1.6 %shard_map.41 = (f32[24,128]{1,0:T(8,128)S(1)}, f32[24,128]{1,0:T(8,128)S(1)}) custom-call(s32[2]{0:T(128)S(1)} %pad_add_fusion.flags, f32[8,176,128]{2,1,0:T(8,128)S(1)} %all-to-all-done.parts), custom_call_target="tpu_custom_call" | custom-call | tf_op jit(solution)/shard_map/pallas_call | solution.py:496
  78.3 9.5 %collective-permute-start.8 = (f32[24,128]{1,0:T(8,128)S(1)}, f32[24,128]{1,0:T(8,128)S(1)}, u32[]{:S(2)}, u32[]{:S(2)}) collective-permute-start(f32[24,128]{1,0:T(8,128)S(1)} %get-tuple-element.25), channel_id=1, source_target_pairs={{0,464},{1,64},{2,320},{3,322},{4,38},{5,209},{6,70},{7,210},{8,29... | collective-permute-start | bytes 36872 | tf_op jit(solution)/shard_map/ppermute | solution.py:504
  87.7 1.9 %collective-permute-start.9 = (f32[24,128]{1,0:T(8,128)S(1)}, f32[24,128]{1,0:T(8,128)S(1)}, u32[]{:S(2)}, u32[]{:S(2)}) collective-permute-start(f32[24,128]{1,0:T(8,128)S(1)} %get-tuple-element.26), channel_id=1, source_target_pairs={{0,14},{1,2},{2,10},{3,74},{4,193},{5,38},{6,194},{7,70},{8,217},{... | collective-permute-start | bytes 36872 | tf_op jit(solution)/shard_map/ppermute | solution.py:503
  90.3 0.0 collective-permute-done.8
  90.3 5.8 %collective-permute-done.9 = f32[24,128]{1,0:T(8,128)S(1)} collective-permute-done((f32[24,128]{1,0:T(8,128)S(1)}, f32[24,128]{1,0:T(8,128)S(1)}, u32[]{:S(2)}, u32[]{:S(2)}) %collective-permute-start.9) | collective-permute-done | bytes 12320 | tf_op jit(solution)/shard_map/ppermute | solution.py:503
  96.1 0.1 fusion
  96.2 0.7 maximum_maximum_fusion
  (1 shorter events, 0.0 us)
Async XLA Ops:
  0.0 23.9 %collective-permute-start.2 = (f32[144,512]{1,0:T(8,128)}, f32[144,512]{1,0:T(8,128)S(1)}, u32[]{:S(2)}, u32[]{:S(2)}) collective-permute-start(f32[144,512]{1,0:T(8,128)} %bitcast.9), channel_id=1, source_target_pairs={{32,0},{48,16},{64,32},{80,48},{96,64},{112,80},{128,96},{144,112}... | collective-permute-start | bytes 884744 | tf_op jit(solution)/shard_map/ppermute | solution.py:421
  11.6 25.9 %collective-permute-start = (f32[144,512]{1,0:T(8,128)}, f32[144,512]{1,0:T(8,128)S(1)}, u32[]{:S(2)}, u32[]{:S(2)}) collective-permute-start(f32[144,512]{1,0:T(8,128)} %bitcast.10), channel_id=1, source_target_pairs={{208,0},{224,16},{240,32},{0,48},{16,64},{32,80},{48,96},{64,112},... | collective-permute-start | bytes 884744 | tf_op jit(solution)/shard_map/ppermute | solution.py:421
  23.9 18.1 %collective-permute-start.3 = (f32[144,512]{1,0:T(8,128)S(1)}, f32[144,512]{1,0:T(8,128)S(1)}, u32[]{:S(2)}, u32[]{:S(2)}) collective-permute-start(f32[144,512]{1,0:T(8,128)S(1)} %collective-permute-done.2.plus2), channel_id=1, source_target_pairs={{32,0},{48,16},{64,32},{80,48},{96,64},{112,80},{128,96},{144,112}... | collective-permute-start | bytes 884744 | tf_op jit(solution)/shard_map/ppermute | solution.py:421
  30.0 14.8 %collective-permute-start.5 = (f32[144,512]{1,0:T(8,128)S(1)}, f32[144,512]{1,0:T(8,128)S(1)}, u32[]{:S(2)}, u32[]{:S(2)}) collective-permute-start(f32[144,512]{1,0:T(8,128)S(1)} %collective-permute-done.2.plus2), channel_id=1, source_target_pairs={{256,0},{272,16},{288,32},{304,48},{320,64},{336,80},{352,96},{368... | collective-permute-start | bytes 884744 | tf_op jit(solution)/shard_map/ppermute | solution.py:424
  37.5 10.0 %collective-permute-start.1 = (f32[144,512]{1,0:T(8,128)S(1)}, f32[144,512]{1,0:T(8,128)S(1)}, u32[]{:S(2)}, u32[]{:S(2)}) collective-permute-start(f32[144,512]{1,0:T(8,128)S(1)} %collective-permute-done.minus3), channel_id=1, source_target_pairs={{256,0},{272,16},{288,32},{304,48},{320,64},{336,80},{352,96},{368... | collective-permute-start | bytes 884744 | tf_op jit(solution)/shard_map/ppermute | solution.py:424
  39.9 10.9 %collective-permute-start.4 = (f32[144,512]{1,0:T(8,128)S(1)}, f32[144,512]{1,0:T(8,128)S(1)}, u32[]{:S(2)}, u32[]{:S(2)}) collective-permute-start(f32[144,512]{1,0:T(8,128)S(1)} %collective-permute-done.minus3), channel_id=1, source_target_pairs={{240,0},{0,16},{16,32},{32,48},{48,64},{64,80},{80,96},{96,112},{1... | collective-permute-start | bytes 884744 | tf_op jit(solution)/shard_map/ppermute | solution.py:421
  42.0 11.8 %collective-permute-start.6 = (f32[144,512]{1,0:T(8,128)S(1)}, f32[144,512]{1,0:T(8,128)S(1)}, u32[]{:S(2)}, u32[]{:S(2)}) collective-permute-start(f32[144,512]{1,0:T(8,128)S(1)} %collective-permute-done.3.plus4), channel_id=1, source_target_pairs={{256,0},{272,16},{288,32},{304,48},{320,64},{336,80},{352,96},{368... | collective-permute-start | bytes 884744 | tf_op jit(solution)/shard_map/ppermute | solution.py:424
  44.8 0.7 copy-start
  45.5 1.0 copy-start.1
  55.2 5.3 %collective-permute-start.7 = (f32[8,176,128]{2,1,0:T(8,128)S(1)}, f32[8,176,128]{2,1,0:T(8,128)S(1)}, u32[]{:S(2)}, u32[]{:S(2)}) collective-permute-start(f32[8,176,128]{2,1,0:T(8,128)S(1)} %get-tuple-element.24), channel_id=1, source_target_pairs={{0,1},{1,0},{2,3},{3,2},{4,5},{5,4},{6,7},{7,6},{8,9},{9,8},{10,11... | collective-permute-start | bytes 2162696 | tf_op jit(solution)/shard_map/ppermute | solution.py:484
  61.5 15.1 %all-to-all-start = ((f32[8,176,128]{2,1,0:T(8,128)}), f32[8,176,128]{2,1,0:T(8,128)S(1)}, u32[]{:S(2)}, u32[]{:S(2)}) async-start(f32[8,176,128]{2,1,0:T(8,128)} %shard_map.40), calls=%async_computation | async-start | bytes 1441792 | tf_op jit(solution)/shard_map/all_to_all | solution.py:493
  78.3 12.1 %collective-permute-start.8 = (f32[24,128]{1,0:T(8,128)S(1)}, f32[24,128]{1,0:T(8,128)S(1)}, u32[]{:S(2)}, u32[]{:S(2)}) collective-permute-start(f32[24,128]{1,0:T(8,128)S(1)} %get-tuple-element.25), channel_id=1, source_target_pairs={{0,464},{1,64},{2,320},{3,322},{4,38},{5,209},{6,70},{7,210},{8,29... | collective-permute-start | bytes 36872 | tf_op jit(solution)/shard_map/ppermute | solution.py:504
  87.7 8.3 %collective-permute-start.9 = (f32[24,128]{1,0:T(8,128)S(1)}, f32[24,128]{1,0:T(8,128)S(1)}, u32[]{:S(2)}, u32[]{:S(2)}) collective-permute-start(f32[24,128]{1,0:T(8,128)S(1)} %get-tuple-element.26), channel_id=1, source_target_pairs={{0,14},{1,2},{2,10},{3,74},{4,193},{5,38},{6,194},{7,70},{8,217},{... | collective-permute-start | bytes 36872 | tf_op jit(solution)/shard_map/ppermute | solution.py:503

commit v11 on v10

--- a/solution.py
+++ b/solution.py
@@ -16,18 +16,19 @@
 
 OWN = (0, 2, 4, -3, -4)
 OTHER = (2, 4, -3)
-STACK = (3, 0, 4, 2)
+STACK = (3, 0, 2, 4)
 EARLY = (
-    (3, 1), (0, 1), (4, 1),
-    (3, 2), (0, 2), (4, 2),
-    (0, 3), (4, 3),
-    (3, 5), (0, 5), (4, 5),
-    (0, 7), (4, 7), (2, 7),
+    (3, 1), (0, 1),
+    (3, 2), (0, 2),
+    (0, 3),
+    (3, 5), (0, 5),
+    (0, 7), (2, 7),
 )
+NEXT = ((4, 1), (4, 2), (4, 3), (4, 5), (4, 7))
 LATE = ((0, 6), (2, 6))
-PAIRS = EARLY + LATE
+PAIRS = EARLY + NEXT + LATE
 DIAGONAL = PAIRS.index((4, 2))
-POSITION = (13, 9, 5, 3, 8, 10, 11, 4, 12, 7, 2, 0, 6, 1, 14, 15)
+POSITION = (8, 6, 10, 2, 5, 12, 7, 3, 13, 11, 9, 0, 4, 1, 14, 15)
 CHIPS = SIDE // 2
 SUM_ROWS = 3 * ROWS + 32
 
@@ -219,24 +220,34 @@
 
 
 def early_kernel(
-    flags, mass_ref, other3, plus4, minus3, minus4, first_centered, first_feature, _, __,
+    flags, mass_ref, other3, plus4, minus3, first_centered, first_feature, _, __,
     out, weighted, row_feature, centered, column_feature,
 ):
     core = flags[2]
     mass = mass_ref[...].astype(jnp.float32)
-    order = (2, 3, 7)
     for at, block in enumerate((plus4, minus3, other3)):
         stage_columns(block, mass, at, core, centered, column_feature)
-    for at, block in ((0, minus3), (2, minus4), (3, plus4)):
-        stage_rows(block, mass, at, core, weighted, row_feature)
+    for k, block in ((3, minus3), (2, plus4)):
+        stage_rows(block, mass, STACK.index(k), core, weighted, row_feature)
     put_groups(out, EARLY, (1, 5), core, weighted, first_centered, row_feature, first_feature)
-    put_groups(out, EARLY, order, core, weighted, centered, row_feature, column_feature)
+    put_groups(out, EARLY, (2, 3, 7), core, weighted, centered, row_feature, column_feature)
+
+
+def next_kernel(
+    flags, mass_ref, minus4, first_centered, first_feature, centered, column_feature, _, __, ___,
+    out, weighted, row_feature, own_centered, own_feature,
+):
+    core = flags[2]
+    mass = mass_ref[...].astype(jnp.float32)
+    stage_rows(minus4, mass, STACK.index(4), core, weighted, row_feature)
+    put_groups(out, NEXT, (1, 5), core, weighted, first_centered, row_feature, first_feature)
+    put_groups(out, NEXT, (2, 3, 7), core, weighted, centered, row_feature, column_feature)
 
     @pl.when(flags[1] == 1)
     def _():
-        stage_columns(minus4, mass, 3, core, centered, column_feature)
-        p, q, last = STACK.index(4), STACK.index(2), order.index(2)
-        upper = product(weighted[p * 3 * ROWS : (p + 1) * 3 * ROWS], centered[3])
+        stage_columns(minus4, mass, 0, core, own_centered, own_feature)
+        p, q, last = STACK.index(4), STACK.index(2), 0
+        upper = product(weighted[p * 3 * ROWS : (p + 1) * 3 * ROWS], own_centered[0])
         lower = product(weighted[q * 3 * ROWS : (q + 1) * 3 * ROWS], centered[last])
         i, j = iota((3 * ROWS, 256), 0) % ROWS, iota((3 * ROWS, 256), 1) % ROWS
         at = iota((ROWS, 256), 1)
@@ -259,8 +270,8 @@
     values = product(weighted[3 * ROWS :], centered[0])
     other = flags[0] == 1
     for n in range(2):
-        rows = values[: 3 * ROWS] if n == 0 else jnp.where(other, values[3 * ROWS : 6 * ROWS], values[6 * ROWS :])
-        feature = row_feature[1] if n == 0 else jnp.where(other, row_feature[2], row_feature[3])
+        rows = values[: 3 * ROWS] if n == 0 else jnp.where(other, values[6 * ROWS :], values[3 * ROWS : 6 * ROWS])
+        feature = row_feature[1] if n == 0 else jnp.where(other, row_feature[3], row_feature[2])
         at = jnp.where(core == n, 0, 1)
         last[at, : 3 * ROWS] = rows[:, :128]
         last[at, 3 * ROWS :] = packed(rest_of(rows[:, 128:]) + feature + column_feature[0])
@@ -462,16 +473,31 @@
         compiler_params=params,
         cost_estimate=cost(len(EARLY)),
     )(build_flags, mass, own, plus2, other2)
+    more = [
+        jax.ShapeDtypeStruct((3, 256, 3 * atoms), jnp.bfloat16),
+        jax.ShapeDtypeStruct((3, ROWS, 128), jnp.float32),
+    ]
+    sums, weighted, row_feature, more_centered, more_feature = pl.pallas_call(
+        early_kernel,
+        out_shape=[sums_of(2 * CHIPS)] + staged + more,
+        in_specs=[smem] + [vmem] * 8,
+        out_specs=[vmem] * 5,
+        input_output_aliases={7: 1, 8: 2},
+        compiler_params=params,
+        cost_estimate=cost(len(EARLY)),
+    )(build_flags, mass, other3, plus4, minus3, centered, column_feature, weighted, row_feature)
     sums, weighted, row_feature = pl.pallas_call(
-        early_kernel,
+        next_kernel,
         out_shape=[sums_of(2 * CHIPS)] + staged,
         in_specs=[smem] + [vmem] * 9,
         out_specs=[vmem] * 3,
-        scratch_shapes=columns_scratch(4),
-        input_output_aliases={8: 1, 9: 2},
+        scratch_shapes=columns_scratch(1),
+        input_output_aliases={7: 0, 8: 1, 9: 2},
         compiler_params=params,
-        cost_estimate=cost(len(EARLY) + 1),
-    )(build_flags, mass, other3, plus4, minus3, minus4, centered, column_feature, weighted, row_feature)
+        cost_estimate=cost(len(NEXT) + 1),
+    )(
+        build_flags, mass, minus4, centered, column_feature, more_centered, more_feature, sums, weighted, row_feature
+    )
     send, keep = pl.pallas_call(
         late_kernel,
         out_shape=[sums_of(CHIPS), sums_of(1)],

time: 98.5 us -> 98.5 us (level)
  waiting for transfers between devices: 33.7 us -> 32.1 us
  Pallas kernels: 7.92 us -> 9.51 us
    ppermute x4, waiting for transfers between devices: 18.7 us -> 16.4 us  [along(): return lax.ppermute(block, 'frame', route)]
    pallas_call x1 -> x2, Pallas kernels: 2.93 us -> 4.54 us  [the longest x1 2.36 us: on_device(): pl.pallas_call(early_kernel, out_shape=[sums_of(2 * CHIPS)] + staged + mo...]
  transfers between devices with their start and end apart: 11 -> 11, of which waited for: 6 -> 7; matrix products, arithmetic and copies ran while one was open for 1% -> 1% of each run, Pallas kernels for 4% -> 6%
where the time goes in v11:
time: 98.5 us; the launch traced here: 96.8 us
  starting transfers between devices  49.3 us (50%)
  waiting for transfers between devices  32.1 us (33%)
  Pallas kernels  9.51 us (10%)
  local copies, waits for them, and re-layouts  2.98 us (3%)
  between operations  2.12 us (2%)
    ppermute x4, starting transfers between devices, along(): return lax.ppermute(block, 'frame', route)  21.5 us
    ppermute x4, waiting for transfers between devices, along(): return lax.ppermute(block, 'frame', route)  16.4 us
    ppermute x1, starting transfers between devices, on_device(): two = lax.ppermute(two, ('frame', 'atom'), list(enumerate(second)))  9.48 us
    ppermute x3, starting transfers between devices, across(): lax.ppermute(block, 'frame', [((f + SIDE) % (2 * SIDE), f) for f in range...  7.73 us
    all_to_all x1, waiting for transfers between devices, on_device(): lax.all_to_all(merged, ('frame', 'atom'), 0, 0, axis_index_groups=groups,...  7.37 us
    ppermute x1, waiting for transfers between devices, on_device(): one = lax.ppermute(one, ('frame', 'atom'), list(enumerate(first)))  5.76 us
    all_to_all x1, starting transfers between devices, on_device(): lax.all_to_all(merged, ('frame', 'atom'), 0, 0, axis_index_groups=groups,...  5.43 us
    ppermute x1, starting transfers between devices, on_device(): taken = lax.ppermute(send, 'atom', [(a, a ^ 1) for a in range(SIDE)])  3.24 us
  transfers between devices with their start and end apart: 11, of which 7 were waited for; matrix products, arithmetic and copies ran while one was open for 1% of the time, Pallas kernels for 6%

profile of v11, /device:TPU:7, one launch (start us, length us, event | category | flops | bytes accessed | tf_op | source)
XLA Modules:
  0.0 96.8 jit_solution(12490092970652577025)
XLA Ops:
  0.0 11.6 %collective-permute-start.2 = (f32[144,512]{1,0:T(8,128)}, f32[144,512]{1,0:T(8,128)S(1)}, u32[]{:S(2)}, u32[]{:S(2)}) collective-permute-start(f32[144,512]{1,0:T(8,128)} %bitcast.10), channel_id=1, source_target_pairs={{32,0},{48,16},{64,32},{80,48},{96,64},{112,80},{128,96},{144,112}... | collective-permute-start | bytes 884744 | tf_op jit(solution)/shard_map/ppermute | solution.py:432
  11.6 1.9 %collective-permute-start = (f32[144,512]{1,0:T(8,128)}, f32[144,512]{1,0:T(8,128)S(1)}, u32[]{:S(2)}, u32[]{:S(2)}) collective-permute-start(f32[144,512]{1,0:T(8,128)} %bitcast.11), channel_id=1, source_target_pairs={{208,0},{224,16},{240,32},{0,48},{16,64},{32,80},{48,96},{64,112},... | collective-permute-start | bytes 884744 | tf_op jit(solution)/shard_map/ppermute | solution.py:432
  13.5 10.4 %collective-permute-done.2.plus2 = f32[144,512]{1,0:T(8,128)S(1)} collective-permute-done((f32[144,512]{1,0:T(8,128)}, f32[144,512]{1,0:T(8,128)S(1)}, u32[]{:S(2)}, u32[]{:S(2)}) %collective-permute-start.2) | collective-permute-done | bytes 294944 | tf_op jit(solution)/shard_map/ppermute | solution.py:432
  23.9 6.1 %collective-permute-start.5 = (f32[144,512]{1,0:T(8,128)S(1)}, f32[144,512]{1,0:T(8,128)S(1)}, u32[]{:S(2)}, u32[]{:S(2)}) collective-permute-start(f32[144,512]{1,0:T(8,128)S(1)} %collective-permute-done.2.plus2), channel_id=1, source_target_pairs={{32,0},{48,16},{64,32},{80,48},{96,64},{112,80},{128,96},{144,112}... | collective-permute-start | bytes 884744 | tf_op jit(solution)/shard_map/ppermute | solution.py:432
  30.0 2.5 %collective-permute-start.3 = (f32[144,512]{1,0:T(8,128)S(1)}, f32[144,512]{1,0:T(8,128)S(1)}, u32[]{:S(2)}, u32[]{:S(2)}) collective-permute-start(f32[144,512]{1,0:T(8,128)S(1)} %collective-permute-done.2.plus2), channel_id=1, source_target_pairs={{256,0},{272,16},{288,32},{304,48},{320,64},{336,80},{352,96},{368... | collective-permute-start | bytes 884744 | tf_op jit(solution)/shard_map/ppermute | solution.py:435
  32.5 5.0 %collective-permute-done.minus3 = f32[144,512]{1,0:T(8,128)S(1)} collective-permute-done((f32[144,512]{1,0:T(8,128)}, f32[144,512]{1,0:T(8,128)S(1)}, u32[]{:S(2)}, u32[]{:S(2)}) %collective-permute-start) | collective-permute-done | bytes 294944 | tf_op jit(solution)/shard_map/ppermute | solution.py:432
  37.5 2.4 %collective-permute-start.4 = (f32[144,512]{1,0:T(8,128)S(1)}, f32[144,512]{1,0:T(8,128)S(1)}, u32[]{:S(2)}, u32[]{:S(2)}) collective-permute-start(f32[144,512]{1,0:T(8,128)S(1)} %collective-permute-done.minus3), channel_id=1, source_target_pairs={{256,0},{272,16},{288,32},{304,48},{320,64},{336,80},{352,96},{368... | collective-permute-start | bytes 884744 | tf_op jit(solution)/shard_map/ppermute | solution.py:435
  40.0 1.9 %collective-permute-start.1 = (f32[144,512]{1,0:T(8,128)S(1)}, f32[144,512]{1,0:T(8,128)S(1)}, u32[]{:S(2)}, u32[]{:S(2)}) collective-permute-start(f32[144,512]{1,0:T(8,128)S(1)} %collective-permute-done.minus3), channel_id=1, source_target_pairs={{240,0},{0,16},{16,32},{32,48},{48,64},{64,80},{80,96},{96,112},{1... | collective-permute-start | bytes 884744 | tf_op jit(solution)/shard_map/ppermute | solution.py:432
  41.9 0.0 collective-permute-done.5.plus4
  41.9 2.8 %collective-permute-start.6 = (f32[144,512]{1,0:T(8,128)S(1)}, f32[144,512]{1,0:T(8,128)S(1)}, u32[]{:S(2)}, u32[]{:S(2)}) collective-permute-start(f32[144,512]{1,0:T(8,128)S(1)} %collective-permute-done.5.plus4), channel_id=1, source_target_pairs={{256,0},{272,16},{288,32},{304,48},{320,64},{336,80},{352,96},{368... | collective-permute-start | bytes 884744 | tf_op jit(solution)/shard_map/ppermute | solution.py:435
  44.8 0.1 pad_add_fusion.1.flags
  44.8 0.0 collective-permute-done.3.other2
  44.8 0.0 copy-start
  44.8 0.7 copy-done
  45.5 0.0 copy-start.1
  45.5 1.0 copy-done.1
  46.5 1.0 %shard_map.37 = (bf16[576,1536]{1,0:T(8,128)(2,1)S(1)}, f32[4,48,128]{2,1,0:T(8,128)S(1)}, bf16[2,256,1536]{2,1,0:T(8,128)(2,1)S(1)}, f32[2,48,128]{2,1,0:T(8,128)S(1)}) custom-call(s32[3]{0:T(128)S(1)} %pad_add_fusion.1.flags, s32[1,512]{1,0:T(1,128)S(1)} %bitcast.6, f32[144,512]{1,0:T(8,128)S(1)} %bitcast.12, f32[144,512]{1,0:T(8,128)S(1)} %collective-permute-done.2.plus2, ...), custom_call_target="tpu_custom_call" | custom-call | flops 1019215872 | bytes 4000000 | tf_op jit(solution)/shard_map/pallas_call | solution.py:468
  47.5 0.0 collective-permute-done.4.other3
  47.5 2.4 %shard_map.38 = (f32[16,176,128]{2,1,0:T(8,128)S(1)}, bf16[576,1536]{1,0:T(8,128)(2,1)S(1)}, f32[4,48,128]{2,1,0:T(8,128)S(1)}, bf16[3,256,1536]{2,1,0:T(8,128)(2,1)S(1)}, f32[3,48,128]{2,1,0:T(8,128)S(1)}) custom-call(s32[3]{0:T(128)S(1)} %pad_add_fusion.1.flags, s32[1,512]{1,0:T(1,128)S(1)} %bitcast.7, ...), custom_call_target="tpu_custom_call", output_to_operand_aliasing={{1}: (7, {}), {2}: (8, {})} | custom-call | flops 1019215872 | bytes 4000000 | tf_op jit(solution)/shard_map/pallas_call | solution.py:480
  49.9 1.0 %collective-permute-done.1.minus4 = f32[144,512]{1,0:T(8,128)S(1)} collective-permute-done((f32[144,512]{1,0:T(8,128)S(1)}, f32[144,512]{1,0:T(8,128)S(1)}, u32[]{:S(2)}, u32[]{:S(2)}) %collective-permute-start.1) | collective-permute-done | bytes 294944 | tf_op jit(solution)/shard_map/ppermute | solution.py:432
  50.9 2.2 %shard_map.39 = (f32[16,176,128]{2,1,0:T(8,128)S(1)}, bf16[576,1536]{1,0:T(8,128)(2,1)S(1)}, f32[4,48,128]{2,1,0:T(8,128)S(1)}) custom-call(s32[3]{0:T(128)S(1)} %pad_add_fusion.1.flags, s32[1,512]{1,0:T(1,128)S(1)} %bitcast.8, f32[144,512]{1,0:T(8,128)S(1)} %collective-permute-done.1.minus4, ...), custom_call_target="tpu_custom_call", output_to_operand_aliasing={{0}: (7, {}), {1}: (8, {}), {2}: (9, {})} | custom-call | flops 679477248 | bytes 4000000 | tf_op jit(solution)/shard_map/pallas_call | solution.py:489
  53.0 0.7 collective-permute-done.6.other4
  53.8 1.4 %shard_map.40 = (f32[8,176,128]{2,1,0:T(8,128)S(1)}, f32[1,176,128]{2,1,0:T(8,128)S(1)}) custom-call(s32[3]{0:T(128)S(1)} %pad_add_fusion.1.flags, s32[1,512]{1,0:T(1,128)S(1)} %bitcast.9, bf16[576,1536]{1,0:T(8,128)(2,1)S(1)} %get-tuple-element.31.weighted, f32[4,48,128]{2,1,0:T(8,128)S(1)} %get-tuple-element.32.row_feature, ...), custom_call_target="tpu_custom_call" | custom-call | flops 339738624 | bytes 4000000 | tf_op jit(solution)/shard_map/pallas_call | solution.py:501
  55.2 3.2 %collective-permute-start.7 = (f32[8,176,128]{2,1,0:T(8,128)S(1)}, f32[8,176,128]{2,1,0:T(8,128)S(1)}, u32[]{:S(2)}, u32[]{:S(2)}) collective-permute-start(f32[8,176,128]{2,1,0:T(8,128)S(1)} %get-tuple-element.34), channel_id=1, source_target_pairs={{0,1},{1,0},{2,3},{3,2},{4,5},{5,4},{6,7},{7,6},{8,9},{9,8},{10,11... | collective-permute-start | bytes 2162696 | tf_op jit(solution)/shard_map/ppermute | solution.py:510
  58.5 1.8 %collective-permute-done.7.taken = f32[8,176,128]{2,1,0:T(8,128)S(1)} collective-permute-done((f32[8,176,128]{2,1,0:T(8,128)S(1)}, f32[8,176,128]{2,1,0:T(8,128)S(1)}, u32[]{:S(2)}, u32[]{:S(2)}) %collective-permute-start.7) | collective-permute-done | bytes 720928 | tf_op jit(solution)/shard_map/ppermute | solution.py:510
  60.2 1.0 shard_map.41
  61.2 5.4 %all-to-all-start = ((f32[8,176,128]{2,1,0:T(8,128)}), f32[8,176,128]{2,1,0:T(8,128)S(1)}, u32[]{:S(2)}, u32[]{:S(2)}) async-start(f32[8,176,128]{2,1,0:T(8,128)} %shard_map.41), calls=%async_computation | async-start | bytes 1441792 | tf_op jit(solution)/shard_map/all_to_all | solution.py:519
  66.6 1.3 %dynamic_slice.3 = s32[1]{0:T(128)} dynamic-slice(s32[512]{0:T(512)} %constant.70.clone, s32[]{:T(128)S(6)} %select_n.34), dynamic_slice_sizes={1} | dynamic-slice | bytes 12 | tf_op jit(solution)/shard_map/dynamic_slice | solution.py:424
  69.2 0.1 pad_add_fusion.flags
  69.3 7.4 %all-to-all-done.parts = f32[8,176,128]{2,1,0:T(8,128)S(1)} async-done(((f32[8,176,128]{2,1,0:T(8,128)}), f32[8,176,128]{2,1,0:T(8,128)S(1)}, u32[]{:S(2)}, u32[]{:S(2)}) %all-to-all-start) | async-done | bytes 720928 | tf_op jit(solution)/shard_map/all_to_all | solution.py:519
  76.6 1.6 %shard_map.42 = (f32[24,128]{1,0:T(8,128)S(1)}, f32[24,128]{1,0:T(8,128)S(1)}) custom-call(s32[2]{0:T(128)S(1)} %pad_add_fusion.flags, f32[8,176,128]{2,1,0:T(8,128)S(1)} %all-to-all-done.parts), custom_call_target="tpu_custom_call" | custom-call | tf_op jit(solution)/shard_map/pallas_call | solution.py:522
  78.2 9.5 %collective-permute-start.8 = (f32[24,128]{1,0:T(8,128)S(1)}, f32[24,128]{1,0:T(8,128)S(1)}, u32[]{:S(2)}, u32[]{:S(2)}) collective-permute-start(f32[24,128]{1,0:T(8,128)S(1)} %get-tuple-element.35), channel_id=1, source_target_pairs={{0,464},{1,64},{2,320},{3,322},{4,38},{5,209},{6,70},{7,210},{8,29... | collective-permute-start | bytes 36872 | tf_op jit(solution)/shard_map/ppermute | solution.py:530
  87.7 1.9 %collective-permute-start.9 = (f32[24,128]{1,0:T(8,128)S(1)}, f32[24,128]{1,0:T(8,128)S(1)}, u32[]{:S(2)}, u32[]{:S(2)}) collective-permute-start(f32[24,128]{1,0:T(8,128)S(1)} %get-tuple-element.36), channel_id=1, source_target_pairs={{0,14},{1,2},{2,10},{3,74},{4,193},{5,38},{6,194},{7,70},{8,217},{... | collective-permute-start | bytes 36872 | tf_op jit(solution)/shard_map/ppermute | solution.py:529
  90.3 0.0 collective-permute-done.8
  90.3 5.8 %collective-permute-done.9 = f32[24,128]{1,0:T(8,128)S(1)} collective-permute-done((f32[24,128]{1,0:T(8,128)S(1)}, f32[24,128]{1,0:T(8,128)S(1)}, u32[]{:S(2)}, u32[]{:S(2)}) %collective-permute-start.9) | collective-permute-done | bytes 12320 | tf_op jit(solution)/shard_map/ppermute | solution.py:529
  96.1 0.1 fusion
  96.1 0.7 maximum_maximum_fusion
  (1 shorter events, 0.0 us)
Async XLA Ops:
  0.0 23.9 %collective-permute-start.2 = (f32[144,512]{1,0:T(8,128)}, f32[144,512]{1,0:T(8,128)S(1)}, u32[]{:S(2)}, u32[]{:S(2)}) collective-permute-start(f32[144,512]{1,0:T(8,128)} %bitcast.10), channel_id=1, source_target_pairs={{32,0},{48,16},{64,32},{80,48},{96,64},{112,80},{128,96},{144,112}... | collective-permute-start | bytes 884744 | tf_op jit(solution)/shard_map/ppermute | solution.py:432
  11.6 25.9 %collective-permute-start = (f32[144,512]{1,0:T(8,128)}, f32[144,512]{1,0:T(8,128)S(1)}, u32[]{:S(2)}, u32[]{:S(2)}) collective-permute-start(f32[144,512]{1,0:T(8,128)} %bitcast.11), channel_id=1, source_target_pairs={{208,0},{224,16},{240,32},{0,48},{16,64},{32,80},{48,96},{64,112},... | collective-permute-start | bytes 884744 | tf_op jit(solution)/shard_map/ppermute | solution.py:432
  23.9 18.0 %collective-permute-start.5 = (f32[144,512]{1,0:T(8,128)S(1)}, f32[144,512]{1,0:T(8,128)S(1)}, u32[]{:S(2)}, u32[]{:S(2)}) collective-permute-start(f32[144,512]{1,0:T(8,128)S(1)} %collective-permute-done.2.plus2), channel_id=1, source_target_pairs={{32,0},{48,16},{64,32},{80,48},{96,64},{112,80},{128,96},{144,112}... | collective-permute-start | bytes 884744 | tf_op jit(solution)/shard_map/ppermute | solution.py:432
  30.0 14.8 %collective-permute-start.3 = (f32[144,512]{1,0:T(8,128)S(1)}, f32[144,512]{1,0:T(8,128)S(1)}, u32[]{:S(2)}, u32[]{:S(2)}) collective-permute-start(f32[144,512]{1,0:T(8,128)S(1)} %collective-permute-done.2.plus2), channel_id=1, source_target_pairs={{256,0},{272,16},{288,32},{304,48},{320,64},{336,80},{352,96},{368... | collective-permute-start | bytes 884744 | tf_op jit(solution)/shard_map/ppermute | solution.py:435
  37.5 10.0 %collective-permute-start.4 = (f32[144,512]{1,0:T(8,128)S(1)}, f32[144,512]{1,0:T(8,128)S(1)}, u32[]{:S(2)}, u32[]{:S(2)}) collective-permute-start(f32[144,512]{1,0:T(8,128)S(1)} %collective-permute-done.minus3), channel_id=1, source_target_pairs={{256,0},{272,16},{288,32},{304,48},{320,64},{336,80},{352,96},{368... | collective-permute-start | bytes 884744 | tf_op jit(solution)/shard_map/ppermute | solution.py:435
  40.0 10.9 %collective-permute-start.1 = (f32[144,512]{1,0:T(8,128)S(1)}, f32[144,512]{1,0:T(8,128)S(1)}, u32[]{:S(2)}, u32[]{:S(2)}) collective-permute-start(f32[144,512]{1,0:T(8,128)S(1)} %collective-permute-done.minus3), channel_id=1, source_target_pairs={{240,0},{0,16},{16,32},{32,48},{48,64},{64,80},{80,96},{96,112},{1... | collective-permute-start | bytes 884744 | tf_op jit(solution)/shard_map/ppermute | solution.py:432
  41.9 11.8 %collective-permute-start.6 = (f32[144,512]{1,0:T(8,128)S(1)}, f32[144,512]{1,0:T(8,128)S(1)}, u32[]{:S(2)}, u32[]{:S(2)}) collective-permute-start(f32[144,512]{1,0:T(8,128)S(1)} %collective-permute-done.5.plus4), channel_id=1, source_target_pairs={{256,0},{272,16},{288,32},{304,48},{320,64},{336,80},{352,96},{368... | collective-permute-start | bytes 884744 | tf_op jit(solution)/shard_map/ppermute | solution.py:435
  44.8 0.7 copy-start
  45.5 1.0 copy-start.1
  55.2 5.0 %collective-permute-start.7 = (f32[8,176,128]{2,1,0:T(8,128)S(1)}, f32[8,176,128]{2,1,0:T(8,128)S(1)}, u32[]{:S(2)}, u32[]{:S(2)}) collective-permute-start(f32[8,176,128]{2,1,0:T(8,128)S(1)} %get-tuple-element.34), channel_id=1, source_target_pairs={{0,1},{1,0},{2,3},{3,2},{4,5},{5,4},{6,7},{7,6},{8,9},{9,8},{10,11... | collective-permute-start | bytes 2162696 | tf_op jit(solution)/shard_map/ppermute | solution.py:510
  61.2 15.4 %all-to-all-start = ((f32[8,176,128]{2,1,0:T(8,128)}), f32[8,176,128]{2,1,0:T(8,128)S(1)}, u32[]{:S(2)}, u32[]{:S(2)}) async-start(f32[8,176,128]{2,1,0:T(8,128)} %shard_map.41), calls=%async_computation | async-start | bytes 1441792 | tf_op jit(solution)/shard_map/all_to_all | solution.py:519
  78.2 12.1 %collective-permute-start.8 = (f32[24,128]{1,0:T(8,128)S(1)}, f32[24,128]{1,0:T(8,128)S(1)}, u32[]{:S(2)}, u32[]{:S(2)}) collective-permute-start(f32[24,128]{1,0:T(8,128)S(1)} %get-tuple-element.35), channel_id=1, source_target_pairs={{0,464},{1,64},{2,320},{3,322},{4,38},{5,209},{6,70},{7,210},{8,29... | collective-permute-start | bytes 36872 | tf_op jit(solution)/shard_map/ppermute | solution.py:530
  87.7 8.3 %collective-permute-start.9 = (f32[24,128]{1,0:T(8,128)S(1)}, f32[24,128]{1,0:T(8,128)S(1)}, u32[]{:S(2)}, u32[]{:S(2)}) collective-permute-start(f32[24,128]{1,0:T(8,128)S(1)} %get-tuple-element.36), channel_id=1, source_target_pairs={{0,14},{1,2},{2,10},{3,74},{4,193},{5,38},{6,194},{7,70},{8,217},{... | collective-permute-start | bytes 36872 | tf_op jit(solution)/shard_map/ppermute | solution.py:529

commit v12 on v11

--- a/solution.py
+++ b/solution.py
@@ -334,7 +334,7 @@
     return jnp.concatenate([x, jnp.zeros((128 - x.shape[0], 128), jnp.float32)], axis=0)
 
 
-def fit_kernel(flags, parts, first, second):
+def fit_kernel(flags, parts, first, second, lower):
     diagonal, swap = flags[1] == 1, flags[0] == 1
     total = parts[0]
     for a in range(1, CHIPS):
@@ -388,19 +388,25 @@
         return jnp.concatenate([high, high, low] if first else [high, low, high], axis=1)
 
     up_rows = parts_of([mass * p for p in off_p], True)
-    low_rows = parts_of([mass * jnp.where(diagonal, q, p) for p, q in zip(off_p, off_q)], True)
     moment = []
     between = []
     for d in range(3):
         up = product(up_rows, parts_of([square_tile(jnp.where(diagonal, off_p[d], off_q[d]))], False))
-        low = product(low_rows, parts_of([square_tile(off_q[d])], False))
-        between.append((up, low))
+        lower[d] = up
+        between.append(up)
+
+    @pl.when(diagonal)
+    def _():
+        low_rows = parts_of([mass * q for q in off_q], True)
+        for d in range(3):
+            lower[d] = product(low_rows, parts_of([square_tile(off_q[d])], False))
+
     for c in range(3):
         main = total[c * ROWS : (c + 1) * ROWS]
         tail = pltpu.roll(rest, (32 - 16 * c) % 128, 1)
         shifted = [main, pltpu.roll(main, 128 - 48, 1), jnp.where(lane < 32, pltpu.roll(main, 128 - 96, 1), tail)]
         for d in range(3):
-            up, low = (b[c * ROWS : (c + 1) * ROWS] for b in between[d])
+            up, low = between[d][c * ROWS : (c + 1) * ROWS], lower[d, c * ROWS : (c + 1) * ROWS]
             value = shifted[d] + jnp.where(upper, up, low)
             end = jnp.sum(jnp.where(lane == 66 + 3 * c + d, rest, 0.0), axis=1, keepdims=True)
             end = end + jnp.sum(mass * off_q[c] * off_q[d], axis=1, keepdims=True)
@@ -524,6 +530,7 @@
         out_shape=(block, block),
         in_specs=[smem, vmem],
         out_specs=(vmem, vmem),
+        scratch_shapes=[pltpu.VMEM((3, 3 * ROWS, 128), jnp.float32)],
         compiler_params=params,
     )(fit_flags, parts)
     one = lax.ppermute(one, ("frame", "atom"), list(enumerate(first)))

time: 98.5 us -> 98.7 us (level)
  no operation moved by 1% of the time
where the time goes in v12:
time: 98.7 us; the launch traced here: 97 us
  starting transfers between devices  49.3 us (50%)
  waiting for transfers between devices  32.1 us (33%)
  Pallas kernels  9.73 us (10%)
  local copies, waits for them, and re-layouts  2.98 us (3%)
  between operations  2.12 us (2%)
    ppermute x4, starting transfers between devices, along(): return lax.ppermute(block, 'frame', route)  21.5 us
    ppermute x4, waiting for transfers between devices, along(): return lax.ppermute(block, 'frame', route)  16.4 us
    ppermute x1, starting transfers between devices, on_device(): two = lax.ppermute(two, ('frame', 'atom'), list(enumerate(second)))  9.48 us
    ppermute x3, starting transfers between devices, across(): lax.ppermute(block, 'frame', [((f + SIDE) % (2 * SIDE), f) for f in range...  7.73 us
    all_to_all x1, waiting for transfers between devices, on_device(): lax.all_to_all(merged, ('frame', 'atom'), 0, 0, axis_index_groups=groups,...  7.37 us
    ppermute x1, waiting for transfers between devices, on_device(): one = lax.ppermute(one, ('frame', 'atom'), list(enumerate(first)))  5.76 us
    all_to_all x1, starting transfers between devices, on_device(): lax.all_to_all(merged, ('frame', 'atom'), 0, 0, axis_index_groups=groups,...  5.43 us
    ppermute x1, starting transfers between devices, on_device(): taken = lax.ppermute(send, 'atom', [(a, a ^ 1) for a in range(SIDE)])  3.24 us
  transfers between devices with their start and end apart: 11, of which 7 were waited for; matrix products, arithmetic and copies ran while one was open for 1% of the time, Pallas kernels for 6%

profile of v12, /device:TPU:7, one launch (start us, length us, event | category | flops | bytes accessed | tf_op | source)
XLA Modules:
  0.0 97.0 jit_solution(285787882338252641)
XLA Ops:
  0.0 11.6 %collective-permute-start.2 = (f32[144,512]{1,0:T(8,128)}, f32[144,512]{1,0:T(8,128)S(1)}, u32[]{:S(2)}, u32[]{:S(2)}) collective-permute-start(f32[144,512]{1,0:T(8,128)} %bitcast.10), channel_id=1, source_target_pairs={{32,0},{48,16},{64,32},{80,48},{96,64},{112,80},{128,96},{144,112}... | collective-permute-start | bytes 884744 | tf_op jit(solution)/shard_map/ppermute | solution.py:438
  11.6 1.9 %collective-permute-start = (f32[144,512]{1,0:T(8,128)}, f32[144,512]{1,0:T(8,128)S(1)}, u32[]{:S(2)}, u32[]{:S(2)}) collective-permute-start(f32[144,512]{1,0:T(8,128)} %bitcast.11), channel_id=1, source_target_pairs={{208,0},{224,16},{240,32},{0,48},{16,64},{32,80},{48,96},{64,112},... | collective-permute-start | bytes 884744 | tf_op jit(solution)/shard_map/ppermute | solution.py:438
  13.5 10.4 %collective-permute-done.2.plus2 = f32[144,512]{1,0:T(8,128)S(1)} collective-permute-done((f32[144,512]{1,0:T(8,128)}, f32[144,512]{1,0:T(8,128)S(1)}, u32[]{:S(2)}, u32[]{:S(2)}) %collective-permute-start.2) | collective-permute-done | bytes 294944 | tf_op jit(solution)/shard_map/ppermute | solution.py:438
  23.9 6.1 %collective-permute-start.5 = (f32[144,512]{1,0:T(8,128)S(1)}, f32[144,512]{1,0:T(8,128)S(1)}, u32[]{:S(2)}, u32[]{:S(2)}) collective-permute-start(f32[144,512]{1,0:T(8,128)S(1)} %collective-permute-done.2.plus2), channel_id=1, source_target_pairs={{32,0},{48,16},{64,32},{80,48},{96,64},{112,80},{128,96},{144,112}... | collective-permute-start | bytes 884744 | tf_op jit(solution)/shard_map/ppermute | solution.py:438
  30.0 2.5 %collective-permute-start.3 = (f32[144,512]{1,0:T(8,128)S(1)}, f32[144,512]{1,0:T(8,128)S(1)}, u32[]{:S(2)}, u32[]{:S(2)}) collective-permute-start(f32[144,512]{1,0:T(8,128)S(1)} %collective-permute-done.2.plus2), channel_id=1, source_target_pairs={{256,0},{272,16},{288,32},{304,48},{320,64},{336,80},{352,96},{368... | collective-permute-start | bytes 884744 | tf_op jit(solution)/shard_map/ppermute | solution.py:441
  32.5 5.0 %collective-permute-done.minus3 = f32[144,512]{1,0:T(8,128)S(1)} collective-permute-done((f32[144,512]{1,0:T(8,128)}, f32[144,512]{1,0:T(8,128)S(1)}, u32[]{:S(2)}, u32[]{:S(2)}) %collective-permute-start) | collective-permute-done | bytes 294944 | tf_op jit(solution)/shard_map/ppermute | solution.py:438
  37.5 2.4 %collective-permute-start.4 = (f32[144,512]{1,0:T(8,128)S(1)}, f32[144,512]{1,0:T(8,128)S(1)}, u32[]{:S(2)}, u32[]{:S(2)}) collective-permute-start(f32[144,512]{1,0:T(8,128)S(1)} %collective-permute-done.minus3), channel_id=1, source_target_pairs={{256,0},{272,16},{288,32},{304,48},{320,64},{336,80},{352,96},{368... | collective-permute-start | bytes 884744 | tf_op jit(solution)/shard_map/ppermute | solution.py:441
  40.0 1.9 %collective-permute-start.1 = (f32[144,512]{1,0:T(8,128)S(1)}, f32[144,512]{1,0:T(8,128)S(1)}, u32[]{:S(2)}, u32[]{:S(2)}) collective-permute-start(f32[144,512]{1,0:T(8,128)S(1)} %collective-permute-done.minus3), channel_id=1, source_target_pairs={{240,0},{0,16},{16,32},{32,48},{48,64},{64,80},{80,96},{96,112},{1... | collective-permute-start | bytes 884744 | tf_op jit(solution)/shard_map/ppermute | solution.py:438
  41.9 0.0 collective-permute-done.5.plus4
  41.9 2.8 %collective-permute-start.6 = (f32[144,512]{1,0:T(8,128)S(1)}, f32[144,512]{1,0:T(8,128)S(1)}, u32[]{:S(2)}, u32[]{:S(2)}) collective-permute-start(f32[144,512]{1,0:T(8,128)S(1)} %collective-permute-done.5.plus4), channel_id=1, source_target_pairs={{256,0},{272,16},{288,32},{304,48},{320,64},{336,80},{352,96},{368... | collective-permute-start | bytes 884744 | tf_op jit(solution)/shard_map/ppermute | solution.py:441
  44.8 0.1 pad_add_fusion.1.flags
  44.8 0.0 collective-permute-done.3.other2
  44.8 0.0 copy-start
  44.8 0.7 copy-done
  45.5 0.0 copy-start.1
  45.5 1.0 copy-done.1
  46.5 1.0 %shard_map.37 = (bf16[576,1536]{1,0:T(8,128)(2,1)S(1)}, f32[4,48,128]{2,1,0:T(8,128)S(1)}, bf16[2,256,1536]{2,1,0:T(8,128)(2,1)S(1)}, f32[2,48,128]{2,1,0:T(8,128)S(1)}) custom-call(s32[3]{0:T(128)S(1)} %pad_add_fusion.1.flags, s32[1,512]{1,0:T(1,128)S(1)} %bitcast.6, f32[144,512]{1,0:T(8,128)S(1)} %bitcast.12, f32[144,512]{1,0:T(8,128)S(1)} %collective-permute-done.2.plus2, ...), custom_call_target="tpu_custom_call" | custom-call | flops 1019215872 | bytes 4000000 | tf_op jit(solution)/shard_map/pallas_call | solution.py:474
  47.5 0.0 collective-permute-done.4.other3
  47.5 2.4 %shard_map.38 = (f32[16,176,128]{2,1,0:T(8,128)S(1)}, bf16[576,1536]{1,0:T(8,128)(2,1)S(1)}, f32[4,48,128]{2,1,0:T(8,128)S(1)}, bf16[3,256,1536]{2,1,0:T(8,128)(2,1)S(1)}, f32[3,48,128]{2,1,0:T(8,128)S(1)}) custom-call(s32[3]{0:T(128)S(1)} %pad_add_fusion.1.flags, s32[1,512]{1,0:T(1,128)S(1)} %bitcast.7, ...), custom_call_target="tpu_custom_call", output_to_operand_aliasing={{1}: (7, {}), {2}: (8, {})} | custom-call | flops 1019215872 | bytes 4000000 | tf_op jit(solution)/shard_map/pallas_call | solution.py:486
  49.9 1.0 %collective-permute-done.1.minus4 = f32[144,512]{1,0:T(8,128)S(1)} collective-permute-done((f32[144,512]{1,0:T(8,128)S(1)}, f32[144,512]{1,0:T(8,128)S(1)}, u32[]{:S(2)}, u32[]{:S(2)}) %collective-permute-start.1) | collective-permute-done | bytes 294944 | tf_op jit(solution)/shard_map/ppermute | solution.py:438
  50.9 2.2 %shard_map.39 = (f32[16,176,128]{2,1,0:T(8,128)S(1)}, bf16[576,1536]{1,0:T(8,128)(2,1)S(1)}, f32[4,48,128]{2,1,0:T(8,128)S(1)}) custom-call(s32[3]{0:T(128)S(1)} %pad_add_fusion.1.flags, s32[1,512]{1,0:T(1,128)S(1)} %bitcast.8, f32[144,512]{1,0:T(8,128)S(1)} %collective-permute-done.1.minus4, ...), custom_call_target="tpu_custom_call", output_to_operand_aliasing={{0}: (7, {}), {1}: (8, {}), {2}: (9, {})} | custom-call | flops 679477248 | bytes 4000000 | tf_op jit(solution)/shard_map/pallas_call | solution.py:495
  53.0 0.7 collective-permute-done.6.other4
  53.8 1.4 %shard_map.40 = (f32[8,176,128]{2,1,0:T(8,128)S(1)}, f32[1,176,128]{2,1,0:T(8,128)S(1)}) custom-call(s32[3]{0:T(128)S(1)} %pad_add_fusion.1.flags, s32[1,512]{1,0:T(1,128)S(1)} %bitcast.9, bf16[576,1536]{1,0:T(8,128)(2,1)S(1)} %get-tuple-element.31.weighted, f32[4,48,128]{2,1,0:T(8,128)S(1)} %get-tuple-element.32.row_feature, ...), custom_call_target="tpu_custom_call" | custom-call | flops 339738624 | bytes 4000000 | tf_op jit(solution)/shard_map/pallas_call | solution.py:507
  55.2 3.2 %collective-permute-start.7 = (f32[8,176,128]{2,1,0:T(8,128)S(1)}, f32[8,176,128]{2,1,0:T(8,128)S(1)}, u32[]{:S(2)}, u32[]{:S(2)}) collective-permute-start(f32[8,176,128]{2,1,0:T(8,128)S(1)} %get-tuple-element.34), channel_id=1, source_target_pairs={{0,1},{1,0},{2,3},{3,2},{4,5},{5,4},{6,7},{7,6},{8,9},{9,8},{10,11... | collective-permute-start | bytes 2162696 | tf_op jit(solution)/shard_map/ppermute | solution.py:516
  58.5 1.8 %collective-permute-done.7.taken = f32[8,176,128]{2,1,0:T(8,128)S(1)} collective-permute-done((f32[8,176,128]{2,1,0:T(8,128)S(1)}, f32[8,176,128]{2,1,0:T(8,128)S(1)}, u32[]{:S(2)}, u32[]{:S(2)}) %collective-permute-start.7) | collective-permute-done | bytes 720928 | tf_op jit(solution)/shard_map/ppermute | solution.py:516
  60.2 1.0 shard_map.41
  61.2 5.4 %all-to-all-start = ((f32[8,176,128]{2,1,0:T(8,128)}), f32[8,176,128]{2,1,0:T(8,128)S(1)}, u32[]{:S(2)}, u32[]{:S(2)}) async-start(f32[8,176,128]{2,1,0:T(8,128)} %shard_map.41), calls=%async_computation | async-start | bytes 1441792 | tf_op jit(solution)/shard_map/all_to_all | solution.py:525
  66.6 1.3 %dynamic_slice.3 = s32[1]{0:T(128)} dynamic-slice(s32[512]{0:T(512)} %constant.70.clone, s32[]{:T(128)S(6)} %select_n.34), dynamic_slice_sizes={1} | dynamic-slice | bytes 12 | tf_op jit(solution)/shard_map/dynamic_slice | solution.py:430
  69.2 0.1 pad_add_fusion.flags
  69.3 7.4 %all-to-all-done.parts = f32[8,176,128]{2,1,0:T(8,128)S(1)} async-done(((f32[8,176,128]{2,1,0:T(8,128)}), f32[8,176,128]{2,1,0:T(8,128)S(1)}, u32[]{:S(2)}, u32[]{:S(2)}) %all-to-all-start) | async-done | bytes 720928 | tf_op jit(solution)/shard_map/all_to_all | solution.py:525
  76.6 1.8 %shard_map.42 = (f32[24,128]{1,0:T(8,128)S(1)}, f32[24,128]{1,0:T(8,128)S(1)}) custom-call(s32[2]{0:T(128)S(1)} %pad_add_fusion.flags, f32[8,176,128]{2,1,0:T(8,128)S(1)} %all-to-all-done.parts), custom_call_target="tpu_custom_call" | custom-call | tf_op jit(solution)/shard_map/pallas_call | solution.py:528
  78.4 9.5 %collective-permute-start.8 = (f32[24,128]{1,0:T(8,128)S(1)}, f32[24,128]{1,0:T(8,128)S(1)}, u32[]{:S(2)}, u32[]{:S(2)}) collective-permute-start(f32[24,128]{1,0:T(8,128)S(1)} %get-tuple-element.35), channel_id=1, source_target_pairs={{0,464},{1,64},{2,320},{3,322},{4,38},{5,209},{6,70},{7,210},{8,29... | collective-permute-start | bytes 36872 | tf_op jit(solution)/shard_map/ppermute | solution.py:537
  87.9 1.9 %collective-permute-start.9 = (f32[24,128]{1,0:T(8,128)S(1)}, f32[24,128]{1,0:T(8,128)S(1)}, u32[]{:S(2)}, u32[]{:S(2)}) collective-permute-start(f32[24,128]{1,0:T(8,128)S(1)} %get-tuple-element.36), channel_id=1, source_target_pairs={{0,14},{1,2},{2,10},{3,74},{4,193},{5,38},{6,194},{7,70},{8,217},{... | collective-permute-start | bytes 36872 | tf_op jit(solution)/shard_map/ppermute | solution.py:536
  90.5 0.0 collective-permute-done.8
  90.5 5.8 %collective-permute-done.9 = f32[24,128]{1,0:T(8,128)S(1)} collective-permute-done((f32[24,128]{1,0:T(8,128)S(1)}, f32[24,128]{1,0:T(8,128)S(1)}, u32[]{:S(2)}, u32[]{:S(2)}) %collective-permute-start.9) | collective-permute-done | bytes 12320 | tf_op jit(solution)/shard_map/ppermute | solution.py:536
  96.3 0.1 fusion
  96.4 0.7 maximum_maximum_fusion
  (1 shorter events, 0.0 us)
Async XLA Ops:
  0.0 23.9 %collective-permute-start.2 = (f32[144,512]{1,0:T(8,128)}, f32[144,512]{1,0:T(8,128)S(1)}, u32[]{:S(2)}, u32[]{:S(2)}) collective-permute-start(f32[144,512]{1,0:T(8,128)} %bitcast.10), channel_id=1, source_target_pairs={{32,0},{48,16},{64,32},{80,48},{96,64},{112,80},{128,96},{144,112}... | collective-permute-start | bytes 884744 | tf_op jit(solution)/shard_map/ppermute | solution.py:438
  11.6 25.9 %collective-permute-start = (f32[144,512]{1,0:T(8,128)}, f32[144,512]{1,0:T(8,128)S(1)}, u32[]{:S(2)}, u32[]{:S(2)}) collective-permute-start(f32[144,512]{1,0:T(8,128)} %bitcast.11), channel_id=1, source_target_pairs={{208,0},{224,16},{240,32},{0,48},{16,64},{32,80},{48,96},{64,112},... | collective-permute-start | bytes 884744 | tf_op jit(solution)/shard_map/ppermute | solution.py:438
  23.9 18.0 %collective-permute-start.5 = (f32[144,512]{1,0:T(8,128)S(1)}, f32[144,512]{1,0:T(8,128)S(1)}, u32[]{:S(2)}, u32[]{:S(2)}) collective-permute-start(f32[144,512]{1,0:T(8,128)S(1)} %collective-permute-done.2.plus2), channel_id=1, source_target_pairs={{32,0},{48,16},{64,32},{80,48},{96,64},{112,80},{128,96},{144,112}... | collective-permute-start | bytes 884744 | tf_op jit(solution)/shard_map/ppermute | solution.py:438
  30.0 14.8 %collective-permute-start.3 = (f32[144,512]{1,0:T(8,128)S(1)}, f32[144,512]{1,0:T(8,128)S(1)}, u32[]{:S(2)}, u32[]{:S(2)}) collective-permute-start(f32[144,512]{1,0:T(8,128)S(1)} %collective-permute-done.2.plus2), channel_id=1, source_target_pairs={{256,0},{272,16},{288,32},{304,48},{320,64},{336,80},{352,96},{368... | collective-permute-start | bytes 884744 | tf_op jit(solution)/shard_map/ppermute | solution.py:441
  37.5 10.0 %collective-permute-start.4 = (f32[144,512]{1,0:T(8,128)S(1)}, f32[144,512]{1,0:T(8,128)S(1)}, u32[]{:S(2)}, u32[]{:S(2)}) collective-permute-start(f32[144,512]{1,0:T(8,128)S(1)} %collective-permute-done.minus3), channel_id=1, source_target_pairs={{256,0},{272,16},{288,32},{304,48},{320,64},{336,80},{352,96},{368... | collective-permute-start | bytes 884744 | tf_op jit(solution)/shard_map/ppermute | solution.py:441
  40.0 10.9 %collective-permute-start.1 = (f32[144,512]{1,0:T(8,128)S(1)}, f32[144,512]{1,0:T(8,128)S(1)}, u32[]{:S(2)}, u32[]{:S(2)}) collective-permute-start(f32[144,512]{1,0:T(8,128)S(1)} %collective-permute-done.minus3), channel_id=1, source_target_pairs={{240,0},{0,16},{16,32},{32,48},{48,64},{64,80},{80,96},{96,112},{1... | collective-permute-start | bytes 884744 | tf_op jit(solution)/shard_map/ppermute | solution.py:438
  41.9 11.8 %collective-permute-start.6 = (f32[144,512]{1,0:T(8,128)S(1)}, f32[144,512]{1,0:T(8,128)S(1)}, u32[]{:S(2)}, u32[]{:S(2)}) collective-permute-start(f32[144,512]{1,0:T(8,128)S(1)} %collective-permute-done.5.plus4), channel_id=1, source_target_pairs={{256,0},{272,16},{288,32},{304,48},{320,64},{336,80},{352,96},{368... | collective-permute-start | bytes 884744 | tf_op jit(solution)/shard_map/ppermute | solution.py:441
  44.8 0.7 copy-start
  45.5 1.0 copy-start.1
  55.2 5.0 %collective-permute-start.7 = (f32[8,176,128]{2,1,0:T(8,128)S(1)}, f32[8,176,128]{2,1,0:T(8,128)S(1)}, u32[]{:S(2)}, u32[]{:S(2)}) collective-permute-start(f32[8,176,128]{2,1,0:T(8,128)S(1)} %get-tuple-element.34), channel_id=1, source_target_pairs={{0,1},{1,0},{2,3},{3,2},{4,5},{5,4},{6,7},{7,6},{8,9},{9,8},{10,11... | collective-permute-start | bytes 2162696 | tf_op jit(solution)/shard_map/ppermute | solution.py:516
  61.2 15.4 %all-to-all-start = ((f32[8,176,128]{2,1,0:T(8,128)}), f32[8,176,128]{2,1,0:T(8,128)S(1)}, u32[]{:S(2)}, u32[]{:S(2)}) async-start(f32[8,176,128]{2,1,0:T(8,128)} %shard_map.41), calls=%async_computation | async-start | bytes 1441792 | tf_op jit(solution)/shard_map/all_to_all | solution.py:525
  78.4 12.1 %collective-permute-start.8 = (f32[24,128]{1,0:T(8,128)S(1)}, f32[24,128]{1,0:T(8,128)S(1)}, u32[]{:S(2)}, u32[]{:S(2)}) collective-permute-start(f32[24,128]{1,0:T(8,128)S(1)} %get-tuple-element.35), channel_id=1, source_target_pairs={{0,464},{1,64},{2,320},{3,322},{4,38},{5,209},{6,70},{7,210},{8,29... | collective-permute-start | bytes 36872 | tf_op jit(solution)/shard_map/ppermute | solution.py:537
  87.9 8.3 %collective-permute-start.9 = (f32[24,128]{1,0:T(8,128)S(1)}, f32[24,128]{1,0:T(8,128)S(1)}, u32[]{:S(2)}, u32[]{:S(2)}) collective-permute-start(f32[24,128]{1,0:T(8,128)S(1)} %get-tuple-element.36), channel_id=1, source_target_pairs={{0,14},{1,2},{2,10},{3,74},{4,193},{5,38},{6,194},{7,70},{8,217},{... | collective-permute-start | bytes 36872 | tf_op jit(solution)/shard_map/ppermute | solution.py:536

commit v13 on v11

--- a/solution.py
+++ b/solution.py
@@ -389,19 +389,20 @@
 
     up_rows = parts_of([mass * p for p in off_p], True)
     low_rows = parts_of([mass * jnp.where(diagonal, q, p) for p, q in zip(off_p, off_q)], True)
+    blank = jnp.zeros((256 - 3 * ROWS, 128), jnp.float32)
+    up_columns = parts_of([jnp.where(diagonal, p, q) for p, q in zip(off_p, off_q)] + [blank], False)
+    low_columns = parts_of(off_q + [blank], False)
+    above = iota((3 * ROWS, 256), 0) % ROWS <= iota((3 * ROWS, 256), 1) % ROWS
+    between = jnp.where(above, product(up_rows, up_columns), product(low_rows, low_columns))
+    sums = total[: 3 * ROWS] + between[:, :128]
+    narrow = rest + rest_of(between[:, 128:])
     moment = []
-    between = []
-    for d in range(3):
-        up = product(up_rows, parts_of([square_tile(jnp.where(diagonal, off_p[d], off_q[d]))], False))
-        low = product(low_rows, parts_of([square_tile(off_q[d])], False))
-        between.append((up, low))
     for c in range(3):
-        main = total[c * ROWS : (c + 1) * ROWS]
-        tail = pltpu.roll(rest, (32 - 16 * c) % 128, 1)
+        main = sums[c * ROWS : (c + 1) * ROWS]
+        tail = pltpu.roll(narrow, (32 - 16 * c) % 128, 1)
         shifted = [main, pltpu.roll(main, 128 - 48, 1), jnp.where(lane < 32, pltpu.roll(main, 128 - 96, 1), tail)]
         for d in range(3):
-            up, low = (b[c * ROWS : (c + 1) * ROWS] for b in between[d])
-            value = shifted[d] + jnp.where(upper, up, low)
+            value = shifted[d]
             end = jnp.sum(jnp.where(lane == 66 + 3 * c + d, rest, 0.0), axis=1, keepdims=True)
             end = end + jnp.sum(mass * off_q[c] * off_q[d], axis=1, keepdims=True)
             moment.append(jnp.where(corner, end, value) / whole)

time: 98.5 us -> 98.5 us (level)
  no operation moved by 1% of the time
where the time goes in v13:
time: 98.5 us; the launch traced here: 96.8 us
  starting transfers between devices  49.3 us (50%)
  waiting for transfers between devices  32.1 us (33%)
  Pallas kernels  9.48 us (10%)
  local copies, waits for them, and re-layouts  2.98 us (3%)
  between operations  2.12 us (2%)
    ppermute x4, starting transfers between devices, along(): return lax.ppermute(block, 'frame', route)  21.5 us
    ppermute x4, waiting for transfers between devices, along(): return lax.ppermute(block, 'frame', route)  16.4 us
    ppermute x1, starting transfers between devices, on_device(): two = lax.ppermute(two, ('frame', 'atom'), list(enumerate(second)))  9.47 us
    ppermute x3, starting transfers between devices, across(): lax.ppermute(block, 'frame', [((f + SIDE) % (2 * SIDE), f) for f in range...  7.73 us
    all_to_all x1, waiting for transfers between devices, on_device(): lax.all_to_all(merged, ('frame', 'atom'), 0, 0, axis_index_groups=groups,...  7.37 us
    ppermute x1, waiting for transfers between devices, on_device(): one = lax.ppermute(one, ('frame', 'atom'), list(enumerate(first)))  5.76 us
    all_to_all x1, starting transfers between devices, on_device(): lax.all_to_all(merged, ('frame', 'atom'), 0, 0, axis_index_groups=groups,...  5.43 us
    ppermute x1, starting transfers between devices, on_device(): taken = lax.ppermute(send, 'atom', [(a, a ^ 1) for a in range(SIDE)])  3.24 us
  transfers between devices with their start and end apart: 11, of which 7 were waited for; matrix products, arithmetic and copies ran while one was open for 1% of the time, Pallas kernels for 6%

profile of v13, /device:TPU:7, one launch (start us, length us, event | category | flops | bytes accessed | tf_op | source)
XLA Modules:
  0.0 96.8 jit_solution(5694950223779216032)
XLA Ops:
  0.0 11.6 %collective-permute-start.2 = (f32[144,512]{1,0:T(8,128)}, f32[144,512]{1,0:T(8,128)S(1)}, u32[]{:S(2)}, u32[]{:S(2)}) collective-permute-start(f32[144,512]{1,0:T(8,128)} %bitcast.10), channel_id=1, source_target_pairs={{32,0},{48,16},{64,32},{80,48},{96,64},{112,80},{128,96},{144,112}... | collective-permute-start | bytes 884744 | tf_op jit(solution)/shard_map/ppermute | solution.py:433
  11.6 1.9 %collective-permute-start = (f32[144,512]{1,0:T(8,128)}, f32[144,512]{1,0:T(8,128)S(1)}, u32[]{:S(2)}, u32[]{:S(2)}) collective-permute-start(f32[144,512]{1,0:T(8,128)} %bitcast.11), channel_id=1, source_target_pairs={{208,0},{224,16},{240,32},{0,48},{16,64},{32,80},{48,96},{64,112},... | collective-permute-start | bytes 884744 | tf_op jit(solution)/shard_map/ppermute | solution.py:433
  13.5 10.4 %collective-permute-done.2.plus2 = f32[144,512]{1,0:T(8,128)S(1)} collective-permute-done((f32[144,512]{1,0:T(8,128)}, f32[144,512]{1,0:T(8,128)S(1)}, u32[]{:S(2)}, u32[]{:S(2)}) %collective-permute-start.2) | collective-permute-done | bytes 294944 | tf_op jit(solution)/shard_map/ppermute | solution.py:433
  23.9 6.1 %collective-permute-start.5 = (f32[144,512]{1,0:T(8,128)S(1)}, f32[144,512]{1,0:T(8,128)S(1)}, u32[]{:S(2)}, u32[]{:S(2)}) collective-permute-start(f32[144,512]{1,0:T(8,128)S(1)} %collective-permute-done.2.plus2), channel_id=1, source_target_pairs={{32,0},{48,16},{64,32},{80,48},{96,64},{112,80},{128,96},{144,112}... | collective-permute-start | bytes 884744 | tf_op jit(solution)/shard_map/ppermute | solution.py:433
  30.0 2.5 %collective-permute-start.3 = (f32[144,512]{1,0:T(8,128)S(1)}, f32[144,512]{1,0:T(8,128)S(1)}, u32[]{:S(2)}, u32[]{:S(2)}) collective-permute-start(f32[144,512]{1,0:T(8,128)S(1)} %collective-permute-done.2.plus2), channel_id=1, source_target_pairs={{256,0},{272,16},{288,32},{304,48},{320,64},{336,80},{352,96},{368... | collective-permute-start | bytes 884744 | tf_op jit(solution)/shard_map/ppermute | solution.py:436
  32.5 5.0 %collective-permute-done.minus3 = f32[144,512]{1,0:T(8,128)S(1)} collective-permute-done((f32[144,512]{1,0:T(8,128)}, f32[144,512]{1,0:T(8,128)S(1)}, u32[]{:S(2)}, u32[]{:S(2)}) %collective-permute-start) | collective-permute-done | bytes 294944 | tf_op jit(solution)/shard_map/ppermute | solution.py:433
  37.5 2.4 %collective-permute-start.4 = (f32[144,512]{1,0:T(8,128)S(1)}, f32[144,512]{1,0:T(8,128)S(1)}, u32[]{:S(2)}, u32[]{:S(2)}) collective-permute-start(f32[144,512]{1,0:T(8,128)S(1)} %collective-permute-done.minus3), channel_id=1, source_target_pairs={{256,0},{272,16},{288,32},{304,48},{320,64},{336,80},{352,96},{368... | collective-permute-start | bytes 884744 | tf_op jit(solution)/shard_map/ppermute | solution.py:436
  40.0 1.9 %collective-permute-start.1 = (f32[144,512]{1,0:T(8,128)S(1)}, f32[144,512]{1,0:T(8,128)S(1)}, u32[]{:S(2)}, u32[]{:S(2)}) collective-permute-start(f32[144,512]{1,0:T(8,128)S(1)} %collective-permute-done.minus3), channel_id=1, source_target_pairs={{240,0},{0,16},{16,32},{32,48},{48,64},{64,80},{80,96},{96,112},{1... | collective-permute-start | bytes 884744 | tf_op jit(solution)/shard_map/ppermute | solution.py:433
  41.9 0.0 collective-permute-done.5.plus4
  41.9 2.8 %collective-permute-start.6 = (f32[144,512]{1,0:T(8,128)S(1)}, f32[144,512]{1,0:T(8,128)S(1)}, u32[]{:S(2)}, u32[]{:S(2)}) collective-permute-start(f32[144,512]{1,0:T(8,128)S(1)} %collective-permute-done.5.plus4), channel_id=1, source_target_pairs={{256,0},{272,16},{288,32},{304,48},{320,64},{336,80},{352,96},{368... | collective-permute-start | bytes 884744 | tf_op jit(solution)/shard_map/ppermute | solution.py:436
  44.8 0.1 pad_add_fusion.1.flags
  44.8 0.0 collective-permute-done.3.other2
  44.8 0.0 copy-start
  44.8 0.7 copy-done
  45.5 0.0 copy-start.1
  45.5 1.0 copy-done.1
  46.5 1.0 %shard_map.37 = (bf16[576,1536]{1,0:T(8,128)(2,1)S(1)}, f32[4,48,128]{2,1,0:T(8,128)S(1)}, bf16[2,256,1536]{2,1,0:T(8,128)(2,1)S(1)}, f32[2,48,128]{2,1,0:T(8,128)S(1)}) custom-call(s32[3]{0:T(128)S(1)} %pad_add_fusion.1.flags, s32[1,512]{1,0:T(1,128)S(1)} %bitcast.6, f32[144,512]{1,0:T(8,128)S(1)} %bitcast.12, f32[144,512]{1,0:T(8,128)S(1)} %collective-permute-done.2.plus2, ...), custom_call_target="tpu_custom_call" | custom-call | flops 1019215872 | bytes 4000000 | tf_op jit(solution)/shard_map/pallas_call | solution.py:469
  47.5 0.0 collective-permute-done.4.other3
  47.5 2.4 %shard_map.38 = (f32[16,176,128]{2,1,0:T(8,128)S(1)}, bf16[576,1536]{1,0:T(8,128)(2,1)S(1)}, f32[4,48,128]{2,1,0:T(8,128)S(1)}, bf16[3,256,1536]{2,1,0:T(8,128)(2,1)S(1)}, f32[3,48,128]{2,1,0:T(8,128)S(1)}) custom-call(s32[3]{0:T(128)S(1)} %pad_add_fusion.1.flags, s32[1,512]{1,0:T(1,128)S(1)} %bitcast.7, ...), custom_call_target="tpu_custom_call", output_to_operand_aliasing={{1}: (7, {}), {2}: (8, {})} | custom-call | flops 1019215872 | bytes 4000000 | tf_op jit(solution)/shard_map/pallas_call | solution.py:481
  49.9 1.0 %collective-permute-done.1.minus4 = f32[144,512]{1,0:T(8,128)S(1)} collective-permute-done((f32[144,512]{1,0:T(8,128)S(1)}, f32[144,512]{1,0:T(8,128)S(1)}, u32[]{:S(2)}, u32[]{:S(2)}) %collective-permute-start.1) | collective-permute-done | bytes 294944 | tf_op jit(solution)/shard_map/ppermute | solution.py:433
  50.9 2.2 %shard_map.39 = (f32[16,176,128]{2,1,0:T(8,128)S(1)}, bf16[576,1536]{1,0:T(8,128)(2,1)S(1)}, f32[4,48,128]{2,1,0:T(8,128)S(1)}) custom-call(s32[3]{0:T(128)S(1)} %pad_add_fusion.1.flags, s32[1,512]{1,0:T(1,128)S(1)} %bitcast.8, f32[144,512]{1,0:T(8,128)S(1)} %collective-permute-done.1.minus4, ...), custom_call_target="tpu_custom_call", output_to_operand_aliasing={{0}: (7, {}), {1}: (8, {}), {2}: (9, {})} | custom-call | flops 679477248 | bytes 4000000 | tf_op jit(solution)/shard_map/pallas_call | solution.py:490
  53.0 0.7 collective-permute-done.6.other4
  53.8 1.4 %shard_map.40 = (f32[8,176,128]{2,1,0:T(8,128)S(1)}, f32[1,176,128]{2,1,0:T(8,128)S(1)}) custom-call(s32[3]{0:T(128)S(1)} %pad_add_fusion.1.flags, s32[1,512]{1,0:T(1,128)S(1)} %bitcast.9, bf16[576,1536]{1,0:T(8,128)(2,1)S(1)} %get-tuple-element.31.weighted, f32[4,48,128]{2,1,0:T(8,128)S(1)} %get-tuple-element.32.row_feature, ...), custom_call_target="tpu_custom_call" | custom-call | flops 339738624 | bytes 4000000 | tf_op jit(solution)/shard_map/pallas_call | solution.py:502
  55.2 3.2 %collective-permute-start.7 = (f32[8,176,128]{2,1,0:T(8,128)S(1)}, f32[8,176,128]{2,1,0:T(8,128)S(1)}, u32[]{:S(2)}, u32[]{:S(2)}) collective-permute-start(f32[8,176,128]{2,1,0:T(8,128)S(1)} %get-tuple-element.34), channel_id=1, source_target_pairs={{0,1},{1,0},{2,3},{3,2},{4,5},{5,4},{6,7},{7,6},{8,9},{9,8},{10,11... | collective-permute-start | bytes 2162696 | tf_op jit(solution)/shard_map/ppermute | solution.py:511
  58.5 1.8 %collective-permute-done.7.taken = f32[8,176,128]{2,1,0:T(8,128)S(1)} collective-permute-done((f32[8,176,128]{2,1,0:T(8,128)S(1)}, f32[8,176,128]{2,1,0:T(8,128)S(1)}, u32[]{:S(2)}, u32[]{:S(2)}) %collective-permute-start.7) | collective-permute-done | bytes 720928 | tf_op jit(solution)/shard_map/ppermute | solution.py:511
  60.2 1.0 shard_map.41
  61.2 5.4 %all-to-all-start = ((f32[8,176,128]{2,1,0:T(8,128)}), f32[8,176,128]{2,1,0:T(8,128)S(1)}, u32[]{:S(2)}, u32[]{:S(2)}) async-start(f32[8,176,128]{2,1,0:T(8,128)} %shard_map.41), calls=%async_computation | async-start | bytes 1441792 | tf_op jit(solution)/shard_map/all_to_all | solution.py:520
  66.6 1.3 %dynamic_slice.3 = s32[1]{0:T(128)} dynamic-slice(s32[512]{0:T(512)} %constant.70.clone, s32[]{:T(128)S(6)} %select_n.34), dynamic_slice_sizes={1} | dynamic-slice | bytes 12 | tf_op jit(solution)/shard_map/dynamic_slice | solution.py:425
  69.2 0.1 pad_add_fusion.flags
  69.3 7.4 %all-to-all-done.parts = f32[8,176,128]{2,1,0:T(8,128)S(1)} async-done(((f32[8,176,128]{2,1,0:T(8,128)}), f32[8,176,128]{2,1,0:T(8,128)S(1)}, u32[]{:S(2)}, u32[]{:S(2)}) %all-to-all-start) | async-done | bytes 720928 | tf_op jit(solution)/shard_map/all_to_all | solution.py:520
  76.6 1.5 %shard_map.42 = (f32[24,128]{1,0:T(8,128)S(1)}, f32[24,128]{1,0:T(8,128)S(1)}) custom-call(s32[2]{0:T(128)S(1)} %pad_add_fusion.flags, f32[8,176,128]{2,1,0:T(8,128)S(1)} %all-to-all-done.parts), custom_call_target="tpu_custom_call" | custom-call | tf_op jit(solution)/shard_map/pallas_call | solution.py:523
  78.2 9.5 %collective-permute-start.8 = (f32[24,128]{1,0:T(8,128)S(1)}, f32[24,128]{1,0:T(8,128)S(1)}, u32[]{:S(2)}, u32[]{:S(2)}) collective-permute-start(f32[24,128]{1,0:T(8,128)S(1)} %get-tuple-element.35), channel_id=1, source_target_pairs={{0,464},{1,64},{2,320},{3,322},{4,38},{5,209},{6,70},{7,210},{8,29... | collective-permute-start | bytes 36872 | tf_op jit(solution)/shard_map/ppermute | solution.py:531
  87.7 1.9 %collective-permute-start.9 = (f32[24,128]{1,0:T(8,128)S(1)}, f32[24,128]{1,0:T(8,128)S(1)}, u32[]{:S(2)}, u32[]{:S(2)}) collective-permute-start(f32[24,128]{1,0:T(8,128)S(1)} %get-tuple-element.36), channel_id=1, source_target_pairs={{0,14},{1,2},{2,10},{3,74},{4,193},{5,38},{6,194},{7,70},{8,217},{... | collective-permute-start | bytes 36872 | tf_op jit(solution)/shard_map/ppermute | solution.py:530
  90.3 0.0 collective-permute-done.8
  90.3 5.8 %collective-permute-done.9 = f32[24,128]{1,0:T(8,128)S(1)} collective-permute-done((f32[24,128]{1,0:T(8,128)S(1)}, f32[24,128]{1,0:T(8,128)S(1)}, u32[]{:S(2)}, u32[]{:S(2)}) %collective-permute-start.9) | collective-permute-done | bytes 12320 | tf_op jit(solution)/shard_map/ppermute | solution.py:530
  96.0 0.1 fusion
  96.1 0.7 maximum_maximum_fusion
  (1 shorter events, 0.0 us)
Async XLA Ops:
  0.0 23.9 %collective-permute-start.2 = (f32[144,512]{1,0:T(8,128)}, f32[144,512]{1,0:T(8,128)S(1)}, u32[]{:S(2)}, u32[]{:S(2)}) collective-permute-start(f32[144,512]{1,0:T(8,128)} %bitcast.10), channel_id=1, source_target_pairs={{32,0},{48,16},{64,32},{80,48},{96,64},{112,80},{128,96},{144,112}... | collective-permute-start | bytes 884744 | tf_op jit(solution)/shard_map/ppermute | solution.py:433
  11.6 25.9 %collective-permute-start = (f32[144,512]{1,0:T(8,128)}, f32[144,512]{1,0:T(8,128)S(1)}, u32[]{:S(2)}, u32[]{:S(2)}) collective-permute-start(f32[144,512]{1,0:T(8,128)} %bitcast.11), channel_id=1, source_target_pairs={{208,0},{224,16},{240,32},{0,48},{16,64},{32,80},{48,96},{64,112},... | collective-permute-start | bytes 884744 | tf_op jit(solution)/shard_map/ppermute | solution.py:433
  23.9 18.0 %collective-permute-start.5 = (f32[144,512]{1,0:T(8,128)S(1)}, f32[144,512]{1,0:T(8,128)S(1)}, u32[]{:S(2)}, u32[]{:S(2)}) collective-permute-start(f32[144,512]{1,0:T(8,128)S(1)} %collective-permute-done.2.plus2), channel_id=1, source_target_pairs={{32,0},{48,16},{64,32},{80,48},{96,64},{112,80},{128,96},{144,112}... | collective-permute-start | bytes 884744 | tf_op jit(solution)/shard_map/ppermute | solution.py:433
  30.0 14.8 %collective-permute-start.3 = (f32[144,512]{1,0:T(8,128)S(1)}, f32[144,512]{1,0:T(8,128)S(1)}, u32[]{:S(2)}, u32[]{:S(2)}) collective-permute-start(f32[144,512]{1,0:T(8,128)S(1)} %collective-permute-done.2.plus2), channel_id=1, source_target_pairs={{256,0},{272,16},{288,32},{304,48},{320,64},{336,80},{352,96},{368... | collective-permute-start | bytes 884744 | tf_op jit(solution)/shard_map/ppermute | solution.py:436
  37.5 10.0 %collective-permute-start.4 = (f32[144,512]{1,0:T(8,128)S(1)}, f32[144,512]{1,0:T(8,128)S(1)}, u32[]{:S(2)}, u32[]{:S(2)}) collective-permute-start(f32[144,512]{1,0:T(8,128)S(1)} %collective-permute-done.minus3), channel_id=1, source_target_pairs={{256,0},{272,16},{288,32},{304,48},{320,64},{336,80},{352,96},{368... | collective-permute-start | bytes 884744 | tf_op jit(solution)/shard_map/ppermute | solution.py:436
  40.0 10.9 %collective-permute-start.1 = (f32[144,512]{1,0:T(8,128)S(1)}, f32[144,512]{1,0:T(8,128)S(1)}, u32[]{:S(2)}, u32[]{:S(2)}) collective-permute-start(f32[144,512]{1,0:T(8,128)S(1)} %collective-permute-done.minus3), channel_id=1, source_target_pairs={{240,0},{0,16},{16,32},{32,48},{48,64},{64,80},{80,96},{96,112},{1... | collective-permute-start | bytes 884744 | tf_op jit(solution)/shard_map/ppermute | solution.py:433
  41.9 11.8 %collective-permute-start.6 = (f32[144,512]{1,0:T(8,128)S(1)}, f32[144,512]{1,0:T(8,128)S(1)}, u32[]{:S(2)}, u32[]{:S(2)}) collective-permute-start(f32[144,512]{1,0:T(8,128)S(1)} %collective-permute-done.5.plus4), channel_id=1, source_target_pairs={{256,0},{272,16},{288,32},{304,48},{320,64},{336,80},{352,96},{368... | collective-permute-start | bytes 884744 | tf_op jit(solution)/shard_map/ppermute | solution.py:436
  44.8 0.7 copy-start
  45.5 1.0 copy-start.1
  55.2 5.0 %collective-permute-start.7 = (f32[8,176,128]{2,1,0:T(8,128)S(1)}, f32[8,176,128]{2,1,0:T(8,128)S(1)}, u32[]{:S(2)}, u32[]{:S(2)}) collective-permute-start(f32[8,176,128]{2,1,0:T(8,128)S(1)} %get-tuple-element.34), channel_id=1, source_target_pairs={{0,1},{1,0},{2,3},{3,2},{4,5},{5,4},{6,7},{7,6},{8,9},{9,8},{10,11... | collective-permute-start | bytes 2162696 | tf_op jit(solution)/shard_map/ppermute | solution.py:511
  61.2 15.4 %all-to-all-start = ((f32[8,176,128]{2,1,0:T(8,128)}), f32[8,176,128]{2,1,0:T(8,128)S(1)}, u32[]{:S(2)}, u32[]{:S(2)}) async-start(f32[8,176,128]{2,1,0:T(8,128)} %shard_map.41), calls=%async_computation | async-start | bytes 1441792 | tf_op jit(solution)/shard_map/all_to_all | solution.py:520
  78.2 12.1 %collective-permute-start.8 = (f32[24,128]{1,0:T(8,128)S(1)}, f32[24,128]{1,0:T(8,128)S(1)}, u32[]{:S(2)}, u32[]{:S(2)}) collective-permute-start(f32[24,128]{1,0:T(8,128)S(1)} %get-tuple-element.35), channel_id=1, source_target_pairs={{0,464},{1,64},{2,320},{3,322},{4,38},{5,209},{6,70},{7,210},{8,29... | collective-permute-start | bytes 36872 | tf_op jit(solution)/shard_map/ppermute | solution.py:531
  87.7 8.3 %collective-permute-start.9 = (f32[24,128]{1,0:T(8,128)S(1)}, f32[24,128]{1,0:T(8,128)S(1)}, u32[]{:S(2)}, u32[]{:S(2)}) collective-permute-start(f32[24,128]{1,0:T(8,128)S(1)} %get-tuple-element.36), channel_id=1, source_target_pairs={{0,14},{1,2},{2,10},{3,74},{4,193},{5,38},{6,194},{7,70},{8,217},{... | collective-permute-start | bytes 36872 | tf_op jit(solution)/shard_map/ppermute | solution.py:530

commit v14 on v11

--- a/solution.py
+++ b/solution.py
@@ -102,11 +102,21 @@
     assert len(at) == len(ends) and all(len(v) == 2 for v in at.values())
     swapped = [None] * len(ends)
     for seed in range(len(ends)):
-        device, enter = seed, 0
+        ring, device, enter = [], seed, 0
         while swapped[device] is None:
             swapped[device] = enter
+            ring.append(device)
             node = place(ends[device][1 - enter])
             device, enter = [e for e in at[node] if e != (device, 1 - enter)][0]
+        cost = [0, 0]
+        for d in ring:
+            column, z = divmod(d // SIDE, SIDE)
+            far = [distance(column, z, d % SIDE // 2, ends[d][e]) for e in (swapped[d], 1 - swapped[d])]
+            cost[0] += 2 ** (2 * far[0] + far[1])
+            cost[1] += 2 ** (2 * far[1] + far[0])
+        if cost[1] < cost[0]:
+            for d in ring:
+                swapped[d] = 1 - swapped[d]
     first = [place(ends[d][swapped[d]]) for d in range(len(ends))]
     second = [place(ends[d][1 - swapped[d]]) for d in range(len(ends))]
     assert len(set(first)) == len(set(second)) == len(ends)

time: 98.5 us -> 98.5 us (level)
  no operation moved by 1% of the time
where the time goes in v14:
time: 98.5 us; the launch traced here: 96.8 us
  starting transfers between devices  49.3 us (50%)
  waiting for transfers between devices  32.1 us (33%)
  Pallas kernels  9.51 us (10%)
  local copies, waits for them, and re-layouts  2.98 us (3%)
  between operations  2.12 us (2%)
    ppermute x4, starting transfers between devices, along(): return lax.ppermute(block, 'frame', route)  21.5 us
    ppermute x4, waiting for transfers between devices, along(): return lax.ppermute(block, 'frame', route)  16.4 us
    ppermute x1, starting transfers between devices, on_device(): two = lax.ppermute(two, ('frame', 'atom'), list(enumerate(second)))  9.48 us
    ppermute x3, starting transfers between devices, across(): lax.ppermute(block, 'frame', [((f + SIDE) % (2 * SIDE), f) for f in range...  7.73 us
    all_to_all x1, waiting for transfers between devices, on_device(): lax.all_to_all(merged, ('frame', 'atom'), 0, 0, axis_index_groups=groups,...  7.37 us
    ppermute x1, waiting for transfers between devices, on_device(): one = lax.ppermute(one, ('frame', 'atom'), list(enumerate(first)))  5.76 us
    all_to_all x1, starting transfers between devices, on_device(): lax.all_to_all(merged, ('frame', 'atom'), 0, 0, axis_index_groups=groups,...  5.43 us
    ppermute x1, starting transfers between devices, on_device(): taken = lax.ppermute(send, 'atom', [(a, a ^ 1) for a in range(SIDE)])  3.24 us
  transfers between devices with their start and end apart: 11, of which 7 were waited for; matrix products, arithmetic and copies ran while one was open for 1% of the time, Pallas kernels for 6%

profile of v14, /device:TPU:7, one launch (start us, length us, event | category | flops | bytes accessed | tf_op | source)
XLA Modules:
  0.0 96.8 jit_solution(5840640494787315978)
XLA Ops:
  0.0 11.6 %collective-permute-start.2 = (f32[144,512]{1,0:T(8,128)}, f32[144,512]{1,0:T(8,128)S(1)}, u32[]{:S(2)}, u32[]{:S(2)}) collective-permute-start(f32[144,512]{1,0:T(8,128)} %bitcast.10), channel_id=1, source_target_pairs={{32,0},{48,16},{64,32},{80,48},{96,64},{112,80},{128,96},{144,112}... | collective-permute-start | bytes 884744 | tf_op jit(solution)/shard_map/ppermute | solution.py:442
  11.6 1.9 %collective-permute-start = (f32[144,512]{1,0:T(8,128)}, f32[144,512]{1,0:T(8,128)S(1)}, u32[]{:S(2)}, u32[]{:S(2)}) collective-permute-start(f32[144,512]{1,0:T(8,128)} %bitcast.11), channel_id=1, source_target_pairs={{208,0},{224,16},{240,32},{0,48},{16,64},{32,80},{48,96},{64,112},... | collective-permute-start | bytes 884744 | tf_op jit(solution)/shard_map/ppermute | solution.py:442
  13.5 10.4 %collective-permute-done.2.plus2 = f32[144,512]{1,0:T(8,128)S(1)} collective-permute-done((f32[144,512]{1,0:T(8,128)}, f32[144,512]{1,0:T(8,128)S(1)}, u32[]{:S(2)}, u32[]{:S(2)}) %collective-permute-start.2) | collective-permute-done | bytes 294944 | tf_op jit(solution)/shard_map/ppermute | solution.py:442
  23.9 6.1 %collective-permute-start.5 = (f32[144,512]{1,0:T(8,128)S(1)}, f32[144,512]{1,0:T(8,128)S(1)}, u32[]{:S(2)}, u32[]{:S(2)}) collective-permute-start(f32[144,512]{1,0:T(8,128)S(1)} %collective-permute-done.2.plus2), channel_id=1, source_target_pairs={{32,0},{48,16},{64,32},{80,48},{96,64},{112,80},{128,96},{144,112}... | collective-permute-start | bytes 884744 | tf_op jit(solution)/shard_map/ppermute | solution.py:442
  30.0 2.5 %collective-permute-start.3 = (f32[144,512]{1,0:T(8,128)S(1)}, f32[144,512]{1,0:T(8,128)S(1)}, u32[]{:S(2)}, u32[]{:S(2)}) collective-permute-start(f32[144,512]{1,0:T(8,128)S(1)} %collective-permute-done.2.plus2), channel_id=1, source_target_pairs={{256,0},{272,16},{288,32},{304,48},{320,64},{336,80},{352,96},{368... | collective-permute-start | bytes 884744 | tf_op jit(solution)/shard_map/ppermute | solution.py:445
  32.5 5.0 %collective-permute-done.minus3 = f32[144,512]{1,0:T(8,128)S(1)} collective-permute-done((f32[144,512]{1,0:T(8,128)}, f32[144,512]{1,0:T(8,128)S(1)}, u32[]{:S(2)}, u32[]{:S(2)}) %collective-permute-start) | collective-permute-done | bytes 294944 | tf_op jit(solution)/shard_map/ppermute | solution.py:442
  37.5 2.4 %collective-permute-start.4 = (f32[144,512]{1,0:T(8,128)S(1)}, f32[144,512]{1,0:T(8,128)S(1)}, u32[]{:S(2)}, u32[]{:S(2)}) collective-permute-start(f32[144,512]{1,0:T(8,128)S(1)} %collective-permute-done.minus3), channel_id=1, source_target_pairs={{256,0},{272,16},{288,32},{304,48},{320,64},{336,80},{352,96},{368... | collective-permute-start | bytes 884744 | tf_op jit(solution)/shard_map/ppermute | solution.py:445
  40.0 1.9 %collective-permute-start.1 = (f32[144,512]{1,0:T(8,128)S(1)}, f32[144,512]{1,0:T(8,128)S(1)}, u32[]{:S(2)}, u32[]{:S(2)}) collective-permute-start(f32[144,512]{1,0:T(8,128)S(1)} %collective-permute-done.minus3), channel_id=1, source_target_pairs={{240,0},{0,16},{16,32},{32,48},{48,64},{64,80},{80,96},{96,112},{1... | collective-permute-start | bytes 884744 | tf_op jit(solution)/shard_map/ppermute | solution.py:442
  41.9 0.0 collective-permute-done.5.plus4
  41.9 2.8 %collective-permute-start.6 = (f32[144,512]{1,0:T(8,128)S(1)}, f32[144,512]{1,0:T(8,128)S(1)}, u32[]{:S(2)}, u32[]{:S(2)}) collective-permute-start(f32[144,512]{1,0:T(8,128)S(1)} %collective-permute-done.5.plus4), channel_id=1, source_target_pairs={{256,0},{272,16},{288,32},{304,48},{320,64},{336,80},{352,96},{368... | collective-permute-start | bytes 884744 | tf_op jit(solution)/shard_map/ppermute | solution.py:445
  44.8 0.1 pad_add_fusion.1.flags
  44.8 0.0 collective-permute-done.3.other2
  44.8 0.0 copy-start
  44.8 0.7 copy-done
  45.5 0.0 copy-start.1
  45.5 1.0 copy-done.1
  46.5 1.0 %shard_map.37 = (bf16[576,1536]{1,0:T(8,128)(2,1)S(1)}, f32[4,48,128]{2,1,0:T(8,128)S(1)}, bf16[2,256,1536]{2,1,0:T(8,128)(2,1)S(1)}, f32[2,48,128]{2,1,0:T(8,128)S(1)}) custom-call(s32[3]{0:T(128)S(1)} %pad_add_fusion.1.flags, s32[1,512]{1,0:T(1,128)S(1)} %bitcast.6, f32[144,512]{1,0:T(8,128)S(1)} %bitcast.12, f32[144,512]{1,0:T(8,128)S(1)} %collective-permute-done.2.plus2, ...), custom_call_target="tpu_custom_call" | custom-call | flops 1019215872 | bytes 4000000 | tf_op jit(solution)/shard_map/pallas_call | solution.py:478
  47.5 0.0 collective-permute-done.4.other3
  47.5 2.4 %shard_map.38 = (f32[16,176,128]{2,1,0:T(8,128)S(1)}, bf16[576,1536]{1,0:T(8,128)(2,1)S(1)}, f32[4,48,128]{2,1,0:T(8,128)S(1)}, bf16[3,256,1536]{2,1,0:T(8,128)(2,1)S(1)}, f32[3,48,128]{2,1,0:T(8,128)S(1)}) custom-call(s32[3]{0:T(128)S(1)} %pad_add_fusion.1.flags, s32[1,512]{1,0:T(1,128)S(1)} %bitcast.7, ...), custom_call_target="tpu_custom_call", output_to_operand_aliasing={{1}: (7, {}), {2}: (8, {})} | custom-call | flops 1019215872 | bytes 4000000 | tf_op jit(solution)/shard_map/pallas_call | solution.py:490
  49.9 1.0 %collective-permute-done.1.minus4 = f32[144,512]{1,0:T(8,128)S(1)} collective-permute-done((f32[144,512]{1,0:T(8,128)S(1)}, f32[144,512]{1,0:T(8,128)S(1)}, u32[]{:S(2)}, u32[]{:S(2)}) %collective-permute-start.1) | collective-permute-done | bytes 294944 | tf_op jit(solution)/shard_map/ppermute | solution.py:442
  50.9 2.2 %shard_map.39 = (f32[16,176,128]{2,1,0:T(8,128)S(1)}, bf16[576,1536]{1,0:T(8,128)(2,1)S(1)}, f32[4,48,128]{2,1,0:T(8,128)S(1)}) custom-call(s32[3]{0:T(128)S(1)} %pad_add_fusion.1.flags, s32[1,512]{1,0:T(1,128)S(1)} %bitcast.8, f32[144,512]{1,0:T(8,128)S(1)} %collective-permute-done.1.minus4, ...), custom_call_target="tpu_custom_call", output_to_operand_aliasing={{0}: (7, {}), {1}: (8, {}), {2}: (9, {})} | custom-call | flops 679477248 | bytes 4000000 | tf_op jit(solution)/shard_map/pallas_call | solution.py:499
  53.0 0.7 collective-permute-done.6.other4
  53.8 1.4 %shard_map.40 = (f32[8,176,128]{2,1,0:T(8,128)S(1)}, f32[1,176,128]{2,1,0:T(8,128)S(1)}) custom-call(s32[3]{0:T(128)S(1)} %pad_add_fusion.1.flags, s32[1,512]{1,0:T(1,128)S(1)} %bitcast.9, bf16[576,1536]{1,0:T(8,128)(2,1)S(1)} %get-tuple-element.31.weighted, f32[4,48,128]{2,1,0:T(8,128)S(1)} %get-tuple-element.32.row_feature, ...), custom_call_target="tpu_custom_call" | custom-call | flops 339738624 | bytes 4000000 | tf_op jit(solution)/shard_map/pallas_call | solution.py:511
  55.2 3.2 %collective-permute-start.7 = (f32[8,176,128]{2,1,0:T(8,128)S(1)}, f32[8,176,128]{2,1,0:T(8,128)S(1)}, u32[]{:S(2)}, u32[]{:S(2)}) collective-permute-start(f32[8,176,128]{2,1,0:T(8,128)S(1)} %get-tuple-element.34), channel_id=1, source_target_pairs={{0,1},{1,0},{2,3},{3,2},{4,5},{5,4},{6,7},{7,6},{8,9},{9,8},{10,11... | collective-permute-start | bytes 2162696 | tf_op jit(solution)/shard_map/ppermute | solution.py:520
  58.5 1.8 %collective-permute-done.7.taken = f32[8,176,128]{2,1,0:T(8,128)S(1)} collective-permute-done((f32[8,176,128]{2,1,0:T(8,128)S(1)}, f32[8,176,128]{2,1,0:T(8,128)S(1)}, u32[]{:S(2)}, u32[]{:S(2)}) %collective-permute-start.7) | collective-permute-done | bytes 720928 | tf_op jit(solution)/shard_map/ppermute | solution.py:520
  60.2 1.0 shard_map.41
  61.2 5.4 %all-to-all-start = ((f32[8,176,128]{2,1,0:T(8,128)}), f32[8,176,128]{2,1,0:T(8,128)S(1)}, u32[]{:S(2)}, u32[]{:S(2)}) async-start(f32[8,176,128]{2,1,0:T(8,128)} %shard_map.41), calls=%async_computation | async-start | bytes 1441792 | tf_op jit(solution)/shard_map/all_to_all | solution.py:529
  66.6 1.3 %dynamic_slice.3 = s32[1]{0:T(128)} dynamic-slice(s32[512]{0:T(512)} %constant.70.clone, s32[]{:T(128)S(6)} %select_n.34), dynamic_slice_sizes={1} | dynamic-slice | bytes 12 | tf_op jit(solution)/shard_map/dynamic_slice | solution.py:434
  69.2 0.1 pad_add_fusion.flags
  69.3 7.4 %all-to-all-done.parts = f32[8,176,128]{2,1,0:T(8,128)S(1)} async-done(((f32[8,176,128]{2,1,0:T(8,128)}), f32[8,176,128]{2,1,0:T(8,128)S(1)}, u32[]{:S(2)}, u32[]{:S(2)}) %all-to-all-start) | async-done | bytes 720928 | tf_op jit(solution)/shard_map/all_to_all | solution.py:529
  76.6 1.6 %shard_map.42 = (f32[24,128]{1,0:T(8,128)S(1)}, f32[24,128]{1,0:T(8,128)S(1)}) custom-call(s32[2]{0:T(128)S(1)} %pad_add_fusion.flags, f32[8,176,128]{2,1,0:T(8,128)S(1)} %all-to-all-done.parts), custom_call_target="tpu_custom_call" | custom-call | tf_op jit(solution)/shard_map/pallas_call | solution.py:532
  78.2 9.5 %collective-permute-start.8 = (f32[24,128]{1,0:T(8,128)S(1)}, f32[24,128]{1,0:T(8,128)S(1)}, u32[]{:S(2)}, u32[]{:S(2)}) collective-permute-start(f32[24,128]{1,0:T(8,128)S(1)} %get-tuple-element.35), channel_id=1, source_target_pairs={{0,14},{1,2},{2,320},{3,74},{4,193},{5,38},{6,194},{7,70},{8,217},... | collective-permute-start | bytes 36872 | tf_op jit(solution)/shard_map/ppermute | solution.py:540
  87.7 1.9 %collective-permute-start.9 = (f32[24,128]{1,0:T(8,128)S(1)}, f32[24,128]{1,0:T(8,128)S(1)}, u32[]{:S(2)}, u32[]{:S(2)}) collective-permute-start(f32[24,128]{1,0:T(8,128)S(1)} %get-tuple-element.36), channel_id=1, source_target_pairs={{0,464},{1,64},{2,10},{3,322},{4,38},{5,209},{6,70},{7,210},{8,294... | collective-permute-start | bytes 36872 | tf_op jit(solution)/shard_map/ppermute | solution.py:539
  90.3 0.0 collective-permute-done.8
  90.3 5.8 %collective-permute-done.9 = f32[24,128]{1,0:T(8,128)S(1)} collective-permute-done((f32[24,128]{1,0:T(8,128)S(1)}, f32[24,128]{1,0:T(8,128)S(1)}, u32[]{:S(2)}, u32[]{:S(2)}) %collective-permute-start.9) | collective-permute-done | bytes 12320 | tf_op jit(solution)/shard_map/ppermute | solution.py:539
  96.1 0.1 fusion
  96.1 0.7 maximum_maximum_fusion
  (1 shorter events, 0.0 us)
Async XLA Ops:
  0.0 23.9 %collective-permute-start.2 = (f32[144,512]{1,0:T(8,128)}, f32[144,512]{1,0:T(8,128)S(1)}, u32[]{:S(2)}, u32[]{:S(2)}) collective-permute-start(f32[144,512]{1,0:T(8,128)} %bitcast.10), channel_id=1, source_target_pairs={{32,0},{48,16},{64,32},{80,48},{96,64},{112,80},{128,96},{144,112}... | collective-permute-start | bytes 884744 | tf_op jit(solution)/shard_map/ppermute | solution.py:442
  11.6 25.9 %collective-permute-start = (f32[144,512]{1,0:T(8,128)}, f32[144,512]{1,0:T(8,128)S(1)}, u32[]{:S(2)}, u32[]{:S(2)}) collective-permute-start(f32[144,512]{1,0:T(8,128)} %bitcast.11), channel_id=1, source_target_pairs={{208,0},{224,16},{240,32},{0,48},{16,64},{32,80},{48,96},{64,112},... | collective-permute-start | bytes 884744 | tf_op jit(solution)/shard_map/ppermute | solution.py:442
  23.9 18.0 %collective-permute-start.5 = (f32[144,512]{1,0:T(8,128)S(1)}, f32[144,512]{1,0:T(8,128)S(1)}, u32[]{:S(2)}, u32[]{:S(2)}) collective-permute-start(f32[144,512]{1,0:T(8,128)S(1)} %collective-permute-done.2.plus2), channel_id=1, source_target_pairs={{32,0},{48,16},{64,32},{80,48},{96,64},{112,80},{128,96},{144,112}... | collective-permute-start | bytes 884744 | tf_op jit(solution)/shard_map/ppermute | solution.py:442
  30.0 14.8 %collective-permute-start.3 = (f32[144,512]{1,0:T(8,128)S(1)}, f32[144,512]{1,0:T(8,128)S(1)}, u32[]{:S(2)}, u32[]{:S(2)}) collective-permute-start(f32[144,512]{1,0:T(8,128)S(1)} %collective-permute-done.2.plus2), channel_id=1, source_target_pairs={{256,0},{272,16},{288,32},{304,48},{320,64},{336,80},{352,96},{368... | collective-permute-start | bytes 884744 | tf_op jit(solution)/shard_map/ppermute | solution.py:445
  37.5 10.0 %collective-permute-start.4 = (f32[144,512]{1,0:T(8,128)S(1)}, f32[144,512]{1,0:T(8,128)S(1)}, u32[]{:S(2)}, u32[]{:S(2)}) collective-permute-start(f32[144,512]{1,0:T(8,128)S(1)} %collective-permute-done.minus3), channel_id=1, source_target_pairs={{256,0},{272,16},{288,32},{304,48},{320,64},{336,80},{352,96},{368... | collective-permute-start | bytes 884744 | tf_op jit(solution)/shard_map/ppermute | solution.py:445
  40.0 10.9 %collective-permute-start.1 = (f32[144,512]{1,0:T(8,128)S(1)}, f32[144,512]{1,0:T(8,128)S(1)}, u32[]{:S(2)}, u32[]{:S(2)}) collective-permute-start(f32[144,512]{1,0:T(8,128)S(1)} %collective-permute-done.minus3), channel_id=1, source_target_pairs={{240,0},{0,16},{16,32},{32,48},{48,64},{64,80},{80,96},{96,112},{1... | collective-permute-start | bytes 884744 | tf_op jit(solution)/shard_map/ppermute | solution.py:442
  41.9 11.8 %collective-permute-start.6 = (f32[144,512]{1,0:T(8,128)S(1)}, f32[144,512]{1,0:T(8,128)S(1)}, u32[]{:S(2)}, u32[]{:S(2)}) collective-permute-start(f32[144,512]{1,0:T(8,128)S(1)} %collective-permute-done.5.plus4), channel_id=1, source_target_pairs={{256,0},{272,16},{288,32},{304,48},{320,64},{336,80},{352,96},{368... | collective-permute-start | bytes 884744 | tf_op jit(solution)/shard_map/ppermute | solution.py:445
  44.8 0.7 copy-start
  45.5 1.0 copy-start.1
  55.2 5.0 %collective-permute-start.7 = (f32[8,176,128]{2,1,0:T(8,128)S(1)}, f32[8,176,128]{2,1,0:T(8,128)S(1)}, u32[]{:S(2)}, u32[]{:S(2)}) collective-permute-start(f32[8,176,128]{2,1,0:T(8,128)S(1)} %get-tuple-element.34), channel_id=1, source_target_pairs={{0,1},{1,0},{2,3},{3,2},{4,5},{5,4},{6,7},{7,6},{8,9},{9,8},{10,11... | collective-permute-start | bytes 2162696 | tf_op jit(solution)/shard_map/ppermute | solution.py:520
  61.2 15.4 %all-to-all-start = ((f32[8,176,128]{2,1,0:T(8,128)}), f32[8,176,128]{2,1,0:T(8,128)S(1)}, u32[]{:S(2)}, u32[]{:S(2)}) async-start(f32[8,176,128]{2,1,0:T(8,128)} %shard_map.41), calls=%async_computation | async-start | bytes 1441792 | tf_op jit(solution)/shard_map/all_to_all | solution.py:529
  78.2 12.1 %collective-permute-start.8 = (f32[24,128]{1,0:T(8,128)S(1)}, f32[24,128]{1,0:T(8,128)S(1)}, u32[]{:S(2)}, u32[]{:S(2)}) collective-permute-start(f32[24,128]{1,0:T(8,128)S(1)} %get-tuple-element.35), channel_id=1, source_target_pairs={{0,14},{1,2},{2,320},{3,74},{4,193},{5,38},{6,194},{7,70},{8,217},... | collective-permute-start | bytes 36872 | tf_op jit(solution)/shard_map/ppermute | solution.py:540
  87.7 8.3 %collective-permute-start.9 = (f32[24,128]{1,0:T(8,128)S(1)}, f32[24,128]{1,0:T(8,128)S(1)}, u32[]{:S(2)}, u32[]{:S(2)}) collective-permute-start(f32[24,128]{1,0:T(8,128)S(1)} %get-tuple-element.36), channel_id=1, source_target_pairs={{0,464},{1,64},{2,10},{3,322},{4,38},{5,209},{6,70},{7,210},{8,294... | collective-permute-start | bytes 36872 | tf_op jit(solution)/shard_map/ppermute | solution.py:539

commit v15 on v14

--- a/solution.py
+++ b/solution.py
@@ -112,8 +112,8 @@
         for d in ring:
             column, z = divmod(d // SIDE, SIDE)
             far = [distance(column, z, d % SIDE // 2, ends[d][e]) for e in (swapped[d], 1 - swapped[d])]
-            cost[0] += 2 ** (2 * far[0] + far[1])
-            cost[1] += 2 ** (2 * far[1] + far[0])
+            cost[0] += 2 ** (far[0] + 2 * far[1])
+            cost[1] += 2 ** (far[1] + 2 * far[0])
         if cost[1] < cost[0]:
             for d in ring:
                 swapped[d] = 1 - swapped[d]

time: 98.5 us -> 100 us (1.015); the launches traced: 96.8 us -> 99.5 us
  waiting for transfers between devices: 32.1 us -> 34.8 us
    ppermute x1, waiting for transfers between devices: 5.76 us -> 8.44 us  [on_device(): one = lax.ppermute(one, ('frame', 'atom'), list(enumerate(first)))]
where the time goes in v15:
time: 100 us; the launch traced here: 99.5 us
  starting transfers between devices  49.3 us (49%)
  waiting for transfers between devices  34.8 us (35%)
  Pallas kernels  9.51 us (10%)
  local copies, waits for them, and re-layouts  2.98 us (3%)
  between operations  2.12 us (2%)
    ppermute x4, starting transfers between devices, along(): return lax.ppermute(block, 'frame', route)  21.5 us
    ppermute x4, waiting for transfers between devices, along(): return lax.ppermute(block, 'frame', route)  16.4 us
    ppermute x1, starting transfers between devices, on_device(): two = lax.ppermute(two, ('frame', 'atom'), list(enumerate(second)))  9.48 us
    ppermute x1, waiting for transfers between devices, on_device(): one = lax.ppermute(one, ('frame', 'atom'), list(enumerate(first)))  8.44 us
    ppermute x3, starting transfers between devices, across(): lax.ppermute(block, 'frame', [((f + SIDE) % (2 * SIDE), f) for f in range...  7.73 us
    all_to_all x1, waiting for transfers between devices, on_device(): lax.all_to_all(merged, ('frame', 'atom'), 0, 0, axis_index_groups=groups,...  7.37 us
    all_to_all x1, starting transfers between devices, on_device(): lax.all_to_all(merged, ('frame', 'atom'), 0, 0, axis_index_groups=groups,...  5.43 us
    ppermute x1, starting transfers between devices, on_device(): taken = lax.ppermute(send, 'atom', [(a, a ^ 1) for a in range(SIDE)])  3.24 us
  transfers between devices with their start and end apart: 11, of which 7 were waited for; matrix products, arithmetic and copies ran while one was open for 1% of the time, Pallas kernels for 6%

profile of v15, /device:TPU:7, one launch (start us, length us, event | category | flops | bytes accessed | tf_op | source)
XLA Modules:
  0.0 99.5 jit_solution(3374601181877157)
XLA Ops:
  0.0 11.6 %collective-permute-start.2 = (f32[144,512]{1,0:T(8,128)}, f32[144,512]{1,0:T(8,128)S(1)}, u32[]{:S(2)}, u32[]{:S(2)}) collective-permute-start(f32[144,512]{1,0:T(8,128)} %bitcast.10), channel_id=1, source_target_pairs={{32,0},{48,16},{64,32},{80,48},{96,64},{112,80},{128,96},{144,112}... | collective-permute-start | bytes 884744 | tf_op jit(solution)/shard_map/ppermute | solution.py:442
  11.6 1.9 %collective-permute-start = (f32[144,512]{1,0:T(8,128)}, f32[144,512]{1,0:T(8,128)S(1)}, u32[]{:S(2)}, u32[]{:S(2)}) collective-permute-start(f32[144,512]{1,0:T(8,128)} %bitcast.11), channel_id=1, source_target_pairs={{208,0},{224,16},{240,32},{0,48},{16,64},{32,80},{48,96},{64,112},... | collective-permute-start | bytes 884744 | tf_op jit(solution)/shard_map/ppermute | solution.py:442
  13.5 10.4 %collective-permute-done.2.plus2 = f32[144,512]{1,0:T(8,128)S(1)} collective-permute-done((f32[144,512]{1,0:T(8,128)}, f32[144,512]{1,0:T(8,128)S(1)}, u32[]{:S(2)}, u32[]{:S(2)}) %collective-permute-start.2) | collective-permute-done | bytes 294944 | tf_op jit(solution)/shard_map/ppermute | solution.py:442
  23.9 6.1 %collective-permute-start.5 = (f32[144,512]{1,0:T(8,128)S(1)}, f32[144,512]{1,0:T(8,128)S(1)}, u32[]{:S(2)}, u32[]{:S(2)}) collective-permute-start(f32[144,512]{1,0:T(8,128)S(1)} %collective-permute-done.2.plus2), channel_id=1, source_target_pairs={{32,0},{48,16},{64,32},{80,48},{96,64},{112,80},{128,96},{144,112}... | collective-permute-start | bytes 884744 | tf_op jit(solution)/shard_map/ppermute | solution.py:442
  30.0 2.5 %collective-permute-start.3 = (f32[144,512]{1,0:T(8,128)S(1)}, f32[144,512]{1,0:T(8,128)S(1)}, u32[]{:S(2)}, u32[]{:S(2)}) collective-permute-start(f32[144,512]{1,0:T(8,128)S(1)} %collective-permute-done.2.plus2), channel_id=1, source_target_pairs={{256,0},{272,16},{288,32},{304,48},{320,64},{336,80},{352,96},{368... | collective-permute-start | bytes 884744 | tf_op jit(solution)/shard_map/ppermute | solution.py:445
  32.5 5.0 %collective-permute-done.minus3 = f32[144,512]{1,0:T(8,128)S(1)} collective-permute-done((f32[144,512]{1,0:T(8,128)}, f32[144,512]{1,0:T(8,128)S(1)}, u32[]{:S(2)}, u32[]{:S(2)}) %collective-permute-start) | collective-permute-done | bytes 294944 | tf_op jit(solution)/shard_map/ppermute | solution.py:442
  37.5 2.4 %collective-permute-start.4 = (f32[144,512]{1,0:T(8,128)S(1)}, f32[144,512]{1,0:T(8,128)S(1)}, u32[]{:S(2)}, u32[]{:S(2)}) collective-permute-start(f32[144,512]{1,0:T(8,128)S(1)} %collective-permute-done.minus3), channel_id=1, source_target_pairs={{256,0},{272,16},{288,32},{304,48},{320,64},{336,80},{352,96},{368... | collective-permute-start | bytes 884744 | tf_op jit(solution)/shard_map/ppermute | solution.py:445
  40.0 1.9 %collective-permute-start.1 = (f32[144,512]{1,0:T(8,128)S(1)}, f32[144,512]{1,0:T(8,128)S(1)}, u32[]{:S(2)}, u32[]{:S(2)}) collective-permute-start(f32[144,512]{1,0:T(8,128)S(1)} %collective-permute-done.minus3), channel_id=1, source_target_pairs={{240,0},{0,16},{16,32},{32,48},{48,64},{64,80},{80,96},{96,112},{1... | collective-permute-start | bytes 884744 | tf_op jit(solution)/shard_map/ppermute | solution.py:442
  41.9 0.0 collective-permute-done.5.plus4
  41.9 2.8 %collective-permute-start.6 = (f32[144,512]{1,0:T(8,128)S(1)}, f32[144,512]{1,0:T(8,128)S(1)}, u32[]{:S(2)}, u32[]{:S(2)}) collective-permute-start(f32[144,512]{1,0:T(8,128)S(1)} %collective-permute-done.5.plus4), channel_id=1, source_target_pairs={{256,0},{272,16},{288,32},{304,48},{320,64},{336,80},{352,96},{368... | collective-permute-start | bytes 884744 | tf_op jit(solution)/shard_map/ppermute | solution.py:445
  44.8 0.1 pad_add_fusion.1.flags
  44.8 0.0 collective-permute-done.3.other2
  44.8 0.0 copy-start
  44.8 0.7 copy-done
  45.5 0.0 copy-start.1
  45.5 1.0 copy-done.1
  46.5 1.0 %shard_map.37 = (bf16[576,1536]{1,0:T(8,128)(2,1)S(1)}, f32[4,48,128]{2,1,0:T(8,128)S(1)}, bf16[2,256,1536]{2,1,0:T(8,128)(2,1)S(1)}, f32[2,48,128]{2,1,0:T(8,128)S(1)}) custom-call(s32[3]{0:T(128)S(1)} %pad_add_fusion.1.flags, s32[1,512]{1,0:T(1,128)S(1)} %bitcast.6, f32[144,512]{1,0:T(8,128)S(1)} %bitcast.12, f32[144,512]{1,0:T(8,128)S(1)} %collective-permute-done.2.plus2, ...), custom_call_target="tpu_custom_call" | custom-call | flops 1019215872 | bytes 4000000 | tf_op jit(solution)/shard_map/pallas_call | solution.py:478
  47.5 0.0 collective-permute-done.4.other3
  47.5 2.4 %shard_map.38 = (f32[16,176,128]{2,1,0:T(8,128)S(1)}, bf16[576,1536]{1,0:T(8,128)(2,1)S(1)}, f32[4,48,128]{2,1,0:T(8,128)S(1)}, bf16[3,256,1536]{2,1,0:T(8,128)(2,1)S(1)}, f32[3,48,128]{2,1,0:T(8,128)S(1)}) custom-call(s32[3]{0:T(128)S(1)} %pad_add_fusion.1.flags, s32[1,512]{1,0:T(1,128)S(1)} %bitcast.7, ...), custom_call_target="tpu_custom_call", output_to_operand_aliasing={{1}: (7, {}), {2}: (8, {})} | custom-call | flops 1019215872 | bytes 4000000 | tf_op jit(solution)/shard_map/pallas_call | solution.py:490
  49.9 1.0 collective-permute-done.1.minus4
  50.9 2.2 %shard_map.39 = (f32[16,176,128]{2,1,0:T(8,128)S(1)}, bf16[576,1536]{1,0:T(8,128)(2,1)S(1)}, f32[4,48,128]{2,1,0:T(8,128)S(1)}) custom-call(s32[3]{0:T(128)S(1)} %pad_add_fusion.1.flags, s32[1,512]{1,0:T(1,128)S(1)} %bitcast.8, f32[144,512]{1,0:T(8,128)S(1)} %collective-permute-done.1.minus4, ...), custom_call_target="tpu_custom_call", output_to_operand_aliasing={{0}: (7, {}), {1}: (8, {}), {2}: (9, {})} | custom-call | flops 679477248 | bytes 4000000 | tf_op jit(solution)/shard_map/pallas_call | solution.py:499
  53.0 0.7 collective-permute-done.6.other4
  53.8 1.4 %shard_map.40 = (f32[8,176,128]{2,1,0:T(8,128)S(1)}, f32[1,176,128]{2,1,0:T(8,128)S(1)}) custom-call(s32[3]{0:T(128)S(1)} %pad_add_fusion.1.flags, s32[1,512]{1,0:T(1,128)S(1)} %bitcast.9, bf16[576,1536]{1,0:T(8,128)(2,1)S(1)} %get-tuple-element.31.weighted, f32[4,48,128]{2,1,0:T(8,128)S(1)} %get-tuple-element.32.row_feature, ...), custom_call_target="tpu_custom_call" | custom-call | flops 339738624 | bytes 4000000 | tf_op jit(solution)/shard_map/pallas_call | solution.py:511
  55.2 3.2 %collective-permute-start.7 = (f32[8,176,128]{2,1,0:T(8,128)S(1)}, f32[8,176,128]{2,1,0:T(8,128)S(1)}, u32[]{:S(2)}, u32[]{:S(2)}) collective-permute-start(f32[8,176,128]{2,1,0:T(8,128)S(1)} %get-tuple-element.34), channel_id=1, source_target_pairs={{0,1},{1,0},{2,3},{3,2},{4,5},{5,4},{6,7},{7,6},{8,9},{9,8},{10,11... | collective-permute-start | bytes 2162696 | tf_op jit(solution)/shard_map/ppermute | solution.py:520
  58.5 1.8 %collective-permute-done.7.taken = f32[8,176,128]{2,1,0:T(8,128)S(1)} collective-permute-done((f32[8,176,128]{2,1,0:T(8,128)S(1)}, f32[8,176,128]{2,1,0:T(8,128)S(1)}, u32[]{:S(2)}, u32[]{:S(2)}) %collective-permute-start.7) | collective-permute-done | bytes 720928 | tf_op jit(solution)/shard_map/ppermute | solution.py:520
  60.2 1.0 shard_map.41
  61.2 5.4 %all-to-all-start = ((f32[8,176,128]{2,1,0:T(8,128)}), f32[8,176,128]{2,1,0:T(8,128)S(1)}, u32[]{:S(2)}, u32[]{:S(2)}) async-start(f32[8,176,128]{2,1,0:T(8,128)} %shard_map.41), calls=%async_computation | async-start | bytes 1441792 | tf_op jit(solution)/shard_map/all_to_all | solution.py:529
  66.6 1.3 %dynamic_slice.3 = s32[1]{0:T(128)} dynamic-slice(s32[512]{0:T(512)} %constant.70.clone, s32[]{:T(128)S(6)} %select_n.34), dynamic_slice_sizes={1} | dynamic-slice | bytes 12 | tf_op jit(solution)/shard_map/dynamic_slice | solution.py:434
  69.2 0.1 pad_add_fusion.flags
  69.3 7.4 %all-to-all-done.parts = f32[8,176,128]{2,1,0:T(8,128)S(1)} async-done(((f32[8,176,128]{2,1,0:T(8,128)}), f32[8,176,128]{2,1,0:T(8,128)S(1)}, u32[]{:S(2)}, u32[]{:S(2)}) %all-to-all-start) | async-done | bytes 720928 | tf_op jit(solution)/shard_map/all_to_all | solution.py:529
  76.6 1.6 %shard_map.42 = (f32[24,128]{1,0:T(8,128)S(1)}, f32[24,128]{1,0:T(8,128)S(1)}) custom-call(s32[2]{0:T(128)S(1)} %pad_add_fusion.flags, f32[8,176,128]{2,1,0:T(8,128)S(1)} %all-to-all-done.parts), custom_call_target="tpu_custom_call" | custom-call | tf_op jit(solution)/shard_map/pallas_call | solution.py:532
  78.2 9.5 %collective-permute-start.8 = (f32[24,128]{1,0:T(8,128)S(1)}, f32[24,128]{1,0:T(8,128)S(1)}, u32[]{:S(2)}, u32[]{:S(2)}) collective-permute-start(f32[24,128]{1,0:T(8,128)S(1)} %get-tuple-element.35), channel_id=1, source_target_pairs={{0,464},{1,64},{2,10},{3,322},{4,38},{5,209},{6,70},{7,210},{8,294... | collective-permute-start | bytes 36872 | tf_op jit(solution)/shard_map/ppermute | solution.py:540
  87.7 1.9 %collective-permute-start.9 = (f32[24,128]{1,0:T(8,128)S(1)}, f32[24,128]{1,0:T(8,128)S(1)}, u32[]{:S(2)}, u32[]{:S(2)}) collective-permute-start(f32[24,128]{1,0:T(8,128)S(1)} %get-tuple-element.36), channel_id=1, source_target_pairs={{0,14},{1,2},{2,320},{3,74},{4,193},{5,38},{6,194},{7,70},{8,217},... | collective-permute-start | bytes 36872 | tf_op jit(solution)/shard_map/ppermute | solution.py:539
  90.3 0.0 collective-permute-done.8
  90.3 8.4 %collective-permute-done.9 = f32[24,128]{1,0:T(8,128)S(1)} collective-permute-done((f32[24,128]{1,0:T(8,128)S(1)}, f32[24,128]{1,0:T(8,128)S(1)}, u32[]{:S(2)}, u32[]{:S(2)}) %collective-permute-start.9) | collective-permute-done | bytes 12320 | tf_op jit(solution)/shard_map/ppermute | solution.py:539
  98.7 0.1 fusion
  98.8 0.7 maximum_maximum_fusion
  (1 shorter events, 0.0 us)
Async XLA Ops:
  0.0 23.9 %collective-permute-start.2 = (f32[144,512]{1,0:T(8,128)}, f32[144,512]{1,0:T(8,128)S(1)}, u32[]{:S(2)}, u32[]{:S(2)}) collective-permute-start(f32[144,512]{1,0:T(8,128)} %bitcast.10), channel_id=1, source_target_pairs={{32,0},{48,16},{64,32},{80,48},{96,64},{112,80},{128,96},{144,112}... | collective-permute-start | bytes 884744 | tf_op jit(solution)/shard_map/ppermute | solution.py:442
  11.6 25.9 %collective-permute-start = (f32[144,512]{1,0:T(8,128)}, f32[144,512]{1,0:T(8,128)S(1)}, u32[]{:S(2)}, u32[]{:S(2)}) collective-permute-start(f32[144,512]{1,0:T(8,128)} %bitcast.11), channel_id=1, source_target_pairs={{208,0},{224,16},{240,32},{0,48},{16,64},{32,80},{48,96},{64,112},... | collective-permute-start | bytes 884744 | tf_op jit(solution)/shard_map/ppermute | solution.py:442
  23.9 18.0 %collective-permute-start.5 = (f32[144,512]{1,0:T(8,128)S(1)}, f32[144,512]{1,0:T(8,128)S(1)}, u32[]{:S(2)}, u32[]{:S(2)}) collective-permute-start(f32[144,512]{1,0:T(8,128)S(1)} %collective-permute-done.2.plus2), channel_id=1, source_target_pairs={{32,0},{48,16},{64,32},{80,48},{96,64},{112,80},{128,96},{144,112}... | collective-permute-start | bytes 884744 | tf_op jit(solution)/shard_map/ppermute | solution.py:442
  30.0 14.8 %collective-permute-start.3 = (f32[144,512]{1,0:T(8,128)S(1)}, f32[144,512]{1,0:T(8,128)S(1)}, u32[]{:S(2)}, u32[]{:S(2)}) collective-permute-start(f32[144,512]{1,0:T(8,128)S(1)} %collective-permute-done.2.plus2), channel_id=1, source_target_pairs={{256,0},{272,16},{288,32},{304,48},{320,64},{336,80},{352,96},{368... | collective-permute-start | bytes 884744 | tf_op jit(solution)/shard_map/ppermute | solution.py:445
  37.5 10.0 %collective-permute-start.4 = (f32[144,512]{1,0:T(8,128)S(1)}, f32[144,512]{1,0:T(8,128)S(1)}, u32[]{:S(2)}, u32[]{:S(2)}) collective-permute-start(f32[144,512]{1,0:T(8,128)S(1)} %collective-permute-done.minus3), channel_id=1, source_target_pairs={{256,0},{272,16},{288,32},{304,48},{320,64},{336,80},{352,96},{368... | collective-permute-start | bytes 884744 | tf_op jit(solution)/shard_map/ppermute | solution.py:445
  40.0 10.9 %collective-permute-start.1 = (f32[144,512]{1,0:T(8,128)S(1)}, f32[144,512]{1,0:T(8,128)S(1)}, u32[]{:S(2)}, u32[]{:S(2)}) collective-permute-start(f32[144,512]{1,0:T(8,128)S(1)} %collective-permute-done.minus3), channel_id=1, source_target_pairs={{240,0},{0,16},{16,32},{32,48},{48,64},{64,80},{80,96},{96,112},{1... | collective-permute-start | bytes 884744 | tf_op jit(solution)/shard_map/ppermute | solution.py:442
  41.9 11.8 %collective-permute-start.6 = (f32[144,512]{1,0:T(8,128)S(1)}, f32[144,512]{1,0:T(8,128)S(1)}, u32[]{:S(2)}, u32[]{:S(2)}) collective-permute-start(f32[144,512]{1,0:T(8,128)S(1)} %collective-permute-done.5.plus4), channel_id=1, source_target_pairs={{256,0},{272,16},{288,32},{304,48},{320,64},{336,80},{352,96},{368... | collective-permute-start | bytes 884744 | tf_op jit(solution)/shard_map/ppermute | solution.py:445
  44.8 0.7 copy-start
  45.5 1.0 copy-start.1
  55.2 5.0 %collective-permute-start.7 = (f32[8,176,128]{2,1,0:T(8,128)S(1)}, f32[8,176,128]{2,1,0:T(8,128)S(1)}, u32[]{:S(2)}, u32[]{:S(2)}) collective-permute-start(f32[8,176,128]{2,1,0:T(8,128)S(1)} %get-tuple-element.34), channel_id=1, source_target_pairs={{0,1},{1,0},{2,3},{3,2},{4,5},{5,4},{6,7},{7,6},{8,9},{9,8},{10,11... | collective-permute-start | bytes 2162696 | tf_op jit(solution)/shard_map/ppermute | solution.py:520
  61.2 15.4 %all-to-all-start = ((f32[8,176,128]{2,1,0:T(8,128)}), f32[8,176,128]{2,1,0:T(8,128)S(1)}, u32[]{:S(2)}, u32[]{:S(2)}) async-start(f32[8,176,128]{2,1,0:T(8,128)} %shard_map.41), calls=%async_computation | async-start | bytes 1441792 | tf_op jit(solution)/shard_map/all_to_all | solution.py:529
  78.2 12.1 %collective-permute-start.8 = (f32[24,128]{1,0:T(8,128)S(1)}, f32[24,128]{1,0:T(8,128)S(1)}, u32[]{:S(2)}, u32[]{:S(2)}) collective-permute-start(f32[24,128]{1,0:T(8,128)S(1)} %get-tuple-element.35), channel_id=1, source_target_pairs={{0,464},{1,64},{2,10},{3,322},{4,38},{5,209},{6,70},{7,210},{8,294... | collective-permute-start | bytes 36872 | tf_op jit(solution)/shard_map/ppermute | solution.py:540
  87.7 11.0 %collective-permute-start.9 = (f32[24,128]{1,0:T(8,128)S(1)}, f32[24,128]{1,0:T(8,128)S(1)}, u32[]{:S(2)}, u32[]{:S(2)}) collective-permute-start(f32[24,128]{1,0:T(8,128)S(1)} %get-tuple-element.36), channel_id=1, source_target_pairs={{0,14},{1,2},{2,320},{3,74},{4,193},{5,38},{6,194},{7,70},{8,217},... | collective-permute-start | bytes 36872 | tf_op jit(solution)/shard_map/ppermute | solution.py:539
